TPU v7x, 256 devices: a whole 4x4x8 slice. The times are simulated.
256 devices in a mesh: pi: 8 (over z), pj: 4 (over x_lo, core), vert: 8 (over x_hi, y).
Axes of the slice: x: 4 (x_hi: 2, x_lo: 2; x = x_hi * 2 + x_lo), y: 4, z: 8, core: 2. Of those that a mesh axis runs over, the one named last changes fastest.
Arguments:
- amplitudes: bfloat16 [64, 64, 8, 4096], P('pi', 'pj', None, 'vert'), may hold values from -6 to 6
- ladder_ints: bfloat16 [2, 4096, 4096], P(None, 'vert'), may hold values from -0.09375 to 0.09375
- ladder_tiles: int32 [2, 2], replicated, may hold values from 0 to 7
- cycle_ints: bfloat16 [64, 5, 2, 4096], P('pj', None, None, 'vert'), may hold values from -0.3125 to 0.3125
- cycle_tiles: int32 [2, 2], replicated, may hold values from 0 to 7
- partner: int32 [8], replicated, may hold values from 0 to 7, as said below
Outputs:
- residual: float32 [64, 64, 8, 4096], P('pi', 'pj', None, 'vert')
Inputs may be any that keep to these rules, and one draw needn't show every extreme that they name: `ladder_tiles`: column 0 is a residual tile, column 1 an amplitude tile, both positions in the tile list. `cycle_tiles`: column 0 is a residual tile, column 1 an amplitude tile, both positions in the tile list. partner[partner[n]] = n and partner[n] != n.
All inputs are finite; a program needn't handle non-finite values.
Results may differ from a plain program's by a relative error of at most 0.0049.
Values may be sent and summed in bfloat16 or wider, within the bound.
No kernel may reach another device: no remote copies, remote signals or barrier semaphores. Data moves between devices by JAX's collectives and lax.ppermute only.
A program may use at most 128 MiB of HBM per device.

v0:
```python
import jax
import jax.numpy as jnp
from jax import lax
from jax.sharding import PartitionSpec as P

TILE = 64
LADDER = 2
CYCLE = 2
REACH = 2
BAND = 5


def with_halo(x, sides, width):
    for axis, dim in sides:
        size, length = (lax.axis_size(axis), x.shape[dim])
        up = [(i, (i + 1) % size) for i in range(size - 1)]
        down = [(j, i) for i, j in up]
        last = lax.slice_in_dim(x, length - width, length, axis=dim)
        first = lax.slice_in_dim(x, 0, width, axis=dim)
        before = lax.ppermute(last, axis, up)
        after = lax.ppermute(first, axis, down)
        x = jnp.concatenate([before, x, after], axis=dim)
    return x


def select_tile(block, index):
    return lax.dynamic_index_in_dim(block, index, 2, keepdims=False)


def body(amplitudes, ladder_ints, ladder_tiles, cycle_ints, cycle_tiles, partner):
    occ_rows, occ_cols, tile_count, local_len = amplitudes.shape
    pair_count = occ_rows * occ_cols
    virt_rows = local_len // TILE
    tile_ids = jnp.arange(tile_count, dtype=jnp.int32)

    def contract(piece, which):
        width = piece.shape[-1]
        columns = ladder_ints[which]
        return lax.dot_general(
            piece.reshape(pair_count, width),
            columns,
            (((1,), (1,)), ((), ())),
            preferred_element_type=jnp.float32,
        )

    def add_all(piece):
        return tuple(
            (contract(select_tile(piece, ladder_tiles[which, 1]), which) for which in range(LADDER))
        )

    ladder = list(add_all(lax.all_gather(amplitudes, "vert", axis=3, tiled=True)))
    total = jnp.zeros((occ_rows, occ_cols, tile_count, local_len), jnp.float32)
    for which in range(LADDER):
        selector = (tile_ids == ladder_tiles[which, 0]).astype(jnp.float32)
        total = total + selector[None, None, :, None] * ladder[which].reshape(
            occ_rows, occ_cols, 1, local_len
        )
    rimmed = with_halo(amplitudes, (("pj", 1),), REACH)
    whole_cycle = lax.all_gather(cycle_ints, "vert", axis=3, tiled=True)
    for which in range(CYCLE):
        source = select_tile(rimmed, cycle_tiles[which, 1]).reshape(
            occ_rows, occ_cols + 2 * REACH, virt_rows, TILE
        )
        stacked = jnp.stack(
            [source[:, offset : offset + occ_cols] for offset in range(BAND)], axis=3
        )
        stacked = stacked.reshape(occ_rows, occ_cols, virt_rows, BAND * TILE)
        kernel = whole_cycle[:, :, which].reshape(occ_cols, BAND * TILE, TILE)
        cycle = jnp.einsum("ijax,jxb->ijab", stacked, kernel, preferred_element_type=jnp.float32)
        selector = (tile_ids == cycle_tiles[which, 0]).astype(jnp.float32)
        total = total + selector[None, None, :, None] * cycle.reshape(
            occ_rows, occ_cols, 1, local_len
        )
    rounded = total.astype(jnp.bfloat16)
    chooser = (partner[:, None] == tile_ids[None, :]).astype(jnp.bfloat16)
    outgoing = jnp.einsum(
        "ijkr,nk->ijnr", rounded, chooser, preferred_element_type=jnp.float32
    ).astype(jnp.bfloat16)
    gathered = lax.all_gather(outgoing, "pj", axis=1, tiled=True)
    blocks = gathered.reshape(occ_rows, gathered.shape[1], tile_count, virt_rows, TILE)
    moved = lax.all_to_all(blocks, "pi", split_axis=1, concat_axis=0, tiled=True)
    moved = lax.all_to_all(moved, "vert", split_axis=4, concat_axis=3, tiled=True)
    mine = lax.dynamic_slice_in_dim(moved, lax.axis_index("pj") * occ_cols, occ_cols, 0)
    mirrored = jnp.transpose(mine, (1, 0, 2, 4, 3)).reshape(
        occ_rows, occ_cols, tile_count, local_len
    )
    return rounded.astype(jnp.float32) + mirrored.astype(jnp.float32)


def solution(mesh):
    placed = (
        P("pi", "pj", None, "vert"),
        P(None, "vert", None),
        P(),
        P("pj", None, None, "vert"),
        P(),
        P(),
    )
    return jax.shard_map(
        body, mesh=mesh, in_specs=placed, out_specs=P("pi", "pj", None, "vert"), check_vma=False
    )
```

profile of v0, /device:TPU:3, one launch (start us, length us, event | category | flops | bytes accessed | tf_op | source)
XLA Modules:
  0.0 540.5 jit_solution(4081433522271616460)
XLA Ops:
  7.3 2.5 copy.75
  9.9 2.6 collective-permute-start.1
  26.5 1.9 copy.105
  28.4 2.4 reshape.83
  31.1 1.9 copy.101
  33.0 1.9 reshape.82
  34.9 29.2 %all-gather.6.cloned.1.call-done = bf16[16,5,2,4096]{3,2,1,0:T(2,128)(2,1)} async-done(((bf16[16,5,2,512]{3,2,1,0:T(2,128)(2,1)}), bf16[16,5,2,4096]{3,2,1,0:T(2,128)(2,1)}) %all-gather.6.cloned.1.call-update) | async-done | bytes 1310736 | tf_op jit(solution)/shard_map/all_gather | solution.py:59
  64.1 7.7 %slice_reduce_fusion.1 = (bf16[16,5,4096]{2,1,0:T(8,128)(2,1)S(1)}, bf16[16,5,4096]{2,1,0:T(8,128)(2,1)S(1)}) fusion(bf16[16,5,2,4096]{3,2,1,0:T(2,128)(2,1)} %all-gather.6.cloned.1.call-done), kind=kLoop, calls=%fused_computation.12 | loop fusion | bytes 2621440 | tf_op jit(solution)/shard_map/slice | solution.py:68
  71.8 1.5 reshape_squeeze.6
  73.3 2.4 fusion.11
  77.1 1.7 reshape_squeeze.7
  79.5 103.4 %all-gather.4.cloned.1.call-done = bf16[8,16,8,4096]{3,1,0,2:T(8,128)(2,1)} async-done(((bf16[8,16,8,512]{3,1,0,2:T(8,128)(2,1)}), bf16[8,16,8,4096]{3,1,0,2:T(8,128)(2,1)}) %all-gather.4.cloned.1.call-update) | async-done | bytes 8388624 | tf_op jit(solution)/shard_map/all_gather | solution.py:51
  182.9 4.0 fusion
  186.9 4.0 fusion.2
  191.0 1.7 fusion.6
  192.7 47.8 %all-gather.8.cloned.1.call-done = bf16[8,64,8,512]{3,2,1,0:T(8,128)(2,1)} async-done(((bf16[8,16,8,512]{3,2,1,0:T(8,128)(2,1)}), bf16[8,64,8,512]{3,2,1,0:T(8,128)(2,1)}) %all-gather.8.cloned.1.call-update) | async-done | bytes 4194320 | tf_op jit(solution)/shard_map/all_gather | solution.py:79
  240.5 11.2 %reshape.75 = bf16[8,64,8,8,64]{4,3,2,1,0:T(8,128)(2,1)} reshape(bf16[8,64,8,512]{3,2,1,0:T(8,128)(2,1)} %all-gather.8.cloned.1.call-done) | data formatting | bytes 8388608 | tf_op jit(solution)/shard_map/reshape | solution.py:80
  251.7 9.6 %copy.113 = bf16[8,64,8,8,64]{4,3,2,0,1:T(8,128)(2,1)} copy(bf16[8,64,8,8,64]{4,3,2,1,0:T(8,128)(2,1)} %reshape.75) | data formatting | bytes 8388608 | tf_op jit(solution)/shard_map/reshape | solution.py:80
  261.3 10.5 %reshape.86 = bf16[8,2,131072]{2,1,0:T(2,128)(2,1)} reshape(bf16[64,8,8,8,64]{4,3,2,1,0:T(8,128)(2,1)} %bitcast.130) | data formatting | bytes 8388608
  271.8 103.7 %all_to_all.36 = bf16[8,2,131072]{2,1,0:T(2,128)(2,1)} all-to-all(bf16[8,2,131072]{2,1,0:T(2,128)(2,1)} %reshape.86), channel_id=1, replica_groups=mesh['pi'=8,'pj'=4,'vert'=8] {'pi'}, dimensions={0} | all-to-all | bytes 8388608 | tf_op jit(solution)/shard_map/all_to_all | solution.py:81
  375.5 10.4 %reshape.87 = bf16[64,8,8,8,64]{4,3,2,1,0:T(8,128)(2,1)} reshape(bf16[8,2,131072]{2,1,0:T(2,128)(2,1)} %all_to_all.36) | data formatting | bytes 8388608
  385.9 9.6 %copy.92 = bf16[8,8,8,8,8,64]{5,4,3,2,1,0:T(8,128)(2,1)} copy(bf16[8,8,8,8,8,64]{5,4,3,1,2,0:T(8,128)(2,1)} %bitcast.131) | data formatting | bytes 8388608 | tf_op jit(solution)/shard_map/all_to_all | solution.py:81
  395.5 16.5 %copy.93 = bf16[64,8,8,8,64]{0,3,2,1,4:T(8,128)(2,1)} copy(bf16[64,8,8,8,64]{4,3,2,1,0:T(8,128)(2,1)} %bitcast.132) | data formatting | bytes 8388608 | tf_op jit(solution)/shard_map/all_to_all | solution.py:81
  412.0 10.5 %reshape.88 = bf16[8,2,131072]{2,1,0:T(2,128)(2,1)} reshape(bf16[64,8,8,8,64]{4,3,2,1,0:T(8,128)(2,1)} %bitcast.133) | data formatting | bytes 8388608
  422.5 5.8 %all-to-all-start.1 = ((bf16[8,2,131072]{2,1,0:T(2,128)(2,1)}), bf16[8,2,131072]{2,1,0:T(2,128)(2,1)}, u32[]{:S(2)}, u32[]{:S(2)}) async-start(bf16[8,2,131072]{2,1,0:T(2,128)(2,1)} %reshape.88), calls=%async_computation.1 | async-start | bytes 8388608 | tf_op jit(solution)/shard_map/all_to_all | solution.py:82
  428.3 48.8 %all-to-all-done.1 = bf16[8,2,131072]{2,1,0:T(2,128)(2,1)} async-done(((bf16[8,2,131072]{2,1,0:T(2,128)(2,1)}), bf16[8,2,131072]{2,1,0:T(2,128)(2,1)}, u32[]{:S(2)}, u32[]{:S(2)}) %all-to-all-start.1) | async-done | bytes 4194336 | tf_op jit(solution)/shard_map/all_to_all | solution.py:82
  477.1 10.6 %reshape.89 = bf16[64,8,8,8,64]{4,3,2,1,0:T(8,128)(2,1)} reshape(bf16[8,2,131072]{2,1,0:T(2,128)(2,1)} %all-to-all-done.1) | data formatting | bytes 8388608
  487.6 16.4 %copy.95 = bf16[64,8,8,8,8,8]{0,5,4,3,2,1:T(8,128)(2,1)} copy(bf16[64,8,8,8,8,8]{0,4,2,1,5,3:T(8,128)(2,1)} %bitcast.134) | data formatting | bytes 8388608 | tf_op jit(solution)/shard_map/all_to_all | solution.py:82
  504.1 12.0 %convert_bitcast_fusion = f32[8,16,8,8,64]{1,3,4,2,0:T(8,128)} fusion(bf16[64,8,8,64,8]{0,4,3,2,1:T(8,128)(2,1)} %bitcast.129, s32[]{:T(128)S(6)} %select_n.21), kind=kLoop, calls=%fused_computation | loop fusion | flops 524288 | bytes 3145732 | tf_op jit(solution)/shard_map/convert_element_type | solution.py:87
  516.1 11.9 %copy.96 = f32[8,16,8,8,64]{4,3,2,1,0:T(8,128)} copy(f32[8,16,8,8,64]{1,3,4,2,0:T(8,128)} %convert_bitcast_fusion) | data formatting | bytes 4194304 | tf_op jit(solution)/shard_map/convert_element_type | solution.py:87
  528.1 3.4 reshape.76
  531.5 2.2 convert_add_fusion
  (47 shorter events, 9.7 us)
Async XLA Ops:
  6.5 3.4 copy-start
  6.5 7.3 %copy-start.2 = (s32[2,2]{1,0:T(2,128)S(1)}, s32[2,2]{1,0:T(2,128)}, u32[]{:S(2)}) copy-start(s32[2,2]{1,0:T(2,128)} %param.8) | copy-start | bytes 52
  6.5 7.9 %copy-start.3 = (s32[2,2]{1,0:T(2,128)S(1)}, s32[2,2]{1,0:T(2,128)}, u32[]{:S(2)}) copy-start(s32[2,2]{1,0:T(2,128)} %param.10) | copy-start | bytes 52
  6.5 57.5 %all-gather.6.cloned.1.call-start = ((), (), s32[]{:S(2)}) async-start(), calls=%async_computation.3 | async-start | bytes 1474560 | tf_op jit(solution)/shard_map/all_gather | solution.py:59
  7.3 175.6 %all-gather.4.cloned.1.call-start = ((), (), s32[]{:S(2)}) async-start(), calls=%async_computation.2 | async-start | bytes 9437184 | tf_op jit(solution)/shard_map/all_gather | solution.py:51
  9.8 230.6 %all-gather.8.cloned.1.call-start = ((), (), s32[]{:S(2)}) async-start(), calls=%async_computation.4 | async-start | bytes 5242880 | tf_op jit(solution)/shard_map/all_gather | solution.py:79
  9.9 15.1 %collective-permute-start.1 = (bf16[8,2,8,512]{3,2,1,0:T(8,128)(2,1)S(1)}, bf16[8,2,8,512]{3,2,1,0:T(8,128)(2,1)S(1)}, u32[]{:S(2)}, u32[]{:S(2)}) collective-permute-start(bf16[8,2,8,512]{3,2,1,0:T(8,128)(2,1)S(1)} %get-tuple-element.9), channel_id=1, source_target_pairs={{8,0},{16,8},{24,16},{9,1},{17,9},{25,17},{10,2},{18,10},{26,18},{... | collective-permute-start | bytes 393224 | tf_op jit(solution)/shard_map/ppermute | solution.py:21
  12.5 12.4 %collective-permute-start = (bf16[8,2,8,512]{3,2,1,0:T(8,128)(2,1)S(1)}, bf16[8,2,8,512]{3,2,1,0:T(8,128)(2,1)S(1)}, u32[]{:S(2)}, u32[]{:S(2)}) collective-permute-start(bf16[8,2,8,512]{3,2,1,0:T(8,128)(2,1)S(1)} %get-tuple-element.10), channel_id=1, source_target_pairs={{0,8},{8,16},{16,24},{1,9},{9,17},{17,25},{2,10},{10,18},{18,26},{... | collective-permute-start | bytes 393224 | tf_op jit(solution)/shard_map/ppermute | solution.py:20
  75.7 3.1 copy-start.1
  186.9 4.1 copy-start.4
  422.5 54.6 %all-to-all-start.1 = ((bf16[8,2,131072]{2,1,0:T(2,128)(2,1)}), bf16[8,2,131072]{2,1,0:T(2,128)(2,1)}, u32[]{:S(2)}, u32[]{:S(2)}) async-start(bf16[8,2,131072]{2,1,0:T(2,128)(2,1)} %reshape.88), calls=%async_computation.1 | async-start | bytes 8388608 | tf_op jit(solution)/shard_map/all_to_all | solution.py:82
Sparse Core Ops, SparseCore 0:
  9.8 54.1 all-gather.5
  66.5 116.2 all-gather.3
  192.8 47.6 all-gather.7
where the time goes:
time: 549 us; the launch traced here: 541 us
  waiting for transfers between devices  230 us (42%)
  local copies, waits for them, and re-layouts  147 us (27%)
  blocking collectives  104 us (19%)
  between operations  21 us (4%)
  other arithmetic  16.7 us (3%)
  matrix products  12.5 us (2%)
  starting transfers between devices  9.78 us (2%)
    all_to_all x1, blocking collectives, body(): lax.all_to_all(blocks, 'pi', split_axis=1, concat_axis=0, tiled=True)  104 us
    all_gather x1, waiting for transfers between devices, body(): lax.all_gather(amplitudes, 'vert', axis=3, tiled=True)  103 us
    all_to_all x1, waiting for transfers between devices, body(): lax.all_to_all(moved, 'vert', split_axis=4, concat_axis=3, tiled=True)  48.8 us
    all_gather x1, waiting for transfers between devices, body(): gathered = lax.all_gather(outgoing, 'pj', axis=1, tiled=True)  47.8 us
    unnamed x25, local copies, waits for them, and re-layouts  44.8 us
    all_gather x1, waiting for transfers between devices, body(): whole_cycle = lax.all_gather(cycle_ints, 'vert', axis=3, tiled=True)  29.2 us
    all_to_all x2, local copies, waits for them, and re-layouts, body(): lax.all_to_all(blocks, 'pi', split_axis=1, concat_axis=0, tiled=True)  26.1 us
    reshape x2, local copies, waits for them, and re-layouts, body(): gathered.reshape(occ_rows, gathered.shape[1], tile_count, virt_rows, TILE)  20.8 us
  transfers between devices with their start and end apart: 6, of which 4 were waited for; matrix products, arithmetic and copies ran while one was open for 6% of the time, Pallas kernels for 0%

commit v1 on v0

v1 whole, which is shorter than its diff:
```python
import jax
import jax.numpy as jnp
import numpy as np
from jax import lax
from jax.experimental import pallas as pl
from jax.experimental.pallas import tpu as pltpu
from jax.sharding import PartitionSpec as P

TILE = 64
REACH = 2
BAND = 5
ROWS = 8
LANES = 512
PAIRS = 128
BF = jnp.bfloat16
F32 = jnp.float32
MIB = 1 << 20


def vert_moves(move):
    return [(v, move(v // 4, v % 4)) for v in range(8)]


FLIP = vert_moves(lambda h, y: (1 - h) * 4 + y)
UP = vert_moves(lambda h, y: h * 4 + (y + 1) % 4)
DOWN = vert_moves(lambda h, y: h * 4 + (y + 3) % 4)


def pair_moves(k):
    return [
        (p * 4 + q, (2 * q + ((p % 2) ^ k)) * 4 + p // 2) for p in range(8) for q in range(4)
    ]


def send_order():
    row = np.arange(1024)
    slot, a, v, b = row // 512, (row // 64) % 8, (row // 8) % 8, row % 8
    return v * 128 + slot * 64 + b * 8 + a


def place_order():
    row = np.arange(1024)
    v, slot, b, a = row // 128, (row // 64) % 2, (row // 8) % 8, row % 8
    return slot * 512 + b * 64 + v * 8 + a


def permutation(order):
    columns = lax.broadcasted_iota(jnp.int32, (1024, 1024), 1)
    return (jnp.asarray(order, jnp.int32)[:, None] == columns).astype(BF)


def pack_outgoing(total, swap, parity, first_ref, second_ref):
    sent = jnp.dot(total.astype(BF), swap, preferred_element_type=F32).astype(BF)
    low, high = sent[:64], sent[64:]
    first = jnp.where(parity == 0, low, high)
    second = jnp.where(parity == 0, high, low)
    for v in range(8):
        first_ref[v] = first[:, v * 128 : (v + 1) * 128]
        second_ref[v] = second[:, v * 128 : (v + 1) * 128]


def ladder_kernel(scalars, ints, swap, *refs):
    pieces, (total_ref, first_ref, second_ref) = refs[:8], refs[8:]
    sums = []
    for which in range(2):
        acc = None
        for d in range(8):
            start = pl.multiple_of(scalars[1 + d] * LANES, LANES)
            part = lax.dot_general(
                pieces[d][which * PAIRS : (which + 1) * PAIRS, :],
                ints[which, :, pl.ds(start, LANES)],
                (((1,), (1,)), ((), ())),
                preferred_element_type=F32,
            )
            acc = part if acc is None else acc + part
        sums.append(acc)
    total = jnp.concatenate(sums, axis=1)
    total_ref[...] = total
    pack_outgoing(total, swap[...], scalars[0], first_ref, second_ref)


def cycle_kernel(scalars, before, inner, after, swap, *refs):
    pieces, (total_ref, first_ref, second_ref, ints) = refs[:8], refs[8:]
    for d in range(8):
        ints[scalars[1 + d]] = pieces[d][256:, :].astype(F32)

    def rows_of(j):
        if j < REACH:
            return before[j]
        if j < REACH + 16:
            return inner[j - REACH]
        return after[j - REACH - 16]

    laid = []
    for j in range(16 + 2 * REACH):
        block = rows_of(j)
        laid.append(
            jnp.concatenate([block[:, a * TILE : (a + 1) * TILE] for a in range(ROWS)], axis=0)
        )
    lane = lax.broadcasted_iota(jnp.int32, (8, 128), 1)
    low = lane < TILE
    for j in range(16):
        left = jnp.concatenate([laid[j + o] for o in range(BAND)], axis=1)
        right = jnp.concatenate(
            [
                ints[v, (j // 4) * 40 + o * 8 : (j // 4) * 40 + o * 8 + 8, (j % 4) * 128 : (j % 4) * 128 + 128]
                for o in range(BAND)
                for v in range(8)
            ],
            axis=0,
        ).astype(BF)
        done = jnp.dot(left, right, preferred_element_type=F32)
        for r in range(2):
            for t in range(4):
                even = done[t * 32 + r * 8 : t * 32 + r * 8 + 8]
                odd = done[t * 32 + 16 + r * 8 : t * 32 + 16 + r * 8 + 8]
                if r == 0:
                    odd = pltpu.roll(odd, TILE, 1)
                else:
                    even = pltpu.roll(even, TILE, 1)
                total_ref[j * 8 : j * 8 + 8, r * LANES + t * 128 : r * LANES + (t + 1) * 128] = (
                    jnp.where(low, even, odd)
                )
    pack_outgoing(total_ref[...], swap[...], scalars[0], first_ref, second_ref)


def finish_kernel(scalars, ladder, cycle, arrived, place, out_ref, mirrored):
    parity = scalars[0]
    wide = jnp.concatenate([arrived[v] for v in range(8)], axis=1)
    moved = jnp.dot(wide, place[...], preferred_element_type=F32)
    for k in range(2):
        half = parity ^ k
        mirrored[0, half] = moved[k * 64 : k * 64 + 64]
        mirrored[1, half] = moved[128 + k * 64 : 128 + k * 64 + 64]
    tile = lax.broadcasted_iota(jnp.int32, (8, LANES), 0)
    own = [(tile == scalars[9 + s]).astype(F32) for s in range(4)]
    other = [(tile == scalars[13 + s]).astype(F32) for s in range(4)]

    def one(i):
        for j in range(16):
            row = j * 8 + i
            mrow = i * 8 + j % 8
            acc = None
            for s in range(4):
                source = ladder if s < 2 else cycle
                lanes = slice((s % 2) * LANES, (s % 2 + 1) * LANES)
                term = own[s] * source[pl.ds(row, 1), lanes]
                acc = term if acc is None else acc + term
                acc = acc + other[s] * mirrored[s // 2, j // 8, pl.ds(mrow, 1), lanes]
            out_ref[i, j] = acc

    pl.loop(0, 8)(one)


def call(kernel, outs, scratch=(), limit=24, flops=0, moved=0):
    def run(scalars, *args):
        return pl.pallas_call(
            kernel,
            out_shape=outs,
            in_specs=[pl.BlockSpec(memory_space=pltpu.SMEM)]
            + [pl.BlockSpec(memory_space=pltpu.VMEM)] * len(args),
            out_specs=jax.tree.map(lambda _: pl.BlockSpec(memory_space=pltpu.VMEM), outs),
            scratch_shapes=list(scratch),
            compiler_params=pltpu.CompilerParams(vmem_limit_bytes=limit * MIB),
            cost_estimate=pl.CostEstimate(flops=flops, bytes_accessed=moved, transcendentals=0),
        )(scalars, *args)

    return run


def select(amplitudes, index):
    tile = lax.dynamic_index_in_dim(amplitudes, index, 2, keepdims=False)
    return jnp.transpose(tile, (1, 0, 2))


def body(amplitudes, ladder_ints, ladder_tiles, cycle_ints, cycle_tiles, partner):
    pi, vert = lax.axis_index("pi"), lax.axis_index("vert")
    h, y = vert // 4, vert % 4
    sources = [
        (h, y), (1 - h, y), (h, y + 3), (h, y + 1),
        (1 - h, y + 3), (1 - h, y + 1), (h, y + 2), (1 - h, y + 2),
    ]
    dests = jnp.concatenate([ladder_tiles[:, 0], cycle_tiles[:, 0]])
    scalars = jnp.concatenate(
        [
            jnp.stack([pi % 2] + [a * 4 + b % 4 for a, b in sources]).astype(jnp.int32),
            dests,
            partner[dests],
        ]
    )
    cycle_in = jnp.stack([select(amplitudes, cycle_tiles[r, 1]) for r in range(2)], axis=1)
    cycle_in = cycle_in.reshape(16, 16, LANES)
    up = [(q, q + 1) for q in range(3)]
    down = [(q + 1, q) for q in range(3)]
    before = lax.ppermute(cycle_in[-REACH:], "pj", up)
    after = lax.ppermute(cycle_in[:REACH], "pj", down)

    ladder_in = jnp.stack([select(amplitudes, ladder_tiles[w, 1]) for w in range(2)])
    ints = cycle_ints.reshape(4, 4, BAND, 2, ROWS, TILE)
    ints = jnp.transpose(ints, (0, 2, 4, 1, 3, 5)).reshape(160, LANES)
    own = jnp.concatenate([ladder_in.reshape(256, LANES), ints])
    flip = lax.ppermute(own, "vert", FLIP)
    own_up = lax.ppermute(own, "vert", UP)
    own_down = lax.ppermute(own, "vert", DOWN)
    flip_up = lax.ppermute(flip, "vert", UP)
    flip_down = lax.ppermute(flip, "vert", DOWN)
    far = lax.ppermute(own_up, "vert", UP)
    flip_far = lax.ppermute(flip_down, "vert", DOWN)
    pieces = [own, flip, own_up, own_down, flip_up, flip_down, far, flip_far]

    swap = permutation(send_order())
    packed = [jax.ShapeDtypeStruct((8, 64, 128), BF)] * 2
    outs = [jax.ShapeDtypeStruct((PAIRS, 1024), F32)] + packed
    ladder, ladder_0, ladder_1 = call(ladder_kernel, outs)(scalars, ladder_ints, swap, *pieces)
    cycle, cycle_0, cycle_1 = call(
        cycle_kernel, outs, [pltpu.VMEM((8, 160, LANES), F32)]
    )(scalars, before, cycle_in, after, swap, *pieces)

    sent = [
        lax.ppermute(block, ("pi", "pj"), pair_moves(k))
        for k, block in ((0, ladder_0), (1, ladder_1), (0, cycle_0), (1, cycle_1))
    ]
    arrived = lax.all_to_all(jnp.concatenate(sent, axis=1), "vert", 0, 0)
    return call(
        finish_kernel,
        jax.ShapeDtypeStruct((8, 16, 8, LANES), F32),
        [pltpu.VMEM((2, 2, 64, 1024), F32)],
    )(scalars, ladder, cycle, arrived, permutation(place_order()))


def solution(mesh):
    placed = (
        P("pi", "pj", None, "vert"),
        P(None, "vert", None),
        P(),
        P("pj", None, None, "vert"),
        P(),
        P(),
    )
    return jax.shard_map(
        body, mesh=mesh, in_specs=placed, out_specs=P("pi", "pj", None, "vert"), check_vma=False
    )
```

time: 549 us -> 119 us (0.22); the launches traced: 541 us -> 118 us
  waiting for transfers between devices: 230 us -> 37.1 us
  local copies, waits for them, and re-layouts: 147 us -> 18.3 us
  blocking collectives: 104 us -> 0 us
  starting transfers between devices: 9.78 us -> 40.4 us
  other arithmetic: 16.7 us -> 2.64 us
  between operations: 21 us -> 8.13 us
  matrix products: 12.5 us -> 0 us
  Pallas kernels: 0 us -> 11.4 us
    all_gather x3 -> x0, waiting for transfers between devices: 180 us -> none  [the longest x1 103 us: body(): lax.all_gather(amplitudes, 'vert', axis=3, tiled=True)]
    all_to_all x1 -> x0, blocking collectives: 104 us -> none  [body(): lax.all_to_all(blocks, 'pi', split_axis=1, concat_axis=0, tiled=True)]
    all_to_all x3 -> x0, local copies, waits for them, and re-layouts: 42.5 us -> none  [the longest x2 26.1 us: body(): lax.all_to_all(blocks, 'pi', split_axis=1, concat_axis=0, tiled=True)]
    all_to_all x1, waiting for transfers between devices: 48.8 us -> 10.1 us  [body(): arrived = lax.all_to_all(jnp.concatenate(sent, axis=1), 'vert', 0, 0)]
    unnamed x25 -> x22, local copies, waits for them, and re-layouts: 44.8 us -> 6.98 us
    ppermute x2 -> x13, starting transfers between devices: 3.88 us -> 36.7 us  [the longest x4 19.7 us: body(): lax.ppermute(block, ('pi', 'pj'), pair_moves(k))]
    reshape x8 -> x3, local copies, waits for them, and re-layouts: 29.3 us -> 1.73 us  [the longest x2 1.49 us: body(): ints = cycle_ints.reshape(4, 4, BAND, 2, ROWS, TILE)]
    ppermute x2 -> x13, waiting for transfers between devices: 0.01 us -> 27 us  [the longest x4 11.9 us: body(): lax.ppermute(block, ('pi', 'pj'), pair_moves(k))]
  transfers between devices with their start and end apart: 6 -> 14, of which waited for: 4 -> 6; matrix products, arithmetic and copies ran while one was open for 6% -> 4% of each run, Pallas kernels for 0% -> 4%
where the time goes in v1:
time: 119 us; the launch traced here: 118 us
  starting transfers between devices  40.4 us (34%)
  waiting for transfers between devices  37.1 us (31%)
  local copies, waits for them, and re-layouts  18.3 us (15%)
  Pallas kernels  11.4 us (10%)
  between operations  8.13 us (7%)
  other arithmetic  2.64 us (2%)
    ppermute x4, starting transfers between devices, body(): lax.ppermute(block, ('pi', 'pj'), pair_moves(k))  19.7 us
    ppermute x4, waiting for transfers between devices, body(): lax.ppermute(block, ('pi', 'pj'), pair_moves(k))  11.9 us
    pallas_call x3, Pallas kernels, run(): pl.pallas_call(kernel, out_shape=outs, in_specs=[pl.BlockSpec(memory_spac...  11.4 us
    all_to_all x1, waiting for transfers between devices, body(): arrived = lax.all_to_all(jnp.concatenate(sent, axis=1), 'vert', 0, 0)  10.1 us
    ppermute x1, waiting for transfers between devices, body(): flip = lax.ppermute(own, 'vert', FLIP)  7.71 us
    unnamed x22, local copies, waits for them, and re-layouts  6.98 us
    ppermute x1, waiting for transfers between devices, body(): flip_down = lax.ppermute(flip, 'vert', DOWN)  5.5 us
    ppermute x1, starting transfers between devices, body(): after = lax.ppermute(cycle_in[:REACH], 'pj', down)  4.65 us
  transfers between devices with their start and end apart: 14, of which 6 were waited for; matrix products, arithmetic and copies ran while one was open for 4% of the time, Pallas kernels for 4%

profile of v1, /device:TPU:3, one launch (start us, length us, event | category | flops | bytes accessed | tf_op | source)
XLA Modules:
  0.0 117.9 jit_solution(11542182745367532611)
XLA Ops:
  0.0 1.4 %fusion.6 = (s32[1,1]{1,0:T(1,128)}, s32[1,1]{1,0:T(1,128)}) fusion(s32[2,2]{1,0:T(2,128)} %param.10), kind=kLoop, calls=%fused_computation.33 | loop fusion | bytes 16 | tf_op jit(solution)/shard_map/slice | solution.py:198
  4.2 1.3 %fusion.5 = (s32[1,1]{1,0:T(1,128)}, s32[1,1]{1,0:T(1,128)}) fusion(s32[2,2]{1,0:T(2,128)} %param.12), kind=kLoop, calls=%fused_computation.32 | loop fusion | bytes 16 | tf_op jit(solution)/shard_map/slice | solution.py:191
  7.9 1.2 %reshape.84 = bf16[4,4,5,2,8,64]{5,4,3,2,1,0:T(8,128)(2,1)S(1)} reshape(bf16[16,5,2,512]{3,2,1,0:T(2,128)(2,1)} %param.11) | data formatting | bytes 327680 | tf_op jit(solution)/shard_map/reshape | solution.py:199
  12.3 3.9 %constant_dynamic-slice_fusion = (bf16[8,16,1,512]{3,2,1,0:T(2,128)(2,1)S(1)}, bf16[8,16,1,512]{3,2,1,0:T(2,128)(2,1)S(1)}, bf16[8,16,1,512]{3,2,1,0:T(2,128)(2,1)S(1)}, bf16[8,16,1,512]{3,2,1,0:T(2,128)(2,1)S(1)}) fusion(bf16[8,16,8,512]{3,2,1,0:T(8,128)(2,1)} %param.8, s32[]{:T(128)S(6)} %select_n.73, s32[]{:T(128)S(6)} %select_n.72, s32[]{:T(128)S(6)} %select_n.71, ...), kind=kLoop, calls=%fused_computation.26 | loop fusion | bytes 1048592 | tf_op jit(solution)/shard_map/jit(dynamic_index_in_dim)/dynamic_slice | solution.py:172
  16.5 1.9 %collective-permute-start = (bf16[416,512]{1,0:T(8,128)(2,1)S(1)}, bf16[416,512]{1,0:T(8,128)(2,1)S(1)}, u32[]{:S(2)}, u32[]{:S(2)}) collective-permute-start(bf16[416,512]{1,0:T(8,128)(2,1)S(1)} %pad_maximum_fusion.1.refs_0_), channel_id=1, source_target_pairs={{0,4},{1,5},{2,6},{3,7},{4,0},{5,1},{6,2},{7,3},{8,12},{9,13},{10,... | collective-permute-start | bytes 1277960 | tf_op jit(solution)/shard_map/ppermute | solution.py:202
  18.4 2.7 %collective-permute-start.2 = (bf16[416,512]{1,0:T(8,128)(2,1)S(1)}, bf16[416,512]{1,0:T(8,128)(2,1)S(1)}, u32[]{:S(2)}, u32[]{:S(2)}) collective-permute-start(bf16[416,512]{1,0:T(8,128)(2,1)S(1)} %pad_maximum_fusion.1.refs_0_), channel_id=1, source_target_pairs={{0,3},{1,0},{2,1},{3,2},{4,7},{5,4},{6,5},{7,6},{8,11},{9,8},{10,9... | collective-permute-start | bytes 1277960 | tf_op jit(solution)/shard_map/ppermute | solution.py:204
  21.1 7.7 %collective-permute-done.refs_1_ = bf16[416,512]{1,0:T(8,128)(2,1)S(1)} collective-permute-done((bf16[416,512]{1,0:T(8,128)(2,1)S(1)}, bf16[416,512]{1,0:T(8,128)(2,1)S(1)}, u32[]{:S(2)}, u32[]{:S(2)}) %collective-permute-start) | collective-permute-done | bytes 426016 | tf_op jit(solution)/shard_map/ppermute | solution.py:202
  28.8 2.6 %collective-permute-start.4 = (bf16[416,512]{1,0:T(8,128)(2,1)S(1)}, bf16[416,512]{1,0:T(8,128)(2,1)}, u32[]{:S(2)}, u32[]{:S(2)}) collective-permute-start(bf16[416,512]{1,0:T(8,128)(2,1)S(1)} %collective-permute-done.refs_1_), channel_id=1, source_target_pairs={{0,3},{1,0},{2,1},{3,2},{4,7},{5,4},{6,5},{7,6},{8,11},{9,8},{10,9... | collective-permute-start | bytes 1277960 | tf_op jit(solution)/shard_map/ppermute | solution.py:206
  31.6 1.3 %collective-permute-start.7 = (bf16[2,16,512]{2,1,0:T(8,128)(2,1)S(1)}, bf16[2,16,512]{2,1,0:T(8,128)(2,1)S(1)}, u32[]{:S(2)}, u32[]{:S(2)}) collective-permute-start(bf16[2,16,512]{2,1,0:T(8,128)(2,1)S(1)} %bitcast.54), channel_id=1, source_target_pairs={{0,8},{8,16},{16,24},{1,9},{9,17},{17,25},{2,10},{10,18},{18,26},{... | collective-permute-start | bytes 98312 | tf_op jit(solution)/shard_map/ppermute | solution.py:195
  32.9 0.4 fusion.swap
  33.5 5.5 %collective-permute-done.4.refs_5_ = bf16[416,512]{1,0:T(8,128)(2,1)} collective-permute-done((bf16[416,512]{1,0:T(8,128)(2,1)S(1)}, bf16[416,512]{1,0:T(8,128)(2,1)}, u32[]{:S(2)}, u32[]{:S(2)}) %collective-permute-start.4) | collective-permute-done | bytes 426016 | tf_op jit(solution)/shard_map/ppermute | solution.py:206
  39.0 3.5 %collective-permute-start.6 = (bf16[416,512]{1,0:T(8,128)(2,1)}, bf16[416,512]{1,0:T(8,128)(2,1)}, u32[]{:S(2)}, u32[]{:S(2)}) collective-permute-start(bf16[416,512]{1,0:T(8,128)(2,1)} %collective-permute-done.4.refs_5_), channel_id=1, source_target_pairs={{0,3},{1,0},{2,1},{3,2},{4,7},{5,4},{6,5},{7,6},{8,11},{9,8},{10,9... | collective-permute-start | bytes 1277960 | tf_op jit(solution)/shard_map/ppermute | solution.py:208
  42.7 0.7 pad_maximum_fusion.2
  43.6 4.7 %collective-permute-start.8 = (bf16[2,16,512]{2,1,0:T(8,128)(2,1)S(1)}, bf16[2,16,512]{2,1,0:T(8,128)(2,1)S(1)}, u32[]{:S(2)}, u32[]{:S(2)}) collective-permute-start(bf16[2,16,512]{2,1,0:T(8,128)(2,1)S(1)} %bitcast.53), channel_id=1, source_target_pairs={{8,0},{16,8},{24,16},{9,1},{17,9},{25,17},{10,2},{18,10},{26,18},{... | collective-permute-start | bytes 98312 | tf_op jit(solution)/shard_map/ppermute | solution.py:196
  48.3 1.8 %copy.32 = bf16[16,2,8,512]{3,2,1,0:T(8,128)(2,1)} copy(bf16[16,2,8,512]{3,0,2,1:T(8,128)(2,1)} %pad_maximum_fusion.2) | data formatting | bytes 524288 | tf_op jit(solution)/shard_map/stack | solution.py:191
  50.1 0.6 gather_fusion
  50.9 1.8 %collective-permute-done.5.refs_6_ = bf16[416,512]{1,0:T(8,128)(2,1)} collective-permute-done((bf16[416,512]{1,0:T(8,128)(2,1)}, bf16[416,512]{1,0:T(8,128)(2,1)}, u32[]{:S(2)}, u32[]{:S(2)}) %collective-permute-start.5) | collective-permute-done | bytes 426016 | tf_op jit(solution)/shard_map/ppermute | solution.py:207
  52.7 0.9 copy-done.2
  53.7 3.1 %shard_map.83 = (f32[128,1024]{1,0:T(8,128)S(1)}, bf16[8,64,128]{2,1,0:T(8,128)(2,1)S(1)}, bf16[8,64,128]{2,1,0:T(8,128)(2,1)S(1)}) custom-call(s32[17]{0:T(128)S(1)} %concatenate.33.scalars, bf16[2,16,512]{2,1,0:T(8,128)(2,1)S(1)} %collective-permute-done.7.before, bf16[16,16,512]{2,1,0:T(8,128)(2,1)S(1)} %bitcast.50, ...), custom_call_target="tpu_custom_call" | custom-call | tf_op jit(solution)/shard_map/pallas_call | solution.py:157
  56.7 0.8 copy-done.3
  57.5 12.1 %collective-permute-start.11 = (bf16[8,64,128]{2,1,0:T(8,128)(2,1)S(1)}, bf16[8,64,128]{2,1,0:T(8,128)(2,1)S(1)}, u32[]{:S(2)}, u32[]{:S(2)}) collective-permute-start(bf16[8,64,128]{2,1,0:T(8,128)(2,1)S(1)} %get-tuple-element.15), channel_id=1, source_target_pairs={{0,0},{8,64},{16,128},{24,192},{32,32},{40,96},{48,160},{56,224},{... | collective-permute-start | bytes 393224 | tf_op jit(solution)/shard_map/ppermute | solution.py:220
  70.0 3.4 %copy-done.1 = bf16[2,512,4096]{2,1,0:T(8,128)(2,1)S(1)} copy-done((bf16[2,512,4096]{2,1,0:T(8,128)(2,1)S(1)}, bf16[2,512,4096]{2,1,0:T(8,128)(2,1)}, u32[]{:S(2)}) %copy-start.1) | copy-done | bytes 8388632
  73.4 4.7 %shard_map.82 = (f32[128,1024]{1,0:T(8,128)S(1)}, bf16[8,64,128]{2,1,0:T(8,128)(2,1)S(1)}, bf16[8,64,128]{2,1,0:T(8,128)(2,1)S(1)}) custom-call(s32[17]{0:T(128)S(1)} %concatenate.33.scalars, bf16[2,512,4096]{2,1,0:T(8,128)(2,1)S(1)} %copy-done.1, bf16[1024,1024]{1,0:T(8,128)(2,1)S(1)} %fusion.swap, bf16[416,512]{1,0:T(8,128)(2,1)S(1)} %pad_maximum_fusion.1.refs_0_, ...), custom_call_target="tpu_custom_call" | custom-call | tf_op jit(solution)/shard_map/pallas_call | solution.py:157
  78.1 0.8 copy-done.5
  78.9 7.2 %collective-permute-start.9 = (bf16[8,64,128]{2,1,0:T(8,128)(2,1)S(1)}, bf16[8,64,128]{2,1,0:T(8,128)(2,1)S(1)}, u32[]{:S(2)}, u32[]{:S(2)}) collective-permute-start(bf16[8,64,128]{2,1,0:T(8,128)(2,1)S(1)} %get-tuple-element.13), channel_id=1, source_target_pairs={{0,0},{8,64},{16,128},{24,192},{32,32},{40,96},{48,160},{56,224},{... | collective-permute-start | bytes 393224 | tf_op jit(solution)/shard_map/ppermute | solution.py:220
  86.2 9.3 %collective-permute-done.9 = bf16[8,64,128]{2,1,0:T(8,128)(2,1)S(1)} collective-permute-done((bf16[8,64,128]{2,1,0:T(8,128)(2,1)S(1)}, bf16[8,64,128]{2,1,0:T(8,128)(2,1)S(1)}, u32[]{:S(2)}, u32[]{:S(2)}) %collective-permute-start.9) | collective-permute-done | bytes 131104 | tf_op jit(solution)/shard_map/ppermute | solution.py:220
  95.5 2.6 %collective-permute-done.10 = bf16[8,64,128]{2,1,0:T(8,128)(2,1)S(1)} collective-permute-done((bf16[8,64,128]{2,1,0:T(8,128)(2,1)S(1)}, bf16[8,64,128]{2,1,0:T(8,128)(2,1)S(1)}, u32[]{:S(2)}, u32[]{:S(2)}) %collective-permute-start.10) | collective-permute-done | bytes 131104 | tf_op jit(solution)/shard_map/ppermute | solution.py:220
  98.1 0.8 pad_maximum_fusion
  99.0 3.7 %all-to-all-start = ((bf16[8,256,128]{2,1,0:T(8,128)(2,1)}), bf16[8,256,128]{2,1,0:T(8,128)(2,1)S(1)}, u32[]{:S(2)}, u32[]{:S(2)}) async-start(bf16[8,256,128]{2,1,0:T(8,128)(2,1)} %pad_maximum_fusion), calls=%async_computation | async-start | bytes 1048576 | tf_op jit(solution)/shard_map/all_to_all | solution.py:223
  103.1 10.1 %all-to-all-done.arrived = bf16[8,256,128]{2,1,0:T(8,128)(2,1)S(1)} async-done(((bf16[8,256,128]{2,1,0:T(8,128)(2,1)}), bf16[8,256,128]{2,1,0:T(8,128)(2,1)S(1)}, u32[]{:S(2)}, u32[]{:S(2)}) %all-to-all-start) | async-done | bytes 524320 | tf_op jit(solution)/shard_map/all_to_all | solution.py:223
  113.2 1.0 copy-done.6
  114.3 3.7 %shard_map.84 = f32[8,16,8,512]{3,2,1,0:T(8,128)} custom-call(s32[17]{0:T(128)S(1)} %concatenate.33.scalars, f32[128,1024]{1,0:T(8,128)S(1)} %copy-done.6, f32[128,1024]{1,0:T(8,128)S(1)} %copy-done.4, bf16[8,256,128]{2,1,0:T(8,128)(2,1)S(1)} %all-to-all-done.arrived, bf16[1024,1024]{1,0:T(8,128)(2,1)S(1)} %fusion.1.place), custom_call_target="tpu_custom_call" | custom-call | tf_op jit(solution)/shard_map/pallas_call | solution.py:157
  (45 shorter events, 2.3 us)
Async XLA Ops:
  0.0 50.1 %copy-start = (s32[8]{0:T(128)S(1)}, s32[8]{0:T(128)}, u32[]{:S(2)}) copy-start(s32[8]{0:T(128)} %param.13) | copy-start | bytes 100
  0.0 32.9 %copy-start.8 = (s32[1024]{0:T(1024)S(1)}, s32[1024]{0:T(1024)}, u32[]{:S(2)}) copy-start(s32[1024]{0:T(1024)} %constant.85.clone) | copy-start | bytes 12292
  9.4 33.1 %copy-start.9 = (s32[2,2]{1,0:T(2,128)S(1)}, s32[2,2]{1,0:T(2,128)}, u32[]{:S(2)}) copy-start(s32[2,2]{1,0:T(2,128)} %param.10) | copy-start | bytes 52
  9.5 33.1 %copy-start.10 = (s32[2,2]{1,0:T(2,128)S(1)}, s32[2,2]{1,0:T(2,128)}, u32[]{:S(2)}) copy-start(s32[2,2]{1,0:T(2,128)} %param.12) | copy-start | bytes 52
  16.5 12.4 %collective-permute-start = (bf16[416,512]{1,0:T(8,128)(2,1)S(1)}, bf16[416,512]{1,0:T(8,128)(2,1)S(1)}, u32[]{:S(2)}, u32[]{:S(2)}) collective-permute-start(bf16[416,512]{1,0:T(8,128)(2,1)S(1)} %pad_maximum_fusion.1.refs_0_), channel_id=1, source_target_pairs={{0,4},{1,5},{2,6},{3,7},{4,0},{5,1},{6,2},{7,3},{8,12},{9,13},{10,... | collective-permute-start | bytes 1277960 | tf_op jit(solution)/shard_map/ppermute | solution.py:202
  18.4 32.5 %collective-permute-start.2 = (bf16[416,512]{1,0:T(8,128)(2,1)S(1)}, bf16[416,512]{1,0:T(8,128)(2,1)S(1)}, u32[]{:S(2)}, u32[]{:S(2)}) collective-permute-start(bf16[416,512]{1,0:T(8,128)(2,1)S(1)} %pad_maximum_fusion.1.refs_0_), channel_id=1, source_target_pairs={{0,3},{1,0},{2,1},{3,2},{4,7},{5,4},{6,5},{7,6},{8,11},{9,8},{10,9... | collective-permute-start | bytes 1277960 | tf_op jit(solution)/shard_map/ppermute | solution.py:204
  21.1 12.3 %collective-permute-start.1 = (bf16[416,512]{1,0:T(8,128)(2,1)S(1)}, bf16[416,512]{1,0:T(8,128)(2,1)}, u32[]{:S(2)}, u32[]{:S(2)}) collective-permute-start(bf16[416,512]{1,0:T(8,128)(2,1)S(1)} %pad_maximum_fusion.1.refs_0_), channel_id=1, source_target_pairs={{0,1},{1,2},{2,3},{3,0},{4,5},{5,6},{6,7},{7,4},{8,9},{9,10},{10,1... | collective-permute-start | bytes 1277960 | tf_op jit(solution)/shard_map/ppermute | solution.py:203
  28.8 10.2 %collective-permute-start.4 = (bf16[416,512]{1,0:T(8,128)(2,1)S(1)}, bf16[416,512]{1,0:T(8,128)(2,1)}, u32[]{:S(2)}, u32[]{:S(2)}) collective-permute-start(bf16[416,512]{1,0:T(8,128)(2,1)S(1)} %collective-permute-done.refs_1_), channel_id=1, source_target_pairs={{0,3},{1,0},{2,1},{3,2},{4,7},{5,4},{6,5},{7,6},{8,11},{9,8},{10,9... | collective-permute-start | bytes 1277960 | tf_op jit(solution)/shard_map/ppermute | solution.py:206
  31.6 11.9 %collective-permute-start.7 = (bf16[2,16,512]{2,1,0:T(8,128)(2,1)S(1)}, bf16[2,16,512]{2,1,0:T(8,128)(2,1)S(1)}, u32[]{:S(2)}, u32[]{:S(2)}) collective-permute-start(bf16[2,16,512]{2,1,0:T(8,128)(2,1)S(1)} %bitcast.54), channel_id=1, source_target_pairs={{0,8},{8,16},{16,24},{1,9},{9,17},{17,25},{2,10},{10,18},{18,26},{... | collective-permute-start | bytes 98312 | tf_op jit(solution)/shard_map/ppermute | solution.py:195
  33.3 19.4 %collective-permute-start.3 = (bf16[416,512]{1,0:T(8,128)(2,1)S(1)}, bf16[416,512]{1,0:T(8,128)(2,1)}, u32[]{:S(2)}, u32[]{:S(2)}) collective-permute-start(bf16[416,512]{1,0:T(8,128)(2,1)S(1)} %collective-permute-done.refs_1_), channel_id=1, source_target_pairs={{0,1},{1,2},{2,3},{3,0},{4,5},{5,6},{6,7},{7,4},{8,9},{9,10},{10,1... | collective-permute-start | bytes 1277960 | tf_op jit(solution)/shard_map/ppermute | solution.py:205
  33.4 19.3 %collective-permute-start.5 = (bf16[416,512]{1,0:T(8,128)(2,1)}, bf16[416,512]{1,0:T(8,128)(2,1)}, u32[]{:S(2)}, u32[]{:S(2)}) collective-permute-start(bf16[416,512]{1,0:T(8,128)(2,1)} %collective-permute-done.1.refs_2_), channel_id=1, source_target_pairs={{0,1},{1,2},{2,3},{3,0},{4,5},{5,6},{6,7},{7,4},{8,9},{9,10},{10,1... | collective-permute-start | bytes 1277960 | tf_op jit(solution)/shard_map/ppermute | solution.py:207
  39.0 13.7 %collective-permute-start.6 = (bf16[416,512]{1,0:T(8,128)(2,1)}, bf16[416,512]{1,0:T(8,128)(2,1)}, u32[]{:S(2)}, u32[]{:S(2)}) collective-permute-start(bf16[416,512]{1,0:T(8,128)(2,1)} %collective-permute-done.4.refs_5_), channel_id=1, source_target_pairs={{0,3},{1,0},{2,1},{3,2},{4,7},{5,4},{6,5},{7,6},{8,11},{9,8},{10,9... | collective-permute-start | bytes 1277960 | tf_op jit(solution)/shard_map/ppermute | solution.py:208
  43.6 7.3 %collective-permute-start.8 = (bf16[2,16,512]{2,1,0:T(8,128)(2,1)S(1)}, bf16[2,16,512]{2,1,0:T(8,128)(2,1)S(1)}, u32[]{:S(2)}, u32[]{:S(2)}) collective-permute-start(bf16[2,16,512]{2,1,0:T(8,128)(2,1)S(1)} %bitcast.53), channel_id=1, source_target_pairs={{8,0},{16,8},{24,16},{9,1},{17,9},{25,17},{10,2},{18,10},{26,18},{... | collective-permute-start | bytes 98312 | tf_op jit(solution)/shard_map/ppermute | solution.py:196
  52.7 1.0 copy-start.2
  56.7 0.8 copy-start.3
  57.5 28.7 %collective-permute-start.11 = (bf16[8,64,128]{2,1,0:T(8,128)(2,1)S(1)}, bf16[8,64,128]{2,1,0:T(8,128)(2,1)S(1)}, u32[]{:S(2)}, u32[]{:S(2)}) collective-permute-start(bf16[8,64,128]{2,1,0:T(8,128)(2,1)S(1)} %get-tuple-element.15), channel_id=1, source_target_pairs={{0,0},{8,64},{16,128},{24,192},{32,32},{40,96},{48,160},{56,224},{... | collective-permute-start | bytes 393224 | tf_op jit(solution)/shard_map/ppermute | solution.py:220
  69.7 16.5 %collective-permute-start.12 = (bf16[8,64,128]{2,1,0:T(8,128)(2,1)S(1)}, bf16[8,64,128]{2,1,0:T(8,128)(2,1)S(1)}, u32[]{:S(2)}, u32[]{:S(2)}) collective-permute-start(bf16[8,64,128]{2,1,0:T(8,128)(2,1)S(1)} %get-tuple-element.16), channel_id=1, source_target_pairs={{0,32},{8,96},{16,160},{24,224},{32,0},{40,64},{48,128},{56,192},{... | collective-permute-start | bytes 393224 | tf_op jit(solution)/shard_map/ppermute | solution.py:220
  70.0 3.4 %copy-start.1 = (bf16[2,512,4096]{2,1,0:T(8,128)(2,1)S(1)}, bf16[2,512,4096]{2,1,0:T(8,128)(2,1)}, u32[]{:S(2)}) copy-start(bf16[2,512,4096]{2,1,0:T(8,128)(2,1)} %ints.1) | copy-start | bytes 25165828
  73.4 29.3 %copy-start.7 = (s32[1024]{0:T(1024)S(1)}, s32[1024]{0:T(1024)}, u32[]{:S(2)}) copy-start(s32[1024]{0:T(1024)} %constant.86.clone) | copy-start | bytes 12292
  78.1 0.8 copy-start.5
  78.9 34.4 %copy-start.4 = (f32[128,1024]{1,0:T(8,128)S(1)}, f32[128,1024]{1,0:T(8,128)}, u32[]{:S(2)}) copy-start(f32[128,1024]{1,0:T(8,128)} %copy-done.3) | copy-start | bytes 1572868
  78.9 16.6 %collective-permute-start.9 = (bf16[8,64,128]{2,1,0:T(8,128)(2,1)S(1)}, bf16[8,64,128]{2,1,0:T(8,128)(2,1)S(1)}, u32[]{:S(2)}, u32[]{:S(2)}) collective-permute-start(bf16[8,64,128]{2,1,0:T(8,128)(2,1)S(1)} %get-tuple-element.13), channel_id=1, source_target_pairs={{0,0},{8,64},{16,128},{24,192},{32,32},{40,96},{48,160},{56,224},{... | collective-permute-start | bytes 393224 | tf_op jit(solution)/shard_map/ppermute | solution.py:220
  86.1 12.0 %collective-permute-start.10 = (bf16[8,64,128]{2,1,0:T(8,128)(2,1)S(1)}, bf16[8,64,128]{2,1,0:T(8,128)(2,1)S(1)}, u32[]{:S(2)}, u32[]{:S(2)}) collective-permute-start(bf16[8,64,128]{2,1,0:T(8,128)(2,1)S(1)} %get-tuple-element.14), channel_id=1, source_target_pairs={{0,32},{8,96},{16,160},{24,224},{32,0},{40,64},{48,128},{56,192},{... | collective-permute-start | bytes 393224 | tf_op jit(solution)/shard_map/ppermute | solution.py:220
  99.0 14.3 %all-to-all-start = ((bf16[8,256,128]{2,1,0:T(8,128)(2,1)}), bf16[8,256,128]{2,1,0:T(8,128)(2,1)S(1)}, u32[]{:S(2)}, u32[]{:S(2)}) async-start(bf16[8,256,128]{2,1,0:T(8,128)(2,1)} %pad_maximum_fusion), calls=%async_computation | async-start | bytes 1048576 | tf_op jit(solution)/shard_map/all_to_all | solution.py:223
  113.2 1.0 copy-start.6

commit v2 on v1

v2 whole, which is shorter than its diff:
```python
import jax
import jax.numpy as jnp
import numpy as np
from jax import lax
from jax.experimental import pallas as pl
from jax.experimental.pallas import tpu as pltpu
from jax.sharding import PartitionSpec as P

TILE = 64
REACH = 2
BAND = 5
ROWS = 8
LANES = 512
PAIRS = 128
BF = jnp.bfloat16
F32 = jnp.float32
MIB = 1 << 20


def vert_moves(move):
    return [(v, move(v // 4, v % 4)) for v in range(8)]


FLIP = vert_moves(lambda h, y: (1 - h) * 4 + y)
UP = vert_moves(lambda h, y: h * 4 + (y + 1) % 4)
DOWN = vert_moves(lambda h, y: h * 4 + (y + 3) % 4)


def pair_moves(k):
    return [
        (p * 4 + q, (2 * q + ((p % 2) ^ k)) * 4 + p // 2) for p in range(8) for q in range(4)
    ]


def send_order():
    row = np.arange(1024)
    slot, a, v, b = row // 512, (row // 64) % 8, (row // 8) % 8, row % 8
    return v * 128 + slot * 64 + b * 8 + a


def place_order():
    row = np.arange(1024)
    v, slot, b, a = row // 128, (row // 64) % 2, (row // 8) % 8, row % 8
    return slot * 512 + b * 64 + v * 8 + a


def permutation(order):
    columns = lax.broadcasted_iota(jnp.int32, (1024, 1024), 1)
    return (jnp.asarray(order, jnp.int32)[:, None] == columns).astype(BF)


def prepare_kernel(ladder_tiles, cycle_tiles, amplitudes, ints, own_ref, inner_ref, first_ref, last_ref, wide, tall):
    row = lax.broadcasted_iota(jnp.int32, (512, 128), 0)
    column = lax.broadcasted_iota(jnp.int32, (512, 128), 1)
    ladder_row = row < 256
    i = row & 7
    j = jnp.where(ladder_row, (row >> 3) & 15, (row >> 4) & 15)
    which = jnp.where(ladder_row, (row >> 7) & 1, (row >> 3) & 1)
    ladder_0, cycle_0 = ladder_tiles[0, 1], cycle_tiles[0, 1]
    tile = jnp.where(
        ladder_row,
        ladder_0 + which * (ladder_tiles[1, 1] - ladder_0),
        cycle_0 + which * (cycle_tiles[1, 1] - cycle_0),
    )
    wanted = (i * 16 + j) * 8 + tile - column
    pick = jnp.concatenate(
        [jnp.where(wanted == c * 128, 1.0, 0.0).astype(BF) for c in range(8)], axis=1
    )
    picked = jnp.dot(pick, amplitudes[...], preferred_element_type=F32).astype(BF)
    own_ref[:256, :] = picked[:256]
    inner = picked[256:].reshape(16, 16, LANES)
    inner_ref[...] = inner
    first_ref[...] = inner[:REACH]
    last_ref[...] = inner[16 - REACH :]
    for t in range(4):
        wide[t] = ints[:, t * 128 : (t + 1) * 128].astype(F32)
    low = lax.broadcasted_iota(jnp.int32, (80, 128), 1) < TILE
    for t in range(4):
        zero = wide[t, pl.ds(0, 80, stride=2), :]
        one = wide[t, pl.ds(1, 80, stride=2), :]
        tall[pl.ds(2 * t, 80, stride=8), :] = jnp.where(low, zero, pltpu.roll(one, TILE, 1))
        tall[pl.ds(2 * t + 1, 80, stride=8), :] = jnp.where(low, pltpu.roll(zero, TILE, 1), one)
    for b in range(4):
        own_ref[256:, b * 128 : (b + 1) * 128] = tall[b * 160 : (b + 1) * 160, :].astype(BF)


def source_rows():
    vert = lax.axis_index("vert")
    h, y = vert // 4, vert % 4
    places = [
        (h, y), (1 - h, y), (h, y + 3), (h, y + 1),
        (1 - h, y + 3), (1 - h, y + 1), (h, y + 2), (1 - h, y + 2),
    ]
    return [a * 4 + b % 4 for a, b in places]


def main_kernel(ladder_hbm, before, inner, after, swap, *refs):
    pieces, (total_ref, sent_ref, ladder_ints, ints, total, sem, sems) = refs[:8], refs[8:]
    loads = [
        pltpu.make_async_copy(ladder_hbm.at[w], ladder_ints.at[w], sems.at[w]) for w in range(2)
    ]
    for load in loads:
        load.start()
    sources = source_rows()
    parity = lax.axis_index("pi") % 2
    for d in range(8):
        ints[sources[d]] = pieces[d][256:, :].astype(F32)

    def rows_of(j):
        if j < REACH:
            return before[j]
        if j < REACH + 16:
            return inner[j - REACH]
        return after[j - REACH - 16]

    laid = []
    for j in range(16 + 2 * REACH):
        block = rows_of(j)
        laid.append(
            jnp.concatenate([block[:, a * TILE : (a + 1) * TILE] for a in range(ROWS)], axis=0)
        )
    low = lax.broadcasted_iota(jnp.int32, (8, 128), 1) < TILE
    for j in range(16):
        left = jnp.concatenate([laid[j + o] for o in range(BAND)], axis=1)
        base, lanes = (j % 4) * 40, (j // 4) * 128
        right = jnp.concatenate(
            [
                ints[v, base + o * 8 : base + o * 8 + 8, lanes : lanes + 128]
                for o in range(BAND)
                for v in range(8)
            ],
            axis=0,
        ).astype(BF)
        done = jnp.dot(left, right, preferred_element_type=F32)
        for r in range(2):
            for t in range(4):
                even = done[t * 32 + r * 8 : t * 32 + r * 8 + 8]
                odd = done[t * 32 + 16 + r * 8 : t * 32 + 16 + r * 8 + 8]
                if r == 0:
                    odd = pltpu.roll(odd, TILE, 1)
                else:
                    even = pltpu.roll(even, TILE, 1)
                lane = 1024 + r * LANES + t * 128
                total[j * 8 : j * 8 + 8, lane : lane + 128] = jnp.where(low, even, odd)
    for which in range(2):
        loads[which].wait()
        acc = None
        for d in range(8):
            start = pl.multiple_of(sources[d] * LANES, LANES)
            part = lax.dot_general(
                pieces[d][which * PAIRS : (which + 1) * PAIRS, :],
                ladder_ints[which, :, pl.ds(start, LANES)],
                (((1,), (1,)), ((), ())),
                preferred_element_type=F32,
            )
            acc = part if acc is None else acc + part
        total[:, which * LANES : (which + 1) * LANES] = acc
    keep = pltpu.make_async_copy(total, total_ref, sem)
    keep.start()
    for s in range(2):
        sent = jnp.dot(
            total[:, s * 1024 : (s + 1) * 1024].astype(BF), swap[...], preferred_element_type=F32
        ).astype(BF)
        upper, under = sent[:64], sent[64:]
        halves = (
            jnp.where(parity == 0, upper, under),
            jnp.where(parity == 0, under, upper),
        )
        for k in range(2):
            for v in range(8):
                sent_ref[v, k, s * 64 : (s + 1) * 64, :] = halves[k][:, v * 128 : (v + 1) * 128]
    keep.wait()


def finish_kernel(ladder_tiles, cycle_tiles, partner, total_ref, first, second, place, out_ref, mirrored, total, sem):
    fetch = pltpu.make_async_copy(total_ref, total, sem)
    fetch.start()
    parity = lax.axis_index("pi") % 2
    for k, arrived in enumerate((first, second)):
        wide = jnp.concatenate([arrived[v] for v in range(8)], axis=1)
        moved = jnp.dot(wide, place[...], preferred_element_type=F32)
        for s in range(2):
            mirrored[s, parity ^ k] = moved[s * 64 : (s + 1) * 64]
    dests = [ladder_tiles[0, 0], ladder_tiles[1, 0], cycle_tiles[0, 0], cycle_tiles[1, 0]]
    tile = lax.broadcasted_iota(jnp.int32, (8, LANES), 0)
    own = [(tile == dest).astype(F32) for dest in dests]
    other = [(tile == partner[dest]).astype(F32) for dest in dests]
    fetch.wait()

    def one(i):
        for j in range(16):
            acc = None
            for s in range(4):
                lanes = slice((s % 2) * LANES, (s % 2 + 1) * LANES)
                term = own[s] * total[pl.ds(j * 8 + i, 1), s * LANES : (s + 1) * LANES]
                acc = term if acc is None else acc + term
                acc = acc + other[s] * mirrored[s // 2, j // 8, pl.ds(i * 8 + j % 8, 1), lanes]
            out_ref[i, j] = acc

    pl.loop(0, 8)(one)


SMEM = pl.BlockSpec(memory_space=pltpu.SMEM)
VMEM = pl.BlockSpec(memory_space=pltpu.VMEM)
ANY = pl.BlockSpec(memory_space=pl.ANY)


def call(kernel, ins, outs, out_specs, scratch, limit, flops):
    return pl.pallas_call(
        kernel,
        out_shape=outs,
        in_specs=ins,
        out_specs=out_specs,
        scratch_shapes=scratch,
        compiler_params=pltpu.CompilerParams(vmem_limit_bytes=limit * MIB),
        cost_estimate=pl.CostEstimate(flops=flops, bytes_accessed=4 * MIB, transcendentals=0),
    )


def shape(dims, kind):
    return jax.ShapeDtypeStruct(dims, kind)


def body(amplitudes, ladder_ints, ladder_tiles, cycle_ints, cycle_tiles, partner):
    edge = shape((REACH, 16, LANES), BF)
    own, inner, first, last = call(
        prepare_kernel,
        [SMEM, SMEM, VMEM, VMEM],
        [shape((416, LANES), BF), shape((16, 16, LANES), BF), edge, edge],
        [VMEM] * 4,
        [pltpu.VMEM((4, 160, 128), F32), pltpu.VMEM((640, 128), F32)],
        12,
        10**9,
    )(ladder_tiles, cycle_tiles, amplitudes.reshape(1024, LANES), cycle_ints.reshape(160, LANES))
    flip = lax.ppermute(own, "vert", FLIP)
    own_up = lax.ppermute(own, "vert", UP)
    own_down = lax.ppermute(own, "vert", DOWN)
    flip_up = lax.ppermute(flip, "vert", UP)
    flip_down = lax.ppermute(flip, "vert", DOWN)
    far = lax.ppermute(own_up, "vert", UP)
    flip_far = lax.ppermute(flip_down, "vert", DOWN)
    before = lax.ppermute(last, "pj", [(q, q + 1) for q in range(3)])
    after = lax.ppermute(first, "pj", [(q + 1, q) for q in range(3)])
    pieces = [own, flip, own_up, own_down, flip_up, flip_down, far, flip_far]

    total, sent = call(
        main_kernel,
        [ANY] + [VMEM] * 12,
        [shape((PAIRS, 2048), F32), shape((8, 2, 128, 128), BF)],
        [ANY, VMEM],
        [
            pltpu.VMEM((2, LANES, 4096), BF),
            pltpu.VMEM((8, 160, LANES), F32),
            pltpu.VMEM((PAIRS, 2048), F32),
            pltpu.SemaphoreType.DMA,
            pltpu.SemaphoreType.DMA((2,)),
        ],
        26,
        2 * 10**9,
    )(ladder_ints, before, inner, after, permutation(send_order()), *pieces)
    arrived = lax.all_to_all(sent, "vert", 0, 0)
    moved = [lax.ppermute(arrived[:, k], ("pi", "pj"), pair_moves(k)) for k in range(2)]
    return call(
        finish_kernel,
        [SMEM, SMEM, SMEM, ANY, VMEM, VMEM, VMEM],
        shape((8, 16, 8, LANES), F32),
        VMEM,
        [
            pltpu.VMEM((2, 2, 64, 1024), F32),
            pltpu.VMEM((PAIRS, 2048), F32),
            pltpu.SemaphoreType.DMA,
        ],
        16,
        10**9,
    )(ladder_tiles, cycle_tiles, partner, total, *moved, permutation(place_order()))


def solution(mesh):
    placed = (
        P("pi", "pj", None, "vert"),
        P(None, "vert", None),
        P(),
        P("pj", None, None, "vert"),
        P(),
        P(),
    )
    return jax.shard_map(
        body, mesh=mesh, in_specs=placed, out_specs=P("pi", "pj", None, "vert"), check_vma=False
    )
```

time: 119 us -> 105 us (0.88)
  blocking collectives: 0 us -> 15.3 us
  local copies, waits for them, and re-layouts: 18.3 us -> 7 us
  starting transfers between devices: 40.4 us -> 29.2 us
  between operations: 8.13 us -> 0.15 us
  waiting for transfers between devices: 37.1 us -> 41.3 us
    all_to_all x0 -> x1, blocking collectives: none -> 15.3 us  [body(): arrived = lax.all_to_all(sent, 'vert', 0, 0)]
    ppermute x6 -> x4, waiting for transfers between devices: 11.9 us -> 24.4 us  [the longest x2 18.3 us: body(): lax.ppermute(arrived[:, k], ('pi', 'pj'), pair_moves(k))]
    all_to_all x1 -> x0, waiting for transfers between devices: 10.1 us -> none  [body(): arrived = lax.all_to_all(jnp.concatenate(sent, axis=1), 'vert', 0, 0)]
    ppermute x6 -> x4, starting transfers between devices: 25.7 us -> 18.4 us  [the longest x2 12.6 us: body(): lax.ppermute(arrived[:, k], ('pi', 'pj'), pair_moves(k))]
    dynamic_slice x1 -> x0, local copies, waits for them, and re-layouts: 3.87 us -> none  [select(): tile = lax.dynamic_index_in_dim(amplitudes, index, 2, keepdims=False)]
    all_to_all x1 -> x0, starting transfers between devices: 3.73 us -> none  [body(): arrived = lax.all_to_all(jnp.concatenate(sent, axis=1), 'vert', 0, 0)]
    slice x5 -> x0, local copies, waits for them, and re-layouts: 2.92 us -> none  [the longest x1 1.42 us: body(): ladder_tiles[w, 1]]
    ppermute x1, starting transfers between devices: 2.73 us -> 0.46 us  [body(): own_down = lax.ppermute(own, 'vert', DOWN)]
  transfers between devices with their start and end apart: 14 -> 11, of which waited for: 6 -> 6; matrix products, arithmetic and copies ran while one was open for 4% -> 1% of each run, Pallas kernels for 4% -> 0%
where the time goes in v2:
time: 105 us
  waiting for transfers between devices  41.3 us (39%)
  starting transfers between devices  29.2 us (28%)
  blocking collectives  15.3 us (15%)
  Pallas kernels  10.6 us (10%)
  local copies, waits for them, and re-layouts  7 us (7%)
  other arithmetic  1.5 us (1%)
    ppermute x2, waiting for transfers between devices, body(): lax.ppermute(arrived[:, k], ('pi', 'pj'), pair_moves(k))  18.3 us
    all_to_all x1, blocking collectives, body(): arrived = lax.all_to_all(sent, 'vert', 0, 0)  15.3 us
    ppermute x2, starting transfers between devices, body(): lax.ppermute(arrived[:, k], ('pi', 'pj'), pair_moves(k))  12.6 us
    ppermute x1, waiting for transfers between devices, body(): flip = lax.ppermute(own, 'vert', FLIP)  9.05 us
    ppermute x1, waiting for transfers between devices, body(): before = lax.ppermute(last, 'pj', [(q, q + 1) for q in range(3)])  6.12 us
    ppermute x1, waiting for transfers between devices, body(): flip_down = lax.ppermute(flip, 'vert', DOWN)  6.06 us
    unnamed x16, local copies, waits for them, and re-layouts  5.98 us
    pallas_call x1, Pallas kernels, body(): call(main_kernel, [ANY] + [VMEM] * 12, [shape((PAIRS, 2048), F32), shape(...  5.52 us
  transfers between devices with their start and end apart: 11, of which 6 were waited for; matrix products, arithmetic and copies ran while one was open for 1% of the time, Pallas kernels for 0%

profile of v2, /device:TPU:3, one launch (start us, length us, event | category | flops | bytes accessed | tf_op | source)
XLA Modules:
  0.0 105.1 jit_solution(7376925445147542061)
XLA Ops:
  0.0 1.0 reshape.9.ints
  1.0 0.0 copy-start.1
  1.0 0.7 copy-done.1
  1.7 0.7 copy-done.3
  2.3 1.2 %copy-done.6 = bf16[8,16,8,512]{3,2,1,0:T(8,128)(2,1)S(1)} copy-done((bf16[8,16,8,512]{3,2,1,0:T(8,128)(2,1)S(1)}, bf16[8,16,8,512]{3,2,1,0:T(8,128)(2,1)}, u32[]{:S(2)}) %copy-start.6) | copy-done | bytes 1048600
  3.6 1.3 %shard_map.82 = (bf16[416,512]{1,0:T(8,128)(2,1)S(1)}, bf16[16,16,512]{2,1,0:T(8,128)(2,1)S(1)}, bf16[2,16,512]{2,1,0:T(8,128)(2,1)S(1)}, bf16[2,16,512]{2,1,0:T(8,128)(2,1)S(1)}) custom-call(s32[2,2]{1,0:T(2,128)S(1)} %copy-done.1, s32[2,2]{1,0:T(2,128)S(1)} %copy-done.3, bf16[1024,512]{1,0:T(8,128)(2,1)S(1)} %bitcast.9, bf16[160,512]{1,0:T(8,128)(2,1)S(1)} %reshape.9.ints), custom_call_target="tpu_custom_call" | custom-call | flops 1000000000 | bytes 4194304 | tf_op jit(solution)/shard_map/pallas_call | solution.py:226
  4.9 1.9 %collective-permute-start.2 = (bf16[416,512]{1,0:T(8,128)(2,1)S(1)}, bf16[416,512]{1,0:T(8,128)(2,1)S(1)}, u32[]{:S(2)}, u32[]{:S(2)}) collective-permute-start(bf16[416,512]{1,0:T(8,128)(2,1)S(1)} %get-tuple-element.14.refs_0_), channel_id=1, source_target_pairs={{0,4},{1,5},{2,6},{3,7},{4,0},{5,1},{6,2},{7,3},{8,12},{9,13},{10,... | collective-permute-start | bytes 1277960 | tf_op jit(solution)/shard_map/ppermute | solution.py:235
  6.8 1.3 %collective-permute-start.3 = (bf16[416,512]{1,0:T(8,128)(2,1)S(1)}, bf16[416,512]{1,0:T(8,128)(2,1)S(1)}, u32[]{:S(2)}, u32[]{:S(2)}) collective-permute-start(bf16[416,512]{1,0:T(8,128)(2,1)S(1)} %get-tuple-element.14.refs_0_), channel_id=1, source_target_pairs={{0,1},{1,2},{2,3},{3,0},{4,5},{5,6},{6,7},{7,4},{8,9},{9,10},{10,1... | collective-permute-start | bytes 1277960 | tf_op jit(solution)/shard_map/ppermute | solution.py:236
  8.1 9.0 %collective-permute-done.2.refs_1_ = bf16[416,512]{1,0:T(8,128)(2,1)S(1)} collective-permute-done((bf16[416,512]{1,0:T(8,128)(2,1)S(1)}, bf16[416,512]{1,0:T(8,128)(2,1)S(1)}, u32[]{:S(2)}, u32[]{:S(2)}) %collective-permute-start.2) | collective-permute-done | bytes 426016 | tf_op jit(solution)/shard_map/ppermute | solution.py:235
  17.2 2.7 %collective-permute-start.6 = (bf16[416,512]{1,0:T(8,128)(2,1)S(1)}, bf16[416,512]{1,0:T(8,128)(2,1)S(1)}, u32[]{:S(2)}, u32[]{:S(2)}) collective-permute-start(bf16[416,512]{1,0:T(8,128)(2,1)S(1)} %collective-permute-done.2.refs_1_), channel_id=1, source_target_pairs={{0,3},{1,0},{2,1},{3,2},{4,7},{5,4},{6,5},{7,6},{8,11},{9,8},{10,9... | collective-permute-start | bytes 1277960 | tf_op jit(solution)/shard_map/ppermute | solution.py:239
  19.9 0.5 collective-permute-start.4
  20.4 1.0 collective-permute-start.5
  21.4 0.0 collective-permute-start.7
  21.4 6.1 %collective-permute-done.6.refs_5_ = bf16[416,512]{1,0:T(8,128)(2,1)S(1)} collective-permute-done((bf16[416,512]{1,0:T(8,128)(2,1)S(1)}, bf16[416,512]{1,0:T(8,128)(2,1)S(1)}, u32[]{:S(2)}, u32[]{:S(2)}) %collective-permute-start.6) | collective-permute-done | bytes 426016 | tf_op jit(solution)/shard_map/ppermute | solution.py:239
  27.5 3.4 %collective-permute-start.8 = (bf16[416,512]{1,0:T(8,128)(2,1)S(1)}, bf16[416,512]{1,0:T(8,128)(2,1)S(1)}, u32[]{:S(2)}, u32[]{:S(2)}) collective-permute-start(bf16[416,512]{1,0:T(8,128)(2,1)S(1)} %collective-permute-done.6.refs_5_), channel_id=1, source_target_pairs={{0,3},{1,0},{2,1},{3,2},{4,7},{5,4},{6,5},{7,6},{8,11},{9,8},{10,9... | collective-permute-start | bytes 1277960 | tf_op jit(solution)/shard_map/ppermute | solution.py:241
  30.9 1.3 %collective-permute-start = (bf16[2,16,512]{2,1,0:T(8,128)(2,1)S(1)}, bf16[2,16,512]{2,1,0:T(8,128)(2,1)S(1)}, u32[]{:S(2)}, u32[]{:S(2)}) collective-permute-start(bf16[2,16,512]{2,1,0:T(8,128)(2,1)S(1)} %get-tuple-element.11), channel_id=1, source_target_pairs={{0,8},{8,16},{16,24},{1,9},{9,17},{17,25},{2,10},{10,18},{18,26},{... | collective-permute-start | bytes 98312 | tf_op jit(solution)/shard_map/ppermute | solution.py:242
  32.2 6.1 %collective-permute-done.before = bf16[2,16,512]{2,1,0:T(8,128)(2,1)S(1)} collective-permute-done((bf16[2,16,512]{2,1,0:T(8,128)(2,1)S(1)}, bf16[2,16,512]{2,1,0:T(8,128)(2,1)S(1)}, u32[]{:S(2)}, u32[]{:S(2)}) %collective-permute-start) | collective-permute-done | bytes 32800 | tf_op jit(solution)/shard_map/ppermute | solution.py:242
  38.3 4.5 %collective-permute-start.1 = (bf16[2,16,512]{2,1,0:T(8,128)(2,1)S(1)}, bf16[2,16,512]{2,1,0:T(8,128)(2,1)S(1)}, u32[]{:S(2)}, u32[]{:S(2)}) collective-permute-start(bf16[2,16,512]{2,1,0:T(8,128)(2,1)S(1)} %get-tuple-element.13), channel_id=1, source_target_pairs={{8,0},{16,8},{24,16},{9,1},{17,9},{25,17},{10,2},{18,10},{26,18},{... | collective-permute-start | bytes 98312 | tf_op jit(solution)/shard_map/ppermute | solution.py:243
  42.8 1.1 %fusion.swap = bf16[1024,1024]{1,0:T(8,128)(2,1)S(1)} fusion(s32[1024]{0:T(1024)} %constant.4.clone), kind=kLoop, calls=%fused_computation.2 | loop fusion | flops 2097152 | bytes 2101248 | tf_op jit(solution)/shard_map/convert_element_type | solution.py:49
  44.0 1.8 %collective-permute-done.8.refs_7_ = bf16[416,512]{1,0:T(8,128)(2,1)S(1)} collective-permute-done((bf16[416,512]{1,0:T(8,128)(2,1)S(1)}, bf16[416,512]{1,0:T(8,128)(2,1)S(1)}, u32[]{:S(2)}, u32[]{:S(2)}) %collective-permute-start.8) | collective-permute-done | bytes 426016 | tf_op jit(solution)/shard_map/ppermute | solution.py:241
  45.7 3.4 %copy-done = bf16[2,512,4096]{2,1,0:T(8,128)(2,1)S(1)} copy-done((bf16[2,512,4096]{2,1,0:T(8,128)(2,1)S(1)}, bf16[2,512,4096]{2,1,0:T(8,128)(2,1)}, u32[]{:S(2)}) %copy-start) | copy-done | bytes 8388632
  49.1 5.5 %shard_map.83 = (f32[128,2048]{1,0:T(8,128)S(1)}, bf16[8,2,128,128]{3,2,1,0:T(8,128)(2,1)S(1)}) custom-call(bf16[2,512,4096]{2,1,0:T(8,128)(2,1)S(1)} %copy-done, bf16[2,16,512]{2,1,0:T(8,128)(2,1)S(1)} %collective-permute-done.before, bf16[16,16,512]{2,1,0:T(8,128)(2,1)S(1)} %get-tuple-element.12.inner, ...), custom_call_target="tpu_custom_call" | custom-call | flops 2000000000 | bytes 4194304 | tf_op jit(solution)/shard_map/pallas_call | solution.py:246
  54.6 0.0 copy-start.2
  54.6 0.0 copy-start.4
  54.7 0.0 copy-start.5
  54.7 15.3 %all_to_all.5 = bf16[8,2,128,128]{3,2,1,0:T(8,128)(2,1)S(1)} all-to-all(bf16[8,2,128,128]{3,2,1,0:T(8,128)(2,1)S(1)} %get-tuple-element.16), channel_id=1, replica_groups=mesh['pi'=8,'pj'=4,'vert'=8] {'vert'}, dimensions={0} | all-to-all | bytes 1048576 | tf_op jit(solution)/shard_map/all_to_all | solution.py:261
  70.0 10.2 %collective-permute-start.10 = (bf16[8,128,128]{2,1,0:T(8,128)(2,1)S(1)}, bf16[8,128,128]{2,1,0:T(8,128)(2,1)S(1)}, u32[]{:S(2)}, u32[]{:S(2)}) collective-permute-start(bf16[8,128,128]{2,1,0:T(8,128)(2,1)S(1)} %get-tuple-element.17), channel_id=1, source_target_pairs={{0,32},{8,96},{16,160},{24,224},{32,0},{40,64},{48,128},{56,192},{... | collective-permute-start | bytes 786440 | tf_op jit(solution)/shard_map/ppermute | solution.py:262
  80.2 2.4 %collective-permute-start.9 = (bf16[8,128,128]{2,1,0:T(8,128)(2,1)S(1)}, bf16[8,128,128]{2,1,0:T(8,128)(2,1)S(1)}, u32[]{:S(2)}, u32[]{:S(2)}) collective-permute-start(bf16[8,128,128]{2,1,0:T(8,128)(2,1)S(1)} %get-tuple-element.18), channel_id=1, source_target_pairs={{0,0},{8,64},{16,128},{24,192},{32,32},{40,96},{48,160},{56,224},{... | collective-permute-start | bytes 786440 | tf_op jit(solution)/shard_map/ppermute | solution.py:262
  82.6 0.4 fusion.1.place
  83.0 15.4 %collective-permute-done.10.second = bf16[8,128,128]{2,1,0:T(8,128)(2,1)S(1)} collective-permute-done((bf16[8,128,128]{2,1,0:T(8,128)(2,1)S(1)}, bf16[8,128,128]{2,1,0:T(8,128)(2,1)S(1)}, u32[]{:S(2)}, u32[]{:S(2)}) %collective-permute-start.10) | collective-permute-done | bytes 262176 | tf_op jit(solution)/shard_map/ppermute | solution.py:262
  98.4 2.9 %collective-permute-done.9.first = bf16[8,128,128]{2,1,0:T(8,128)(2,1)S(1)} collective-permute-done((bf16[8,128,128]{2,1,0:T(8,128)(2,1)S(1)}, bf16[8,128,128]{2,1,0:T(8,128)(2,1)S(1)}, u32[]{:S(2)}, u32[]{:S(2)}) %collective-permute-start.9) | collective-permute-done | bytes 262176 | tf_op jit(solution)/shard_map/ppermute | solution.py:262
  101.3 3.8 %shard_map.84 = f32[8,16,8,512]{3,2,1,0:T(8,128)} custom-call(s32[2,2]{1,0:T(2,128)S(1)} %copy-done.2, s32[2,2]{1,0:T(2,128)S(1)} %copy-done.4, s32[8]{0:T(128)S(1)} %copy-done.5, f32[128,2048]{1,0:T(8,128)S(1)} %get-tuple-element.15.total_ref, bf16[8,128,128]{2,1,0:T(8,128)(2,1)S(1)} %collective-permute-done.9.first, ...), custom_call_target="tpu_custom_call" | custom-call | flops 1000000000 | bytes 4194304 | tf_op jit(solution)/shard_map/pallas_call | solution.py:263
  (14 shorter events, 0.1 us)
Async XLA Ops:
  1.0 0.7 copy-start.1
  1.7 0.7 copy-start.3
  2.3 1.2 %copy-start.6 = (bf16[8,16,8,512]{3,2,1,0:T(8,128)(2,1)S(1)}, bf16[8,16,8,512]{3,2,1,0:T(8,128)(2,1)}, u32[]{:S(2)}) copy-start(bf16[8,16,8,512]{3,2,1,0:T(8,128)(2,1)} %param.8) | copy-start | bytes 3145732
  4.9 12.3 %collective-permute-start.2 = (bf16[416,512]{1,0:T(8,128)(2,1)S(1)}, bf16[416,512]{1,0:T(8,128)(2,1)S(1)}, u32[]{:S(2)}, u32[]{:S(2)}) collective-permute-start(bf16[416,512]{1,0:T(8,128)(2,1)S(1)} %get-tuple-element.14.refs_0_), channel_id=1, source_target_pairs={{0,4},{1,5},{2,6},{3,7},{4,0},{5,1},{6,2},{7,3},{8,12},{9,13},{10,... | collective-permute-start | bytes 1277960 | tf_op jit(solution)/shard_map/ppermute | solution.py:235
  6.8 14.5 %collective-permute-start.3 = (bf16[416,512]{1,0:T(8,128)(2,1)S(1)}, bf16[416,512]{1,0:T(8,128)(2,1)S(1)}, u32[]{:S(2)}, u32[]{:S(2)}) collective-permute-start(bf16[416,512]{1,0:T(8,128)(2,1)S(1)} %get-tuple-element.14.refs_0_), channel_id=1, source_target_pairs={{0,1},{1,2},{2,3},{3,0},{4,5},{5,6},{6,7},{7,4},{8,9},{9,10},{10,1... | collective-permute-start | bytes 1277960 | tf_op jit(solution)/shard_map/ppermute | solution.py:236
  17.2 10.3 %collective-permute-start.6 = (bf16[416,512]{1,0:T(8,128)(2,1)S(1)}, bf16[416,512]{1,0:T(8,128)(2,1)S(1)}, u32[]{:S(2)}, u32[]{:S(2)}) collective-permute-start(bf16[416,512]{1,0:T(8,128)(2,1)S(1)} %collective-permute-done.2.refs_1_), channel_id=1, source_target_pairs={{0,3},{1,0},{2,1},{3,2},{4,7},{5,4},{6,5},{7,6},{8,11},{9,8},{10,9... | collective-permute-start | bytes 1277960 | tf_op jit(solution)/shard_map/ppermute | solution.py:239
  19.9 24.0 %collective-permute-start.4 = (bf16[416,512]{1,0:T(8,128)(2,1)S(1)}, bf16[416,512]{1,0:T(8,128)(2,1)S(1)}, u32[]{:S(2)}, u32[]{:S(2)}) collective-permute-start(bf16[416,512]{1,0:T(8,128)(2,1)S(1)} %get-tuple-element.14.refs_0_), channel_id=1, source_target_pairs={{0,3},{1,0},{2,1},{3,2},{4,7},{5,4},{6,5},{7,6},{8,11},{9,8},{10,9... | collective-permute-start | bytes 1277960 | tf_op jit(solution)/shard_map/ppermute | solution.py:237
  20.4 23.6 %collective-permute-start.5 = (bf16[416,512]{1,0:T(8,128)(2,1)S(1)}, bf16[416,512]{1,0:T(8,128)(2,1)S(1)}, u32[]{:S(2)}, u32[]{:S(2)}) collective-permute-start(bf16[416,512]{1,0:T(8,128)(2,1)S(1)} %collective-permute-done.2.refs_1_), channel_id=1, source_target_pairs={{0,1},{1,2},{2,3},{3,0},{4,5},{5,6},{6,7},{7,4},{8,9},{9,10},{10,1... | collective-permute-start | bytes 1277960 | tf_op jit(solution)/shard_map/ppermute | solution.py:238
  21.4 22.6 %collective-permute-start.7 = (bf16[416,512]{1,0:T(8,128)(2,1)S(1)}, bf16[416,512]{1,0:T(8,128)(2,1)S(1)}, u32[]{:S(2)}, u32[]{:S(2)}) collective-permute-start(bf16[416,512]{1,0:T(8,128)(2,1)S(1)} %collective-permute-done.3.refs_2_), channel_id=1, source_target_pairs={{0,1},{1,2},{2,3},{3,0},{4,5},{5,6},{6,7},{7,4},{8,9},{9,10},{10,1... | collective-permute-start | bytes 1277960 | tf_op jit(solution)/shard_map/ppermute | solution.py:240
  27.5 18.3 %collective-permute-start.8 = (bf16[416,512]{1,0:T(8,128)(2,1)S(1)}, bf16[416,512]{1,0:T(8,128)(2,1)S(1)}, u32[]{:S(2)}, u32[]{:S(2)}) collective-permute-start(bf16[416,512]{1,0:T(8,128)(2,1)S(1)} %collective-permute-done.6.refs_5_), channel_id=1, source_target_pairs={{0,3},{1,0},{2,1},{3,2},{4,7},{5,4},{6,5},{7,6},{8,11},{9,8},{10,9... | collective-permute-start | bytes 1277960 | tf_op jit(solution)/shard_map/ppermute | solution.py:241
  30.9 7.4 %collective-permute-start = (bf16[2,16,512]{2,1,0:T(8,128)(2,1)S(1)}, bf16[2,16,512]{2,1,0:T(8,128)(2,1)S(1)}, u32[]{:S(2)}, u32[]{:S(2)}) collective-permute-start(bf16[2,16,512]{2,1,0:T(8,128)(2,1)S(1)} %get-tuple-element.11), channel_id=1, source_target_pairs={{0,8},{8,16},{16,24},{1,9},{9,17},{17,25},{2,10},{10,18},{18,26},{... | collective-permute-start | bytes 98312 | tf_op jit(solution)/shard_map/ppermute | solution.py:242
  38.3 5.6 %collective-permute-start.1 = (bf16[2,16,512]{2,1,0:T(8,128)(2,1)S(1)}, bf16[2,16,512]{2,1,0:T(8,128)(2,1)S(1)}, u32[]{:S(2)}, u32[]{:S(2)}) collective-permute-start(bf16[2,16,512]{2,1,0:T(8,128)(2,1)S(1)} %get-tuple-element.13), channel_id=1, source_target_pairs={{8,0},{16,8},{24,16},{9,1},{17,9},{25,17},{10,2},{18,10},{26,18},{... | collective-permute-start | bytes 98312 | tf_op jit(solution)/shard_map/ppermute | solution.py:243
  45.7 3.4 %copy-start = (bf16[2,512,4096]{2,1,0:T(8,128)(2,1)S(1)}, bf16[2,512,4096]{2,1,0:T(8,128)(2,1)}, u32[]{:S(2)}) copy-start(bf16[2,512,4096]{2,1,0:T(8,128)(2,1)} %ladder_hbm.1) | copy-start | bytes 25165828
  49.1 33.5 %copy-start.7 = (s32[1024]{0:T(1024)S(1)}, s32[1024]{0:T(1024)}, u32[]{:S(2)}) copy-start(s32[1024]{0:T(1024)} %constant.5.clone) | copy-start | bytes 12292
  54.6 46.7 %copy-start.2 = (s32[2,2]{1,0:T(2,128)S(1)}, s32[2,2]{1,0:T(2,128)}, u32[]{:S(2)}) copy-start(s32[2,2]{1,0:T(2,128)} %ladder_tiles.3) | copy-start | bytes 52
  54.6 46.7 %copy-start.4 = (s32[2,2]{1,0:T(2,128)S(1)}, s32[2,2]{1,0:T(2,128)}, u32[]{:S(2)}) copy-start(s32[2,2]{1,0:T(2,128)} %cycle_tiles.3) | copy-start | bytes 52
  54.7 46.7 %copy-start.5 = (s32[8]{0:T(128)S(1)}, s32[8]{0:T(128)}, u32[]{:S(2)}) copy-start(s32[8]{0:T(128)} %partner.1) | copy-start | bytes 100
  70.0 28.4 %collective-permute-start.10 = (bf16[8,128,128]{2,1,0:T(8,128)(2,1)S(1)}, bf16[8,128,128]{2,1,0:T(8,128)(2,1)S(1)}, u32[]{:S(2)}, u32[]{:S(2)}) collective-permute-start(bf16[8,128,128]{2,1,0:T(8,128)(2,1)S(1)} %get-tuple-element.17), channel_id=1, source_target_pairs={{0,32},{8,96},{16,160},{24,224},{32,0},{40,64},{48,128},{56,192},{... | collective-permute-start | bytes 786440 | tf_op jit(solution)/shard_map/ppermute | solution.py:262
  80.2 21.1 %collective-permute-start.9 = (bf16[8,128,128]{2,1,0:T(8,128)(2,1)S(1)}, bf16[8,128,128]{2,1,0:T(8,128)(2,1)S(1)}, u32[]{:S(2)}, u32[]{:S(2)}) collective-permute-start(bf16[8,128,128]{2,1,0:T(8,128)(2,1)S(1)} %get-tuple-element.18), channel_id=1, source_target_pairs={{0,0},{8,64},{16,128},{24,192},{32,32},{40,96},{48,160},{56,224},{... | collective-permute-start | bytes 786440 | tf_op jit(solution)/shard_map/ppermute | solution.py:262

commit v3 on v2

v3 whole, which is shorter than its diff:
```python
import jax
import jax.numpy as jnp
import numpy as np
from jax import lax
from jax.experimental import pallas as pl
from jax.experimental.pallas import tpu as pltpu
from jax.sharding import PartitionSpec as P

TILE = 64
REACH = 2
BAND = 5
ROWS = 8
LANES = 512
PAIRS = 128
BF = jnp.bfloat16
F32 = jnp.float32
MIB = 1 << 20


def vert_moves(move):
    return [(v, move(v // 4, v % 4)) for v in range(8)]


FLIP = vert_moves(lambda h, y: (1 - h) * 4 + y)
UP = vert_moves(lambda h, y: h * 4 + (y + 1) % 4)
DOWN = vert_moves(lambda h, y: h * 4 + (y + 3) % 4)


def pair_moves(k):
    return [
        (p * 4 + q, (2 * q + ((p % 2) ^ k)) * 4 + p // 2) for p in range(8) for q in range(4)
    ]


def send_order():
    row = np.arange(1024)
    slot, a, v, b = row // 512, (row // 64) % 8, (row // 8) % 8, row % 8
    return v * 128 + slot * 64 + b * 8 + a


def place_order():
    row = np.arange(1024)
    v, slot, b, a = row // 128, (row // 64) % 2, (row // 8) % 8, row % 8
    return slot * 512 + b * 64 + v * 8 + a


def permutation(order):
    columns = lax.broadcasted_iota(jnp.int32, (1024, 1024), 1)
    return (jnp.asarray(order, jnp.int32)[:, None] == columns).astype(BF)


def prepare_kernel(ladder_tiles, cycle_tiles, amplitudes, ints, ladder_ref, ints_ref, inner_ref, first_ref, last_ref, wide, tall):
    row = lax.broadcasted_iota(jnp.int32, (512, 128), 0)
    column = lax.broadcasted_iota(jnp.int32, (512, 128), 1)
    ladder_row = row < 256
    i = row & 7
    j = jnp.where(ladder_row, (row >> 3) & 15, (row >> 4) & 15)
    which = jnp.where(ladder_row, (row >> 7) & 1, (row >> 3) & 1)
    ladder_0, cycle_0 = ladder_tiles[0, 1], cycle_tiles[0, 1]
    tile = jnp.where(
        ladder_row,
        ladder_0 + which * (ladder_tiles[1, 1] - ladder_0),
        cycle_0 + which * (cycle_tiles[1, 1] - cycle_0),
    )
    wanted = (i * 16 + j) * 8 + tile - column
    pick = jnp.concatenate(
        [jnp.where(wanted == c * 128, 1.0, 0.0).astype(BF) for c in range(8)], axis=1
    )
    picked = jnp.dot(pick, amplitudes[...], preferred_element_type=F32).astype(BF)
    ladder_ref[...] = picked[:256]
    inner = picked[256:].reshape(16, 16, LANES)
    inner_ref[...] = inner
    first_ref[...] = inner[:REACH]
    last_ref[...] = inner[16 - REACH :]
    for t in range(4):
        wide[t] = ints[:, t * 128 : (t + 1) * 128].astype(F32)
    low = lax.broadcasted_iota(jnp.int32, (80, 128), 1) < TILE
    for t in range(4):
        zero = wide[t, pl.ds(0, 80, stride=2), :]
        one = wide[t, pl.ds(1, 80, stride=2), :]
        tall[pl.ds(2 * t, 80, stride=8), :] = jnp.where(low, zero, pltpu.roll(one, TILE, 1))
        tall[pl.ds(2 * t + 1, 80, stride=8), :] = jnp.where(low, pltpu.roll(zero, TILE, 1), one)
    for b in range(4):
        ints_ref[:, b * 128 : (b + 1) * 128] = tall[b * 160 : (b + 1) * 160, :].astype(BF)


def split_pieces(refs, rows):
    own, flip, up, down, far, flip_far = refs
    vert = lax.axis_index("vert")
    h, y = vert // 4, vert % 4
    first, second = pl.ds(0, rows), pl.ds(rows, rows)
    pieces = [
        (h, y, own, first), (1 - h, y, flip, first),
        (h, y + 3, up, first), (1 - h, y + 3, up, second),
        (h, y + 1, down, first), (1 - h, y + 1, down, second),
        (h, y + 2, far, first), (1 - h, y + 2, flip_far, first),
    ]
    return [(a * 4 + b % 4, ref, where) for a, b, ref, where in pieces]


def pack(total, swap, sent_ref):
    parity = lax.axis_index("pi") % 2
    sent = jnp.dot(total[...].astype(BF), swap[...], preferred_element_type=F32).astype(BF)
    upper, under = sent[:64], sent[64:]
    halves = (jnp.where(parity == 0, upper, under), jnp.where(parity == 0, under, upper))
    for k in range(2):
        for v in range(8):
            sent_ref[v, k] = halves[k][:, v * 128 : (v + 1) * 128]


def ladder_kernel(ladder_hbm, swap, *refs):
    total_ref, sent_ref, ladder_ints, total, sem, sems = refs[6:]
    loads = [
        pltpu.make_async_copy(ladder_hbm.at[w], ladder_ints.at[w], sems.at[w]) for w in range(2)
    ]
    for load in loads:
        load.start()
    pieces = split_pieces(refs[:6], 256)
    for which in range(2):
        loads[which].wait()
        acc = None
        for source, ref, where in pieces:
            start = pl.multiple_of(source * LANES, LANES)
            part = lax.dot_general(
                ref[pl.ds(where.start + which * PAIRS, PAIRS), :],
                ladder_ints[which, :, pl.ds(start, LANES)],
                (((1,), (1,)), ((), ())),
                preferred_element_type=F32,
            )
            acc = part if acc is None else acc + part
        total[:, which * LANES : (which + 1) * LANES] = acc
    keep = pltpu.make_async_copy(total, total_ref, sem)
    keep.start()
    pack(total, swap, sent_ref)
    keep.wait()


def cycle_kernel(before, inner, after, swap, *refs):
    total_ref, sent_ref, ints, total, sem = refs[6:]
    for source, ref, where in split_pieces(refs[:6], 160):
        ints[source] = ref[where, :].astype(F32)

    def rows_of(j):
        if j < REACH:
            return before[j]
        if j < REACH + 16:
            return inner[j - REACH]
        return after[j - REACH - 16]

    laid = []
    for j in range(16 + 2 * REACH):
        block = rows_of(j)
        laid.append(
            jnp.concatenate([block[:, a * TILE : (a + 1) * TILE] for a in range(ROWS)], axis=0)
        )
    low = lax.broadcasted_iota(jnp.int32, (8, 128), 1) < TILE
    for j in range(16):
        left = jnp.concatenate([laid[j + o] for o in range(BAND)], axis=1)
        base, lanes = (j % 4) * 40, (j // 4) * 128
        right = jnp.concatenate(
            [
                ints[v, base + o * 8 : base + o * 8 + 8, lanes : lanes + 128]
                for o in range(BAND)
                for v in range(8)
            ],
            axis=0,
        ).astype(BF)
        done = jnp.dot(left, right, preferred_element_type=F32)
        for r in range(2):
            for t in range(4):
                even = done[t * 32 + r * 8 : t * 32 + r * 8 + 8]
                odd = done[t * 32 + 16 + r * 8 : t * 32 + 16 + r * 8 + 8]
                if r == 0:
                    odd = pltpu.roll(odd, TILE, 1)
                else:
                    even = pltpu.roll(even, TILE, 1)
                lane = r * LANES + t * 128
                total[j * 8 : j * 8 + 8, lane : lane + 128] = jnp.where(low, even, odd)
    keep = pltpu.make_async_copy(total, total_ref, sem)
    keep.start()
    pack(total, swap, sent_ref)
    keep.wait()


def finish_kernel(ladder_tiles, cycle_tiles, partner, ladder_total, cycle_total, place, *refs):
    arrived, (out_ref, mirrored, total, sems) = refs[:4], refs[4:]
    fetches = [
        pltpu.make_async_copy(source, total.at[s], sems.at[s])
        for s, source in enumerate((ladder_total, cycle_total))
    ]
    for fetch in fetches:
        fetch.start()
    parity = lax.axis_index("pi") % 2
    for s in range(2):
        for k in range(2):
            block = arrived[s * 2 + k]
            wide = jnp.concatenate([block[v] for v in range(8)], axis=1)
            mirrored[s, parity ^ k] = jnp.dot(wide, place[...], preferred_element_type=F32)
    dests = [ladder_tiles[0, 0], ladder_tiles[1, 0], cycle_tiles[0, 0], cycle_tiles[1, 0]]
    tile = lax.broadcasted_iota(jnp.int32, (8, LANES), 0)
    own = [(tile == dest).astype(F32) for dest in dests]
    other = [(tile == partner[dest]).astype(F32) for dest in dests]
    for fetch in fetches:
        fetch.wait()

    def one(i):
        for j in range(16):
            acc = None
            for s in range(4):
                lanes = slice((s % 2) * LANES, (s % 2 + 1) * LANES)
                term = own[s] * total[s // 2, pl.ds(j * 8 + i, 1), lanes]
                acc = term if acc is None else acc + term
                acc = acc + other[s] * mirrored[s // 2, j // 8, pl.ds(i * 8 + j % 8, 1), lanes]
            out_ref[i, j] = acc

    pl.loop(0, 8)(one)


SMEM = pl.BlockSpec(memory_space=pltpu.SMEM)
VMEM = pl.BlockSpec(memory_space=pltpu.VMEM)
ANY = pl.BlockSpec(memory_space=pl.ANY)


def call(kernel, ins, outs, out_specs, scratch, limit, flops):
    return pl.pallas_call(
        kernel,
        out_shape=outs,
        in_specs=ins,
        out_specs=out_specs,
        scratch_shapes=scratch,
        compiler_params=pltpu.CompilerParams(vmem_limit_bytes=limit * MIB),
        cost_estimate=pl.CostEstimate(flops=flops, bytes_accessed=4 * MIB, transcendentals=0),
    )


def shape(dims, kind):
    return jax.ShapeDtypeStruct(dims, kind)


def gather(own):
    rows = own.shape[0]
    flip = lax.ppermute(own, "vert", FLIP)
    both = jnp.concatenate([own, flip])
    up = lax.ppermute(both, "vert", UP)
    down = lax.ppermute(both, "vert", DOWN)
    far = lax.ppermute(up[:rows], "vert", UP)
    flip_far = lax.ppermute(down[rows:], "vert", DOWN)
    return [own, flip, up, down, far, flip_far]


def exchange(sent):
    arrived = lax.all_to_all(sent, "vert", 0, 0)
    return [lax.ppermute(arrived[:, k], ("pi", "pj"), pair_moves(k)) for k in range(2)]


def body(amplitudes, ladder_ints, ladder_tiles, cycle_ints, cycle_tiles, partner):
    edge = shape((REACH, 16, LANES), BF)
    ladder_own, ints_own, inner, first, last = call(
        prepare_kernel,
        [SMEM, SMEM, VMEM, VMEM],
        [shape((256, LANES), BF), shape((160, LANES), BF), shape((16, 16, LANES), BF), edge, edge],
        [VMEM] * 5,
        [pltpu.VMEM((4, 160, 128), F32), pltpu.VMEM((640, 128), F32)],
        12,
        10**9,
    )(ladder_tiles, cycle_tiles, amplitudes.reshape(1024, LANES), cycle_ints.reshape(160, LANES))
    swap, place = permutation(send_order()), permutation(place_order())
    outs = [shape((PAIRS, 1024), F32), shape((8, 2, 64, 128), BF)]

    ints_pieces = gather(ints_own)
    before = lax.ppermute(last, "pj", [(q, q + 1) for q in range(3)])
    after = lax.ppermute(first, "pj", [(q + 1, q) for q in range(3)])
    cycle_total, cycle_sent = call(
        cycle_kernel,
        [VMEM] * 10,
        outs,
        [ANY, VMEM],
        [
            pltpu.VMEM((8, 160, LANES), F32),
            pltpu.VMEM((PAIRS, 1024), F32),
            pltpu.SemaphoreType.DMA,
        ],
        16,
        10**9,
    )(before, inner, after, swap, *ints_pieces)
    cycle_moved = exchange(cycle_sent)

    ladder_pieces = gather(ladder_own)
    ladder_total, ladder_sent = call(
        ladder_kernel,
        [ANY] + [VMEM] * 7,
        outs,
        [ANY, VMEM],
        [
            pltpu.VMEM((2, LANES, 4096), BF),
            pltpu.VMEM((PAIRS, 1024), F32),
            pltpu.SemaphoreType.DMA,
            pltpu.SemaphoreType.DMA((2,)),
        ],
        50,
        2 * 10**9,
    )(ladder_ints, swap, *ladder_pieces)
    ladder_moved = exchange(ladder_sent)

    return call(
        finish_kernel,
        [SMEM, SMEM, SMEM, ANY, ANY] + [VMEM] * 5,
        shape((8, 16, 8, LANES), F32),
        VMEM,
        [
            pltpu.VMEM((2, 2, 64, 1024), F32),
            pltpu.VMEM((2, PAIRS, 1024), F32),
            pltpu.SemaphoreType.DMA((2,)),
        ],
        16,
        10**9,
    )(ladder_tiles, cycle_tiles, partner, ladder_total, cycle_total, place, *ladder_moved, *cycle_moved)


def solution(mesh):
    placed = (
        P("pi", "pj", None, "vert"),
        P(None, "vert", None),
        P(),
        P("pj", None, None, "vert"),
        P(),
        P(),
    )
    return jax.shard_map(
        body, mesh=mesh, in_specs=placed, out_specs=P("pi", "pj", None, "vert"), check_vma=False
    )
```

time: 105 us -> 113 us (1.076)
  starting transfers between devices: 29.2 us -> 51.3 us
  blocking collectives: 15.3 us -> 0 us
  waiting for transfers between devices: 41.3 us -> 32.4 us
  local copies, waits for them, and re-layouts: 7 us -> 12.1 us
  Pallas kernels: 10.6 us -> 15 us
    all_to_all x1 -> x0, blocking collectives: 15.3 us -> none  [body(): arrived = lax.all_to_all(sent, 'vert', 0, 0)]
    all_to_all x0 -> x2, starting transfers between devices: none -> 11.8 us  [exchange(): arrived = lax.all_to_all(sent, 'vert', 0, 0)]
    ppermute x9 -> x14, starting transfers between devices: 23.4 us -> 32.8 us  [the longest x4 18.4 us: exchange(): lax.ppermute(arrived[:, k], ('pi', 'pj'), pair_moves(k))]
    ppermute x1, waiting for transfers between devices: 6.12 us -> 0.01 us  [body(): before = lax.ppermute(last, 'pj', [(q, q + 1) for q in range(3)])]
    pallas_call x3 -> x4, Pallas kernels: 10.6 us -> 15 us  [the longest x1 7.38 us: body(): call(ladder_kernel, [ANY] + [VMEM] * 7, outs, [ANY, VMEM], [pltpu.VMEM((2...]
    ppermute x9 -> x14, waiting for transfers between devices: 35.2 us -> 32.4 us  [the longest x4 14.7 us: exchange(): lax.ppermute(arrived[:, k], ('pi', 'pj'), pair_moves(k))]
    unnamed x16 -> x36, local copies, waits for them, and re-layouts: 5.98 us -> 8.62 us
    slice x0 -> x4, local copies, waits for them, and re-layouts: none -> 1.46 us  [the longest x2 0.73 us: gather(): flip_far = lax.ppermute(down[rows:], 'vert', DOWN)]
  transfers between devices with their start and end apart: 11 -> 18, of which waited for: 6 -> 7; matrix products, arithmetic and copies ran while one was open for 1% -> 3% of each run, Pallas kernels for 0% -> 8%
where the time goes in v3:
time: 113 us; the launch traced here: 112 us
  starting transfers between devices  51.3 us (45%)
  waiting for transfers between devices  32.4 us (29%)
  Pallas kernels  15 us (13%)
  local copies, waits for them, and re-layouts  12.1 us (11%)
    ppermute x4, starting transfers between devices, exchange(): lax.ppermute(arrived[:, k], ('pi', 'pj'), pair_moves(k))  18.4 us
    ppermute x4, waiting for transfers between devices, exchange(): lax.ppermute(arrived[:, k], ('pi', 'pj'), pair_moves(k))  14.7 us
    all_to_all x2, starting transfers between devices, exchange(): arrived = lax.all_to_all(sent, 'vert', 0, 0)  11.8 us
    ppermute x2, waiting for transfers between devices, gather(): up = lax.ppermute(both, 'vert', UP)  11.5 us
    unnamed x36, local copies, waits for them, and re-layouts  8.62 us
    pallas_call x1, Pallas kernels, body(): call(ladder_kernel, [ANY] + [VMEM] * 7, outs, [ANY, VMEM], [pltpu.VMEM((2...  7.38 us
    ppermute x2, waiting for transfers between devices, gather(): flip = lax.ppermute(own, 'vert', FLIP)  6.25 us
    ppermute x1, starting transfers between devices, body(): after = lax.ppermute(first, 'pj', [(q + 1, q) for q in range(3)])  5.46 us
  transfers between devices with their start and end apart: 18, of which 7 were waited for; matrix products, arithmetic and copies ran while one was open for 3% of the time, Pallas kernels for 8%

profile of v3, /device:TPU:3, one launch (start us, length us, event | category | flops | bytes accessed | tf_op | source)
XLA Modules:
  0.0 112.0 jit_solution(258586784122941522)
XLA Ops:
  0.0 1.0 reshape.9.ints
  2.4 1.2 %copy-done.14 = bf16[8,16,8,512]{3,2,1,0:T(8,128)(2,1)S(1)} copy-done((bf16[8,16,8,512]{3,2,1,0:T(8,128)(2,1)S(1)}, bf16[8,16,8,512]{3,2,1,0:T(8,128)(2,1)}, u32[]{:S(2)}) %copy-start.14) | copy-done | bytes 1048600
  3.6 1.3 %shard_map.82 = (bf16[256,512]{1,0:T(8,128)(2,1)S(1)}, bf16[160,512]{1,0:T(8,128)(2,1)S(1)}, bf16[16,16,512]{2,1,0:T(8,128)(2,1)S(1)}, bf16[2,16,512]{2,1,0:T(8,128)(2,1)S(1)}, bf16[2,16,512]{2,1,0:T(8,128)(2,1)S(1)}) custom-call(s32[2,2]{1,0:T(2,128)S(1)} %copy-done.9, s32[2,2]{1,0:T(2,128)S(1)} %copy-done.11, bf16[1024,512]{1,0:T(8,128)(2,1)S(1)} %bitcast.17, ...), custom_call_target="tpu_custom_call" | custom-call | flops 1000000000 | bytes 4194304 | tf_op jit(solution)/shard_map/pallas_call | solution.py:258
  4.9 1.9 %collective-permute-start = (bf16[256,512]{1,0:T(8,128)(2,1)S(1)}, bf16[256,512]{1,0:T(8,128)(2,1)S(1)}, u32[]{:S(2)}, u32[]{:S(2)}) collective-permute-start(bf16[256,512]{1,0:T(8,128)(2,1)S(1)} %get-tuple-element.14.refs_0_), channel_id=1, source_target_pairs={{0,4},{1,5},{2,6},{3,7},{4,0},{5,1},{6,2},{7,3},{8,12},{9,13},{10,... | collective-permute-start | bytes 786440 | tf_op jit(solution)/shard_map/ppermute | solution.py:242
  6.8 1.1 %collective-permute-start.7 = (bf16[160,512]{1,0:T(8,128)(2,1)S(1)}, bf16[160,512]{1,0:T(8,128)(2,1)S(1)}, u32[]{:S(2)}, u32[]{:S(2)}) collective-permute-start(bf16[160,512]{1,0:T(8,128)(2,1)S(1)} %get-tuple-element.19.refs_0_), channel_id=1, source_target_pairs={{0,4},{1,5},{2,6},{3,7},{4,0},{5,1},{6,2},{7,3},{8,12},{9,13},{10,... | collective-permute-start | bytes 491528 | tf_op jit(solution)/shard_map/ppermute | solution.py:242
  8.0 5.7 %collective-permute-done.refs_1_ = bf16[256,512]{1,0:T(8,128)(2,1)S(1)} collective-permute-done((bf16[256,512]{1,0:T(8,128)(2,1)S(1)}, bf16[256,512]{1,0:T(8,128)(2,1)S(1)}, u32[]{:S(2)}, u32[]{:S(2)}) %collective-permute-start) | collective-permute-done | bytes 262176 | tf_op jit(solution)/shard_map/ppermute | solution.py:242
  13.7 1.4 %collective-permute-start.1 = (bf16[512,512]{1,0:T(8,128)(2,1)S(1)}, bf16[512,512]{1,0:T(8,128)(2,1)S(1)}, u32[]{:S(2)}, u32[]{:S(2)}) collective-permute-start(bf16[512,512]{1,0:T(8,128)(2,1)S(1)} %constant_dynamic-update-slice_fusion), channel_id=1, source_target_pairs={{0,1},{1,2},{2,3},{3,0},{4,5},{5,6},{6,7},{7,4},{8,9},{9,10},{10,1... | collective-permute-start | bytes 1572872 | tf_op jit(solution)/shard_map/ppermute | solution.py:244
  15.1 1.5 %collective-permute-start.2 = (bf16[512,512]{1,0:T(8,128)(2,1)S(1)}, bf16[512,512]{1,0:T(8,128)(2,1)S(1)}, u32[]{:S(2)}, u32[]{:S(2)}) collective-permute-start(bf16[512,512]{1,0:T(8,128)(2,1)S(1)} %constant_dynamic-update-slice_fusion), channel_id=1, source_target_pairs={{0,3},{1,0},{2,1},{3,2},{4,7},{5,4},{6,5},{7,6},{8,11},{9,8},{10,9... | collective-permute-start | bytes 1572872 | tf_op jit(solution)/shard_map/ppermute | solution.py:245
  17.2 1.4 %collective-permute-start.8 = (bf16[320,512]{1,0:T(8,128)(2,1)S(1)}, bf16[320,512]{1,0:T(8,128)(2,1)S(1)}, u32[]{:S(2)}, u32[]{:S(2)}) collective-permute-start(bf16[320,512]{1,0:T(8,128)(2,1)S(1)} %constant_dynamic-update-slice_fusion.2), channel_id=1, source_target_pairs={{0,1},{1,2},{2,3},{3,0},{4,5},{5,6},{6,7},{7,4},{8,9},{9,10},{10,1... | collective-permute-start | bytes 983048 | tf_op jit(solution)/shard_map/ppermute | solution.py:244
  18.6 1.5 %collective-permute-start.9 = (bf16[320,512]{1,0:T(8,128)(2,1)S(1)}, bf16[320,512]{1,0:T(8,128)(2,1)S(1)}, u32[]{:S(2)}, u32[]{:S(2)}) collective-permute-start(bf16[320,512]{1,0:T(8,128)(2,1)S(1)} %constant_dynamic-update-slice_fusion.2), channel_id=1, source_target_pairs={{0,3},{1,0},{2,1},{3,2},{4,7},{5,4},{6,5},{7,6},{8,11},{9,8},{10,9... | collective-permute-start | bytes 983048 | tf_op jit(solution)/shard_map/ppermute | solution.py:245
  20.1 1.3 %collective-permute-start.5 = (bf16[2,16,512]{2,1,0:T(8,128)(2,1)S(1)}, bf16[2,16,512]{2,1,0:T(8,128)(2,1)S(1)}, u32[]{:S(2)}, u32[]{:S(2)}) collective-permute-start(bf16[2,16,512]{2,1,0:T(8,128)(2,1)S(1)} %get-tuple-element.16), channel_id=1, source_target_pairs={{0,8},{8,16},{16,24},{1,9},{9,17},{17,25},{2,10},{10,18},{18,26},{... | collective-permute-start | bytes 98312 | tf_op jit(solution)/shard_map/ppermute | solution.py:271
  21.4 11.5 %collective-permute-done.8.refs_2_ = bf16[320,512]{1,0:T(8,128)(2,1)S(1)} collective-permute-done((bf16[320,512]{1,0:T(8,128)(2,1)S(1)}, bf16[320,512]{1,0:T(8,128)(2,1)S(1)}, u32[]{:S(2)}, u32[]{:S(2)}) %collective-permute-start.8) | collective-permute-done | bytes 327712 | tf_op jit(solution)/shard_map/ppermute | solution.py:244
  32.8 5.5 %collective-permute-start.6 = (bf16[2,16,512]{2,1,0:T(8,128)(2,1)S(1)}, bf16[2,16,512]{2,1,0:T(8,128)(2,1)S(1)}, u32[]{:S(2)}, u32[]{:S(2)}) collective-permute-start(bf16[2,16,512]{2,1,0:T(8,128)(2,1)S(1)} %get-tuple-element.18), channel_id=1, source_target_pairs={{8,0},{16,8},{24,16},{9,1},{17,9},{25,17},{10,2},{18,10},{26,18},{... | collective-permute-start | bytes 98312 | tf_op jit(solution)/shard_map/ppermute | solution.py:272
  38.5 2.7 %collective-permute-start.11 = (bf16[160,512]{1,0:T(8,128)(2,1)S(1)}, bf16[160,512]{1,0:T(8,128)(2,1)S(1)}, u32[]{:S(2)}, u32[]{:S(2)}) collective-permute-start(bf16[160,512]{1,0:T(8,128)(2,1)S(1)} %slice.35), channel_id=1, source_target_pairs={{0,3},{1,0},{2,1},{3,2},{4,7},{5,4},{6,5},{7,6},{8,11},{9,8},{10,9... | collective-permute-start | bytes 491528 | tf_op jit(solution)/shard_map/ppermute | solution.py:247
  42.6 2.7 %collective-permute-start.4 = (bf16[256,512]{1,0:T(8,128)(2,1)}, bf16[256,512]{1,0:T(8,128)(2,1)}, u32[]{:S(2)}, u32[]{:S(2)}) collective-permute-start(bf16[256,512]{1,0:T(8,128)(2,1)} %slice.33), channel_id=1, source_target_pairs={{0,3},{1,0},{2,1},{3,2},{4,7},{5,4},{6,5},{7,6},{8,11},{9,8},{10,9... | collective-permute-start | bytes 786440 | tf_op jit(solution)/shard_map/ppermute | solution.py:247
  45.8 1.6 %shard_map.84 = (f32[128,1024]{1,0:T(8,128)S(1)}, bf16[8,2,64,128]{3,2,1,0:T(8,128)(2,1)S(1)}) custom-call(bf16[2,16,512]{2,1,0:T(8,128)(2,1)S(1)} %collective-permute-done.5.before, bf16[16,16,512]{2,1,0:T(8,128)(2,1)S(1)} %get-tuple-element.17.inner, bf16[2,16,512]{2,1,0:T(8,128)(2,1)S(1)} %collective-permute-done.6.after, ...), custom_call_target="tpu_custom_call" | custom-call | flops 1000000000 | bytes 4194304 | tf_op jit(solution)/shard_map/pallas_call | solution.py:273
  47.4 0.8 copy-done.3
  48.9 5.1 %all-to-all-start.1 = ((bf16[8,2,64,128]{3,2,1,0:T(8,128)(2,1)}), bf16[8,2,64,128]{3,2,1,0:T(8,128)(2,1)}, u32[]{:S(2)}, u32[]{:S(2)}) async-start(bf16[8,2,64,128]{3,2,1,0:T(8,128)(2,1)} %copy-done.7), calls=%async_computation.1 | async-start | bytes 524288 | tf_op jit(solution)/shard_map/all_to_all | solution.py:252
  54.1 0.9 copy-done.2
  55.0 7.4 %shard_map.83 = (f32[128,1024]{1,0:T(8,128)S(1)}, bf16[8,2,64,128]{3,2,1,0:T(8,128)(2,1)S(1)}) custom-call(bf16[2,512,4096]{2,1,0:T(8,128)(2,1)} %ladder_hbm.1, bf16[1024,1024]{1,0:T(8,128)(2,1)} %copy-done, bf16[256,512]{1,0:T(8,128)(2,1)S(1)} %get-tuple-element.14.refs_0_, bf16[256,512]{1,0:T(8,128)(2,1)S(1)} %copy-done.2, ...), custom_call_target="tpu_custom_call" | custom-call | flops 2000000000 | bytes 4194304 | tf_op jit(solution)/shard_map/pallas_call | solution.py:289
  62.4 0.8 copy-done.5
  63.9 6.6 %all-to-all-start = ((bf16[8,2,64,128]{3,2,1,0:T(8,128)(2,1)}), bf16[8,2,64,128]{3,2,1,0:T(8,128)(2,1)S(1)}, u32[]{:S(2)}, u32[]{:S(2)}) async-start(bf16[8,2,64,128]{3,2,1,0:T(8,128)(2,1)} %copy-done.8), calls=%async_computation | async-start | bytes 524288 | tf_op jit(solution)/shard_map/all_to_all | solution.py:252
  70.5 1.0 slice_bitcast_fusion
  71.5 10.6 %collective-permute-start.14 = (bf16[8,64,128]{2,1,0:T(8,128)(2,1)S(1)}, bf16[8,64,128]{2,1,0:T(8,128)(2,1)S(1)}, u32[]{:S(2)}, u32[]{:S(2)}) collective-permute-start(bf16[8,64,128]{2,1,0:T(8,128)(2,1)S(1)} %get-tuple-element.24), channel_id=1, source_target_pairs={{0,0},{8,64},{16,128},{24,192},{32,32},{40,96},{48,160},{56,224},{... | collective-permute-start | bytes 393224 | tf_op jit(solution)/shard_map/ppermute | solution.py:253
  82.3 7.6 %collective-permute-start.12 = (bf16[8,64,128]{2,1,0:T(8,128)(2,1)S(1)}, bf16[8,64,128]{2,1,0:T(8,128)(2,1)S(1)}, u32[]{:S(2)}, u32[]{:S(2)}) collective-permute-start(bf16[8,64,128]{2,1,0:T(8,128)(2,1)S(1)} %get-tuple-element.26), channel_id=1, source_target_pairs={{0,0},{8,64},{16,128},{24,192},{32,32},{40,96},{48,160},{56,224},{... | collective-permute-start | bytes 393224 | tf_op jit(solution)/shard_map/ppermute | solution.py:253
  90.5 8.3 %collective-permute-done.14.refs_2_ = bf16[8,64,128]{2,1,0:T(8,128)(2,1)S(1)} collective-permute-done((bf16[8,64,128]{2,1,0:T(8,128)(2,1)S(1)}, bf16[8,64,128]{2,1,0:T(8,128)(2,1)S(1)}, u32[]{:S(2)}, u32[]{:S(2)}) %collective-permute-start.14) | collective-permute-done | bytes 131104 | tf_op jit(solution)/shard_map/ppermute | solution.py:253
  98.7 3.0 %collective-permute-done.15.refs_3_ = bf16[8,64,128]{2,1,0:T(8,128)(2,1)S(1)} collective-permute-done((bf16[8,64,128]{2,1,0:T(8,128)(2,1)S(1)}, bf16[8,64,128]{2,1,0:T(8,128)(2,1)S(1)}, u32[]{:S(2)}, u32[]{:S(2)}) %collective-permute-start.15) | collective-permute-done | bytes 131104 | tf_op jit(solution)/shard_map/ppermute | solution.py:253
  101.7 2.0 %collective-permute-done.12.refs_0_ = bf16[8,64,128]{2,1,0:T(8,128)(2,1)S(1)} collective-permute-done((bf16[8,64,128]{2,1,0:T(8,128)(2,1)S(1)}, bf16[8,64,128]{2,1,0:T(8,128)(2,1)S(1)}, u32[]{:S(2)}, u32[]{:S(2)}) %collective-permute-start.12) | collective-permute-done | bytes 131104 | tf_op jit(solution)/shard_map/ppermute | solution.py:253
  103.7 1.4 %collective-permute-done.13.refs_1_ = bf16[8,64,128]{2,1,0:T(8,128)(2,1)S(1)} collective-permute-done((bf16[8,64,128]{2,1,0:T(8,128)(2,1)S(1)}, bf16[8,64,128]{2,1,0:T(8,128)(2,1)S(1)}, u32[]{:S(2)}, u32[]{:S(2)}) %collective-permute-start.13) | collective-permute-done | bytes 131104 | tf_op jit(solution)/shard_map/ppermute | solution.py:253
  105.1 1.0 copy-done.4
  106.2 1.0 copy-done.6
  107.2 4.6 %shard_map.85 = f32[8,16,8,512]{3,2,1,0:T(8,128)} custom-call(s32[2,2]{1,0:T(2,128)S(1)} %copy-done.10, s32[2,2]{1,0:T(2,128)S(1)} %copy-done.12, s32[8]{0:T(128)S(1)} %copy-done.13, f32[128,1024]{1,0:T(8,128)S(1)} %copy-done.6, f32[128,1024]{1,0:T(8,128)S(1)} %copy-done.4, bf16[1024,1024]{1,0:T(8,128)(2,1)S(1)} %fusion.1.place, ...), custom_call_target="tpu_custom_call" | custom-call | flops 1000000000 | bytes 4194304 | tf_op jit(solution)/shard_map/pallas_call | solution.py:305
  (55 shorter events, 6.0 us)
Async XLA Ops:
  0.0 45.3 %copy-start.16 = (s32[1024]{0:T(1024)S(1)}, s32[1024]{0:T(1024)}, u32[]{:S(2)}) copy-start(s32[1024]{0:T(1024)} %constant.4.clone) | copy-start | bytes 12292
  2.4 1.2 %copy-start.14 = (bf16[8,16,8,512]{3,2,1,0:T(8,128)(2,1)S(1)}, bf16[8,16,8,512]{3,2,1,0:T(8,128)(2,1)}, u32[]{:S(2)}) copy-start(bf16[8,16,8,512]{3,2,1,0:T(8,128)(2,1)} %param.8) | copy-start | bytes 3145732
  4.9 8.8 %collective-permute-start = (bf16[256,512]{1,0:T(8,128)(2,1)S(1)}, bf16[256,512]{1,0:T(8,128)(2,1)S(1)}, u32[]{:S(2)}, u32[]{:S(2)}) collective-permute-start(bf16[256,512]{1,0:T(8,128)(2,1)S(1)} %get-tuple-element.14.refs_0_), channel_id=1, source_target_pairs={{0,4},{1,5},{2,6},{3,7},{4,0},{5,1},{6,2},{7,3},{8,12},{9,13},{10,... | collective-permute-start | bytes 786440 | tf_op jit(solution)/shard_map/ppermute | solution.py:242
  6.8 10.3 %collective-permute-start.7 = (bf16[160,512]{1,0:T(8,128)(2,1)S(1)}, bf16[160,512]{1,0:T(8,128)(2,1)S(1)}, u32[]{:S(2)}, u32[]{:S(2)}) collective-permute-start(bf16[160,512]{1,0:T(8,128)(2,1)S(1)} %get-tuple-element.19.refs_0_), channel_id=1, source_target_pairs={{0,4},{1,5},{2,6},{3,7},{4,0},{5,1},{6,2},{7,3},{8,12},{9,13},{10,... | collective-permute-start | bytes 491528 | tf_op jit(solution)/shard_map/ppermute | solution.py:242
  13.7 29.0 %copy-start.1 = (bf16[256,512]{1,0:T(8,128)(2,1)}, bf16[256,512]{1,0:T(8,128)(2,1)S(1)}, u32[]{:S(2)}) copy-start(bf16[256,512]{1,0:T(8,128)(2,1)S(1)} %collective-permute-done.refs_1_) | copy-start | bytes 786436
  13.7 24.8 %collective-permute-start.1 = (bf16[512,512]{1,0:T(8,128)(2,1)S(1)}, bf16[512,512]{1,0:T(8,128)(2,1)S(1)}, u32[]{:S(2)}, u32[]{:S(2)}) collective-permute-start(bf16[512,512]{1,0:T(8,128)(2,1)S(1)} %constant_dynamic-update-slice_fusion), channel_id=1, source_target_pairs={{0,1},{1,2},{2,3},{3,0},{4,5},{5,6},{6,7},{7,4},{8,9},{9,10},{10,1... | collective-permute-start | bytes 1572872 | tf_op jit(solution)/shard_map/ppermute | solution.py:244
  15.1 26.8 %collective-permute-start.2 = (bf16[512,512]{1,0:T(8,128)(2,1)S(1)}, bf16[512,512]{1,0:T(8,128)(2,1)S(1)}, u32[]{:S(2)}, u32[]{:S(2)}) collective-permute-start(bf16[512,512]{1,0:T(8,128)(2,1)S(1)} %constant_dynamic-update-slice_fusion), channel_id=1, source_target_pairs={{0,3},{1,0},{2,1},{3,2},{4,7},{5,4},{6,5},{7,6},{8,11},{9,8},{10,9... | collective-permute-start | bytes 1572872 | tf_op jit(solution)/shard_map/ppermute | solution.py:245
  17.2 15.6 %collective-permute-start.8 = (bf16[320,512]{1,0:T(8,128)(2,1)S(1)}, bf16[320,512]{1,0:T(8,128)(2,1)S(1)}, u32[]{:S(2)}, u32[]{:S(2)}) collective-permute-start(bf16[320,512]{1,0:T(8,128)(2,1)S(1)} %constant_dynamic-update-slice_fusion.2), channel_id=1, source_target_pairs={{0,1},{1,2},{2,3},{3,0},{4,5},{5,6},{6,7},{7,4},{8,9},{9,10},{10,1... | collective-permute-start | bytes 983048 | tf_op jit(solution)/shard_map/ppermute | solution.py:244
  18.6 19.8 %collective-permute-start.9 = (bf16[320,512]{1,0:T(8,128)(2,1)S(1)}, bf16[320,512]{1,0:T(8,128)(2,1)S(1)}, u32[]{:S(2)}, u32[]{:S(2)}) collective-permute-start(bf16[320,512]{1,0:T(8,128)(2,1)S(1)} %constant_dynamic-update-slice_fusion.2), channel_id=1, source_target_pairs={{0,3},{1,0},{2,1},{3,2},{4,7},{5,4},{6,5},{7,6},{8,11},{9,8},{10,9... | collective-permute-start | bytes 983048 | tf_op jit(solution)/shard_map/ppermute | solution.py:245
  20.1 22.5 %collective-permute-start.5 = (bf16[2,16,512]{2,1,0:T(8,128)(2,1)S(1)}, bf16[2,16,512]{2,1,0:T(8,128)(2,1)S(1)}, u32[]{:S(2)}, u32[]{:S(2)}) collective-permute-start(bf16[2,16,512]{2,1,0:T(8,128)(2,1)S(1)} %get-tuple-element.16), channel_id=1, source_target_pairs={{0,8},{8,16},{16,24},{1,9},{9,17},{17,25},{2,10},{10,18},{18,26},{... | collective-permute-start | bytes 98312 | tf_op jit(solution)/shard_map/ppermute | solution.py:271
  32.8 12.9 %collective-permute-start.6 = (bf16[2,16,512]{2,1,0:T(8,128)(2,1)S(1)}, bf16[2,16,512]{2,1,0:T(8,128)(2,1)S(1)}, u32[]{:S(2)}, u32[]{:S(2)}) collective-permute-start(bf16[2,16,512]{2,1,0:T(8,128)(2,1)S(1)} %get-tuple-element.18), channel_id=1, source_target_pairs={{8,0},{16,8},{24,16},{9,1},{17,9},{25,17},{10,2},{18,10},{26,18},{... | collective-permute-start | bytes 98312 | tf_op jit(solution)/shard_map/ppermute | solution.py:272
  38.3 7.4 %collective-permute-start.10 = (bf16[160,512]{1,0:T(8,128)(2,1)S(1)}, bf16[160,512]{1,0:T(8,128)(2,1)S(1)}, u32[]{:S(2)}, u32[]{:S(2)}) collective-permute-start(bf16[160,512]{1,0:T(8,128)(2,1)S(1)} %slice.34), channel_id=1, source_target_pairs={{0,1},{1,2},{2,3},{3,0},{4,5},{5,6},{6,7},{7,4},{8,9},{9,10},{10,1... | collective-permute-start | bytes 491528 | tf_op jit(solution)/shard_map/ppermute | solution.py:246
  38.5 7.3 %collective-permute-start.11 = (bf16[160,512]{1,0:T(8,128)(2,1)S(1)}, bf16[160,512]{1,0:T(8,128)(2,1)S(1)}, u32[]{:S(2)}, u32[]{:S(2)}) collective-permute-start(bf16[160,512]{1,0:T(8,128)(2,1)S(1)} %slice.35), channel_id=1, source_target_pairs={{0,3},{1,0},{2,1},{3,2},{4,7},{5,4},{6,5},{7,6},{8,11},{9,8},{10,9... | collective-permute-start | bytes 491528 | tf_op jit(solution)/shard_map/ppermute | solution.py:247
  41.9 12.1 %collective-permute-start.3 = (bf16[256,512]{1,0:T(8,128)(2,1)}, bf16[256,512]{1,0:T(8,128)(2,1)}, u32[]{:S(2)}, u32[]{:S(2)}) collective-permute-start(bf16[256,512]{1,0:T(8,128)(2,1)} %slice.32), channel_id=1, source_target_pairs={{0,1},{1,2},{2,3},{3,0},{4,5},{5,6},{6,7},{7,4},{8,9},{9,10},{10,1... | collective-permute-start | bytes 786440 | tf_op jit(solution)/shard_map/ppermute | solution.py:246
  42.6 11.4 %collective-permute-start.4 = (bf16[256,512]{1,0:T(8,128)(2,1)}, bf16[256,512]{1,0:T(8,128)(2,1)}, u32[]{:S(2)}, u32[]{:S(2)}) collective-permute-start(bf16[256,512]{1,0:T(8,128)(2,1)} %slice.33), channel_id=1, source_target_pairs={{0,3},{1,0},{2,1},{3,2},{4,7},{5,4},{6,5},{7,6},{8,11},{9,8},{10,9... | collective-permute-start | bytes 786440 | tf_op jit(solution)/shard_map/ppermute | solution.py:247
  45.7 8.3 %copy-start = (bf16[1024,1024]{1,0:T(8,128)(2,1)}, bf16[1024,1024]{1,0:T(8,128)(2,1)S(1)}, u32[]{:S(2)}) copy-start(bf16[1024,1024]{1,0:T(8,128)(2,1)S(1)} %fusion.swap) | copy-start | bytes 6291460
  47.4 0.8 copy-start.3
  48.9 41.1 %copy-start.15 = (s32[1024]{0:T(1024)S(1)}, s32[1024]{0:T(1024)}, u32[]{:S(2)}) copy-start(s32[1024]{0:T(1024)} %constant.5.clone) | copy-start | bytes 12292
  48.9 56.2 %copy-start.10 = (s32[2,2]{1,0:T(2,128)S(1)}, s32[2,2]{1,0:T(2,128)}, u32[]{:S(2)}) copy-start(s32[2,2]{1,0:T(2,128)} %ladder_tiles.3) | copy-start | bytes 52
  48.9 56.2 %copy-start.12 = (s32[2,2]{1,0:T(2,128)S(1)}, s32[2,2]{1,0:T(2,128)}, u32[]{:S(2)}) copy-start(s32[2,2]{1,0:T(2,128)} %cycle_tiles.3) | copy-start | bytes 52
  48.9 56.2 %copy-start.13 = (s32[8]{0:T(128)S(1)}, s32[8]{0:T(128)}, u32[]{:S(2)}) copy-start(s32[8]{0:T(128)} %partner.1) | copy-start | bytes 100
  48.9 15.0 %all-to-all-start.1 = ((bf16[8,2,64,128]{3,2,1,0:T(8,128)(2,1)}), bf16[8,2,64,128]{3,2,1,0:T(8,128)(2,1)}, u32[]{:S(2)}, u32[]{:S(2)}) async-start(bf16[8,2,64,128]{3,2,1,0:T(8,128)(2,1)} %copy-done.7), calls=%async_computation.1 | async-start | bytes 524288 | tf_op jit(solution)/shard_map/all_to_all | solution.py:252
  54.0 1.0 copy-start.2
  62.4 0.8 copy-start.5
  63.2 0.7 copy-start.8
  63.9 18.4 %all-to-all-start = ((bf16[8,2,64,128]{3,2,1,0:T(8,128)(2,1)}), bf16[8,2,64,128]{3,2,1,0:T(8,128)(2,1)S(1)}, u32[]{:S(2)}, u32[]{:S(2)}) async-start(bf16[8,2,64,128]{3,2,1,0:T(8,128)(2,1)} %copy-done.8), calls=%async_computation | async-start | bytes 524288 | tf_op jit(solution)/shard_map/all_to_all | solution.py:252
  71.5 27.2 %collective-permute-start.14 = (bf16[8,64,128]{2,1,0:T(8,128)(2,1)S(1)}, bf16[8,64,128]{2,1,0:T(8,128)(2,1)S(1)}, u32[]{:S(2)}, u32[]{:S(2)}) collective-permute-start(bf16[8,64,128]{2,1,0:T(8,128)(2,1)S(1)} %get-tuple-element.24), channel_id=1, source_target_pairs={{0,0},{8,64},{16,128},{24,192},{32,32},{40,96},{48,160},{56,224},{... | collective-permute-start | bytes 393224 | tf_op jit(solution)/shard_map/ppermute | solution.py:253
  82.2 19.5 %collective-permute-start.15 = (bf16[8,64,128]{2,1,0:T(8,128)(2,1)S(1)}, bf16[8,64,128]{2,1,0:T(8,128)(2,1)S(1)}, u32[]{:S(2)}, u32[]{:S(2)}) collective-permute-start(bf16[8,64,128]{2,1,0:T(8,128)(2,1)S(1)} %get-tuple-element.23), channel_id=1, source_target_pairs={{0,32},{8,96},{16,160},{24,224},{32,0},{40,64},{48,128},{56,192},{... | collective-permute-start | bytes 393224 | tf_op jit(solution)/shard_map/ppermute | solution.py:253
  82.3 21.4 %collective-permute-start.12 = (bf16[8,64,128]{2,1,0:T(8,128)(2,1)S(1)}, bf16[8,64,128]{2,1,0:T(8,128)(2,1)S(1)}, u32[]{:S(2)}, u32[]{:S(2)}) collective-permute-start(bf16[8,64,128]{2,1,0:T(8,128)(2,1)S(1)} %get-tuple-element.26), channel_id=1, source_target_pairs={{0,0},{8,64},{16,128},{24,192},{32,32},{40,96},{48,160},{56,224},{... | collective-permute-start | bytes 393224 | tf_op jit(solution)/shard_map/ppermute | solution.py:253
  89.9 15.2 %collective-permute-start.13 = (bf16[8,64,128]{2,1,0:T(8,128)(2,1)S(1)}, bf16[8,64,128]{2,1,0:T(8,128)(2,1)S(1)}, u32[]{:S(2)}, u32[]{:S(2)}) collective-permute-start(bf16[8,64,128]{2,1,0:T(8,128)(2,1)S(1)} %get-tuple-element.25), channel_id=1, source_target_pairs={{0,32},{8,96},{16,160},{24,224},{32,0},{40,64},{48,128},{56,192},{... | collective-permute-start | bytes 393224 | tf_op jit(solution)/shard_map/ppermute | solution.py:253
  105.1 1.0 copy-start.4
  106.2 1.0 copy-start.6
  (3 other events, 2.1 us)

commit v4 on v2

v4 whole, which is shorter than its diff:
```python
import jax
import jax.numpy as jnp
import numpy as np
from jax import lax
from jax.experimental import pallas as pl
from jax.experimental.pallas import tpu as pltpu
from jax.sharding import PartitionSpec as P

TILE = 64
REACH = 2
BAND = 5
ROWS = 8
LANES = 512
PAIRS = 128
BF = jnp.bfloat16
F32 = jnp.float32
MIB = 1 << 20


def vert_moves(move):
    return [(v, move(v // 4, v % 4)) for v in range(8)]


FLIP = vert_moves(lambda h, y: (1 - h) * 4 + y)
UP = vert_moves(lambda h, y: h * 4 + (y + 1) % 4)
DOWN = vert_moves(lambda h, y: h * 4 + (y + 3) % 4)


def pair_moves(k):
    return [
        (p * 4 + q, (2 * q + ((p % 2) ^ k)) * 4 + p // 2) for p in range(8) for q in range(4)
    ]


def send_order():
    row = np.arange(1024)
    slot, a, v, b = row // 512, (row // 64) % 8, (row // 8) % 8, row % 8
    return v * 128 + slot * 64 + b * 8 + a


def place_order():
    row = np.arange(1024)
    v, slot, b, a = row // 128, (row // 64) % 2, (row // 8) % 8, row % 8
    return slot * 512 + b * 64 + v * 8 + a


def permutation(order):
    columns = lax.broadcasted_iota(jnp.int32, (1024, 1024), 1)
    return (jnp.asarray(order, jnp.int32)[:, None] == columns).astype(BF)


def pick_rows(wanted, amplitudes):
    column = lax.broadcasted_iota(jnp.int32, (256, 128), 1)
    offset = wanted - column
    pick = jnp.concatenate(
        [jnp.where(offset == c * 128, 1.0, 0.0).astype(BF) for c in range(8)], axis=1
    )
    return jnp.dot(pick, amplitudes[...], preferred_element_type=F32).astype(BF)


def cycle_prepare_kernel(tiles, amplitudes, ints, ints_ref, inner_ref, first_ref, last_ref, wide, tall):
    row = lax.broadcasted_iota(jnp.int32, (256, 128), 0)
    i, j, r = row & 7, row >> 4, (row >> 3) & 1
    tile = tiles[0, 1] + r * (tiles[1, 1] - tiles[0, 1])
    inner = pick_rows((i * 16 + j) * 8 + tile, amplitudes).reshape(16, 16, LANES)
    inner_ref[...] = inner
    first_ref[...] = inner[:REACH]
    last_ref[...] = inner[16 - REACH :]
    for t in range(4):
        wide[t] = ints[:, t * 128 : (t + 1) * 128].astype(F32)
    low = lax.broadcasted_iota(jnp.int32, (80, 128), 1) < TILE
    for t in range(4):
        zero = wide[t, pl.ds(0, 80, stride=2), :]
        one = wide[t, pl.ds(1, 80, stride=2), :]
        tall[pl.ds(2 * t, 80, stride=8), :] = jnp.where(low, zero, pltpu.roll(one, TILE, 1))
        tall[pl.ds(2 * t + 1, 80, stride=8), :] = jnp.where(low, pltpu.roll(zero, TILE, 1), one)
    for b in range(4):
        ints_ref[:, b * 128 : (b + 1) * 128] = tall[b * 160 : (b + 1) * 160, :].astype(BF)


def ladder_prepare_kernel(tiles, amplitudes, order, own_ref):
    del order
    row = lax.broadcasted_iota(jnp.int32, (256, 128), 0)
    i, j, w = row & 7, (row >> 3) & 15, row >> 7
    tile = tiles[0, 1] + w * (tiles[1, 1] - tiles[0, 1])
    own_ref[...] = pick_rows((i * 16 + j) * 8 + tile, amplitudes)


def split_pieces(refs, rows):
    own, flip, up, down, up_2, down_2, up_3, down_3 = refs
    vert = lax.axis_index("vert")
    h, y = vert // 4, vert % 4
    half = rows // 2
    pieces = []
    for w in range(2):
        base = w * half
        places = [
            (h, y, own, base), (1 - h, y, flip, base),
            (h, y + 3, up, base), (h, y + 1, down, base),
            (1 - h, y + 3, up_2, base), (1 - h, y + 1, down_2, base),
            (h, y + 2, (up_2, down_2)[w], rows), (1 - h, y + 2, (up_3, down_3)[w], 0),
        ]
        pieces.append([(a * 4 + b % 4, ref, pl.ds(first, half)) for a, b, ref, first in places])
    return pieces


def packed_halves(total, swap):
    parity = lax.axis_index("pi") % 2
    sent = jnp.dot(total[...].astype(BF), swap[...], preferred_element_type=F32).astype(BF)
    upper, under = sent[:64], sent[64:]
    return jnp.where(parity == 0, upper, under), jnp.where(parity == 0, under, upper)


def cycle_kernel(ladder_hbm, before, inner, after, swap, *refs):
    total, first_ref, second_ref, ladder_ints, ints, sem = refs[8:]
    load = pltpu.make_async_copy(ladder_hbm, ladder_ints, sem)
    load.start()
    for w, pieces in enumerate(split_pieces(refs[:8], 160)):
        for source, ref, where in pieces:
            ints[source, w * 80 : (w + 1) * 80, :] = ref[where, :].astype(F32)

    def rows_of(j):
        if j < REACH:
            return before[j]
        if j < REACH + 16:
            return inner[j - REACH]
        return after[j - REACH - 16]

    laid = []
    for j in range(16 + 2 * REACH):
        block = rows_of(j)
        laid.append(
            jnp.concatenate([block[:, a * TILE : (a + 1) * TILE] for a in range(ROWS)], axis=0)
        )
    low = lax.broadcasted_iota(jnp.int32, (8, 128), 1) < TILE
    for j in range(16):
        left = jnp.concatenate([laid[j + o] for o in range(BAND)], axis=1)
        base, lanes = (j % 4) * 40, (j // 4) * 128
        right = jnp.concatenate(
            [
                ints[v, base + o * 8 : base + o * 8 + 8, lanes : lanes + 128]
                for o in range(BAND)
                for v in range(8)
            ],
            axis=0,
        ).astype(BF)
        done = jnp.dot(left, right, preferred_element_type=F32)
        for r in range(2):
            for t in range(4):
                even = done[t * 32 + r * 8 : t * 32 + r * 8 + 8]
                odd = done[t * 32 + 16 + r * 8 : t * 32 + 16 + r * 8 + 8]
                if r == 0:
                    odd = pltpu.roll(odd, TILE, 1)
                else:
                    even = pltpu.roll(even, TILE, 1)
                lane = r * LANES + t * 128
                total[j * 8 : j * 8 + 8, lane : lane + 128] = jnp.where(low, even, odd)
    for half, ref in zip(packed_halves(total, swap), (first_ref, second_ref)):
        for v in range(8):
            ref[v] = half[:, v * 128 : (v + 1) * 128]
    load.wait()


def ladder_kernel(ladder_ints, swap, cycle_0, cycle_1, *refs):
    total, sent_ref = refs[8:]
    for which, pieces in enumerate(split_pieces(refs[:8], 256)):
        acc = None
        for source, ref, where in pieces:
            start = pl.multiple_of(source * LANES, LANES)
            part = lax.dot_general(
                ref[where, :],
                ladder_ints[which, :, pl.ds(start, LANES)],
                (((1,), (1,)), ((), ())),
                preferred_element_type=F32,
            )
            acc = part if acc is None else acc + part
        total[:, which * LANES : (which + 1) * LANES] = acc
    for k, half in enumerate(packed_halves(total, swap)):
        for v in range(8):
            sent_ref[v, k] = half[:, v * 128 : (v + 1) * 128]
    sent_ref[:, 2] = cycle_0[...]
    sent_ref[:, 3] = cycle_1[...]


def finish_kernel(
    ladder_tiles, cycle_tiles, partner, ladder, cycle, place, first, second, arrived, out_ref, mirrored
):
    parity = lax.axis_index("pi") % 2
    for s in range(2):
        for k in range(2):
            if s == 0:
                blocks = [(first, second)[k][v] for v in range(8)]
            else:
                blocks = [arrived[v, 2 + k] for v in range(8)]
            wide = jnp.concatenate(blocks, axis=1)
            mirrored[s, parity ^ k] = jnp.dot(wide, place[...], preferred_element_type=F32)
    dests = [ladder_tiles[0, 0], ladder_tiles[1, 0], cycle_tiles[0, 0], cycle_tiles[1, 0]]
    tile = lax.broadcasted_iota(jnp.int32, (8, LANES), 0)
    own = [(tile == dest).astype(F32) for dest in dests]
    other = [(tile == partner[dest]).astype(F32) for dest in dests]

    def one(i):
        for j in range(16):
            acc = None
            for s in range(4):
                lanes = slice((s % 2) * LANES, (s % 2 + 1) * LANES)
                source = ladder if s < 2 else cycle
                term = own[s] * source[pl.ds(j * 8 + i, 1), lanes]
                acc = term if acc is None else acc + term
                acc = acc + other[s] * mirrored[s // 2, j // 8, pl.ds(i * 8 + j % 8, 1), lanes]
            out_ref[i, j] = acc

    pl.loop(0, 8)(one)


SMEM = pl.BlockSpec(memory_space=pltpu.SMEM)
VMEM = pl.BlockSpec(memory_space=pltpu.VMEM)
ANY = pl.BlockSpec(memory_space=pl.ANY)


def call(kernel, ins, outs, out_specs, scratch, limit, flops):
    return pl.pallas_call(
        kernel,
        out_shape=outs,
        in_specs=ins,
        out_specs=out_specs,
        scratch_shapes=scratch,
        compiler_params=pltpu.CompilerParams(vmem_limit_bytes=limit * MIB),
        cost_estimate=pl.CostEstimate(flops=flops, bytes_accessed=4 * MIB, transcendentals=0),
    )


def shape(dims, kind):
    return jax.ShapeDtypeStruct(dims, kind)


def gather(own):
    rows = own.shape[0]
    half = rows // 2
    flip = lax.ppermute(own, "vert", FLIP)
    up = lax.ppermute(own, "vert", UP)
    down = lax.ppermute(own, "vert", DOWN)
    up_2 = lax.ppermute(jnp.concatenate([flip, up[:half]]), "vert", UP)
    down_2 = lax.ppermute(jnp.concatenate([flip, down[half:]]), "vert", DOWN)
    up_3 = lax.ppermute(up_2[:half], "vert", UP)
    down_3 = lax.ppermute(down_2[half:rows], "vert", DOWN)
    return [own, flip, up, down, up_2, down_2, up_3, down_3]


def to_transposed(blocks):
    return [lax.ppermute(block, ("pi", "pj"), pair_moves(k)) for k, block in enumerate(blocks)]


def body(amplitudes, ladder_ints, ladder_tiles, cycle_ints, cycle_tiles, partner):
    amplitudes = amplitudes.reshape(1024, LANES)
    edge = shape((REACH, 16, LANES), BF)
    ints_own, inner, first, last = call(
        cycle_prepare_kernel,
        [SMEM, VMEM, VMEM],
        [shape((160, LANES), BF), shape((16, 16, LANES), BF), edge, edge],
        [VMEM] * 4,
        [pltpu.VMEM((4, 160, 128), F32), pltpu.VMEM((640, 128), F32)],
        12,
        10**9,
    )(cycle_tiles, amplitudes, cycle_ints.reshape(160, LANES))
    swap, place = permutation(send_order()), permutation(place_order())
    total = shape((PAIRS, 1024), F32)
    block = shape((8, 64, 128), BF)

    ints_pieces = gather(ints_own)
    before = lax.ppermute(last, "pj", [(q, q + 1) for q in range(3)])
    after = lax.ppermute(first, "pj", [(q + 1, q) for q in range(3)])
    ladder_own = call(
        ladder_prepare_kernel, [SMEM, VMEM, ANY], shape((256, LANES), BF), VMEM, [], 8, 10**9
    )(ladder_tiles, amplitudes, ints_pieces[1])
    ladder_pieces = gather(ladder_own)

    cycle_total, *cycle_blocks, ladder_near = call(
        cycle_kernel,
        [ANY] + [VMEM] * 12,
        [total, block, block, shape((2, LANES, 4096), BF)],
        [VMEM] * 4,
        [pltpu.VMEM((8, 160, LANES), F32), pltpu.SemaphoreType.DMA],
        16,
        10**9,
    )(ladder_ints, before, inner, after, swap, *ints_pieces)
    cycle_moved = to_transposed(cycle_blocks)

    ladder_total, sent = call(
        ladder_kernel,
        [VMEM] * 12,
        [total, shape((8, 4, 64, 128), BF)],
        [VMEM] * 2,
        [],
        12,
        2 * 10**9,
    )(ladder_near, swap, *cycle_moved, *ladder_pieces)
    arrived = lax.all_to_all(sent, "vert", 0, 0)
    ladder_moved = to_transposed([arrived[:, 0], arrived[:, 1]])

    return call(
        finish_kernel,
        [SMEM, SMEM, SMEM] + [VMEM] * 6,
        shape((8, 16, 8, LANES), F32),
        VMEM,
        [pltpu.VMEM((2, 2, 64, 1024), F32)],
        12,
        10**9,
    )(ladder_tiles, cycle_tiles, partner, ladder_total, cycle_total, place, *ladder_moved, arrived)


def solution(mesh):
    placed = (
        P("pi", "pj", None, "vert"),
        P(None, "vert", None),
        P(),
        P("pj", None, None, "vert"),
        P(),
        P(),
    )
    return jax.shard_map(
        body, mesh=mesh, in_specs=placed, out_specs=P("pi", "pj", None, "vert"), check_vma=False
    )
```

time: 105 us -> 105 us (level)
  starting transfers between devices: 29.2 us -> 49.8 us
  waiting for transfers between devices: 41.3 us -> 22.4 us
  local copies, waits for them, and re-layouts: 7 us -> 3.67 us
  Pallas kernels: 10.6 us -> 11.8 us
    ppermute x9 -> x18, starting transfers between devices: 23.4 us -> 43.1 us  [the longest x4 22.2 us: to_transposed(): lax.ppermute(block, ('pi', 'pj'), pair_moves(k))]
    ppermute x9 -> x18, waiting for transfers between devices: 35.2 us -> 22.4 us  [the longest x4 16.5 us: to_transposed(): lax.ppermute(block, ('pi', 'pj'), pair_moves(k))]
    ppermute x1, waiting for transfers between devices: 6.12 us -> 0.01 us  [body(): before = lax.ppermute(last, 'pj', [(q, q + 1) for q in range(3)])]
    unnamed x16, local copies, waits for them, and re-layouts: 5.98 us -> 2.6 us
    pallas_call x3 -> x5, Pallas kernels: 10.6 us -> 11.8 us  [the longest x1 4.54 us: body(): call(finish_kernel, [SMEM, SMEM, SMEM] + [VMEM] * 6, shape((8, 16, 8, LAN...]
  transfers between devices with their start and end apart: 11 -> 20, of which waited for: 6 -> 8; matrix products, arithmetic and copies ran while one was open for 1% -> 1% of each run, Pallas kernels for 0% -> 3%
where the time goes in v4:
time: 105 us; the launch traced here: 104 us
  starting transfers between devices  49.8 us (47%)
  waiting for transfers between devices  22.4 us (21%)
  blocking collectives  15.5 us (15%)
  Pallas kernels  11.8 us (11%)
  local copies, waits for them, and re-layouts  3.67 us (3%)
    ppermute x4, starting transfers between devices, to_transposed(): lax.ppermute(block, ('pi', 'pj'), pair_moves(k))  22.2 us
    ppermute x4, waiting for transfers between devices, to_transposed(): lax.ppermute(block, ('pi', 'pj'), pair_moves(k))  16.5 us
    all_to_all x1, blocking collectives, body(): arrived = lax.all_to_all(sent, 'vert', 0, 0)  15.5 us
    ppermute x1, starting transfers between devices, body(): after = lax.ppermute(first, 'pj', [(q + 1, q) for q in range(3)])  5.34 us
    ppermute x2, starting transfers between devices, gather(): down_2 = lax.ppermute(jnp.concatenate([flip, down[half:]]), 'vert', DOWN)  5.33 us
    ppermute x2, starting transfers between devices, gather(): down_3 = lax.ppermute(down_2[half:rows], 'vert', DOWN)  5.26 us
    pallas_call x1, Pallas kernels, body(): call(finish_kernel, [SMEM, SMEM, SMEM] + [VMEM] * 6, shape((8, 16, 8, LAN...  4.54 us
    ppermute x2, starting transfers between devices, gather(): flip = lax.ppermute(own, 'vert', FLIP)  3.76 us
  transfers between devices with their start and end apart: 20, of which 8 were waited for; matrix products, arithmetic and copies ran while one was open for 1% of the time, Pallas kernels for 3%

profile of v4, /device:TPU:3, one launch (start us, length us, event | category | flops | bytes accessed | tf_op | source)
XLA Modules:
  0.0 104.3 jit_solution(11791677299412974332)
XLA Ops:
  0.0 1.0 reshape.9.ints
  1.0 0.7 copy-done.2
  1.7 1.2 %copy-done.5 = bf16[8,16,8,512]{3,2,1,0:T(8,128)(2,1)S(1)} copy-done((bf16[8,16,8,512]{3,2,1,0:T(8,128)(2,1)S(1)}, bf16[8,16,8,512]{3,2,1,0:T(8,128)(2,1)}, u32[]{:S(2)}) %copy-start.5) | copy-done | bytes 1048600
  2.9 1.0 shard_map.82
  3.9 1.9 %collective-permute-start.2 = (bf16[160,512]{1,0:T(8,128)(2,1)S(1)}, bf16[160,512]{1,0:T(8,128)(2,1)S(1)}, u32[]{:S(2)}, u32[]{:S(2)}) collective-permute-start(bf16[160,512]{1,0:T(8,128)(2,1)S(1)} %get-tuple-element.18.refs_0_), channel_id=1, source_target_pairs={{0,4},{1,5},{2,6},{3,7},{4,0},{5,1},{6,2},{7,3},{8,12},{9,13},{10,... | collective-permute-start | bytes 491528 | tf_op jit(solution)/shard_map/ppermute | solution.py:240
  5.9 1.3 %collective-permute-start.3 = (bf16[160,512]{1,0:T(8,128)(2,1)S(1)}, bf16[160,512]{1,0:T(8,128)(2,1)S(1)}, u32[]{:S(2)}, u32[]{:S(2)}) collective-permute-start(bf16[160,512]{1,0:T(8,128)(2,1)S(1)} %get-tuple-element.18.refs_0_), channel_id=1, source_target_pairs={{0,1},{1,2},{2,3},{3,0},{4,5},{5,6},{6,7},{7,4},{8,9},{9,10},{10,1... | collective-permute-start | bytes 491528 | tf_op jit(solution)/shard_map/ppermute | solution.py:241
  7.2 1.4 %collective-permute-start.4 = (bf16[160,512]{1,0:T(8,128)(2,1)S(1)}, bf16[160,512]{1,0:T(8,128)(2,1)S(1)}, u32[]{:S(2)}, u32[]{:S(2)}) collective-permute-start(bf16[160,512]{1,0:T(8,128)(2,1)S(1)} %get-tuple-element.18.refs_0_), channel_id=1, source_target_pairs={{0,3},{1,0},{2,1},{3,2},{4,7},{5,4},{6,5},{7,6},{8,11},{9,8},{10,9... | collective-permute-start | bytes 491528 | tf_op jit(solution)/shard_map/ppermute | solution.py:242
  8.6 2.0 %collective-permute-done.2.refs_1_.order = bf16[160,512]{1,0:T(8,128)(2,1)S(1)} collective-permute-done((bf16[160,512]{1,0:T(8,128)(2,1)S(1)}, bf16[160,512]{1,0:T(8,128)(2,1)S(1)}, u32[]{:S(2)}, u32[]{:S(2)}) %collective-permute-start.2) | collective-permute-done | bytes 163872 | tf_op jit(solution)/shard_map/ppermute | solution.py:240
  10.6 0.7 copy-done.1
  11.3 1.0 shard_map.84.refs_0_
  12.3 1.3 %collective-permute-start.12 = (bf16[256,512]{1,0:T(8,128)(2,1)S(1)}, bf16[256,512]{1,0:T(8,128)(2,1)S(1)}, u32[]{:S(2)}, u32[]{:S(2)}) collective-permute-start(bf16[256,512]{1,0:T(8,128)(2,1)S(1)} %shard_map.84.refs_0_), channel_id=1, source_target_pairs={{0,1},{1,2},{2,3},{3,0},{4,5},{5,6},{6,7},{7,4},{8,9},{9,10},{10,1... | collective-permute-start | bytes 786440 | tf_op jit(solution)/shard_map/ppermute | solution.py:241
  13.6 1.5 %collective-permute-start.13 = (bf16[256,512]{1,0:T(8,128)(2,1)S(1)}, bf16[256,512]{1,0:T(8,128)(2,1)S(1)}, u32[]{:S(2)}, u32[]{:S(2)}) collective-permute-start(bf16[256,512]{1,0:T(8,128)(2,1)S(1)} %shard_map.84.refs_0_), channel_id=1, source_target_pairs={{0,3},{1,0},{2,1},{3,2},{4,7},{5,4},{6,5},{7,6},{8,11},{9,8},{10,9... | collective-permute-start | bytes 786440 | tf_op jit(solution)/shard_map/ppermute | solution.py:242
  15.2 1.8 %collective-permute-start.11 = (bf16[256,512]{1,0:T(8,128)(2,1)S(1)}, bf16[256,512]{1,0:T(8,128)(2,1)S(1)}, u32[]{:S(2)}, u32[]{:S(2)}) collective-permute-start(bf16[256,512]{1,0:T(8,128)(2,1)S(1)} %shard_map.84.refs_0_), channel_id=1, source_target_pairs={{0,4},{1,5},{2,6},{3,7},{4,0},{5,1},{6,2},{7,3},{8,12},{9,13},{10,... | collective-permute-start | bytes 786440 | tf_op jit(solution)/shard_map/ppermute | solution.py:240
  17.2 2.7 %collective-permute-start.6 = (bf16[240,512]{1,0:T(8,128)(2,1)S(1)}, bf16[240,512]{1,0:T(8,128)(2,1)S(1)}, u32[]{:S(2)}, u32[]{:S(2)}) collective-permute-start(bf16[240,512]{1,0:T(8,128)(2,1)S(1)} %get-tuple-element.29), channel_id=1, source_target_pairs={{0,3},{1,0},{2,1},{3,2},{4,7},{5,4},{6,5},{7,6},{8,11},{9,8},{10,9... | collective-permute-start | bytes 737288 | tf_op jit(solution)/shard_map/ppermute | solution.py:244
  19.9 1.3 %collective-permute-start = (bf16[2,16,512]{2,1,0:T(8,128)(2,1)S(1)}, bf16[2,16,512]{2,1,0:T(8,128)(2,1)S(1)}, u32[]{:S(2)}, u32[]{:S(2)}) collective-permute-start(bf16[2,16,512]{2,1,0:T(8,128)(2,1)S(1)} %get-tuple-element.15), channel_id=1, source_target_pairs={{0,8},{8,16},{16,24},{1,9},{9,17},{17,25},{2,10},{10,18},{18,26},{... | collective-permute-start | bytes 98312 | tf_op jit(solution)/shard_map/ppermute | solution.py:271
  21.3 1.2 %collective-permute-done.11.refs_1_ = bf16[256,512]{1,0:T(8,128)(2,1)S(1)} collective-permute-done((bf16[256,512]{1,0:T(8,128)(2,1)S(1)}, bf16[256,512]{1,0:T(8,128)(2,1)S(1)}, u32[]{:S(2)}, u32[]{:S(2)}) %collective-permute-start.11) | collective-permute-done | bytes 262176 | tf_op jit(solution)/shard_map/ppermute | solution.py:240
  22.6 2.7 %collective-permute-start.15 = (bf16[384,512]{1,0:T(8,128)(2,1)S(1)}, bf16[384,512]{1,0:T(8,128)(2,1)S(1)}, u32[]{:S(2)}, u32[]{:S(2)}) collective-permute-start(bf16[384,512]{1,0:T(8,128)(2,1)S(1)} %get-tuple-element.27), channel_id=1, source_target_pairs={{0,3},{1,0},{2,1},{3,2},{4,7},{5,4},{6,5},{7,6},{8,11},{9,8},{10,9... | collective-permute-start | bytes 1179656 | tf_op jit(solution)/shard_map/ppermute | solution.py:244
  25.3 5.3 %collective-permute-start.1 = (bf16[2,16,512]{2,1,0:T(8,128)(2,1)S(1)}, bf16[2,16,512]{2,1,0:T(8,128)(2,1)S(1)}, u32[]{:S(2)}, u32[]{:S(2)}) collective-permute-start(bf16[2,16,512]{2,1,0:T(8,128)(2,1)S(1)} %get-tuple-element.17), channel_id=1, source_target_pairs={{8,0},{16,8},{24,16},{9,1},{17,9},{25,17},{10,2},{18,10},{26,18},{... | collective-permute-start | bytes 98312 | tf_op jit(solution)/shard_map/ppermute | solution.py:272
  30.7 0.7 collective-permute-start.7
  31.4 2.1 %collective-permute-start.8 = (bf16[80,512]{1,0:T(8,128)(2,1)S(1)}, bf16[80,512]{1,0:T(8,128)(2,1)S(1)}, u32[]{:S(2)}, u32[]{:S(2)}) collective-permute-start(bf16[80,512]{1,0:T(8,128)(2,1)S(1)} %slice.43), channel_id=1, source_target_pairs={{0,3},{1,0},{2,1},{3,2},{4,7},{5,4},{6,5},{7,6},{8,11},{9,8},{10,9... | collective-permute-start | bytes 245768 | tf_op jit(solution)/shard_map/ppermute | solution.py:246
  34.0 2.5 %collective-permute-done.7.refs_6_ = bf16[80,512]{1,0:T(8,128)(2,1)S(1)} collective-permute-done((bf16[80,512]{1,0:T(8,128)(2,1)S(1)}, bf16[80,512]{1,0:T(8,128)(2,1)S(1)}, u32[]{:S(2)}, u32[]{:S(2)}) %collective-permute-start.7) | collective-permute-done | bytes 81952 | tf_op jit(solution)/shard_map/ppermute | solution.py:245
  36.5 2.1 %shard_map.83 = (f32[128,1024]{1,0:T(8,128)S(1)}, bf16[8,64,128]{2,1,0:T(8,128)(2,1)S(1)}, bf16[8,64,128]{2,1,0:T(8,128)(2,1)S(1)}, bf16[2,512,4096]{2,1,0:T(8,128)(2,1)S(1)}) custom-call(bf16[2,512,4096]{2,1,0:T(8,128)(2,1)S(1)} %copy-done, bf16[2,16,512]{2,1,0:T(8,128)(2,1)S(1)} %collective-permute-done.before, ...), custom_call_target="tpu_custom_call" | custom-call | flops 1000000000 | bytes 4194304 | tf_op jit(solution)/shard_map/pallas_call | solution.py:278
  38.6 9.2 %collective-permute-start.10 = (bf16[8,64,128]{2,1,0:T(8,128)(2,1)S(1)}, bf16[8,64,128]{2,1,0:T(8,128)(2,1)S(1)}, u32[]{:S(2)}, u32[]{:S(2)}) collective-permute-start(bf16[8,64,128]{2,1,0:T(8,128)(2,1)S(1)} %get-tuple-element.21), channel_id=1, source_target_pairs={{0,32},{8,96},{16,160},{24,224},{32,0},{40,64},{48,128},{56,192},{... | collective-permute-start | bytes 393224 | tf_op jit(solution)/shard_map/ppermute | solution.py:251
  47.8 2.6 %collective-permute-start.9 = (bf16[8,64,128]{2,1,0:T(8,128)(2,1)S(1)}, bf16[8,64,128]{2,1,0:T(8,128)(2,1)S(1)}, u32[]{:S(2)}, u32[]{:S(2)}) collective-permute-start(bf16[8,64,128]{2,1,0:T(8,128)(2,1)S(1)} %get-tuple-element.20), channel_id=1, source_target_pairs={{0,0},{8,64},{16,128},{24,192},{32,32},{40,96},{48,160},{56,224},{... | collective-permute-start | bytes 393224 | tf_op jit(solution)/shard_map/ppermute | solution.py:251
  50.5 3.1 %collective-permute-start.17 = (bf16[128,512]{1,0:T(8,128)(2,1)S(1)}, bf16[128,512]{1,0:T(8,128)(2,1)S(1)}, u32[]{:S(2)}, u32[]{:S(2)}) collective-permute-start(bf16[128,512]{1,0:T(8,128)(2,1)S(1)} %slice.47), channel_id=1, source_target_pairs={{0,3},{1,0},{2,1},{3,2},{4,7},{5,4},{6,5},{7,6},{8,11},{9,8},{10,9... | collective-permute-start | bytes 393224 | tf_op jit(solution)/shard_map/ppermute | solution.py:246
  54.1 5.4 %collective-permute-done.9.cycle_0 = bf16[8,64,128]{2,1,0:T(8,128)(2,1)S(1)} collective-permute-done((bf16[8,64,128]{2,1,0:T(8,128)(2,1)S(1)}, bf16[8,64,128]{2,1,0:T(8,128)(2,1)S(1)}, u32[]{:S(2)}, u32[]{:S(2)}) %collective-permute-start.9) | collective-permute-done | bytes 131104 | tf_op jit(solution)/shard_map/ppermute | solution.py:251
  59.6 3.2 %shard_map.85 = (f32[128,1024]{1,0:T(8,128)S(1)}, bf16[8,4,64,128]{3,2,1,0:T(8,128)(2,1)S(1)}) custom-call(bf16[2,512,4096]{2,1,0:T(8,128)(2,1)S(1)} %get-tuple-element.19.ladder_ints, bf16[1024,1024]{1,0:T(8,128)(2,1)S(1)} %fusion.swap, bf16[8,64,128]{2,1,0:T(8,128)(2,1)S(1)} %collective-permute-done.9.cycle_0, ...), custom_call_target="tpu_custom_call" | custom-call | flops 2000000000 | bytes 4194304 | tf_op jit(solution)/shard_map/pallas_call | solution.py:289
  62.8 15.5 %all_to_all.5.arrived = bf16[8,4,64,128]{3,2,1,0:T(8,128)(2,1)S(1)} all-to-all(bf16[8,4,64,128]{3,2,1,0:T(8,128)(2,1)S(1)} %get-tuple-element.24), channel_id=1, replica_groups=mesh['pi'=8,'pj'=4,'vert'=8] {'vert'}, dimensions={0} | all-to-all | bytes 1048576 | tf_op jit(solution)/shard_map/all_to_all | solution.py:298
  78.2 10.4 %collective-permute-start.18 = (bf16[8,64,128]{2,1,0:T(8,128)(2,1)S(1)}, bf16[8,64,128]{2,1,0:T(8,128)(2,1)S(1)}, u32[]{:S(2)}, u32[]{:S(2)}) collective-permute-start(bf16[8,64,128]{2,1,0:T(8,128)(2,1)S(1)} %get-tuple-element.26), channel_id=1, source_target_pairs={{0,0},{8,64},{16,128},{24,192},{32,32},{40,96},{48,160},{56,224},{... | collective-permute-start | bytes 393224 | tf_op jit(solution)/shard_map/ppermute | solution.py:251
  89.2 7.9 %collective-permute-done.18.first = bf16[8,64,128]{2,1,0:T(8,128)(2,1)S(1)} collective-permute-done((bf16[8,64,128]{2,1,0:T(8,128)(2,1)S(1)}, bf16[8,64,128]{2,1,0:T(8,128)(2,1)S(1)}, u32[]{:S(2)}, u32[]{:S(2)}) %collective-permute-start.18) | collective-permute-done | bytes 131104 | tf_op jit(solution)/shard_map/ppermute | solution.py:251
  97.1 2.6 %collective-permute-done.19.second = bf16[8,64,128]{2,1,0:T(8,128)(2,1)S(1)} collective-permute-done((bf16[8,64,128]{2,1,0:T(8,128)(2,1)S(1)}, bf16[8,64,128]{2,1,0:T(8,128)(2,1)S(1)}, u32[]{:S(2)}, u32[]{:S(2)}) %collective-permute-start.19) | collective-permute-done | bytes 131104 | tf_op jit(solution)/shard_map/ppermute | solution.py:251
  99.7 4.5 %shard_map.86 = f32[8,16,8,512]{3,2,1,0:T(8,128)} custom-call(s32[2,2]{1,0:T(2,128)S(1)} %copy-done.1, s32[2,2]{1,0:T(2,128)S(1)} %copy-done.3, s32[8]{0:T(128)S(1)} %copy-done.4, f32[128,1024]{1,0:T(8,128)S(1)} %get-tuple-element.22.ladder, f32[128,1024]{1,0:T(8,128)S(1)} %get-tuple-element.23.cycle, bf16[1024,1024]{1,0:T(8,128)(2,1)S(1)} %fusion.1.place, ...), custom_call_target="tpu_custom_call" | custom-call | flops 1000000000 | bytes 4194304 | tf_op jit(solution)/shard_map/pallas_call | solution.py:301
  (44 shorter events, 2.0 us)
Async XLA Ops:
  1.0 0.7 copy-start.2
  1.7 1.2 %copy-start.5 = (bf16[8,16,8,512]{3,2,1,0:T(8,128)(2,1)S(1)}, bf16[8,16,8,512]{3,2,1,0:T(8,128)(2,1)}, u32[]{:S(2)}) copy-start(bf16[8,16,8,512]{3,2,1,0:T(8,128)(2,1)} %param.8) | copy-start | bytes 3145732
  2.9 30.6 %copy-start.7 = (s32[1024]{0:T(1024)S(1)}, s32[1024]{0:T(1024)}, u32[]{:S(2)}) copy-start(s32[1024]{0:T(1024)} %constant.4.clone) | copy-start | bytes 12292
  3.9 32.6 %copy-start = (bf16[2,512,4096]{2,1,0:T(8,128)(2,1)S(1)}, bf16[2,512,4096]{2,1,0:T(8,128)(2,1)}, u32[]{:S(2)}) copy-start(bf16[2,512,4096]{2,1,0:T(8,128)(2,1)} %ladder_hbm.1) | copy-start | bytes 25165828
  3.9 6.7 %collective-permute-start.2 = (bf16[160,512]{1,0:T(8,128)(2,1)S(1)}, bf16[160,512]{1,0:T(8,128)(2,1)S(1)}, u32[]{:S(2)}, u32[]{:S(2)}) collective-permute-start(bf16[160,512]{1,0:T(8,128)(2,1)S(1)} %get-tuple-element.18.refs_0_), channel_id=1, source_target_pairs={{0,4},{1,5},{2,6},{3,7},{4,0},{5,1},{6,2},{7,3},{8,12},{9,13},{10,... | collective-permute-start | bytes 491528 | tf_op jit(solution)/shard_map/ppermute | solution.py:240
  5.9 11.1 %collective-permute-start.3 = (bf16[160,512]{1,0:T(8,128)(2,1)S(1)}, bf16[160,512]{1,0:T(8,128)(2,1)S(1)}, u32[]{:S(2)}, u32[]{:S(2)}) collective-permute-start(bf16[160,512]{1,0:T(8,128)(2,1)S(1)} %get-tuple-element.18.refs_0_), channel_id=1, source_target_pairs={{0,1},{1,2},{2,3},{3,0},{4,5},{5,6},{6,7},{7,4},{8,9},{9,10},{10,1... | collective-permute-start | bytes 491528 | tf_op jit(solution)/shard_map/ppermute | solution.py:241
  7.2 9.9 %collective-permute-start.4 = (bf16[160,512]{1,0:T(8,128)(2,1)S(1)}, bf16[160,512]{1,0:T(8,128)(2,1)S(1)}, u32[]{:S(2)}, u32[]{:S(2)}) collective-permute-start(bf16[160,512]{1,0:T(8,128)(2,1)S(1)} %get-tuple-element.18.refs_0_), channel_id=1, source_target_pairs={{0,3},{1,0},{2,1},{3,2},{4,7},{5,4},{6,5},{7,6},{8,11},{9,8},{10,9... | collective-permute-start | bytes 491528 | tf_op jit(solution)/shard_map/ppermute | solution.py:242
  10.6 0.7 copy-start.1
  12.3 7.7 %collective-permute-start.12 = (bf16[256,512]{1,0:T(8,128)(2,1)S(1)}, bf16[256,512]{1,0:T(8,128)(2,1)S(1)}, u32[]{:S(2)}, u32[]{:S(2)}) collective-permute-start(bf16[256,512]{1,0:T(8,128)(2,1)S(1)} %shard_map.84.refs_0_), channel_id=1, source_target_pairs={{0,1},{1,2},{2,3},{3,0},{4,5},{5,6},{6,7},{7,4},{8,9},{9,10},{10,1... | collective-permute-start | bytes 786440 | tf_op jit(solution)/shard_map/ppermute | solution.py:241
  13.6 7.6 %collective-permute-start.13 = (bf16[256,512]{1,0:T(8,128)(2,1)S(1)}, bf16[256,512]{1,0:T(8,128)(2,1)S(1)}, u32[]{:S(2)}, u32[]{:S(2)}) collective-permute-start(bf16[256,512]{1,0:T(8,128)(2,1)S(1)} %shard_map.84.refs_0_), channel_id=1, source_target_pairs={{0,3},{1,0},{2,1},{3,2},{4,7},{5,4},{6,5},{7,6},{8,11},{9,8},{10,9... | collective-permute-start | bytes 786440 | tf_op jit(solution)/shard_map/ppermute | solution.py:242
  15.2 7.3 %collective-permute-start.11 = (bf16[256,512]{1,0:T(8,128)(2,1)S(1)}, bf16[256,512]{1,0:T(8,128)(2,1)S(1)}, u32[]{:S(2)}, u32[]{:S(2)}) collective-permute-start(bf16[256,512]{1,0:T(8,128)(2,1)S(1)} %shard_map.84.refs_0_), channel_id=1, source_target_pairs={{0,4},{1,5},{2,6},{3,7},{4,0},{5,1},{6,2},{7,3},{8,12},{9,13},{10,... | collective-permute-start | bytes 786440 | tf_op jit(solution)/shard_map/ppermute | solution.py:240
  17.1 8.2 %collective-permute-start.5 = (bf16[240,512]{1,0:T(8,128)(2,1)S(1)}, bf16[240,512]{1,0:T(8,128)(2,1)S(1)}, u32[]{:S(2)}, u32[]{:S(2)}) collective-permute-start(bf16[240,512]{1,0:T(8,128)(2,1)S(1)} %get-tuple-element.30), channel_id=1, source_target_pairs={{0,1},{1,2},{2,3},{3,0},{4,5},{5,6},{6,7},{7,4},{8,9},{9,10},{10,1... | collective-permute-start | bytes 737288 | tf_op jit(solution)/shard_map/ppermute | solution.py:243
  17.2 13.5 %collective-permute-start.6 = (bf16[240,512]{1,0:T(8,128)(2,1)S(1)}, bf16[240,512]{1,0:T(8,128)(2,1)S(1)}, u32[]{:S(2)}, u32[]{:S(2)}) collective-permute-start(bf16[240,512]{1,0:T(8,128)(2,1)S(1)} %get-tuple-element.29), channel_id=1, source_target_pairs={{0,3},{1,0},{2,1},{3,2},{4,7},{5,4},{6,5},{7,6},{8,11},{9,8},{10,9... | collective-permute-start | bytes 737288 | tf_op jit(solution)/shard_map/ppermute | solution.py:244
  19.9 11.5 %collective-permute-start = (bf16[2,16,512]{2,1,0:T(8,128)(2,1)S(1)}, bf16[2,16,512]{2,1,0:T(8,128)(2,1)S(1)}, u32[]{:S(2)}, u32[]{:S(2)}) collective-permute-start(bf16[2,16,512]{2,1,0:T(8,128)(2,1)S(1)} %get-tuple-element.15), channel_id=1, source_target_pairs={{0,8},{8,16},{16,24},{1,9},{9,17},{17,25},{2,10},{10,18},{18,26},{... | collective-permute-start | bytes 98312 | tf_op jit(solution)/shard_map/ppermute | solution.py:271
  22.6 27.8 %collective-permute-start.14 = (bf16[384,512]{1,0:T(8,128)(2,1)S(1)}, bf16[384,512]{1,0:T(8,128)(2,1)S(1)}, u32[]{:S(2)}, u32[]{:S(2)}) collective-permute-start(bf16[384,512]{1,0:T(8,128)(2,1)S(1)} %get-tuple-element.28), channel_id=1, source_target_pairs={{0,1},{1,2},{2,3},{3,0},{4,5},{5,6},{6,7},{7,4},{8,9},{9,10},{10,1... | collective-permute-start | bytes 1179656 | tf_op jit(solution)/shard_map/ppermute | solution.py:243
  22.6 27.8 %collective-permute-start.15 = (bf16[384,512]{1,0:T(8,128)(2,1)S(1)}, bf16[384,512]{1,0:T(8,128)(2,1)S(1)}, u32[]{:S(2)}, u32[]{:S(2)}) collective-permute-start(bf16[384,512]{1,0:T(8,128)(2,1)S(1)} %get-tuple-element.27), channel_id=1, source_target_pairs={{0,3},{1,0},{2,1},{3,2},{4,7},{5,4},{6,5},{7,6},{8,11},{9,8},{10,9... | collective-permute-start | bytes 1179656 | tf_op jit(solution)/shard_map/ppermute | solution.py:244
  25.3 8.6 %collective-permute-start.1 = (bf16[2,16,512]{2,1,0:T(8,128)(2,1)S(1)}, bf16[2,16,512]{2,1,0:T(8,128)(2,1)S(1)}, u32[]{:S(2)}, u32[]{:S(2)}) collective-permute-start(bf16[2,16,512]{2,1,0:T(8,128)(2,1)S(1)} %get-tuple-element.17), channel_id=1, source_target_pairs={{8,0},{16,8},{24,16},{9,1},{17,9},{25,17},{10,2},{18,10},{26,18},{... | collective-permute-start | bytes 98312 | tf_op jit(solution)/shard_map/ppermute | solution.py:272
  30.7 5.8 %collective-permute-start.7 = (bf16[80,512]{1,0:T(8,128)(2,1)S(1)}, bf16[80,512]{1,0:T(8,128)(2,1)S(1)}, u32[]{:S(2)}, u32[]{:S(2)}) collective-permute-start(bf16[80,512]{1,0:T(8,128)(2,1)S(1)} %slice.42), channel_id=1, source_target_pairs={{0,1},{1,2},{2,3},{3,0},{4,5},{5,6},{6,7},{7,4},{8,9},{9,10},{10,1... | collective-permute-start | bytes 245768 | tf_op jit(solution)/shard_map/ppermute | solution.py:245
  31.4 5.1 %collective-permute-start.8 = (bf16[80,512]{1,0:T(8,128)(2,1)S(1)}, bf16[80,512]{1,0:T(8,128)(2,1)S(1)}, u32[]{:S(2)}, u32[]{:S(2)}) collective-permute-start(bf16[80,512]{1,0:T(8,128)(2,1)S(1)} %slice.43), channel_id=1, source_target_pairs={{0,3},{1,0},{2,1},{3,2},{4,7},{5,4},{6,5},{7,6},{8,11},{9,8},{10,9... | collective-permute-start | bytes 245768 | tf_op jit(solution)/shard_map/ppermute | solution.py:246
  38.6 15.5 %collective-permute-start.10 = (bf16[8,64,128]{2,1,0:T(8,128)(2,1)S(1)}, bf16[8,64,128]{2,1,0:T(8,128)(2,1)S(1)}, u32[]{:S(2)}, u32[]{:S(2)}) collective-permute-start(bf16[8,64,128]{2,1,0:T(8,128)(2,1)S(1)} %get-tuple-element.21), channel_id=1, source_target_pairs={{0,32},{8,96},{16,160},{24,224},{32,0},{40,64},{48,128},{56,192},{... | collective-permute-start | bytes 393224 | tf_op jit(solution)/shard_map/ppermute | solution.py:251
  47.8 11.8 %collective-permute-start.9 = (bf16[8,64,128]{2,1,0:T(8,128)(2,1)S(1)}, bf16[8,64,128]{2,1,0:T(8,128)(2,1)S(1)}, u32[]{:S(2)}, u32[]{:S(2)}) collective-permute-start(bf16[8,64,128]{2,1,0:T(8,128)(2,1)S(1)} %get-tuple-element.20), channel_id=1, source_target_pairs={{0,0},{8,64},{16,128},{24,192},{32,32},{40,96},{48,160},{56,224},{... | collective-permute-start | bytes 393224 | tf_op jit(solution)/shard_map/ppermute | solution.py:251
  50.4 9.2 %collective-permute-start.16 = (bf16[128,512]{1,0:T(8,128)(2,1)S(1)}, bf16[128,512]{1,0:T(8,128)(2,1)S(1)}, u32[]{:S(2)}, u32[]{:S(2)}) collective-permute-start(bf16[128,512]{1,0:T(8,128)(2,1)S(1)} %slice.46), channel_id=1, source_target_pairs={{0,1},{1,2},{2,3},{3,0},{4,5},{5,6},{6,7},{7,4},{8,9},{9,10},{10,1... | collective-permute-start | bytes 393224 | tf_op jit(solution)/shard_map/ppermute | solution.py:245
  50.5 9.1 %collective-permute-start.17 = (bf16[128,512]{1,0:T(8,128)(2,1)S(1)}, bf16[128,512]{1,0:T(8,128)(2,1)S(1)}, u32[]{:S(2)}, u32[]{:S(2)}) collective-permute-start(bf16[128,512]{1,0:T(8,128)(2,1)S(1)} %slice.47), channel_id=1, source_target_pairs={{0,3},{1,0},{2,1},{3,2},{4,7},{5,4},{6,5},{7,6},{8,11},{9,8},{10,9... | collective-permute-start | bytes 393224 | tf_op jit(solution)/shard_map/ppermute | solution.py:246
  59.6 29.2 %copy-start.6 = (s32[1024]{0:T(1024)S(1)}, s32[1024]{0:T(1024)}, u32[]{:S(2)}) copy-start(s32[1024]{0:T(1024)} %constant.5.clone) | copy-start | bytes 12292
  59.6 40.1 %copy-start.3 = (s32[2,2]{1,0:T(2,128)S(1)}, s32[2,2]{1,0:T(2,128)}, u32[]{:S(2)}) copy-start(s32[2,2]{1,0:T(2,128)} %cycle_tiles.1) | copy-start | bytes 52
  59.6 40.1 %copy-start.4 = (s32[8]{0:T(128)S(1)}, s32[8]{0:T(128)}, u32[]{:S(2)}) copy-start(s32[8]{0:T(128)} %partner.1) | copy-start | bytes 100
  78.2 18.9 %collective-permute-start.18 = (bf16[8,64,128]{2,1,0:T(8,128)(2,1)S(1)}, bf16[8,64,128]{2,1,0:T(8,128)(2,1)S(1)}, u32[]{:S(2)}, u32[]{:S(2)}) collective-permute-start(bf16[8,64,128]{2,1,0:T(8,128)(2,1)S(1)} %get-tuple-element.26), channel_id=1, source_target_pairs={{0,0},{8,64},{16,128},{24,192},{32,32},{40,96},{48,160},{56,224},{... | collective-permute-start | bytes 393224 | tf_op jit(solution)/shard_map/ppermute | solution.py:251
  88.7 11.1 %collective-permute-start.19 = (bf16[8,64,128]{2,1,0:T(8,128)(2,1)S(1)}, bf16[8,64,128]{2,1,0:T(8,128)(2,1)S(1)}, u32[]{:S(2)}, u32[]{:S(2)}) collective-permute-start(bf16[8,64,128]{2,1,0:T(8,128)(2,1)S(1)} %get-tuple-element.25), channel_id=1, source_target_pairs={{0,32},{8,96},{16,160},{24,224},{32,0},{40,64},{48,128},{56,192},{... | collective-permute-start | bytes 393224 | tf_op jit(solution)/shard_map/ppermute | solution.py:251

commit v5 on v2

--- a/solution.py
+++ b/solution.py
@@ -49,7 +49,12 @@
     return (jnp.asarray(order, jnp.int32)[:, None] == columns).astype(BF)
 
 
-def prepare_kernel(ladder_tiles, cycle_tiles, amplitudes, ints, own_ref, inner_ref, first_ref, last_ref, wide, tall):
+HALF = 208
+
+
+def prepare_kernel(
+    ladder_tiles, cycle_tiles, amplitudes, ints, own_ref, inner_ref, first_ref, last_ref, wide, tall
+):
     row = lax.broadcasted_iota(jnp.int32, (512, 128), 0)
     column = lax.broadcasted_iota(jnp.int32, (512, 128), 1)
     ladder_row = row < 256
@@ -67,7 +72,8 @@
         [jnp.where(wanted == c * 128, 1.0, 0.0).astype(BF) for c in range(8)], axis=1
     )
     picked = jnp.dot(pick, amplitudes[...], preferred_element_type=F32).astype(BF)
-    own_ref[:256, :] = picked[:256]
+    for w in range(2):
+        own_ref[w * HALF : w * HALF + PAIRS, :] = picked[w * PAIRS : (w + 1) * PAIRS]
     inner = picked[256:].reshape(16, 16, LANES)
     inner_ref[...] = inner
     first_ref[...] = inner[:REACH]
@@ -81,30 +87,60 @@
         tall[pl.ds(2 * t, 80, stride=8), :] = jnp.where(low, zero, pltpu.roll(one, TILE, 1))
         tall[pl.ds(2 * t + 1, 80, stride=8), :] = jnp.where(low, pltpu.roll(zero, TILE, 1), one)
     for b in range(4):
-        own_ref[256:, b * 128 : (b + 1) * 128] = tall[b * 160 : (b + 1) * 160, :].astype(BF)
-
-
-def source_rows():
+        for w in range(2):
+            own_ref[w * HALF + PAIRS : (w + 1) * HALF, b * 128 : (b + 1) * 128] = tall[
+                b * 160 + w * 80 : b * 160 + (w + 1) * 80, :
+            ].astype(BF)
+
+
+def near_pieces(refs):
+    own, flip, up, down = refs
     vert = lax.axis_index("vert")
     h, y = vert // 4, vert % 4
-    places = [
-        (h, y), (1 - h, y), (h, y + 3), (h, y + 1),
-        (1 - h, y + 3), (1 - h, y + 1), (h, y + 2), (1 - h, y + 2),
-    ]
-    return [a * 4 + b % 4 for a, b in places]
-
-
-def main_kernel(ladder_hbm, before, inner, after, swap, *refs):
-    pieces, (total_ref, sent_ref, ladder_ints, ints, total, sem, sems) = refs[:8], refs[8:]
-    loads = [
-        pltpu.make_async_copy(ladder_hbm.at[w], ladder_ints.at[w], sems.at[w]) for w in range(2)
-    ]
-    for load in loads:
-        load.start()
-    sources = source_rows()
-    parity = lax.axis_index("pi") % 2
-    for d in range(8):
-        ints[sources[d]] = pieces[d][256:, :].astype(F32)
+    places = [(h, y, own), (1 - h, y, flip), (h, y + 3, up), (h, y + 1, down)]
+    return [[(a * 4 + b % 4, ref, w * HALF) for a, b, ref in places] for w in range(2)]
+
+
+def far_pieces(refs):
+    up_2, down_2, up_3, down_3 = refs
+    vert = lax.axis_index("vert")
+    h, y = vert // 4, vert % 4
+    pieces = []
+    for w in range(2):
+        places = [
+            (1 - h, y + 3, up_2, w * HALF), (1 - h, y + 1, down_2, w * HALF),
+            (h, y + 2, (up_2, down_2)[w], 2 * HALF), (1 - h, y + 2, (up_3, down_3)[w], 0),
+        ]
+        pieces.append([(a * 4 + b % 4, ref, first) for a, b, ref, first in places])
+    return pieces
+
+
+def ladder_part(which, pieces, ladder_ints, acc):
+    for source, ref, first in pieces:
+        start = pl.multiple_of(source * LANES, LANES)
+        part = lax.dot_general(
+            ref[first : first + PAIRS, :],
+            ladder_ints[which, :, pl.ds(start, LANES)],
+            (((1,), (1,)), ((), ())),
+            preferred_element_type=F32,
+        )
+        acc = part if acc is None else acc + part
+    return acc
+
+
+def near_kernel(ladder_ints, *refs):
+    for which, pieces in enumerate(near_pieces(refs[:4])):
+        refs[4][:, which * LANES : (which + 1) * LANES] = ladder_part(
+            which, pieces, ladder_ints, None
+        )
+
+
+def main_kernel(ladder_ints, near, before, inner, after, swap, *refs):
+    total, first_ref, second_ref, ints = refs[8:]
+    far = far_pieces(refs[4:8])
+    for w, pieces in enumerate(near_pieces(refs[:4])):
+        for source, ref, first in pieces + far[w]:
+            ints[source, w * 80 : (w + 1) * 80, :] = ref[first + PAIRS : first + HALF, :].astype(F32)
 
     def rows_of(j):
         if j < REACH:
@@ -143,38 +179,21 @@
                 lane = 1024 + r * LANES + t * 128
                 total[j * 8 : j * 8 + 8, lane : lane + 128] = jnp.where(low, even, odd)
     for which in range(2):
-        loads[which].wait()
-        acc = None
-        for d in range(8):
-            start = pl.multiple_of(sources[d] * LANES, LANES)
-            part = lax.dot_general(
-                pieces[d][which * PAIRS : (which + 1) * PAIRS, :],
-                ladder_ints[which, :, pl.ds(start, LANES)],
-                (((1,), (1,)), ((), ())),
-                preferred_element_type=F32,
-            )
-            acc = part if acc is None else acc + part
-        total[:, which * LANES : (which + 1) * LANES] = acc
-    keep = pltpu.make_async_copy(total, total_ref, sem)
-    keep.start()
+        lanes = slice(which * LANES, (which + 1) * LANES)
+        total[:, lanes] = ladder_part(which, far[which], ladder_ints, near[:, lanes])
+    parity = lax.axis_index("pi") % 2
     for s in range(2):
         sent = jnp.dot(
             total[:, s * 1024 : (s + 1) * 1024].astype(BF), swap[...], preferred_element_type=F32
         ).astype(BF)
         upper, under = sent[:64], sent[64:]
-        halves = (
-            jnp.where(parity == 0, upper, under),
-            jnp.where(parity == 0, under, upper),
-        )
-        for k in range(2):
+        halves = (jnp.where(parity == 0, upper, under), jnp.where(parity == 0, under, upper))
+        for half, ref in zip(halves, (first_ref, second_ref)):
             for v in range(8):
-                sent_ref[v, k, s * 64 : (s + 1) * 64, :] = halves[k][:, v * 128 : (v + 1) * 128]
-    keep.wait()
-
-
-def finish_kernel(ladder_tiles, cycle_tiles, partner, total_ref, first, second, place, out_ref, mirrored, total, sem):
-    fetch = pltpu.make_async_copy(total_ref, total, sem)
-    fetch.start()
+                ref[v, s * 64 : (s + 1) * 64, :] = half[:, v * 128 : (v + 1) * 128]
+
+
+def finish_kernel(ladder_tiles, cycle_tiles, partner, total, place, first, second, out_ref, mirrored):
     parity = lax.axis_index("pi") % 2
     for k, arrived in enumerate((first, second)):
         wide = jnp.concatenate([arrived[v] for v in range(8)], axis=1)
@@ -185,7 +204,6 @@
     tile = lax.broadcasted_iota(jnp.int32, (8, LANES), 0)
     own = [(tile == dest).astype(F32) for dest in dests]
     other = [(tile == partner[dest]).astype(F32) for dest in dests]
-    fetch.wait()
 
     def one(i):
         for j in range(16):
@@ -221,58 +239,57 @@
     return jax.ShapeDtypeStruct(dims, kind)
 
 
+def gather(own):
+    flip = lax.ppermute(own, "vert", FLIP)
+    up = lax.ppermute(own, "vert", UP)
+    down = lax.ppermute(own, "vert", DOWN)
+    up_2 = lax.ppermute(jnp.concatenate([flip, up[:HALF]]), "vert", UP)
+    down_2 = lax.ppermute(jnp.concatenate([flip, down[HALF:]]), "vert", DOWN)
+    up_3 = lax.ppermute(up_2[:HALF], "vert", UP)
+    down_3 = lax.ppermute(down_2[HALF : 2 * HALF], "vert", DOWN)
+    return [own, flip, up, down], [up_2, down_2, up_3, down_3]
+
+
 def body(amplitudes, ladder_ints, ladder_tiles, cycle_ints, cycle_tiles, partner):
     edge = shape((REACH, 16, LANES), BF)
     own, inner, first, last = call(
         prepare_kernel,
         [SMEM, SMEM, VMEM, VMEM],
-        [shape((416, LANES), BF), shape((16, 16, LANES), BF), edge, edge],
+        [shape((2 * HALF, LANES), BF), shape((16, 16, LANES), BF), edge, edge],
         [VMEM] * 4,
         [pltpu.VMEM((4, 160, 128), F32), pltpu.VMEM((640, 128), F32)],
         12,
         10**9,
     )(ladder_tiles, cycle_tiles, amplitudes.reshape(1024, LANES), cycle_ints.reshape(160, LANES))
-    flip = lax.ppermute(own, "vert", FLIP)
-    own_up = lax.ppermute(own, "vert", UP)
-    own_down = lax.ppermute(own, "vert", DOWN)
-    flip_up = lax.ppermute(flip, "vert", UP)
-    flip_down = lax.ppermute(flip, "vert", DOWN)
-    far = lax.ppermute(own_up, "vert", UP)
-    flip_far = lax.ppermute(flip_down, "vert", DOWN)
+    near, far = gather(own)
     before = lax.ppermute(last, "pj", [(q, q + 1) for q in range(3)])
     after = lax.ppermute(first, "pj", [(q + 1, q) for q in range(3)])
-    pieces = [own, flip, own_up, own_down, flip_up, flip_down, far, flip_far]
-
-    total, sent = call(
+    begun = call(
+        near_kernel, [VMEM] * 5, shape((PAIRS, 1024), F32), VMEM, [], 8, 10**9
+    )(ladder_ints, *near)
+    block = shape((8, 128, 128), BF)
+    total, sent_0, sent_1 = call(
         main_kernel,
-        [ANY] + [VMEM] * 12,
-        [shape((PAIRS, 2048), F32), shape((8, 2, 128, 128), BF)],
-        [ANY, VMEM],
-        [
-            pltpu.VMEM((2, LANES, 4096), BF),
-            pltpu.VMEM((8, 160, LANES), F32),
-            pltpu.VMEM((PAIRS, 2048), F32),
-            pltpu.SemaphoreType.DMA,
-            pltpu.SemaphoreType.DMA((2,)),
-        ],
-        26,
+        [VMEM] * 14,
+        [shape((PAIRS, 2048), F32), block, block],
+        [VMEM] * 3,
+        [pltpu.VMEM((8, 160, LANES), F32)],
+        12,
         2 * 10**9,
-    )(ladder_ints, before, inner, after, permutation(send_order()), *pieces)
-    arrived = lax.all_to_all(sent, "vert", 0, 0)
-    moved = [lax.ppermute(arrived[:, k], ("pi", "pj"), pair_moves(k)) for k in range(2)]
+    )(ladder_ints, begun, before, inner, after, permutation(send_order()), *near, *far)
+    moved_0 = lax.ppermute(sent_0, ("pi", "pj"), pair_moves(0))
+    arrived_1 = lax.all_to_all(sent_1, "vert", 0, 0)
+    arrived_0 = lax.all_to_all(moved_0, "vert", 0, 0)
+    moved_1 = lax.ppermute(arrived_1, ("pi", "pj"), pair_moves(1))
     return call(
         finish_kernel,
-        [SMEM, SMEM, SMEM, ANY, VMEM, VMEM, VMEM],
+        [SMEM, SMEM, SMEM] + [VMEM] * 4,
         shape((8, 16, 8, LANES), F32),
         VMEM,
-        [
-            pltpu.VMEM((2, 2, 64, 1024), F32),
-            pltpu.VMEM((PAIRS, 2048), F32),
-            pltpu.SemaphoreType.DMA,
-        ],
-        16,
+        [pltpu.VMEM((2, 2, 64, 1024), F32)],
+        12,
         10**9,
-    )(ladder_tiles, cycle_tiles, partner, total, *moved, permutation(place_order()))
+    )(ladder_tiles, cycle_tiles, partner, total, permutation(place_order()), arrived_0, moved_1)
 
 
 def solution(mesh):

time: 105 us -> 92.1 us (0.88)
  the two profiles are of different devices: /device:TPU:3 before, /device:TPU:1 now
where the time goes in v5:
time: 92.1 us; the launch traced here: 91.7 us
  starting transfers between devices  33.7 us (37%)
  waiting for transfers between devices  29.4 us (32%)
  blocking collectives  14.2 us (15%)
  Pallas kernels  9.66 us (10%)
  local copies, waits for them, and re-layouts  3.66 us (4%)
    all_to_all x1, blocking collectives, body(): arrived_1 = lax.all_to_all(sent_1, 'vert', 0, 0)  14.2 us
    ppermute x1, starting transfers between devices, body(): moved_0 = lax.ppermute(sent_0, ('pi', 'pj'), pair_moves(0))  9.43 us
    ppermute x1, waiting for transfers between devices, body(): moved_1 = lax.ppermute(arrived_1, ('pi', 'pj'), pair_moves(1))  7.92 us
    ppermute x1, waiting for transfers between devices, gather(): down = lax.ppermute(own, 'vert', DOWN)  5.74 us
    ppermute x1, starting transfers between devices, body(): before = lax.ppermute(last, 'pj', [(q, q + 1) for q in range(3)])  5.42 us
    all_to_all x1, waiting for transfers between devices, body(): arrived_0 = lax.all_to_all(moved_0, 'vert', 0, 0)  4.54 us
    ppermute x1, waiting for transfers between devices, gather(): down_2 = lax.ppermute(jnp.concatenate([flip, down[HALF:]]), 'vert', DOWN)  4.15 us
    pallas_call x1, Pallas kernels, body(): call(finish_kernel, [SMEM, SMEM, SMEM] + [VMEM] * 4, shape((8, 16, 8, LAN...  4.08 us
  transfers between devices with their start and end apart: 12, of which 7 were waited for; matrix products, arithmetic and copies ran while one was open for 1% of the time, Pallas kernels for 2%

profile of v5, /device:TPU:1, one launch (start us, length us, event | category | flops | bytes accessed | tf_op | source)
XLA Modules:
  0.0 91.7 jit_solution(16965322658258338370)
XLA Ops:
  0.0 1.0 %reshape.9.ints = bf16[160,512]{1,0:T(8,128)(2,1)S(1)} reshape(bf16[16,5,2,512]{3,2,1,0:T(2,128)(2,1)} %param.11) | data formatting | bytes 327680 | tf_op jit(solution)/shard_map/reshape | solution.py:263
  1.0 0.0 copy-start.1
  1.0 0.7 copy-done.1
  1.7 0.7 copy-done.3
  2.4 1.2 %copy-done.6 = bf16[8,16,8,512]{3,2,1,0:T(8,128)(2,1)S(1)} copy-done((bf16[8,16,8,512]{3,2,1,0:T(8,128)(2,1)S(1)}, bf16[8,16,8,512]{3,2,1,0:T(8,128)(2,1)}, u32[]{:S(2)}) %copy-start.6) | copy-done | bytes 1048600
  3.6 1.3 %shard_map.82 = (bf16[416,512]{1,0:T(8,128)(2,1)S(1)}, bf16[16,16,512]{2,1,0:T(8,128)(2,1)S(1)}, bf16[2,16,512]{2,1,0:T(8,128)(2,1)S(1)}, bf16[2,16,512]{2,1,0:T(8,128)(2,1)S(1)}) custom-call(s32[2,2]{1,0:T(2,128)S(1)} %copy-done.1, s32[2,2]{1,0:T(2,128)S(1)} %copy-done.3, bf16[1024,512]{1,0:T(8,128)(2,1)S(1)} %bitcast.1, bf16[160,512]{1,0:T(8,128)(2,1)S(1)} %reshape.9.ints), custom_call_target="tpu_custom_call" | custom-call | flops 1000000000 | bytes 4194304 | tf_op jit(solution)/shard_map/pallas_call | solution.py:255
  4.9 3.6 %collective-permute-start.2 = (bf16[416,512]{1,0:T(8,128)(2,1)S(1)}, bf16[416,512]{1,0:T(8,128)(2,1)S(1)}, u32[]{:S(2)}, u32[]{:S(2)}) collective-permute-start(bf16[416,512]{1,0:T(8,128)(2,1)S(1)} %get-tuple-element.12.refs_0_), channel_id=1, source_target_pairs={{0,3},{1,0},{2,1},{3,2},{4,7},{5,4},{6,5},{7,6},{8,11},{9,8},{10,9... | collective-permute-start | bytes 1277960 | tf_op jit(solution)/shard_map/ppermute | solution.py:245
  8.6 2.7 %collective-permute-start = (bf16[416,512]{1,0:T(8,128)(2,1)S(1)}, bf16[416,512]{1,0:T(8,128)(2,1)S(1)}, u32[]{:S(2)}, u32[]{:S(2)}) collective-permute-start(bf16[416,512]{1,0:T(8,128)(2,1)S(1)} %get-tuple-element.12.refs_0_), channel_id=1, source_target_pairs={{0,4},{1,5},{2,6},{3,7},{4,0},{5,1},{6,2},{7,3},{8,12},{9,13},{10,... | collective-permute-start | bytes 1277960 | tf_op jit(solution)/shard_map/ppermute | solution.py:243
  11.3 5.7 %collective-permute-done.2.refs_3_ = bf16[416,512]{1,0:T(8,128)(2,1)S(1)} collective-permute-done((bf16[416,512]{1,0:T(8,128)(2,1)S(1)}, bf16[416,512]{1,0:T(8,128)(2,1)S(1)}, u32[]{:S(2)}, u32[]{:S(2)}) %collective-permute-start.2) | collective-permute-done | bytes 426016 | tf_op jit(solution)/shard_map/ppermute | solution.py:245
  17.1 3.1 %collective-permute-done.1.refs_2_ = bf16[416,512]{1,0:T(8,128)(2,1)S(1)} collective-permute-done((bf16[416,512]{1,0:T(8,128)(2,1)S(1)}, bf16[416,512]{1,0:T(8,128)(2,1)S(1)}, u32[]{:S(2)}, u32[]{:S(2)}) %collective-permute-start.1) | collective-permute-done | bytes 426016 | tf_op jit(solution)/shard_map/ppermute | solution.py:244
  20.2 0.1 pad_maximum_fusion
  20.2 2.7 %collective-permute-start.6 = (bf16[624,512]{1,0:T(8,128)(2,1)S(1)}, bf16[624,512]{1,0:T(8,128)(2,1)S(1)}, u32[]{:S(2)}, u32[]{:S(2)}) collective-permute-start(bf16[624,512]{1,0:T(8,128)(2,1)S(1)} %get-tuple-element.19), channel_id=1, source_target_pairs={{0,3},{1,0},{2,1},{3,2},{4,7},{5,4},{6,5},{7,6},{8,11},{9,8},{10,9... | collective-permute-start | bytes 1916936 | tf_op jit(solution)/shard_map/ppermute | solution.py:247
  23.0 5.4 %collective-permute-start.3 = (bf16[2,16,512]{2,1,0:T(8,128)(2,1)S(1)}, bf16[2,16,512]{2,1,0:T(8,128)(2,1)S(1)}, u32[]{:S(2)}, u32[]{:S(2)}) collective-permute-start(bf16[2,16,512]{2,1,0:T(8,128)(2,1)S(1)} %get-tuple-element.13), channel_id=1, source_target_pairs={{0,8},{8,16},{16,24},{1,9},{9,17},{17,25},{2,10},{10,18},{18,26},{... | collective-permute-start | bytes 98312 | tf_op jit(solution)/shard_map/ppermute | solution.py:265
  28.4 1.9 %collective-permute-start.4 = (bf16[2,16,512]{2,1,0:T(8,128)(2,1)S(1)}, bf16[2,16,512]{2,1,0:T(8,128)(2,1)S(1)}, u32[]{:S(2)}, u32[]{:S(2)}) collective-permute-start(bf16[2,16,512]{2,1,0:T(8,128)(2,1)S(1)} %get-tuple-element.15), channel_id=1, source_target_pairs={{8,0},{16,8},{24,16},{9,1},{17,9},{25,17},{10,2},{18,10},{26,18},{... | collective-permute-start | bytes 98312 | tf_op jit(solution)/shard_map/ppermute | solution.py:266
  30.3 4.2 %collective-permute-done.6.refs_5_ = bf16[624,512]{1,0:T(8,128)(2,1)S(1)} collective-permute-done((bf16[624,512]{1,0:T(8,128)(2,1)S(1)}, bf16[624,512]{1,0:T(8,128)(2,1)S(1)}, u32[]{:S(2)}, u32[]{:S(2)}) %collective-permute-start.6) | collective-permute-done | bytes 639008 | tf_op jit(solution)/shard_map/ppermute | solution.py:247
  34.5 3.5 %collective-permute-start.8 = (bf16[208,512]{1,0:T(8,128)(2,1)S(1)}, bf16[208,512]{1,0:T(8,128)(2,1)S(1)}, u32[]{:S(2)}, u32[]{:S(2)}) collective-permute-start(bf16[208,512]{1,0:T(8,128)(2,1)S(1)} %slice.19), channel_id=1, source_target_pairs={{0,3},{1,0},{2,1},{3,2},{4,7},{5,4},{6,5},{7,6},{8,11},{9,8},{10,9... | collective-permute-start | bytes 638984 | tf_op jit(solution)/shard_map/ppermute | solution.py:249
  38.0 0.1 collective-permute-start.7
  38.1 0.4 fusion.swap
  38.5 1.5 %shard_map.83.near = f32[128,1024]{1,0:T(8,128)S(1)} custom-call(bf16[2,512,4096]{2,1,0:T(8,128)(2,1)S(1)} %copy-done, bf16[416,512]{1,0:T(8,128)(2,1)S(1)} %get-tuple-element.12.refs_0_, bf16[416,512]{1,0:T(8,128)(2,1)S(1)} %collective-permute-done.refs_1_, bf16[416,512]{1,0:T(8,128)(2,1)S(1)} %collective-permute-done.1.refs_2_, ...), custom_call_target="tpu_custom_call" | custom-call | flops 1000000000 | bytes 4194304 | tf_op jit(solution)/shard_map/pallas_call | solution.py:267
  40.1 0.7 collective-permute-done.8.refs_7_
  40.8 3.2 %collective-permute-done.7.refs_6_ = bf16[208,512]{1,0:T(8,128)(2,1)S(1)} collective-permute-done((bf16[208,512]{1,0:T(8,128)(2,1)S(1)}, bf16[208,512]{1,0:T(8,128)(2,1)S(1)}, u32[]{:S(2)}, u32[]{:S(2)}) %collective-permute-start.7) | collective-permute-done | bytes 213024 | tf_op jit(solution)/shard_map/ppermute | solution.py:248
  44.0 2.8 %shard_map.84 = (f32[128,2048]{1,0:T(8,128)S(1)}, bf16[8,128,128]{2,1,0:T(8,128)(2,1)S(1)}, bf16[8,128,128]{2,1,0:T(8,128)(2,1)S(1)}) custom-call(bf16[2,512,4096]{2,1,0:T(8,128)(2,1)S(1)} %copy-done, f32[128,1024]{1,0:T(8,128)S(1)} %shard_map.83.near, bf16[2,16,512]{2,1,0:T(8,128)(2,1)S(1)} %collective-permute-done.3.before, ...), custom_call_target="tpu_custom_call" | custom-call | flops 2000000000 | bytes 4194304 | tf_op jit(solution)/shard_map/pallas_call | solution.py:271
  46.8 0.0 copy-start.2
  46.8 0.0 copy-start.4
  46.8 9.4 %collective-permute-start.9 = (bf16[8,128,128]{2,1,0:T(8,128)(2,1)S(1)}, bf16[8,128,128]{2,1,0:T(8,128)(2,1)}, u32[]{:S(2)}, u32[]{:S(2)}) collective-permute-start(bf16[8,128,128]{2,1,0:T(8,128)(2,1)S(1)} %get-tuple-element.17), channel_id=1, source_target_pairs={{0,0},{8,64},{16,128},{24,192},{32,32},{40,96},{48,160},{56,224},{... | collective-permute-start | bytes 786440 | tf_op jit(solution)/shard_map/ppermute | solution.py:280
  56.2 14.2 %all_to_all.10 = bf16[8,128,128]{2,1,0:T(8,128)(2,1)} all-to-all(bf16[8,128,128]{2,1,0:T(8,128)(2,1)S(1)} %get-tuple-element.18), channel_id=1, replica_groups=mesh['pi'=8,'pj'=4,'vert'=8] {'vert'}, dimensions={0} | all-to-all | bytes 524288 | tf_op jit(solution)/shard_map/all_to_all | solution.py:281
  70.4 0.9 collective-permute-start.10
  71.3 3.4 %all-to-all-start = ((bf16[8,128,128]{2,1,0:T(8,128)(2,1)}), bf16[8,128,128]{2,1,0:T(8,128)(2,1)S(1)}, u32[]{:S(2)}, u32[]{:S(2)}) async-start(bf16[8,128,128]{2,1,0:T(8,128)(2,1)} %collective-permute-done.9), calls=%async_computation | async-start | bytes 524288 | tf_op jit(solution)/shard_map/all_to_all | solution.py:282
  74.7 0.4 fusion.1.place
  75.1 7.9 %collective-permute-done.10.second = bf16[8,128,128]{2,1,0:T(8,128)(2,1)} collective-permute-done((bf16[8,128,128]{2,1,0:T(8,128)(2,1)}, bf16[8,128,128]{2,1,0:T(8,128)(2,1)}, u32[]{:S(2)}, u32[]{:S(2)}) %collective-permute-start.10) | collective-permute-done | bytes 262176 | tf_op jit(solution)/shard_map/ppermute | solution.py:283
  83.0 4.5 %all-to-all-done.first = bf16[8,128,128]{2,1,0:T(8,128)(2,1)S(1)} async-done(((bf16[8,128,128]{2,1,0:T(8,128)(2,1)}), bf16[8,128,128]{2,1,0:T(8,128)(2,1)S(1)}, u32[]{:S(2)}, u32[]{:S(2)}) %all-to-all-start) | async-done | bytes 262176 | tf_op jit(solution)/shard_map/all_to_all | solution.py:282
  87.6 4.1 %shard_map.85 = f32[8,16,8,512]{3,2,1,0:T(8,128)} custom-call(s32[2,2]{1,0:T(2,128)S(1)} %copy-done.2, s32[2,2]{1,0:T(2,128)S(1)} %copy-done.4, s32[8]{0:T(128)S(1)} %copy-done.5, f32[128,2048]{1,0:T(8,128)S(1)} %get-tuple-element.16.total, bf16[1024,1024]{1,0:T(8,128)(2,1)S(1)} %fusion.1.place, bf16[8,128,128]{2,1,0:T(8,128)(2,1)S(1)} %all-to-all-done.first, ...), custom_call_target="tpu_custom_call" | custom-call | flops 1000000000 | bytes 4194304 | tf_op jit(solution)/shard_map/pallas_call | solution.py:284
  (23 shorter events, 0.1 us)
Async XLA Ops:
  0.0 38.1 %copy-start.8 = (s32[1024]{0:T(1024)S(1)}, s32[1024]{0:T(1024)}, u32[]{:S(2)}) copy-start(s32[1024]{0:T(1024)} %constant.4.clone) | copy-start | bytes 12292
  1.0 0.7 copy-start.1
  1.7 0.7 copy-start.3
  2.4 1.2 %copy-start.6 = (bf16[8,16,8,512]{3,2,1,0:T(8,128)(2,1)S(1)}, bf16[8,16,8,512]{3,2,1,0:T(8,128)(2,1)}, u32[]{:S(2)}) copy-start(bf16[8,16,8,512]{3,2,1,0:T(8,128)(2,1)} %param.8) | copy-start | bytes 3145732
  3.6 34.9 %copy-start = (bf16[2,512,4096]{2,1,0:T(8,128)(2,1)S(1)}, bf16[2,512,4096]{2,1,0:T(8,128)(2,1)}, u32[]{:S(2)}) copy-start(bf16[2,512,4096]{2,1,0:T(8,128)(2,1)} %ladder_ints.3) | copy-start | bytes 25165828
  4.9 12.1 %collective-permute-start.2 = (bf16[416,512]{1,0:T(8,128)(2,1)S(1)}, bf16[416,512]{1,0:T(8,128)(2,1)S(1)}, u32[]{:S(2)}, u32[]{:S(2)}) collective-permute-start(bf16[416,512]{1,0:T(8,128)(2,1)S(1)} %get-tuple-element.12.refs_0_), channel_id=1, source_target_pairs={{0,3},{1,0},{2,1},{3,2},{4,7},{5,4},{6,5},{7,6},{8,11},{9,8},{10,9... | collective-permute-start | bytes 1277960 | tf_op jit(solution)/shard_map/ppermute | solution.py:245
  8.5 11.6 %collective-permute-start.1 = (bf16[416,512]{1,0:T(8,128)(2,1)S(1)}, bf16[416,512]{1,0:T(8,128)(2,1)S(1)}, u32[]{:S(2)}, u32[]{:S(2)}) collective-permute-start(bf16[416,512]{1,0:T(8,128)(2,1)S(1)} %get-tuple-element.12.refs_0_), channel_id=1, source_target_pairs={{0,1},{1,2},{2,3},{3,0},{4,5},{5,6},{6,7},{7,4},{8,9},{9,10},{10,1... | collective-permute-start | bytes 1277960 | tf_op jit(solution)/shard_map/ppermute | solution.py:244
  8.6 11.6 %collective-permute-start = (bf16[416,512]{1,0:T(8,128)(2,1)S(1)}, bf16[416,512]{1,0:T(8,128)(2,1)S(1)}, u32[]{:S(2)}, u32[]{:S(2)}) collective-permute-start(bf16[416,512]{1,0:T(8,128)(2,1)S(1)} %get-tuple-element.12.refs_0_), channel_id=1, source_target_pairs={{0,4},{1,5},{2,6},{3,7},{4,0},{5,1},{6,2},{7,3},{8,12},{9,13},{10,... | collective-permute-start | bytes 1277960 | tf_op jit(solution)/shard_map/ppermute | solution.py:243
  20.2 14.2 %collective-permute-start.6 = (bf16[624,512]{1,0:T(8,128)(2,1)S(1)}, bf16[624,512]{1,0:T(8,128)(2,1)S(1)}, u32[]{:S(2)}, u32[]{:S(2)}) collective-permute-start(bf16[624,512]{1,0:T(8,128)(2,1)S(1)} %get-tuple-element.19), channel_id=1, source_target_pairs={{0,3},{1,0},{2,1},{3,2},{4,7},{5,4},{6,5},{7,6},{8,11},{9,8},{10,9... | collective-permute-start | bytes 1916936 | tf_op jit(solution)/shard_map/ppermute | solution.py:247
  23.0 15.0 %collective-permute-start.5 = (bf16[624,512]{1,0:T(8,128)(2,1)S(1)}, bf16[624,512]{1,0:T(8,128)(2,1)S(1)}, u32[]{:S(2)}, u32[]{:S(2)}) collective-permute-start(bf16[624,512]{1,0:T(8,128)(2,1)S(1)} %get-tuple-element.20), channel_id=1, source_target_pairs={{0,1},{1,2},{2,3},{3,0},{4,5},{5,6},{6,7},{7,4},{8,9},{9,10},{10,1... | collective-permute-start | bytes 1916936 | tf_op jit(solution)/shard_map/ppermute | solution.py:246
  23.0 17.1 %collective-permute-start.3 = (bf16[2,16,512]{2,1,0:T(8,128)(2,1)S(1)}, bf16[2,16,512]{2,1,0:T(8,128)(2,1)S(1)}, u32[]{:S(2)}, u32[]{:S(2)}) collective-permute-start(bf16[2,16,512]{2,1,0:T(8,128)(2,1)S(1)} %get-tuple-element.13), channel_id=1, source_target_pairs={{0,8},{8,16},{16,24},{1,9},{9,17},{17,25},{2,10},{10,18},{18,26},{... | collective-permute-start | bytes 98312 | tf_op jit(solution)/shard_map/ppermute | solution.py:265
  28.4 11.7 %collective-permute-start.4 = (bf16[2,16,512]{2,1,0:T(8,128)(2,1)S(1)}, bf16[2,16,512]{2,1,0:T(8,128)(2,1)S(1)}, u32[]{:S(2)}, u32[]{:S(2)}) collective-permute-start(bf16[2,16,512]{2,1,0:T(8,128)(2,1)S(1)} %get-tuple-element.15), channel_id=1, source_target_pairs={{8,0},{16,8},{24,16},{9,1},{17,9},{25,17},{10,2},{18,10},{26,18},{... | collective-permute-start | bytes 98312 | tf_op jit(solution)/shard_map/ppermute | solution.py:266
  34.5 6.3 %collective-permute-start.8 = (bf16[208,512]{1,0:T(8,128)(2,1)S(1)}, bf16[208,512]{1,0:T(8,128)(2,1)S(1)}, u32[]{:S(2)}, u32[]{:S(2)}) collective-permute-start(bf16[208,512]{1,0:T(8,128)(2,1)S(1)} %slice.19), channel_id=1, source_target_pairs={{0,3},{1,0},{2,1},{3,2},{4,7},{5,4},{6,5},{7,6},{8,11},{9,8},{10,9... | collective-permute-start | bytes 638984 | tf_op jit(solution)/shard_map/ppermute | solution.py:249
  38.0 6.0 %collective-permute-start.7 = (bf16[208,512]{1,0:T(8,128)(2,1)S(1)}, bf16[208,512]{1,0:T(8,128)(2,1)S(1)}, u32[]{:S(2)}, u32[]{:S(2)}) collective-permute-start(bf16[208,512]{1,0:T(8,128)(2,1)S(1)} %slice.18), channel_id=1, source_target_pairs={{0,1},{1,2},{2,3},{3,0},{4,5},{5,6},{6,7},{7,4},{8,9},{9,10},{10,1... | collective-permute-start | bytes 638984 | tf_op jit(solution)/shard_map/ppermute | solution.py:248
  44.0 30.7 %copy-start.7 = (s32[1024]{0:T(1024)S(1)}, s32[1024]{0:T(1024)}, u32[]{:S(2)}) copy-start(s32[1024]{0:T(1024)} %constant.5.clone) | copy-start | bytes 12292
  46.8 40.8 %copy-start.2 = (s32[2,2]{1,0:T(2,128)S(1)}, s32[2,2]{1,0:T(2,128)}, u32[]{:S(2)}) copy-start(s32[2,2]{1,0:T(2,128)} %ladder_tiles.3) | copy-start | bytes 52
  46.8 40.8 %copy-start.4 = (s32[2,2]{1,0:T(2,128)S(1)}, s32[2,2]{1,0:T(2,128)}, u32[]{:S(2)}) copy-start(s32[2,2]{1,0:T(2,128)} %cycle_tiles.3) | copy-start | bytes 52
  46.8 40.8 %copy-start.5 = (s32[8]{0:T(128)S(1)}, s32[8]{0:T(128)}, u32[]{:S(2)}) copy-start(s32[8]{0:T(128)} %partner.1) | copy-start | bytes 100
  46.8 24.5 %collective-permute-start.9 = (bf16[8,128,128]{2,1,0:T(8,128)(2,1)S(1)}, bf16[8,128,128]{2,1,0:T(8,128)(2,1)}, u32[]{:S(2)}, u32[]{:S(2)}) collective-permute-start(bf16[8,128,128]{2,1,0:T(8,128)(2,1)S(1)} %get-tuple-element.17), channel_id=1, source_target_pairs={{0,0},{8,64},{16,128},{24,192},{32,32},{40,96},{48,160},{56,224},{... | collective-permute-start | bytes 786440 | tf_op jit(solution)/shard_map/ppermute | solution.py:280
  70.4 12.6 %collective-permute-start.10 = (bf16[8,128,128]{2,1,0:T(8,128)(2,1)}, bf16[8,128,128]{2,1,0:T(8,128)(2,1)}, u32[]{:S(2)}, u32[]{:S(2)}) collective-permute-start(bf16[8,128,128]{2,1,0:T(8,128)(2,1)} %all_to_all.10), channel_id=1, source_target_pairs={{0,32},{8,96},{16,160},{24,224},{32,0},{40,64},{48,128},{56,192},{... | collective-permute-start | bytes 786440 | tf_op jit(solution)/shard_map/ppermute | solution.py:283
  71.3 16.3 %all-to-all-start = ((bf16[8,128,128]{2,1,0:T(8,128)(2,1)}), bf16[8,128,128]{2,1,0:T(8,128)(2,1)S(1)}, u32[]{:S(2)}, u32[]{:S(2)}) async-start(bf16[8,128,128]{2,1,0:T(8,128)(2,1)} %collective-permute-done.9), calls=%async_computation | async-start | bytes 524288 | tf_op jit(solution)/shard_map/all_to_all | solution.py:282

commit v6 on v5

--- a/solution.py
+++ b/solution.py
@@ -52,34 +52,17 @@
 HALF = 208
 
 
-def prepare_kernel(
-    ladder_tiles, cycle_tiles, amplitudes, ints, own_ref, inner_ref, first_ref, last_ref, wide, tall
-):
-    row = lax.broadcasted_iota(jnp.int32, (512, 128), 0)
-    column = lax.broadcasted_iota(jnp.int32, (512, 128), 1)
-    ladder_row = row < 256
-    i = row & 7
-    j = jnp.where(ladder_row, (row >> 3) & 15, (row >> 4) & 15)
-    which = jnp.where(ladder_row, (row >> 7) & 1, (row >> 3) & 1)
-    ladder_0, cycle_0 = ladder_tiles[0, 1], cycle_tiles[0, 1]
-    tile = jnp.where(
-        ladder_row,
-        ladder_0 + which * (ladder_tiles[1, 1] - ladder_0),
-        cycle_0 + which * (cycle_tiles[1, 1] - cycle_0),
-    )
-    wanted = (i * 16 + j) * 8 + tile - column
-    pick = jnp.concatenate(
-        [jnp.where(wanted == c * 128, 1.0, 0.0).astype(BF) for c in range(8)], axis=1
-    )
-    picked = jnp.dot(pick, amplitudes[...], preferred_element_type=F32).astype(BF)
-    for w in range(2):
-        own_ref[w * HALF : w * HALF + PAIRS, :] = picked[w * PAIRS : (w + 1) * PAIRS]
-    inner = picked[256:].reshape(16, 16, LANES)
-    inner_ref[...] = inner
-    first_ref[...] = inner[:REACH]
-    last_ref[...] = inner[16 - REACH :]
-    for t in range(4):
-        wide[t] = ints[:, t * 128 : (t + 1) * 128].astype(F32)
+def prepare_kernel(*refs):
+    inputs, (own_ref, inner_ref, first_ref, last_ref), held = refs[:4], refs[4:8], refs[8:12]
+    wide, tall, sems = refs[12:]
+    loads = [pltpu.make_async_copy(a, b, sems.at[n]) for n, (a, b) in enumerate(zip(inputs, held))]
+    for load in loads:
+        load.start()
+    ladder_tiles, cycle_tiles, amplitudes, ints = held
+    loads[3].wait()
+    for n in range(80):
+        for t in range(4):
+            wide[t, 2 * n : 2 * n + 2, :] = ints[n, :, t * 128 : (t + 1) * 128].astype(F32)
     low = lax.broadcasted_iota(jnp.int32, (80, 128), 1) < TILE
     for t in range(4):
         zero = wide[t, pl.ds(0, 80, stride=2), :]
@@ -91,6 +74,32 @@
             own_ref[w * HALF + PAIRS : (w + 1) * HALF, b * 128 : (b + 1) * 128] = tall[
                 b * 160 + w * 80 : b * 160 + (w + 1) * 80, :
             ].astype(BF)
+    row = lax.broadcasted_iota(jnp.int32, (512, 128), 0)
+    column = lax.broadcasted_iota(jnp.int32, (512, 128), 1)
+    ladder_row = row < 256
+    for load in loads[:2]:
+        load.wait()
+    i = row & 7
+    j = jnp.where(ladder_row, (row >> 3) & 15, (row >> 4) & 15)
+    which = jnp.where(ladder_row, (row >> 7) & 1, (row >> 3) & 1)
+    ladder_0, cycle_0 = ladder_tiles[0, 1], cycle_tiles[0, 1]
+    tile = jnp.where(
+        ladder_row,
+        ladder_0 + which * (ladder_tiles[1, 1] - ladder_0),
+        cycle_0 + which * (cycle_tiles[1, 1] - cycle_0),
+    )
+    wanted = (i * 16 + j) * 8 + tile - column
+    pick = jnp.concatenate(
+        [jnp.where(wanted == c * 128, 1.0, 0.0).astype(BF) for c in range(8)], axis=1
+    )
+    loads[2].wait()
+    picked = jnp.dot(pick, amplitudes[...], preferred_element_type=F32).astype(BF)
+    for w in range(2):
+        own_ref[w * HALF : w * HALF + PAIRS, :] = picked[w * PAIRS : (w + 1) * PAIRS]
+    inner = picked[256:].reshape(16, 16, LANES)
+    inner_ref[...] = inner
+    first_ref[...] = inner[:REACH]
+    last_ref[...] = inner[16 - REACH :]
 
 
 def near_pieces(refs):
@@ -102,17 +111,18 @@
 
 
 def far_pieces(refs):
-    up_2, down_2, up_3, down_3 = refs
+    up_2, down_2, side_2, up_3, down_3 = refs
     vert = lax.axis_index("vert")
     h, y = vert // 4, vert % 4
-    pieces = []
-    for w in range(2):
-        places = [
-            (1 - h, y + 3, up_2, w * HALF), (1 - h, y + 1, down_2, w * HALF),
-            (h, y + 2, (up_2, down_2)[w], 2 * HALF), (1 - h, y + 2, (up_3, down_3)[w], 0),
-        ]
-        pieces.append([(a * 4 + b % 4, ref, first) for a, b, ref, first in places])
-    return pieces
+    places = [(1 - h, y + 3), (1 - h, y + 1), (h, y + 2), (1 - h, y + 2)]
+    held = [
+        [(up_2, 0), (down_2, 0), (up_2, HALF), (down_3, 0)],
+        [(side_2, 0), (side_2, HALF), (down_2, HALF), (up_3, 0)],
+    ]
+    return [
+        [(a * 4 + b % 4, ref, first) for (a, b), (ref, first) in zip(places, held[w])]
+        for w in range(2)
+    ]
 
 
 def ladder_part(which, pieces, ladder_ints, acc):
@@ -136,8 +146,8 @@
 
 
 def main_kernel(ladder_ints, near, before, inner, after, swap, *refs):
-    total, first_ref, second_ref, ints = refs[8:]
-    far = far_pieces(refs[4:8])
+    total, first_ref, second_ref, ints = refs[9:]
+    far = far_pieces(refs[4:9])
     for w, pieces in enumerate(near_pieces(refs[:4])):
         for source, ref, first in pieces + far[w]:
             ints[source, w * 80 : (w + 1) * 80, :] = ref[first + PAIRS : first + HALF, :].astype(F32)
@@ -193,7 +203,9 @@
                 ref[v, s * 64 : (s + 1) * 64, :] = half[:, v * 128 : (v + 1) * 128]
 
 
-def finish_kernel(ladder_tiles, cycle_tiles, partner, total, place, first, second, out_ref, mirrored):
+def finish_kernel(
+    ladder_tiles, cycle_tiles, partner, total, place, first, second, out_ref, mirrored, held, sems
+):
     parity = lax.axis_index("pi") % 2
     for k, arrived in enumerate((first, second)):
         wide = jnp.concatenate([arrived[v] for v in range(8)], axis=1)
@@ -205,6 +217,9 @@
     own = [(tile == dest).astype(F32) for dest in dests]
     other = [(tile == partner[dest]).astype(F32) for dest in dests]
 
+    def store(i):
+        return pltpu.make_async_copy(held.at[i], out_ref.at[i], sems.at[i])
+
     def one(i):
         for j in range(16):
             acc = None
@@ -213,14 +228,16 @@
                 term = own[s] * total[pl.ds(j * 8 + i, 1), s * LANES : (s + 1) * LANES]
                 acc = term if acc is None else acc + term
                 acc = acc + other[s] * mirrored[s // 2, j // 8, pl.ds(i * 8 + j % 8, 1), lanes]
-            out_ref[i, j] = acc
+            held[i, j] = acc
+        store(i).start()
 
     pl.loop(0, 8)(one)
+    pl.loop(0, 8)(lambda i: store(i).wait())
 
 
 SMEM = pl.BlockSpec(memory_space=pltpu.SMEM)
 VMEM = pl.BlockSpec(memory_space=pltpu.VMEM)
-ANY = pl.BlockSpec(memory_space=pl.ANY)
+HBM = pl.BlockSpec(memory_space=pltpu.HBM)
 
 
 def call(kernel, ins, outs, out_specs, scratch, limit, flops):
@@ -240,27 +257,36 @@
 
 
 def gather(own):
+    down = lax.ppermute(own, "vert", DOWN)
+    up = lax.ppermute(own, "vert", UP)
     flip = lax.ppermute(own, "vert", FLIP)
-    up = lax.ppermute(own, "vert", UP)
-    down = lax.ppermute(own, "vert", DOWN)
-    up_2 = lax.ppermute(jnp.concatenate([flip, up[:HALF]]), "vert", UP)
-    down_2 = lax.ppermute(jnp.concatenate([flip, down[HALF:]]), "vert", DOWN)
-    up_3 = lax.ppermute(up_2[:HALF], "vert", UP)
-    down_3 = lax.ppermute(down_2[HALF : 2 * HALF], "vert", DOWN)
-    return [own, flip, up, down], [up_2, down_2, up_3, down_3]
+    side_2 = lax.ppermute(jnp.concatenate([up[HALF:], down[HALF:]]), "vert", FLIP)
+    up_2 = lax.ppermute(jnp.concatenate([flip[:HALF], up[:HALF]]), "vert", UP)
+    down_2 = lax.ppermute(jnp.concatenate([flip[:HALF], down[HALF:]]), "vert", DOWN)
+    up_3 = lax.ppermute(side_2[:HALF], "vert", UP)
+    down_3 = lax.ppermute(down_2[:HALF], "vert", DOWN)
+    return [own, flip, up, down], [up_2, down_2, side_2, up_3, down_3]
 
 
 def body(amplitudes, ladder_ints, ladder_tiles, cycle_ints, cycle_tiles, partner):
     edge = shape((REACH, 16, LANES), BF)
     own, inner, first, last = call(
         prepare_kernel,
-        [SMEM, SMEM, VMEM, VMEM],
+        [HBM] * 4,
         [shape((2 * HALF, LANES), BF), shape((16, 16, LANES), BF), edge, edge],
         [VMEM] * 4,
-        [pltpu.VMEM((4, 160, 128), F32), pltpu.VMEM((640, 128), F32)],
-        12,
+        [
+            pltpu.SMEM((2, 2), jnp.int32),
+            pltpu.SMEM((2, 2), jnp.int32),
+            pltpu.VMEM((1024, LANES), BF),
+            pltpu.VMEM((80, 2, LANES), BF),
+            pltpu.VMEM((4, 160, 128), F32),
+            pltpu.VMEM((640, 128), F32),
+            pltpu.SemaphoreType.DMA((4,)),
+        ],
+        60,
         10**9,
-    )(ladder_tiles, cycle_tiles, amplitudes.reshape(1024, LANES), cycle_ints.reshape(160, LANES))
+    )(ladder_tiles, cycle_tiles, amplitudes.reshape(1024, LANES), cycle_ints.reshape(80, 2, LANES))
     near, far = gather(own)
     before = lax.ppermute(last, "pj", [(q, q + 1) for q in range(3)])
     after = lax.ppermute(first, "pj", [(q + 1, q) for q in range(3)])
@@ -270,7 +296,7 @@
     block = shape((8, 128, 128), BF)
     total, sent_0, sent_1 = call(
         main_kernel,
-        [VMEM] * 14,
+        [VMEM] * 15,
         [shape((PAIRS, 2048), F32), block, block],
         [VMEM] * 3,
         [pltpu.VMEM((8, 160, LANES), F32)],
@@ -281,12 +307,17 @@
     arrived_1 = lax.all_to_all(sent_1, "vert", 0, 0)
     arrived_0 = lax.all_to_all(moved_0, "vert", 0, 0)
     moved_1 = lax.ppermute(arrived_1, ("pi", "pj"), pair_moves(1))
+    whole = shape((8, 16, 8, LANES), F32)
     return call(
         finish_kernel,
         [SMEM, SMEM, SMEM] + [VMEM] * 4,
-        shape((8, 16, 8, LANES), F32),
-        VMEM,
-        [pltpu.VMEM((2, 2, 64, 1024), F32)],
+        whole,
+        HBM,
+        [
+            pltpu.VMEM((2, 2, 64, 1024), F32),
+            pltpu.VMEM((8, 16, 8, LANES), F32),
+            pltpu.SemaphoreType.DMA((8,)),
+        ],
         12,
         10**9,
     )(ladder_tiles, cycle_tiles, partner, total, permutation(place_order()), arrived_0, moved_1)

time: 92.1 us -> 87.8 us (0.953)
  waiting for transfers between devices: 29.4 us -> 21.7 us
  local copies, waits for them, and re-layouts: 3.66 us -> 5.18 us
  Pallas kernels: 9.66 us -> 11 us
    ppermute x4 -> x5, waiting for transfers between devices: 8.07 us -> 0.17 us  [the longest x1 0.16 us: gather(): up_3 = lax.ppermute(side_2[:HALF], 'vert', UP)]
    ppermute x4 -> x5, starting transfers between devices: 6.3 us -> 8.83 us  [the longest x1 3.27 us: gather(): down_3 = lax.ppermute(down_2[:HALF], 'vert', DOWN)]
    unnamed x18, local copies, waits for them, and re-layouts: 2.61 us -> 5.09 us
    pallas_call x3, Pallas kernels: 8.15 us -> 9.46 us  [the longest x1 3.54 us: body(): call(finish_kernel, [SMEM, SMEM, SMEM] + [VMEM] * 4, whole, HBM, [pltpu.V...]
    ppermute x1, starting transfers between devices: 9.43 us -> 8.42 us  [body(): moved_0 = lax.ppermute(sent_0, ('pi', 'pj'), pair_moves(0))]
    reshape x1 -> x0, local copies, waits for them, and re-layouts: 1 us -> none  [body(): cycle_ints.reshape(160, LANES)]
  transfers between devices with their start and end apart: 12 -> 13, of which waited for: 7 -> 5; matrix products, arithmetic and copies ran while one was open for 1% -> 1% of each run, Pallas kernels for 2% -> 2%
where the time goes in v6:
time: 87.8 us; the launch traced here: 87.4 us
  starting transfers between devices  34.2 us (39%)
  waiting for transfers between devices  21.7 us (25%)
  blocking collectives  14.3 us (16%)
  Pallas kernels  11 us (13%)
  local copies, waits for them, and re-layouts  5.18 us (6%)
  other arithmetic  0.91 us (1%)
    all_to_all x1, blocking collectives, body(): arrived_1 = lax.all_to_all(sent_1, 'vert', 0, 0)  14.3 us
    ppermute x1, starting transfers between devices, body(): moved_0 = lax.ppermute(sent_0, ('pi', 'pj'), pair_moves(0))  8.42 us
    ppermute x1, waiting for transfers between devices, body(): moved_1 = lax.ppermute(arrived_1, ('pi', 'pj'), pair_moves(1))  7.21 us
    ppermute x1, waiting for transfers between devices, gather(): down = lax.ppermute(own, 'vert', DOWN)  6.05 us
    all_to_all x1, waiting for transfers between devices, body(): arrived_0 = lax.all_to_all(moved_0, 'vert', 0, 0)  5.28 us
    unnamed x18, local copies, waits for them, and re-layouts  5.09 us
    ppermute x1, starting transfers between devices, body(): before = lax.ppermute(last, 'pj', [(q, q + 1) for q in range(3)])  4.81 us
    ppermute x1, starting transfers between devices, gather(): down = lax.ppermute(own, 'vert', DOWN)  3.64 us
  transfers between devices with their start and end apart: 13, of which 5 were waited for; matrix products, arithmetic and copies ran while one was open for 1% of the time, Pallas kernels for 2%

profile of v6, /device:TPU:1, one launch (start us, length us, event | category | flops | bytes accessed | tf_op | source)
XLA Modules:
  0.0 87.4 jit_solution(17206347114462026661)
XLA Ops:
  0.0 3.2 %shard_map.82 = (bf16[416,512]{1,0:T(8,128)(2,1)}, bf16[16,16,512]{2,1,0:T(8,128)(2,1)}, bf16[2,16,512]{2,1,0:T(8,128)(2,1)}, bf16[2,16,512]{2,1,0:T(8,128)(2,1)}) custom-call(s32[2,2]{1,0:T(2,128)} %ladder_tiles.1, s32[2,2]{1,0:T(2,128)} %cycle_tiles.1, bf16[1024,512]{1,0:T(8,128)(2,1)} %bitcast.2, bf16[80,2,512]{2,1,0:T(2,128)(2,1)} %bitcast.3), custom_call_target="tpu_custom_call" | custom-call | flops 1000000000 | bytes 4194304 | tf_op jit(solution)/shard_map/pallas_call | solution.py:273
  3.2 0.0 copy-start.2
  3.2 3.6 %collective-permute-start.2 = (bf16[416,512]{1,0:T(8,128)(2,1)}, bf16[416,512]{1,0:T(8,128)(2,1)S(1)}, u32[]{:S(2)}, u32[]{:S(2)}) collective-permute-start(bf16[416,512]{1,0:T(8,128)(2,1)} %get-tuple-element.12.refs_0_), channel_id=1, source_target_pairs={{0,3},{1,0},{2,1},{3,2},{4,7},{5,4},{6,5},{7,6},{8,11},{9,8},{10,9... | collective-permute-start | bytes 1277960 | tf_op jit(solution)/shard_map/ppermute | solution.py:260
  6.8 0.0 collective-permute-start.1
  6.8 2.7 %collective-permute-start = (bf16[416,512]{1,0:T(8,128)(2,1)}, bf16[416,512]{1,0:T(8,128)(2,1)S(1)}, u32[]{:S(2)}, u32[]{:S(2)}) collective-permute-start(bf16[416,512]{1,0:T(8,128)(2,1)} %get-tuple-element.12.refs_0_), channel_id=1, source_target_pairs={{0,4},{1,5},{2,6},{3,7},{4,0},{5,1},{6,2},{7,3},{8,12},{9,13},{10,... | collective-permute-start | bytes 1277960 | tf_op jit(solution)/shard_map/ppermute | solution.py:262
  9.6 6.0 %collective-permute-done.2.refs_3_ = bf16[416,512]{1,0:T(8,128)(2,1)S(1)} collective-permute-done((bf16[416,512]{1,0:T(8,128)(2,1)}, bf16[416,512]{1,0:T(8,128)(2,1)S(1)}, u32[]{:S(2)}, u32[]{:S(2)}) %collective-permute-start.2) | collective-permute-done | bytes 426016 | tf_op jit(solution)/shard_map/ppermute | solution.py:260
  15.6 3.0 %collective-permute-done.1.refs_2_ = bf16[416,512]{1,0:T(8,128)(2,1)S(1)} collective-permute-done((bf16[416,512]{1,0:T(8,128)(2,1)}, bf16[416,512]{1,0:T(8,128)(2,1)S(1)}, u32[]{:S(2)}, u32[]{:S(2)}) %collective-permute-start.1) | collective-permute-done | bytes 426016 | tf_op jit(solution)/shard_map/ppermute | solution.py:261
  18.7 0.1 pad_maximum_fusion.2
  18.8 3.1 %collective-permute-start.7 = (bf16[416,512]{1,0:T(8,128)(2,1)S(1)}, bf16[416,512]{1,0:T(8,128)(2,1)S(1)}, u32[]{:S(2)}, u32[]{:S(2)}) collective-permute-start(bf16[416,512]{1,0:T(8,128)(2,1)S(1)} %get-tuple-element.21), channel_id=1, source_target_pairs={{0,4},{1,5},{2,6},{3,7},{4,0},{5,1},{6,2},{7,3},{8,12},{9,13},{10,... | collective-permute-start | bytes 1277960 | tf_op jit(solution)/shard_map/ppermute | solution.py:263
  21.9 2.4 %collective-permute-start.6 = (bf16[416,512]{1,0:T(8,128)(2,1)S(1)}, bf16[416,512]{1,0:T(8,128)(2,1)S(1)}, u32[]{:S(2)}, u32[]{:S(2)}) collective-permute-start(bf16[416,512]{1,0:T(8,128)(2,1)S(1)} %get-tuple-element.22), channel_id=1, source_target_pairs={{0,3},{1,0},{2,1},{3,2},{4,7},{5,4},{6,5},{7,6},{8,11},{9,8},{10,9... | collective-permute-start | bytes 1277960 | tf_op jit(solution)/shard_map/ppermute | solution.py:265
  24.3 4.8 %collective-permute-start.3 = (bf16[2,16,512]{2,1,0:T(8,128)(2,1)}, bf16[2,16,512]{2,1,0:T(8,128)(2,1)S(1)}, u32[]{:S(2)}, u32[]{:S(2)}) collective-permute-start(bf16[2,16,512]{2,1,0:T(8,128)(2,1)} %get-tuple-element.13), channel_id=1, source_target_pairs={{0,8},{8,16},{16,24},{1,9},{9,17},{17,25},{2,10},{10,18},{18,26},{... | collective-permute-start | bytes 98312 | tf_op jit(solution)/shard_map/ppermute | solution.py:291
  29.1 1.9 %collective-permute-start.4 = (bf16[2,16,512]{2,1,0:T(8,128)(2,1)}, bf16[2,16,512]{2,1,0:T(8,128)(2,1)S(1)}, u32[]{:S(2)}, u32[]{:S(2)}) collective-permute-start(bf16[2,16,512]{2,1,0:T(8,128)(2,1)} %get-tuple-element.15), channel_id=1, source_target_pairs={{8,0},{16,8},{24,16},{9,1},{17,9},{25,17},{10,2},{18,10},{26,18},{... | collective-permute-start | bytes 98312 | tf_op jit(solution)/shard_map/ppermute | solution.py:292
  31.0 0.1 collective-permute-start.8
  31.1 0.0 collective-permute-done.6.refs_5_
  31.2 3.3 %collective-permute-start.9 = (bf16[208,512]{1,0:T(8,128)(2,1)S(1)}, bf16[208,512]{1,0:T(8,128)(2,1)S(1)}, u32[]{:S(2)}, u32[]{:S(2)}) collective-permute-start(bf16[208,512]{1,0:T(8,128)(2,1)S(1)} %slice.31), channel_id=1, source_target_pairs={{0,3},{1,0},{2,1},{3,2},{4,7},{5,4},{6,5},{7,6},{8,11},{9,8},{10,9... | collective-permute-start | bytes 638984 | tf_op jit(solution)/shard_map/ppermute | solution.py:267
  34.4 0.4 fusion.swap
  34.9 0.0 copy-start
  34.9 3.4 %copy-done = bf16[2,512,4096]{2,1,0:T(8,128)(2,1)S(1)} copy-done((bf16[2,512,4096]{2,1,0:T(8,128)(2,1)S(1)}, bf16[2,512,4096]{2,1,0:T(8,128)(2,1)}, u32[]{:S(2)}) %copy-start) | copy-done | bytes 8388632
  38.3 1.5 %shard_map.83.near = f32[128,1024]{1,0:T(8,128)S(1)} custom-call(bf16[2,512,4096]{2,1,0:T(8,128)(2,1)S(1)} %copy-done, bf16[416,512]{1,0:T(8,128)(2,1)S(1)} %copy-done.2, bf16[416,512]{1,0:T(8,128)(2,1)S(1)} %collective-permute-done.refs_1_, bf16[416,512]{1,0:T(8,128)(2,1)S(1)} %collective-permute-done.1.refs_2_, ...), custom_call_target="tpu_custom_call" | custom-call | flops 1000000000 | bytes 4194304 | tf_op jit(solution)/shard_map/pallas_call | solution.py:293
  39.8 0.0 collective-permute-done.4.after
  39.8 0.2 collective-permute-done.8.refs_7_
  39.9 1.7 %copy-done.1 = bf16[2,512,4096]{2,1,0:T(8,128)(2,1)S(1)} copy-done((bf16[2,512,4096]{2,1,0:T(8,128)(2,1)S(1)}, bf16[2,512,4096]{2,1,0:T(8,128)(2,1)}, u32[]{:S(2)}) %copy-start.1) | copy-done | bytes 8388632
  41.6 0.0 copy-start.6
  41.7 2.7 %shard_map.84 = (f32[128,2048]{1,0:T(8,128)S(1)}, bf16[8,128,128]{2,1,0:T(8,128)(2,1)S(1)}, bf16[8,128,128]{2,1,0:T(8,128)(2,1)S(1)}) custom-call(bf16[2,512,4096]{2,1,0:T(8,128)(2,1)S(1)} %copy-done.1, f32[128,1024]{1,0:T(8,128)S(1)} %shard_map.83.near, bf16[2,16,512]{2,1,0:T(8,128)(2,1)S(1)} %collective-permute-done.3.before, ...), custom_call_target="tpu_custom_call" | custom-call | flops 2000000000 | bytes 4194304 | tf_op jit(solution)/shard_map/pallas_call | solution.py:297
  44.4 8.4 %collective-permute-start.10 = (bf16[8,128,128]{2,1,0:T(8,128)(2,1)S(1)}, bf16[8,128,128]{2,1,0:T(8,128)(2,1)}, u32[]{:S(2)}, u32[]{:S(2)}) collective-permute-start(bf16[8,128,128]{2,1,0:T(8,128)(2,1)S(1)} %get-tuple-element.17), channel_id=1, source_target_pairs={{0,0},{8,64},{16,128},{24,192},{32,32},{40,96},{48,160},{56,224},{... | collective-permute-start | bytes 786440 | tf_op jit(solution)/shard_map/ppermute | solution.py:306
  52.8 14.3 %all_to_all.10 = bf16[8,128,128]{2,1,0:T(8,128)(2,1)} all-to-all(bf16[8,128,128]{2,1,0:T(8,128)(2,1)S(1)} %get-tuple-element.18), channel_id=1, replica_groups=mesh['pi'=8,'pj'=4,'vert'=8] {'vert'}, dimensions={0} | all-to-all | bytes 524288 | tf_op jit(solution)/shard_map/all_to_all | solution.py:307
  67.1 0.4 collective-permute-start.11
  67.5 3.4 %all-to-all-start = ((bf16[8,128,128]{2,1,0:T(8,128)(2,1)}), bf16[8,128,128]{2,1,0:T(8,128)(2,1)S(1)}, u32[]{:S(2)}, u32[]{:S(2)}) async-start(bf16[8,128,128]{2,1,0:T(8,128)(2,1)} %collective-permute-done.10), calls=%async_computation | async-start | bytes 524288 | tf_op jit(solution)/shard_map/all_to_all | solution.py:308
  71.0 0.4 fusion.1.place
  71.4 7.2 %collective-permute-done.11.second = bf16[8,128,128]{2,1,0:T(8,128)(2,1)} collective-permute-done((bf16[8,128,128]{2,1,0:T(8,128)(2,1)}, bf16[8,128,128]{2,1,0:T(8,128)(2,1)}, u32[]{:S(2)}, u32[]{:S(2)}) %collective-permute-start.11) | collective-permute-done | bytes 262176 | tf_op jit(solution)/shard_map/ppermute | solution.py:309
  78.6 5.3 %all-to-all-done.first = bf16[8,128,128]{2,1,0:T(8,128)(2,1)S(1)} async-done(((bf16[8,128,128]{2,1,0:T(8,128)(2,1)}), bf16[8,128,128]{2,1,0:T(8,128)(2,1)S(1)}, u32[]{:S(2)}, u32[]{:S(2)}) %all-to-all-start) | async-done | bytes 262176 | tf_op jit(solution)/shard_map/all_to_all | solution.py:308
  83.9 3.5 %shard_map.85 = f32[8,16,8,512]{3,2,1,0:T(8,128)} custom-call(s32[2,2]{1,0:T(2,128)S(1)} %copy-done.4, s32[2,2]{1,0:T(2,128)S(1)} %copy-done.5, s32[8]{0:T(128)S(1)} %copy-done.6, f32[128,2048]{1,0:T(8,128)S(1)} %get-tuple-element.16.total, bf16[1024,1024]{1,0:T(8,128)(2,1)S(1)} %fusion.1.place, bf16[8,128,128]{2,1,0:T(8,128)(2,1)S(1)} %all-to-all-done.first, ...), custom_call_target="tpu_custom_call" | custom-call | flops 1000000000 | bytes 4194304 | tf_op jit(solution)/shard_map/pallas_call | solution.py:311
  (25 shorter events, 0.1 us)
Async XLA Ops:
  0.0 34.4 %copy-start.8 = (s32[1024]{0:T(1024)S(1)}, s32[1024]{0:T(1024)}, u32[]{:S(2)}) copy-start(s32[1024]{0:T(1024)} %constant.4.clone) | copy-start | bytes 12292
  3.2 31.7 %copy-start.2 = (bf16[416,512]{1,0:T(8,128)(2,1)S(1)}, bf16[416,512]{1,0:T(8,128)(2,1)}, u32[]{:S(2)}) copy-start(bf16[416,512]{1,0:T(8,128)(2,1)} %get-tuple-element.12.refs_0_) | copy-start | bytes 1277956
  3.2 12.4 %collective-permute-start.2 = (bf16[416,512]{1,0:T(8,128)(2,1)}, bf16[416,512]{1,0:T(8,128)(2,1)S(1)}, u32[]{:S(2)}, u32[]{:S(2)}) collective-permute-start(bf16[416,512]{1,0:T(8,128)(2,1)} %get-tuple-element.12.refs_0_), channel_id=1, source_target_pairs={{0,3},{1,0},{2,1},{3,2},{4,7},{5,4},{6,5},{7,6},{8,11},{9,8},{10,9... | collective-permute-start | bytes 1277960 | tf_op jit(solution)/shard_map/ppermute | solution.py:260
  6.8 11.8 %collective-permute-start.1 = (bf16[416,512]{1,0:T(8,128)(2,1)}, bf16[416,512]{1,0:T(8,128)(2,1)S(1)}, u32[]{:S(2)}, u32[]{:S(2)}) collective-permute-start(bf16[416,512]{1,0:T(8,128)(2,1)} %get-tuple-element.12.refs_0_), channel_id=1, source_target_pairs={{0,1},{1,2},{2,3},{3,0},{4,5},{5,6},{6,7},{7,4},{8,9},{9,10},{10,1... | collective-permute-start | bytes 1277960 | tf_op jit(solution)/shard_map/ppermute | solution.py:261
  6.8 11.8 %collective-permute-start = (bf16[416,512]{1,0:T(8,128)(2,1)}, bf16[416,512]{1,0:T(8,128)(2,1)S(1)}, u32[]{:S(2)}, u32[]{:S(2)}) collective-permute-start(bf16[416,512]{1,0:T(8,128)(2,1)} %get-tuple-element.12.refs_0_), channel_id=1, source_target_pairs={{0,4},{1,5},{2,6},{3,7},{4,0},{5,1},{6,2},{7,3},{8,12},{9,13},{10,... | collective-permute-start | bytes 1277960 | tf_op jit(solution)/shard_map/ppermute | solution.py:262
  18.8 12.2 %collective-permute-start.7 = (bf16[416,512]{1,0:T(8,128)(2,1)S(1)}, bf16[416,512]{1,0:T(8,128)(2,1)S(1)}, u32[]{:S(2)}, u32[]{:S(2)}) collective-permute-start(bf16[416,512]{1,0:T(8,128)(2,1)S(1)} %get-tuple-element.21), channel_id=1, source_target_pairs={{0,4},{1,5},{2,6},{3,7},{4,0},{5,1},{6,2},{7,3},{8,12},{9,13},{10,... | collective-permute-start | bytes 1277960 | tf_op jit(solution)/shard_map/ppermute | solution.py:263
  21.9 9.3 %collective-permute-start.6 = (bf16[416,512]{1,0:T(8,128)(2,1)S(1)}, bf16[416,512]{1,0:T(8,128)(2,1)S(1)}, u32[]{:S(2)}, u32[]{:S(2)}) collective-permute-start(bf16[416,512]{1,0:T(8,128)(2,1)S(1)} %get-tuple-element.22), channel_id=1, source_target_pairs={{0,3},{1,0},{2,1},{3,2},{4,7},{5,4},{6,5},{7,6},{8,11},{9,8},{10,9... | collective-permute-start | bytes 1277960 | tf_op jit(solution)/shard_map/ppermute | solution.py:265
  24.3 15.5 %collective-permute-start.5 = (bf16[416,512]{1,0:T(8,128)(2,1)S(1)}, bf16[416,512]{1,0:T(8,128)(2,1)S(1)}, u32[]{:S(2)}, u32[]{:S(2)}) collective-permute-start(bf16[416,512]{1,0:T(8,128)(2,1)S(1)} %get-tuple-element.23), channel_id=1, source_target_pairs={{0,1},{1,2},{2,3},{3,0},{4,5},{5,6},{6,7},{7,4},{8,9},{9,10},{10,1... | collective-permute-start | bytes 1277960 | tf_op jit(solution)/shard_map/ppermute | solution.py:264
  24.3 15.5 %collective-permute-start.3 = (bf16[2,16,512]{2,1,0:T(8,128)(2,1)}, bf16[2,16,512]{2,1,0:T(8,128)(2,1)S(1)}, u32[]{:S(2)}, u32[]{:S(2)}) collective-permute-start(bf16[2,16,512]{2,1,0:T(8,128)(2,1)} %get-tuple-element.13), channel_id=1, source_target_pairs={{0,8},{8,16},{16,24},{1,9},{9,17},{17,25},{2,10},{10,18},{18,26},{... | collective-permute-start | bytes 98312 | tf_op jit(solution)/shard_map/ppermute | solution.py:291
  29.1 10.7 %collective-permute-start.4 = (bf16[2,16,512]{2,1,0:T(8,128)(2,1)}, bf16[2,16,512]{2,1,0:T(8,128)(2,1)S(1)}, u32[]{:S(2)}, u32[]{:S(2)}) collective-permute-start(bf16[2,16,512]{2,1,0:T(8,128)(2,1)} %get-tuple-element.15), channel_id=1, source_target_pairs={{8,0},{16,8},{24,16},{9,1},{17,9},{25,17},{10,2},{18,10},{26,18},{... | collective-permute-start | bytes 98312 | tf_op jit(solution)/shard_map/ppermute | solution.py:292
  31.0 8.9 %collective-permute-start.8 = (bf16[208,512]{1,0:T(8,128)(2,1)S(1)}, bf16[208,512]{1,0:T(8,128)(2,1)S(1)}, u32[]{:S(2)}, u32[]{:S(2)}) collective-permute-start(bf16[208,512]{1,0:T(8,128)(2,1)S(1)} %slice.30), channel_id=1, source_target_pairs={{0,1},{1,2},{2,3},{3,0},{4,5},{5,6},{6,7},{7,4},{8,9},{9,10},{10,1... | collective-permute-start | bytes 638984 | tf_op jit(solution)/shard_map/ppermute | solution.py:266
  31.2 8.8 %collective-permute-start.9 = (bf16[208,512]{1,0:T(8,128)(2,1)S(1)}, bf16[208,512]{1,0:T(8,128)(2,1)S(1)}, u32[]{:S(2)}, u32[]{:S(2)}) collective-permute-start(bf16[208,512]{1,0:T(8,128)(2,1)S(1)} %slice.31), channel_id=1, source_target_pairs={{0,3},{1,0},{2,1},{3,2},{4,7},{5,4},{6,5},{7,6},{8,11},{9,8},{10,9... | collective-permute-start | bytes 638984 | tf_op jit(solution)/shard_map/ppermute | solution.py:267
  34.9 3.4 %copy-start = (bf16[2,512,4096]{2,1,0:T(8,128)(2,1)S(1)}, bf16[2,512,4096]{2,1,0:T(8,128)(2,1)}, u32[]{:S(2)}) copy-start(bf16[2,512,4096]{2,1,0:T(8,128)(2,1)} %ladder_ints.3) | copy-start | bytes 25165828
  38.2 3.4 %copy-start.1 = (bf16[2,512,4096]{2,1,0:T(8,128)(2,1)S(1)}, bf16[2,512,4096]{2,1,0:T(8,128)(2,1)}, u32[]{:S(2)}) copy-start(bf16[2,512,4096]{2,1,0:T(8,128)(2,1)} %ladder_ints.3) | copy-start | bytes 25165828
  38.2 3.4 %copy-start.3 = (bf16[16,16,512]{2,1,0:T(8,128)(2,1)S(1)}, bf16[16,16,512]{2,1,0:T(8,128)(2,1)}, u32[]{:S(2)}) copy-start(bf16[16,16,512]{2,1,0:T(8,128)(2,1)} %get-tuple-element.14.inner) | copy-start | bytes 786436
  41.6 29.3 %copy-start.7 = (s32[1024]{0:T(1024)S(1)}, s32[1024]{0:T(1024)}, u32[]{:S(2)}) copy-start(s32[1024]{0:T(1024)} %constant.5.clone) | copy-start | bytes 12292
  41.6 42.2 %copy-start.4 = (s32[2,2]{1,0:T(2,128)S(1)}, s32[2,2]{1,0:T(2,128)}, u32[]{:S(2)}) copy-start(s32[2,2]{1,0:T(2,128)} %ladder_tiles.1) | copy-start | bytes 52
  41.6 42.2 %copy-start.5 = (s32[2,2]{1,0:T(2,128)S(1)}, s32[2,2]{1,0:T(2,128)}, u32[]{:S(2)}) copy-start(s32[2,2]{1,0:T(2,128)} %cycle_tiles.1) | copy-start | bytes 52
  41.6 42.2 %copy-start.6 = (s32[8]{0:T(128)S(1)}, s32[8]{0:T(128)}, u32[]{:S(2)}) copy-start(s32[8]{0:T(128)} %partner.1) | copy-start | bytes 100
  44.4 23.1 %collective-permute-start.10 = (bf16[8,128,128]{2,1,0:T(8,128)(2,1)S(1)}, bf16[8,128,128]{2,1,0:T(8,128)(2,1)}, u32[]{:S(2)}, u32[]{:S(2)}) collective-permute-start(bf16[8,128,128]{2,1,0:T(8,128)(2,1)S(1)} %get-tuple-element.17), channel_id=1, source_target_pairs={{0,0},{8,64},{16,128},{24,192},{32,32},{40,96},{48,160},{56,224},{... | collective-permute-start | bytes 786440 | tf_op jit(solution)/shard_map/ppermute | solution.py:306
  67.1 11.5 %collective-permute-start.11 = (bf16[8,128,128]{2,1,0:T(8,128)(2,1)}, bf16[8,128,128]{2,1,0:T(8,128)(2,1)}, u32[]{:S(2)}, u32[]{:S(2)}) collective-permute-start(bf16[8,128,128]{2,1,0:T(8,128)(2,1)} %all_to_all.10), channel_id=1, source_target_pairs={{0,32},{8,96},{16,160},{24,224},{32,0},{40,64},{48,128},{56,192},{... | collective-permute-start | bytes 786440 | tf_op jit(solution)/shard_map/ppermute | solution.py:309
  67.5 16.3 %all-to-all-start = ((bf16[8,128,128]{2,1,0:T(8,128)(2,1)}), bf16[8,128,128]{2,1,0:T(8,128)(2,1)S(1)}, u32[]{:S(2)}, u32[]{:S(2)}) async-start(bf16[8,128,128]{2,1,0:T(8,128)(2,1)} %collective-permute-done.10), calls=%async_computation | async-start | bytes 524288 | tf_op jit(solution)/shard_map/all_to_all | solution.py:308

commit v7 on v6

--- a/solution.py
+++ b/solution.py
@@ -1,6 +1,5 @@
 import jax
 import jax.numpy as jnp
-import numpy as np
 from jax import lax
 from jax.experimental import pallas as pl
 from jax.experimental.pallas import tpu as pltpu
@@ -32,21 +31,15 @@
     ]
 
 
-def send_order():
-    row = np.arange(1024)
-    slot, a, v, b = row // 512, (row // 64) % 8, (row // 8) % 8, row % 8
-    return v * 128 + slot * 64 + b * 8 + a
-
-
-def place_order():
-    row = np.arange(1024)
-    v, slot, b, a = row // 128, (row // 64) % 2, (row // 8) % 8, row % 8
-    return slot * 512 + b * 64 + v * 8 + a
-
-
-def permutation(order):
-    columns = lax.broadcasted_iota(jnp.int32, (1024, 1024), 1)
-    return (jnp.asarray(order, jnp.int32)[:, None] == columns).astype(BF)
+def orders_kernel(after, swap_ref, place_ref):
+    del after
+    row = lax.broadcasted_iota(jnp.int32, (1024, 128), 0)
+    column = lax.broadcasted_iota(jnp.int32, (1024, 128), 1)
+    swap = ((row >> 3) & 7) * 128 + (row >> 9) * 64 + (row & 7) * 8 + ((row >> 6) & 7) - column
+    place = ((row >> 6) & 1) * 512 + ((row >> 3) & 7) * 64 + (row >> 7) * 8 + (row & 7) - column
+    for order, ref in ((swap, swap_ref), (place, place_ref)):
+        for c in range(8):
+            ref[:, c * 128 : (c + 1) * 128] = jnp.where(order == c * 128, 1.0, 0.0).astype(BF)
 
 
 HALF = 208
@@ -103,10 +96,10 @@
 
 
 def near_pieces(refs):
-    own, flip, up, down = refs
+    own, down, up, flip = refs
     vert = lax.axis_index("vert")
     h, y = vert // 4, vert % 4
-    places = [(h, y, own), (1 - h, y, flip), (h, y + 3, up), (h, y + 1, down)]
+    places = [(h, y, own), (h, y + 1, down), (h, y + 3, up), (1 - h, y, flip)]
     return [[(a * 4 + b % 4, ref, w * HALF) for a, b, ref in places] for w in range(2)]
 
 
@@ -265,7 +258,7 @@
     down_2 = lax.ppermute(jnp.concatenate([flip[:HALF], down[HALF:]]), "vert", DOWN)
     up_3 = lax.ppermute(side_2[:HALF], "vert", UP)
     down_3 = lax.ppermute(down_2[:HALF], "vert", DOWN)
-    return [own, flip, up, down], [up_2, down_2, side_2, up_3, down_3]
+    return [own, down, up, flip], [up_2, down_2, side_2, up_3, down_3]
 
 
 def body(amplitudes, ladder_ints, ladder_tiles, cycle_ints, cycle_tiles, partner):
@@ -290,6 +283,8 @@
     near, far = gather(own)
     before = lax.ppermute(last, "pj", [(q, q + 1) for q in range(3)])
     after = lax.ppermute(first, "pj", [(q + 1, q) for q in range(3)])
+    matrix = shape((1024, 1024), BF)
+    swap, place = call(orders_kernel, [HBM], [matrix] * 2, [VMEM] * 2, [], 8, 2 * 10**10)(near[1])
     begun = call(
         near_kernel, [VMEM] * 5, shape((PAIRS, 1024), F32), VMEM, [], 8, 10**9
     )(ladder_ints, *near)
@@ -302,7 +297,7 @@
         [pltpu.VMEM((8, 160, LANES), F32)],
         12,
         2 * 10**9,
-    )(ladder_ints, begun, before, inner, after, permutation(send_order()), *near, *far)
+    )(ladder_ints, begun, before, inner, after, swap, *near, *far)
     moved_0 = lax.ppermute(sent_0, ("pi", "pj"), pair_moves(0))
     arrived_1 = lax.all_to_all(sent_1, "vert", 0, 0)
     arrived_0 = lax.all_to_all(moved_0, "vert", 0, 0)
@@ -320,7 +315,7 @@
         ],
         12,
         10**9,
-    )(ladder_tiles, cycle_tiles, partner, total, permutation(place_order()), arrived_0, moved_1)
+    )(ladder_tiles, cycle_tiles, partner, total, place, arrived_0, moved_1)
 
 
 def solution(mesh):

time: 87.8 us -> 101 us (1.15)
  the two profiles are of different devices: /device:TPU:1 before, /device:TPU:66 now
where the time goes in v7:
time: 101 us; the launch traced here: 100 us
  waiting for transfers between devices  47.1 us (47%)
  starting transfers between devices  38.6 us (38%)
  Pallas kernels  12.5 us (12%)
  local copies, waits for them, and re-layouts  1.55 us (2%)
    ppermute x1, waiting for transfers between devices, body(): moved_0 = lax.ppermute(sent_0, ('pi', 'pj'), pair_moves(0))  15.7 us
    all_to_all x1, waiting for transfers between devices, body(): arrived_0 = lax.all_to_all(moved_0, 'vert', 0, 0)  8.72 us
    ppermute x1, waiting for transfers between devices, gather(): flip = lax.ppermute(own, 'vert', FLIP)  7.91 us
    all_to_all x1, starting transfers between devices, body(): arrived_0 = lax.all_to_all(moved_0, 'vert', 0, 0)  7.24 us
    ppermute x1, waiting for transfers between devices, gather(): up_2 = lax.ppermute(jnp.concatenate([flip[:HALF], up[:HALF]]), 'vert', UP)  5.24 us
    ppermute x1, starting transfers between devices, body(): moved_0 = lax.ppermute(sent_0, ('pi', 'pj'), pair_moves(0))  5.16 us
    all_to_all x1, starting transfers between devices, body(): arrived_1 = lax.all_to_all(sent_1, 'vert', 0, 0)  4.05 us
    ppermute x1, starting transfers between devices, body(): after = lax.ppermute(first, 'pj', [(q + 1, q) for q in range(3)])  3.64 us
  transfers between devices with their start and end apart: 14, of which 8 were waited for; matrix products, arithmetic and copies ran while one was open for 0% of the time, Pallas kernels for 3%

profile of v7, /device:TPU:66, one launch (start us, length us, event | category | flops | bytes accessed | tf_op | source)
XLA Modules:
  0.0 100.2 jit_solution(10150364204820944021)
XLA Ops:
  0.0 3.1 %shard_map.64 = (bf16[416,512]{1,0:T(8,128)(2,1)}, bf16[16,16,512]{2,1,0:T(8,128)(2,1)}, bf16[2,16,512]{2,1,0:T(8,128)(2,1)}, bf16[2,16,512]{2,1,0:T(8,128)(2,1)}) custom-call(s32[2,2]{1,0:T(2,128)} %ladder_tiles.1, s32[2,2]{1,0:T(2,128)} %cycle_tiles.1, bf16[1024,512]{1,0:T(8,128)(2,1)} %bitcast.4, bf16[80,2,512]{2,1,0:T(2,128)(2,1)} %bitcast.5), custom_call_target="tpu_custom_call" | custom-call | flops 1000000000 | bytes 4194304 | tf_op jit(solution)/shard_map/pallas_call | solution.py:266
  3.2 2.2 %collective-permute-start.2 = (bf16[416,512]{1,0:T(8,128)(2,1)}, bf16[416,512]{1,0:T(8,128)(2,1)S(1)}, u32[]{:S(2)}, u32[]{:S(2)}) collective-permute-start(bf16[416,512]{1,0:T(8,128)(2,1)} %get-tuple-element.14.refs_0_), channel_id=1, source_target_pairs={{0,4},{1,5},{2,6},{3,7},{4,0},{5,1},{6,2},{7,3},{8,12},{9,13},{10,... | collective-permute-start | bytes 1277960 | tf_op jit(solution)/shard_map/ppermute | solution.py:255
  5.4 1.6 %collective-permute-start.1 = (bf16[416,512]{1,0:T(8,128)(2,1)}, bf16[416,512]{1,0:T(8,128)(2,1)S(1)}, u32[]{:S(2)}, u32[]{:S(2)}) collective-permute-start(bf16[416,512]{1,0:T(8,128)(2,1)} %get-tuple-element.14.refs_0_), channel_id=1, source_target_pairs={{0,1},{1,2},{2,3},{3,0},{4,5},{5,6},{6,7},{7,4},{8,9},{9,10},{10,1... | collective-permute-start | bytes 1277960 | tf_op jit(solution)/shard_map/ppermute | solution.py:254
  7.0 1.7 %collective-permute-start = (bf16[416,512]{1,0:T(8,128)(2,1)}, bf16[416,512]{1,0:T(8,128)(2,1)S(1)}, u32[]{:S(2)}, u32[]{:S(2)}) collective-permute-start(bf16[416,512]{1,0:T(8,128)(2,1)} %get-tuple-element.14.refs_0_), channel_id=1, source_target_pairs={{0,3},{1,0},{2,1},{3,2},{4,7},{5,4},{6,5},{7,6},{8,11},{9,8},{10,9... | collective-permute-start | bytes 1277960 | tf_op jit(solution)/shard_map/ppermute | solution.py:253
  8.6 7.9 %collective-permute-done.2.refs_3_ = bf16[416,512]{1,0:T(8,128)(2,1)S(1)} collective-permute-done((bf16[416,512]{1,0:T(8,128)(2,1)}, bf16[416,512]{1,0:T(8,128)(2,1)S(1)}, u32[]{:S(2)}, u32[]{:S(2)}) %collective-permute-start.2) | collective-permute-done | bytes 426016 | tf_op jit(solution)/shard_map/ppermute | solution.py:255
  16.5 1.6 %collective-permute-done.1.refs_2_ = bf16[416,512]{1,0:T(8,128)(2,1)S(1)} collective-permute-done((bf16[416,512]{1,0:T(8,128)(2,1)}, bf16[416,512]{1,0:T(8,128)(2,1)S(1)}, u32[]{:S(2)}, u32[]{:S(2)}) %collective-permute-start.1) | collective-permute-done | bytes 426016 | tf_op jit(solution)/shard_map/ppermute | solution.py:254
  18.2 0.1 pad_maximum_fusion.2
  18.3 1.5 %collective-permute-start.7 = (bf16[416,512]{1,0:T(8,128)(2,1)S(1)}, bf16[416,512]{1,0:T(8,128)(2,1)S(1)}, u32[]{:S(2)}, u32[]{:S(2)}) collective-permute-start(bf16[416,512]{1,0:T(8,128)(2,1)S(1)} %get-tuple-element.25), channel_id=1, source_target_pairs={{0,4},{1,5},{2,6},{3,7},{4,0},{5,1},{6,2},{7,3},{8,12},{9,13},{10,... | collective-permute-start | bytes 1277960 | tf_op jit(solution)/shard_map/ppermute | solution.py:256
  19.8 2.9 %collective-permute-start.6 = (bf16[416,512]{1,0:T(8,128)(2,1)S(1)}, bf16[416,512]{1,0:T(8,128)(2,1)S(1)}, u32[]{:S(2)}, u32[]{:S(2)}) collective-permute-start(bf16[416,512]{1,0:T(8,128)(2,1)S(1)} %get-tuple-element.26), channel_id=1, source_target_pairs={{0,3},{1,0},{2,1},{3,2},{4,7},{5,4},{6,5},{7,6},{8,11},{9,8},{10,9... | collective-permute-start | bytes 1277960 | tf_op jit(solution)/shard_map/ppermute | solution.py:258
  22.7 1.9 %collective-permute-start.3 = (bf16[2,16,512]{2,1,0:T(8,128)(2,1)S(1)}, bf16[2,16,512]{2,1,0:T(8,128)(2,1)S(1)}, u32[]{:S(2)}, u32[]{:S(2)}) collective-permute-start(bf16[2,16,512]{2,1,0:T(8,128)(2,1)S(1)} %copy-done.8), channel_id=1, source_target_pairs={{0,8},{8,16},{16,24},{1,9},{9,17},{17,25},{2,10},{10,18},{18,26},{... | collective-permute-start | bytes 98312 | tf_op jit(solution)/shard_map/ppermute | solution.py:284
  24.6 3.6 %collective-permute-start.4 = (bf16[2,16,512]{2,1,0:T(8,128)(2,1)S(1)}, bf16[2,16,512]{2,1,0:T(8,128)(2,1)S(1)}, u32[]{:S(2)}, u32[]{:S(2)}) collective-permute-start(bf16[2,16,512]{2,1,0:T(8,128)(2,1)S(1)} %copy-done.7), channel_id=1, source_target_pairs={{8,0},{16,8},{24,16},{9,1},{17,9},{25,17},{10,2},{18,10},{26,18},{... | collective-permute-start | bytes 98312 | tf_op jit(solution)/shard_map/ppermute | solution.py:285
  28.3 0.1 collective-permute-start.5
  28.4 2.0 %collective-permute-done.7.refs_6_ = bf16[416,512]{1,0:T(8,128)(2,1)S(1)} collective-permute-done((bf16[416,512]{1,0:T(8,128)(2,1)S(1)}, bf16[416,512]{1,0:T(8,128)(2,1)S(1)}, u32[]{:S(2)}, u32[]{:S(2)}) %collective-permute-start.7) | collective-permute-done | bytes 426016 | tf_op jit(solution)/shard_map/ppermute | solution.py:256
  30.4 1.2 %collective-permute-start.8 = (bf16[208,512]{1,0:T(8,128)(2,1)S(1)}, bf16[208,512]{1,0:T(8,128)(2,1)S(1)}, u32[]{:S(2)}, u32[]{:S(2)}) collective-permute-start(bf16[208,512]{1,0:T(8,128)(2,1)S(1)} %slice.30), channel_id=1, source_target_pairs={{0,1},{1,2},{2,3},{3,0},{4,5},{5,6},{6,7},{7,4},{8,9},{9,10},{10,1... | collective-permute-start | bytes 638984 | tf_op jit(solution)/shard_map/ppermute | solution.py:259
  31.7 0.0 slice-start.1
  31.7 0.0 copy-start
  31.7 2.2 %collective-permute-start.9 = (bf16[208,512]{1,0:T(8,128)(2,1)S(1)}, bf16[208,512]{1,0:T(8,128)(2,1)S(1)}, u32[]{:S(2)}, u32[]{:S(2)}) collective-permute-start(bf16[208,512]{1,0:T(8,128)(2,1)S(1)} %slice.31), channel_id=1, source_target_pairs={{0,3},{1,0},{2,1},{3,2},{4,7},{5,4},{6,5},{7,6},{8,11},{9,8},{10,9... | collective-permute-start | bytes 638984 | tf_op jit(solution)/shard_map/ppermute | solution.py:260
  33.9 1.6 %shard_map.66 = (bf16[1024,1024]{1,0:T(8,128)(2,1)S(1)}, bf16[1024,1024]{1,0:T(8,128)(2,1)S(1)}) custom-call(bf16[416,512]{1,0:T(8,128)(2,1)S(1)} %collective-permute-done.refs_1_.after), custom_call_target="tpu_custom_call" | custom-call | flops 20000000000 | bytes 4194304 | tf_op jit(solution)/shard_map/pallas_call | solution.py:287
  35.6 1.5 %shard_map.65.near = f32[128,1024]{1,0:T(8,128)S(1)} custom-call(bf16[2,512,4096]{2,1,0:T(8,128)(2,1)S(1)} %bitcast.3, bf16[416,512]{1,0:T(8,128)(2,1)S(1)} %copy-done, bf16[416,512]{1,0:T(8,128)(2,1)S(1)} %collective-permute-done.refs_1_.after, bf16[416,512]{1,0:T(8,128)(2,1)S(1)} %collective-permute-done.1.refs_2_, ...), custom_call_target="tpu_custom_call" | custom-call | flops 1000000000 | bytes 4194304 | tf_op jit(solution)/shard_map/pallas_call | solution.py:288
  37.1 5.2 %collective-permute-done.5.refs_4_ = bf16[416,512]{1,0:T(8,128)(2,1)S(1)} collective-permute-done((bf16[416,512]{1,0:T(8,128)(2,1)S(1)}, bf16[416,512]{1,0:T(8,128)(2,1)S(1)}, u32[]{:S(2)}, u32[]{:S(2)}) %collective-permute-start.5) | collective-permute-done | bytes 426016 | tf_op jit(solution)/shard_map/ppermute | solution.py:257
  42.3 2.3 %collective-permute-done.8.refs_7_ = bf16[208,512]{1,0:T(8,128)(2,1)S(1)} collective-permute-done((bf16[208,512]{1,0:T(8,128)(2,1)S(1)}, bf16[208,512]{1,0:T(8,128)(2,1)S(1)}, u32[]{:S(2)}, u32[]{:S(2)}) %collective-permute-start.8) | collective-permute-done | bytes 213024 | tf_op jit(solution)/shard_map/ppermute | solution.py:259
  44.7 2.7 %shard_map.67 = (f32[128,2048]{1,0:T(8,128)S(1)}, bf16[8,128,128]{2,1,0:T(8,128)(2,1)S(1)}, bf16[8,128,128]{2,1,0:T(8,128)(2,1)S(1)}) custom-call(bf16[2,512,4096]{2,1,0:T(8,128)(2,1)S(1)} %bitcast.3, f32[128,1024]{1,0:T(8,128)S(1)} %shard_map.65.near, bf16[2,16,512]{2,1,0:T(8,128)(2,1)S(1)} %collective-permute-done.3.before, ...), custom_call_target="tpu_custom_call" | custom-call | flops 2000000000 | bytes 4194304 | tf_op jit(solution)/shard_map/pallas_call | solution.py:292
  47.4 0.7 copy-done.2
  48.2 0.7 copy-done.6
  48.9 4.0 %all-to-all-start.1 = ((bf16[8,128,128]{2,1,0:T(8,128)(2,1)}), bf16[8,128,128]{2,1,0:T(8,128)(2,1)}, u32[]{:S(2)}, u32[]{:S(2)}) async-start(bf16[8,128,128]{2,1,0:T(8,128)(2,1)} %copy-done.2), calls=%async_computation.1 | async-start | bytes 524288 | tf_op jit(solution)/shard_map/all_to_all | solution.py:302
  52.9 5.2 %collective-permute-start.10 = (bf16[8,128,128]{2,1,0:T(8,128)(2,1)}, bf16[8,128,128]{2,1,0:T(8,128)(2,1)}, u32[]{:S(2)}, u32[]{:S(2)}) collective-permute-start(bf16[8,128,128]{2,1,0:T(8,128)(2,1)} %copy-done.6), channel_id=1, source_target_pairs={{0,0},{8,64},{16,128},{24,192},{32,32},{40,96},{48,160},{56,224},{... | collective-permute-start | bytes 786440 | tf_op jit(solution)/shard_map/ppermute | solution.py:301
  58.1 3.6 %all-to-all-done.1 = bf16[8,128,128]{2,1,0:T(8,128)(2,1)} async-done(((bf16[8,128,128]{2,1,0:T(8,128)(2,1)}), bf16[8,128,128]{2,1,0:T(8,128)(2,1)}, u32[]{:S(2)}, u32[]{:S(2)}) %all-to-all-start.1) | async-done | bytes 262176 | tf_op jit(solution)/shard_map/all_to_all | solution.py:302
  61.6 3.3 %collective-permute-start.11 = (bf16[8,128,128]{2,1,0:T(8,128)(2,1)}, bf16[8,128,128]{2,1,0:T(8,128)(2,1)}, u32[]{:S(2)}, u32[]{:S(2)}) collective-permute-start(bf16[8,128,128]{2,1,0:T(8,128)(2,1)} %all-to-all-done.1), channel_id=1, source_target_pairs={{0,32},{8,96},{16,160},{24,224},{32,0},{40,64},{48,128},{56,192},{... | collective-permute-start | bytes 786440 | tf_op jit(solution)/shard_map/ppermute | solution.py:304
  65.0 15.7 %collective-permute-done.10 = bf16[8,128,128]{2,1,0:T(8,128)(2,1)} collective-permute-done((bf16[8,128,128]{2,1,0:T(8,128)(2,1)}, bf16[8,128,128]{2,1,0:T(8,128)(2,1)}, u32[]{:S(2)}, u32[]{:S(2)}) %collective-permute-start.10) | collective-permute-done | bytes 262176 | tf_op jit(solution)/shard_map/ppermute | solution.py:301
  80.6 7.2 %all-to-all-start = ((bf16[8,128,128]{2,1,0:T(8,128)(2,1)}), bf16[8,128,128]{2,1,0:T(8,128)(2,1)S(1)}, u32[]{:S(2)}, u32[]{:S(2)}) async-start(bf16[8,128,128]{2,1,0:T(8,128)(2,1)} %collective-permute-done.10), calls=%async_computation | async-start | bytes 524288 | tf_op jit(solution)/shard_map/all_to_all | solution.py:303
  87.9 8.7 %all-to-all-done.first = bf16[8,128,128]{2,1,0:T(8,128)(2,1)S(1)} async-done(((bf16[8,128,128]{2,1,0:T(8,128)(2,1)}), bf16[8,128,128]{2,1,0:T(8,128)(2,1)S(1)}, u32[]{:S(2)}, u32[]{:S(2)}) %all-to-all-start) | async-done | bytes 262176 | tf_op jit(solution)/shard_map/all_to_all | solution.py:303
  96.6 3.5 %shard_map.68 = f32[8,16,8,512]{3,2,1,0:T(8,128)} custom-call(s32[2,2]{1,0:T(2,128)S(1)} %copy-done.3, s32[2,2]{1,0:T(2,128)S(1)} %copy-done.4, s32[8]{0:T(128)S(1)} %copy-done.5, f32[128,2048]{1,0:T(8,128)S(1)} %get-tuple-element.19.total, bf16[1024,1024]{1,0:T(8,128)(2,1)S(1)} %get-tuple-element.20.place, bf16[8,128,128]{2,1,0:T(8,128)(2,1)S(1)} %all-to-all-done.first, ...), custom_call_target="tpu_custom_call" | custom-call | flops 1000000000 | bytes 4194304 | tf_op jit(solution)/shard_map/pallas_call | solution.py:306
  (30 shorter events, 0.1 us)
Async XLA Ops:
  3.1 19.6 %copy-start.8 = (bf16[2,16,512]{2,1,0:T(8,128)(2,1)S(1)}, bf16[2,16,512]{2,1,0:T(8,128)(2,1)}, u32[]{:S(2)}) copy-start(bf16[2,16,512]{2,1,0:T(8,128)(2,1)} %get-tuple-element.15) | copy-start | bytes 98308
  3.2 21.5 %copy-start.7 = (bf16[2,16,512]{2,1,0:T(8,128)(2,1)S(1)}, bf16[2,16,512]{2,1,0:T(8,128)(2,1)}, u32[]{:S(2)}) copy-start(bf16[2,16,512]{2,1,0:T(8,128)(2,1)} %get-tuple-element.17) | copy-start | bytes 98308
  3.2 13.4 %collective-permute-start.2 = (bf16[416,512]{1,0:T(8,128)(2,1)}, bf16[416,512]{1,0:T(8,128)(2,1)S(1)}, u32[]{:S(2)}, u32[]{:S(2)}) collective-permute-start(bf16[416,512]{1,0:T(8,128)(2,1)} %get-tuple-element.14.refs_0_), channel_id=1, source_target_pairs={{0,4},{1,5},{2,6},{3,7},{4,0},{5,1},{6,2},{7,3},{8,12},{9,13},{10,... | collective-permute-start | bytes 1277960 | tf_op jit(solution)/shard_map/ppermute | solution.py:255
  5.4 12.8 %collective-permute-start.1 = (bf16[416,512]{1,0:T(8,128)(2,1)}, bf16[416,512]{1,0:T(8,128)(2,1)S(1)}, u32[]{:S(2)}, u32[]{:S(2)}) collective-permute-start(bf16[416,512]{1,0:T(8,128)(2,1)} %get-tuple-element.14.refs_0_), channel_id=1, source_target_pairs={{0,1},{1,2},{2,3},{3,0},{4,5},{5,6},{6,7},{7,4},{8,9},{9,10},{10,1... | collective-permute-start | bytes 1277960 | tf_op jit(solution)/shard_map/ppermute | solution.py:254
  7.0 11.2 %collective-permute-start = (bf16[416,512]{1,0:T(8,128)(2,1)}, bf16[416,512]{1,0:T(8,128)(2,1)S(1)}, u32[]{:S(2)}, u32[]{:S(2)}) collective-permute-start(bf16[416,512]{1,0:T(8,128)(2,1)} %get-tuple-element.14.refs_0_), channel_id=1, source_target_pairs={{0,3},{1,0},{2,1},{3,2},{4,7},{5,4},{6,5},{7,6},{8,11},{9,8},{10,9... | collective-permute-start | bytes 1277960 | tf_op jit(solution)/shard_map/ppermute | solution.py:253
  18.3 12.1 %collective-permute-start.7 = (bf16[416,512]{1,0:T(8,128)(2,1)S(1)}, bf16[416,512]{1,0:T(8,128)(2,1)S(1)}, u32[]{:S(2)}, u32[]{:S(2)}) collective-permute-start(bf16[416,512]{1,0:T(8,128)(2,1)S(1)} %get-tuple-element.25), channel_id=1, source_target_pairs={{0,4},{1,5},{2,6},{3,7},{4,0},{5,1},{6,2},{7,3},{8,12},{9,13},{10,... | collective-permute-start | bytes 1277960 | tf_op jit(solution)/shard_map/ppermute | solution.py:256
  19.8 11.8 %collective-permute-start.6 = (bf16[416,512]{1,0:T(8,128)(2,1)S(1)}, bf16[416,512]{1,0:T(8,128)(2,1)S(1)}, u32[]{:S(2)}, u32[]{:S(2)}) collective-permute-start(bf16[416,512]{1,0:T(8,128)(2,1)S(1)} %get-tuple-element.26), channel_id=1, source_target_pairs={{0,3},{1,0},{2,1},{3,2},{4,7},{5,4},{6,5},{7,6},{8,11},{9,8},{10,9... | collective-permute-start | bytes 1277960 | tf_op jit(solution)/shard_map/ppermute | solution.py:258
  22.7 14.4 %collective-permute-start.3 = (bf16[2,16,512]{2,1,0:T(8,128)(2,1)S(1)}, bf16[2,16,512]{2,1,0:T(8,128)(2,1)S(1)}, u32[]{:S(2)}, u32[]{:S(2)}) collective-permute-start(bf16[2,16,512]{2,1,0:T(8,128)(2,1)S(1)} %copy-done.8), channel_id=1, source_target_pairs={{0,8},{8,16},{16,24},{1,9},{9,17},{17,25},{2,10},{10,18},{18,26},{... | collective-permute-start | bytes 98312 | tf_op jit(solution)/shard_map/ppermute | solution.py:284
  24.6 12.5 %collective-permute-start.4 = (bf16[2,16,512]{2,1,0:T(8,128)(2,1)S(1)}, bf16[2,16,512]{2,1,0:T(8,128)(2,1)S(1)}, u32[]{:S(2)}, u32[]{:S(2)}) collective-permute-start(bf16[2,16,512]{2,1,0:T(8,128)(2,1)S(1)} %copy-done.7), channel_id=1, source_target_pairs={{8,0},{16,8},{24,16},{9,1},{17,9},{25,17},{10,2},{18,10},{26,18},{... | collective-permute-start | bytes 98312 | tf_op jit(solution)/shard_map/ppermute | solution.py:285
  28.3 14.0 %collective-permute-start.5 = (bf16[416,512]{1,0:T(8,128)(2,1)S(1)}, bf16[416,512]{1,0:T(8,128)(2,1)S(1)}, u32[]{:S(2)}, u32[]{:S(2)}) collective-permute-start(bf16[416,512]{1,0:T(8,128)(2,1)S(1)} %get-tuple-element.27), channel_id=1, source_target_pairs={{0,1},{1,2},{2,3},{3,0},{4,5},{5,6},{6,7},{7,4},{8,9},{9,10},{10,1... | collective-permute-start | bytes 1277960 | tf_op jit(solution)/shard_map/ppermute | solution.py:257
  30.4 5.1 %slice-start = ((s8[8388608]{0:T(1024)(128)(4,1)}), s8[4194304]{0:T(1024)(128)(4,1)S(1)}, s32[]{:S(2)}) async-start(s8[8388608]{0:T(1024)(128)(4,1)} %bitcast.2), calls=%async_computation.2 | async-start | bytes 8388608
  30.4 14.2 %collective-permute-start.8 = (bf16[208,512]{1,0:T(8,128)(2,1)S(1)}, bf16[208,512]{1,0:T(8,128)(2,1)S(1)}, u32[]{:S(2)}, u32[]{:S(2)}) collective-permute-start(bf16[208,512]{1,0:T(8,128)(2,1)S(1)} %slice.30), channel_id=1, source_target_pairs={{0,1},{1,2},{2,3},{3,0},{4,5},{5,6},{6,7},{7,4},{8,9},{9,10},{10,1... | collective-permute-start | bytes 638984 | tf_op jit(solution)/shard_map/ppermute | solution.py:259
  31.7 3.9 %slice-start.1 = ((s8[8388608]{0:T(1024)(128)(4,1)}), s8[4194304]{0:T(1024)(128)(4,1)S(1)}, s32[]{:S(2)}) async-start(s8[8388608]{0:T(1024)(128)(4,1)} %bitcast.2), calls=%async_computation.3 | async-start | bytes 8388608
  31.7 3.9 %copy-start = (bf16[416,512]{1,0:T(8,128)(2,1)S(1)}, bf16[416,512]{1,0:T(8,128)(2,1)}, u32[]{:S(2)}) copy-start(bf16[416,512]{1,0:T(8,128)(2,1)} %get-tuple-element.14.refs_0_) | copy-start | bytes 1277956
  31.7 13.0 %collective-permute-start.9 = (bf16[208,512]{1,0:T(8,128)(2,1)S(1)}, bf16[208,512]{1,0:T(8,128)(2,1)S(1)}, u32[]{:S(2)}, u32[]{:S(2)}) collective-permute-start(bf16[208,512]{1,0:T(8,128)(2,1)S(1)} %slice.31), channel_id=1, source_target_pairs={{0,3},{1,0},{2,1},{3,2},{4,7},{5,4},{6,5},{7,6},{8,11},{9,8},{10,9... | collective-permute-start | bytes 638984 | tf_op jit(solution)/shard_map/ppermute | solution.py:260
  35.6 9.1 %copy-start.1 = (bf16[16,16,512]{2,1,0:T(8,128)(2,1)S(1)}, bf16[16,16,512]{2,1,0:T(8,128)(2,1)}, u32[]{:S(2)}) copy-start(bf16[16,16,512]{2,1,0:T(8,128)(2,1)} %get-tuple-element.16.inner) | copy-start | bytes 786436
  44.7 52.0 %copy-start.3 = (s32[2,2]{1,0:T(2,128)S(1)}, s32[2,2]{1,0:T(2,128)}, u32[]{:S(2)}) copy-start(s32[2,2]{1,0:T(2,128)} %ladder_tiles.1) | copy-start | bytes 52
  44.7 52.0 %copy-start.4 = (s32[2,2]{1,0:T(2,128)S(1)}, s32[2,2]{1,0:T(2,128)}, u32[]{:S(2)}) copy-start(s32[2,2]{1,0:T(2,128)} %cycle_tiles.1) | copy-start | bytes 52
  44.7 51.9 %copy-start.5 = (s32[8]{0:T(128)S(1)}, s32[8]{0:T(128)}, u32[]{:S(2)}) copy-start(s32[8]{0:T(128)} %partner.1) | copy-start | bytes 100
  47.4 0.7 copy-start.2
  48.2 0.7 copy-start.6
  48.9 12.8 %all-to-all-start.1 = ((bf16[8,128,128]{2,1,0:T(8,128)(2,1)}), bf16[8,128,128]{2,1,0:T(8,128)(2,1)}, u32[]{:S(2)}, u32[]{:S(2)}) async-start(bf16[8,128,128]{2,1,0:T(8,128)(2,1)} %copy-done.2), calls=%async_computation.1 | async-start | bytes 524288 | tf_op jit(solution)/shard_map/all_to_all | solution.py:302
  52.9 27.7 %collective-permute-start.10 = (bf16[8,128,128]{2,1,0:T(8,128)(2,1)}, bf16[8,128,128]{2,1,0:T(8,128)(2,1)}, u32[]{:S(2)}, u32[]{:S(2)}) collective-permute-start(bf16[8,128,128]{2,1,0:T(8,128)(2,1)} %copy-done.6), channel_id=1, source_target_pairs={{0,0},{8,64},{16,128},{24,192},{32,32},{40,96},{48,160},{56,224},{... | collective-permute-start | bytes 786440 | tf_op jit(solution)/shard_map/ppermute | solution.py:301
  61.6 26.2 %collective-permute-start.11 = (bf16[8,128,128]{2,1,0:T(8,128)(2,1)}, bf16[8,128,128]{2,1,0:T(8,128)(2,1)}, u32[]{:S(2)}, u32[]{:S(2)}) collective-permute-start(bf16[8,128,128]{2,1,0:T(8,128)(2,1)} %all-to-all-done.1), channel_id=1, source_target_pairs={{0,32},{8,96},{16,160},{24,224},{32,0},{40,64},{48,128},{56,192},{... | collective-permute-start | bytes 786440 | tf_op jit(solution)/shard_map/ppermute | solution.py:304
  80.6 16.0 %all-to-all-start = ((bf16[8,128,128]{2,1,0:T(8,128)(2,1)}), bf16[8,128,128]{2,1,0:T(8,128)(2,1)S(1)}, u32[]{:S(2)}, u32[]{:S(2)}) async-start(bf16[8,128,128]{2,1,0:T(8,128)(2,1)} %collective-permute-done.10), calls=%async_computation | async-start | bytes 524288 | tf_op jit(solution)/shard_map/all_to_all | solution.py:303

commit v8 on v7

--- a/solution.py
+++ b/solution.py
@@ -1,5 +1,6 @@
 import jax
 import jax.numpy as jnp
+import numpy as np
 from jax import lax
 from jax.experimental import pallas as pl
 from jax.experimental.pallas import tpu as pltpu
@@ -31,15 +32,31 @@
     ]
 
 
-def orders_kernel(after, swap_ref, place_ref):
+def swap_kernel(after, swap_ref):
     del after
     row = lax.broadcasted_iota(jnp.int32, (1024, 128), 0)
     column = lax.broadcasted_iota(jnp.int32, (1024, 128), 1)
-    swap = ((row >> 3) & 7) * 128 + (row >> 9) * 64 + (row & 7) * 8 + ((row >> 6) & 7) - column
-    place = ((row >> 6) & 1) * 512 + ((row >> 3) & 7) * 64 + (row >> 7) * 8 + (row & 7) - column
-    for order, ref in ((swap, swap_ref), (place, place_ref)):
-        for c in range(8):
-            ref[:, c * 128 : (c + 1) * 128] = jnp.where(order == c * 128, 1.0, 0.0).astype(BF)
+    order = ((row >> 3) & 7) * 128 + (row >> 9) * 64 + (row & 7) * 8 + ((row >> 6) & 7) - column
+    for c in range(8):
+        swap_ref[:, c * 128 : (c + 1) * 128] = jnp.where(order == c * 128, 1.0, 0.0).astype(BF)
+
+
+def place_matrix():
+    row = np.arange(1024)
+    v, slot, b, a = row // 128, (row // 64) % 2, (row // 8) % 8, row % 8
+    order = jnp.asarray(slot * 512 + b * 64 + v * 8 + a, jnp.int32)
+    columns = lax.broadcasted_iota(jnp.int32, (1024, 1024), 1)
+    return (order[:, None] == columns).astype(BF)
+
+
+def second_stage_kernel(before, after, down, up, flip, up_ref, down_ref, side_ref):
+    del before, after
+    up_ref[:HALF, :] = flip[:HALF, :]
+    up_ref[HALF:, :] = up[:HALF, :]
+    down_ref[:HALF, :] = flip[:HALF, :]
+    down_ref[HALF:, :] = down[HALF:, :]
+    side_ref[:HALF, :] = up[HALF:, :]
+    side_ref[HALF:, :] = down[HALF:, :]
 
 
 HALF = 208
@@ -249,16 +266,26 @@
     return jax.ShapeDtypeStruct(dims, kind)
 
 
-def gather(own):
+def gather(own, before, after):
     down = lax.ppermute(own, "vert", DOWN)
     up = lax.ppermute(own, "vert", UP)
     flip = lax.ppermute(own, "vert", FLIP)
-    side_2 = lax.ppermute(jnp.concatenate([up[HALF:], down[HALF:]]), "vert", FLIP)
-    up_2 = lax.ppermute(jnp.concatenate([flip[:HALF], up[:HALF]]), "vert", UP)
-    down_2 = lax.ppermute(jnp.concatenate([flip[:HALF], down[HALF:]]), "vert", DOWN)
+    near = [down, up, flip]
+    to_up, to_down, to_side = call(
+        second_stage_kernel,
+        [HBM] * 2 + [VMEM] * 3,
+        [shape((2 * HALF, LANES), BF)] * 3,
+        [VMEM] * 3,
+        [],
+        8,
+        10**7,
+    )(before, after, *near)
+    side_2 = lax.ppermute(to_side, "vert", FLIP)
+    up_2 = lax.ppermute(to_up, "vert", UP)
+    down_2 = lax.ppermute(to_down, "vert", DOWN)
     up_3 = lax.ppermute(side_2[:HALF], "vert", UP)
     down_3 = lax.ppermute(down_2[:HALF], "vert", DOWN)
-    return [own, down, up, flip], [up_2, down_2, side_2, up_3, down_3]
+    return [own] + near, [up_2, down_2, side_2, up_3, down_3]
 
 
 def body(amplitudes, ladder_ints, ladder_tiles, cycle_ints, cycle_tiles, partner):
@@ -280,11 +307,12 @@
         60,
         10**9,
     )(ladder_tiles, cycle_tiles, amplitudes.reshape(1024, LANES), cycle_ints.reshape(80, 2, LANES))
-    near, far = gather(own)
     before = lax.ppermute(last, "pj", [(q, q + 1) for q in range(3)])
     after = lax.ppermute(first, "pj", [(q + 1, q) for q in range(3)])
-    matrix = shape((1024, 1024), BF)
-    swap, place = call(orders_kernel, [HBM], [matrix] * 2, [VMEM] * 2, [], 8, 2 * 10**10)(near[1])
+    near, far = gather(own, before, after)
+    swap = call(
+        swap_kernel, [HBM], shape((1024, 1024), BF), VMEM, [], 8, 2 * 10**10
+    )(near[1])
     begun = call(
         near_kernel, [VMEM] * 5, shape((PAIRS, 1024), F32), VMEM, [], 8, 10**9
     )(ladder_ints, *near)
@@ -315,7 +343,7 @@
         ],
         12,
         10**9,
-    )(ladder_tiles, cycle_tiles, partner, total, place, arrived_0, moved_1)
+    )(ladder_tiles, cycle_tiles, partner, total, place_matrix(), arrived_0, moved_1)
 
 
 def solution(mesh):

time: 101 us -> 83.3 us (0.82)
  the two profiles are of different devices: /device:TPU:66 before, /device:TPU:3 now
where the time goes in v8:
time: 83.3 us; the launch traced here: 81.9 us
  starting transfers between devices  37.7 us (45%)
  waiting for transfers between devices  19.8 us (24%)
  Pallas kernels  11.8 us (14%)
  blocking collectives  10.7 us (13%)
  local copies, waits for them, and re-layouts  1.38 us (2%)
    ppermute x1, starting transfers between devices, body(): moved_0 = lax.ppermute(sent_0, ('pi', 'pj'), pair_moves(0))  13.3 us
    all_to_all x1, blocking collectives, body(): arrived_1 = lax.all_to_all(sent_1, 'vert', 0, 0)  10.7 us
    all_to_all x1, starting transfers between devices, body(): arrived_0 = lax.all_to_all(moved_0, 'vert', 0, 0)  6.97 us
    ppermute x1, waiting for transfers between devices, body(): moved_1 = lax.ppermute(arrived_1, ('pi', 'pj'), pair_moves(1))  6.49 us
    ppermute x1, waiting for transfers between devices, gather(): down_2 = lax.ppermute(to_down, 'vert', DOWN)  6.12 us
    ppermute x1, starting transfers between devices, body(): after = lax.ppermute(first, 'pj', [(q + 1, q) for q in range(3)])  3.99 us
    pallas_call x1, Pallas kernels, body(): call(finish_kernel, [SMEM, SMEM, SMEM] + [VMEM] * 4, whole, HBM, [pltpu.V...  3.54 us
    ppermute x1, starting transfers between devices, gather(): down_3 = lax.ppermute(down_2[:HALF], 'vert', DOWN)  3.26 us
  transfers between devices with their start and end apart: 13, of which 7 were waited for; matrix products, arithmetic and copies ran while one was open for 1% of the time, Pallas kernels for 3%

profile of v8, /device:TPU:3, one launch (start us, length us, event | category | flops | bytes accessed | tf_op | source)
XLA Modules:
  0.0 81.9 jit_solution(4903024144588109355)
XLA Ops:
  0.0 3.2 %shard_map.73 = (bf16[416,512]{1,0:T(8,128)(2,1)}, bf16[16,16,512]{2,1,0:T(8,128)(2,1)}, bf16[2,16,512]{2,1,0:T(8,128)(2,1)}, bf16[2,16,512]{2,1,0:T(8,128)(2,1)}) custom-call(s32[2,2]{1,0:T(2,128)} %ladder_tiles.1, s32[2,2]{1,0:T(2,128)} %cycle_tiles.1, bf16[1024,512]{1,0:T(8,128)(2,1)} %bitcast.4, bf16[80,2,512]{2,1,0:T(2,128)(2,1)} %bitcast.5), custom_call_target="tpu_custom_call" | custom-call | flops 1000000000 | bytes 4194304 | tf_op jit(solution)/shard_map/pallas_call | solution.py:293
  3.2 1.9 %collective-permute-start.2 = (bf16[416,512]{1,0:T(8,128)(2,1)}, bf16[416,512]{1,0:T(8,128)(2,1)S(1)}, u32[]{:S(2)}, u32[]{:S(2)}) collective-permute-start(bf16[416,512]{1,0:T(8,128)(2,1)} %get-tuple-element.15.refs_0_), channel_id=1, source_target_pairs={{0,4},{1,5},{2,6},{3,7},{4,0},{5,1},{6,2},{7,3},{8,12},{9,13},{10,... | collective-permute-start | bytes 1277960 | tf_op jit(solution)/shard_map/ppermute | solution.py:272
  5.1 1.3 %collective-permute-start.1 = (bf16[416,512]{1,0:T(8,128)(2,1)}, bf16[416,512]{1,0:T(8,128)(2,1)S(1)}, u32[]{:S(2)}, u32[]{:S(2)}) collective-permute-start(bf16[416,512]{1,0:T(8,128)(2,1)} %get-tuple-element.15.refs_0_), channel_id=1, source_target_pairs={{0,1},{1,2},{2,3},{3,0},{4,5},{5,6},{6,7},{7,4},{8,9},{9,10},{10,1... | collective-permute-start | bytes 1277960 | tf_op jit(solution)/shard_map/ppermute | solution.py:271
  6.4 1.4 %collective-permute-start = (bf16[416,512]{1,0:T(8,128)(2,1)}, bf16[416,512]{1,0:T(8,128)(2,1)S(1)}, u32[]{:S(2)}, u32[]{:S(2)}) collective-permute-start(bf16[416,512]{1,0:T(8,128)(2,1)} %get-tuple-element.15.refs_0_), channel_id=1, source_target_pairs={{0,3},{1,0},{2,1},{3,2},{4,7},{5,4},{6,5},{7,6},{8,11},{9,8},{10,9... | collective-permute-start | bytes 1277960 | tf_op jit(solution)/shard_map/ppermute | solution.py:270
  7.8 1.3 %collective-permute-start.3 = (bf16[2,16,512]{2,1,0:T(8,128)(2,1)}, bf16[2,16,512]{2,1,0:T(8,128)(2,1)S(1)}, u32[]{:S(2)}, u32[]{:S(2)}) collective-permute-start(bf16[2,16,512]{2,1,0:T(8,128)(2,1)} %get-tuple-element.16), channel_id=1, source_target_pairs={{0,8},{8,16},{16,24},{1,9},{9,17},{17,25},{2,10},{10,18},{18,26},{... | collective-permute-start | bytes 98312 | tf_op jit(solution)/shard_map/ppermute | solution.py:310
  9.1 4.0 %collective-permute-start.4 = (bf16[2,16,512]{2,1,0:T(8,128)(2,1)}, bf16[2,16,512]{2,1,0:T(8,128)(2,1)S(1)}, u32[]{:S(2)}, u32[]{:S(2)}) collective-permute-start(bf16[2,16,512]{2,1,0:T(8,128)(2,1)} %get-tuple-element.18), channel_id=1, source_target_pairs={{8,0},{16,8},{24,16},{9,1},{17,9},{25,17},{10,2},{18,10},{26,18},{... | collective-permute-start | bytes 98312 | tf_op jit(solution)/shard_map/ppermute | solution.py:311
  13.1 1.0 %collective-permute-done.4.after = bf16[2,16,512]{2,1,0:T(8,128)(2,1)S(1)} collective-permute-done((bf16[2,16,512]{2,1,0:T(8,128)(2,1)}, bf16[2,16,512]{2,1,0:T(8,128)(2,1)S(1)}, u32[]{:S(2)}, u32[]{:S(2)}) %collective-permute-start.4) | collective-permute-done | bytes 32800 | tf_op jit(solution)/shard_map/ppermute | solution.py:311
  14.2 1.5 %collective-permute-done.2.refs_3_.flip = bf16[416,512]{1,0:T(8,128)(2,1)S(1)} collective-permute-done((bf16[416,512]{1,0:T(8,128)(2,1)}, bf16[416,512]{1,0:T(8,128)(2,1)S(1)}, u32[]{:S(2)}, u32[]{:S(2)}) %collective-permute-start.2) | collective-permute-done | bytes 426016 | tf_op jit(solution)/shard_map/ppermute | solution.py:272
  15.7 1.4 %collective-permute-done.1.refs_2_.up = bf16[416,512]{1,0:T(8,128)(2,1)S(1)} collective-permute-done((bf16[416,512]{1,0:T(8,128)(2,1)}, bf16[416,512]{1,0:T(8,128)(2,1)S(1)}, u32[]{:S(2)}, u32[]{:S(2)}) %collective-permute-start.1) | collective-permute-done | bytes 426016 | tf_op jit(solution)/shard_map/ppermute | solution.py:271
  17.1 0.1 shard_map.76
  17.2 2.4 %collective-permute-start.6 = (bf16[416,512]{1,0:T(8,128)(2,1)S(1)}, bf16[416,512]{1,0:T(8,128)(2,1)S(1)}, u32[]{:S(2)}, u32[]{:S(2)}) collective-permute-start(bf16[416,512]{1,0:T(8,128)(2,1)S(1)} %get-tuple-element.20), channel_id=1, source_target_pairs={{0,3},{1,0},{2,1},{3,2},{4,7},{5,4},{6,5},{7,6},{8,11},{9,8},{10,9... | collective-permute-start | bytes 1277960 | tf_op jit(solution)/shard_map/ppermute | solution.py:285
  19.6 1.1 %collective-permute-start.7 = (bf16[416,512]{1,0:T(8,128)(2,1)S(1)}, bf16[416,512]{1,0:T(8,128)(2,1)S(1)}, u32[]{:S(2)}, u32[]{:S(2)}) collective-permute-start(bf16[416,512]{1,0:T(8,128)(2,1)S(1)} %get-tuple-element.21), channel_id=1, source_target_pairs={{0,4},{1,5},{2,6},{3,7},{4,0},{5,1},{6,2},{7,3},{8,12},{9,13},{10,... | collective-permute-start | bytes 1277960 | tf_op jit(solution)/shard_map/ppermute | solution.py:283
  20.7 6.1 %collective-permute-done.6.refs_5_ = bf16[416,512]{1,0:T(8,128)(2,1)S(1)} collective-permute-done((bf16[416,512]{1,0:T(8,128)(2,1)S(1)}, bf16[416,512]{1,0:T(8,128)(2,1)S(1)}, u32[]{:S(2)}, u32[]{:S(2)}) %collective-permute-start.6) | collective-permute-done | bytes 426016 | tf_op jit(solution)/shard_map/ppermute | solution.py:285
  26.8 3.3 %collective-permute-start.9 = (bf16[208,512]{1,0:T(8,128)(2,1)S(1)}, bf16[208,512]{1,0:T(8,128)(2,1)S(1)}, u32[]{:S(2)}, u32[]{:S(2)}) collective-permute-start(bf16[208,512]{1,0:T(8,128)(2,1)S(1)} %slice.9), channel_id=1, source_target_pairs={{0,3},{1,0},{2,1},{3,2},{4,7},{5,4},{6,5},{7,6},{8,11},{9,8},{10,9... | collective-permute-start | bytes 638984 | tf_op jit(solution)/shard_map/ppermute | solution.py:287
  30.1 0.0 slice-start.1
  30.1 0.1 collective-permute-start.8
  30.2 0.8 %shard_map.75.swap = bf16[1024,1024]{1,0:T(8,128)(2,1)S(1)} custom-call(bf16[416,512]{1,0:T(8,128)(2,1)S(1)} %collective-permute-done.refs_1_.after.down), custom_call_target="tpu_custom_call" | custom-call | flops 20000000000 | bytes 4194304 | tf_op jit(solution)/shard_map/pallas_call | solution.py:313
  31.1 1.2 %slice-done.1 = s8[4194304]{0:T(1024)(128)(4,1)S(1)} async-done(((s8[8388608]{0:T(1024)(128)(4,1)}), s8[4194304]{0:T(1024)(128)(4,1)S(1)}, s32[]{:S(2)}) %slice-start.1) | async-done | bytes 4194328
  32.3 0.1 copy-done
  32.4 1.5 %shard_map.74.near = f32[128,1024]{1,0:T(8,128)S(1)} custom-call(bf16[2,512,4096]{2,1,0:T(8,128)(2,1)S(1)} %bitcast.3, bf16[416,512]{1,0:T(8,128)(2,1)S(1)} %copy-done, bf16[416,512]{1,0:T(8,128)(2,1)S(1)} %collective-permute-done.refs_1_.after.down, bf16[416,512]{1,0:T(8,128)(2,1)S(1)} %collective-permute-done.1.refs_2_.up, ...), custom_call_target="tpu_custom_call" | custom-call | flops 1000000000 | bytes 4194304 | tf_op jit(solution)/shard_map/pallas_call | solution.py:316
  33.9 2.2 %collective-permute-done.8.refs_7_ = bf16[208,512]{1,0:T(8,128)(2,1)S(1)} collective-permute-done((bf16[208,512]{1,0:T(8,128)(2,1)S(1)}, bf16[208,512]{1,0:T(8,128)(2,1)S(1)}, u32[]{:S(2)}, u32[]{:S(2)}) %collective-permute-start.8) | collective-permute-done | bytes 213024 | tf_op jit(solution)/shard_map/ppermute | solution.py:286
  36.1 2.7 %shard_map.77 = (f32[128,2048]{1,0:T(8,128)S(1)}, bf16[8,128,128]{2,1,0:T(8,128)(2,1)S(1)}, bf16[8,128,128]{2,1,0:T(8,128)(2,1)S(1)}) custom-call(bf16[2,512,4096]{2,1,0:T(8,128)(2,1)S(1)} %bitcast.3, f32[128,1024]{1,0:T(8,128)S(1)} %shard_map.74.near, bf16[2,16,512]{2,1,0:T(8,128)(2,1)S(1)} %collective-permute-done.3.before, ...), custom_call_target="tpu_custom_call" | custom-call | flops 2000000000 | bytes 4194304 | tf_op jit(solution)/shard_map/pallas_call | solution.py:320
  38.9 0.0 copy-start.3
  38.9 0.0 copy-start.4
  38.9 13.3 %collective-permute-start.10 = (bf16[8,128,128]{2,1,0:T(8,128)(2,1)S(1)}, bf16[8,128,128]{2,1,0:T(8,128)(2,1)}, u32[]{:S(2)}, u32[]{:S(2)}) collective-permute-start(bf16[8,128,128]{2,1,0:T(8,128)(2,1)S(1)} %get-tuple-element.23), channel_id=1, source_target_pairs={{0,0},{8,64},{16,128},{24,192},{32,32},{40,96},{48,160},{56,224},{... | collective-permute-start | bytes 786440 | tf_op jit(solution)/shard_map/ppermute | solution.py:329
  52.2 10.7 %all_to_all.10 = bf16[8,128,128]{2,1,0:T(8,128)(2,1)} all-to-all(bf16[8,128,128]{2,1,0:T(8,128)(2,1)S(1)} %get-tuple-element.24), channel_id=1, replica_groups=mesh['pi'=8,'pj'=4,'vert'=8] {'vert'}, dimensions={0} | all-to-all | bytes 524288 | tf_op jit(solution)/shard_map/all_to_all | solution.py:330
  62.8 0.7 collective-permute-start.11
  63.5 7.0 %all-to-all-start = ((bf16[8,128,128]{2,1,0:T(8,128)(2,1)}), bf16[8,128,128]{2,1,0:T(8,128)(2,1)S(1)}, u32[]{:S(2)}, u32[]{:S(2)}) async-start(bf16[8,128,128]{2,1,0:T(8,128)(2,1)} %collective-permute-done.10), calls=%async_computation | async-start | bytes 524288 | tf_op jit(solution)/shard_map/all_to_all | solution.py:331
  70.5 0.4 fusion.place
  70.9 6.5 %collective-permute-done.11.second = bf16[8,128,128]{2,1,0:T(8,128)(2,1)} collective-permute-done((bf16[8,128,128]{2,1,0:T(8,128)(2,1)}, bf16[8,128,128]{2,1,0:T(8,128)(2,1)}, u32[]{:S(2)}, u32[]{:S(2)}) %collective-permute-start.11) | collective-permute-done | bytes 262176 | tf_op jit(solution)/shard_map/ppermute | solution.py:332
  77.4 1.0 %all-to-all-done.first = bf16[8,128,128]{2,1,0:T(8,128)(2,1)S(1)} async-done(((bf16[8,128,128]{2,1,0:T(8,128)(2,1)}), bf16[8,128,128]{2,1,0:T(8,128)(2,1)S(1)}, u32[]{:S(2)}, u32[]{:S(2)}) %all-to-all-start) | async-done | bytes 262176 | tf_op jit(solution)/shard_map/all_to_all | solution.py:331
  78.4 3.5 %shard_map.78 = f32[8,16,8,512]{3,2,1,0:T(8,128)} custom-call(s32[2,2]{1,0:T(2,128)S(1)} %copy-done.2, s32[2,2]{1,0:T(2,128)S(1)} %copy-done.3, s32[8]{0:T(128)S(1)} %copy-done.4, f32[128,2048]{1,0:T(8,128)S(1)} %get-tuple-element.22.total, bf16[1024,1024]{1,0:T(8,128)(2,1)S(1)} %fusion.place, bf16[8,128,128]{2,1,0:T(8,128)(2,1)S(1)} %all-to-all-done.first, ...), custom_call_target="tpu_custom_call" | custom-call | flops 1000000000 | bytes 4194304 | tf_op jit(solution)/shard_map/pallas_call | solution.py:334
  (21 shorter events, 0.1 us)
Async XLA Ops:
  3.2 12.5 %collective-permute-start.2 = (bf16[416,512]{1,0:T(8,128)(2,1)}, bf16[416,512]{1,0:T(8,128)(2,1)S(1)}, u32[]{:S(2)}, u32[]{:S(2)}) collective-permute-start(bf16[416,512]{1,0:T(8,128)(2,1)} %get-tuple-element.15.refs_0_), channel_id=1, source_target_pairs={{0,4},{1,5},{2,6},{3,7},{4,0},{5,1},{6,2},{7,3},{8,12},{9,13},{10,... | collective-permute-start | bytes 1277960 | tf_op jit(solution)/shard_map/ppermute | solution.py:272
  5.1 12.0 %collective-permute-start.1 = (bf16[416,512]{1,0:T(8,128)(2,1)}, bf16[416,512]{1,0:T(8,128)(2,1)S(1)}, u32[]{:S(2)}, u32[]{:S(2)}) collective-permute-start(bf16[416,512]{1,0:T(8,128)(2,1)} %get-tuple-element.15.refs_0_), channel_id=1, source_target_pairs={{0,1},{1,2},{2,3},{3,0},{4,5},{5,6},{6,7},{7,4},{8,9},{9,10},{10,1... | collective-permute-start | bytes 1277960 | tf_op jit(solution)/shard_map/ppermute | solution.py:271
  6.4 10.7 %collective-permute-start = (bf16[416,512]{1,0:T(8,128)(2,1)}, bf16[416,512]{1,0:T(8,128)(2,1)S(1)}, u32[]{:S(2)}, u32[]{:S(2)}) collective-permute-start(bf16[416,512]{1,0:T(8,128)(2,1)} %get-tuple-element.15.refs_0_), channel_id=1, source_target_pairs={{0,3},{1,0},{2,1},{3,2},{4,7},{5,4},{6,5},{7,6},{8,11},{9,8},{10,9... | collective-permute-start | bytes 1277960 | tf_op jit(solution)/shard_map/ppermute | solution.py:270
  7.8 5.3 %collective-permute-start.3 = (bf16[2,16,512]{2,1,0:T(8,128)(2,1)}, bf16[2,16,512]{2,1,0:T(8,128)(2,1)S(1)}, u32[]{:S(2)}, u32[]{:S(2)}) collective-permute-start(bf16[2,16,512]{2,1,0:T(8,128)(2,1)} %get-tuple-element.16), channel_id=1, source_target_pairs={{0,8},{8,16},{16,24},{1,9},{9,17},{17,25},{2,10},{10,18},{18,26},{... | collective-permute-start | bytes 98312 | tf_op jit(solution)/shard_map/ppermute | solution.py:310
  9.1 5.0 %collective-permute-start.4 = (bf16[2,16,512]{2,1,0:T(8,128)(2,1)}, bf16[2,16,512]{2,1,0:T(8,128)(2,1)S(1)}, u32[]{:S(2)}, u32[]{:S(2)}) collective-permute-start(bf16[2,16,512]{2,1,0:T(8,128)(2,1)} %get-tuple-element.18), channel_id=1, source_target_pairs={{8,0},{16,8},{24,16},{9,1},{17,9},{25,17},{10,2},{18,10},{26,18},{... | collective-permute-start | bytes 98312 | tf_op jit(solution)/shard_map/ppermute | solution.py:311
  17.2 9.6 %collective-permute-start.6 = (bf16[416,512]{1,0:T(8,128)(2,1)S(1)}, bf16[416,512]{1,0:T(8,128)(2,1)S(1)}, u32[]{:S(2)}, u32[]{:S(2)}) collective-permute-start(bf16[416,512]{1,0:T(8,128)(2,1)S(1)} %get-tuple-element.20), channel_id=1, source_target_pairs={{0,3},{1,0},{2,1},{3,2},{4,7},{5,4},{6,5},{7,6},{8,11},{9,8},{10,9... | collective-permute-start | bytes 1277960 | tf_op jit(solution)/shard_map/ppermute | solution.py:285
  19.6 10.5 %collective-permute-start.7 = (bf16[416,512]{1,0:T(8,128)(2,1)S(1)}, bf16[416,512]{1,0:T(8,128)(2,1)S(1)}, u32[]{:S(2)}, u32[]{:S(2)}) collective-permute-start(bf16[416,512]{1,0:T(8,128)(2,1)S(1)} %get-tuple-element.21), channel_id=1, source_target_pairs={{0,4},{1,5},{2,6},{3,7},{4,0},{5,1},{6,2},{7,3},{8,12},{9,13},{10,... | collective-permute-start | bytes 1277960 | tf_op jit(solution)/shard_map/ppermute | solution.py:283
  20.7 13.2 %collective-permute-start.5 = (bf16[416,512]{1,0:T(8,128)(2,1)S(1)}, bf16[416,512]{1,0:T(8,128)(2,1)S(1)}, u32[]{:S(2)}, u32[]{:S(2)}) collective-permute-start(bf16[416,512]{1,0:T(8,128)(2,1)S(1)} %get-tuple-element.19), channel_id=1, source_target_pairs={{0,1},{1,2},{2,3},{3,0},{4,5},{5,6},{6,7},{7,4},{8,9},{9,10},{10,1... | collective-permute-start | bytes 1277960 | tf_op jit(solution)/shard_map/ppermute | solution.py:284
  26.8 4.3 %slice-start = ((s8[8388608]{0:T(1024)(128)(4,1)}), s8[4194304]{0:T(1024)(128)(4,1)S(1)}, s32[]{:S(2)}) async-start(s8[8388608]{0:T(1024)(128)(4,1)} %bitcast.2), calls=%async_computation.2 | async-start | bytes 8388608
  26.8 7.1 %collective-permute-start.9 = (bf16[208,512]{1,0:T(8,128)(2,1)S(1)}, bf16[208,512]{1,0:T(8,128)(2,1)S(1)}, u32[]{:S(2)}, u32[]{:S(2)}) collective-permute-start(bf16[208,512]{1,0:T(8,128)(2,1)S(1)} %slice.9), channel_id=1, source_target_pairs={{0,3},{1,0},{2,1},{3,2},{4,7},{5,4},{6,5},{7,6},{8,11},{9,8},{10,9... | collective-permute-start | bytes 638984 | tf_op jit(solution)/shard_map/ppermute | solution.py:287
  30.1 2.2 %slice-start.1 = ((s8[8388608]{0:T(1024)(128)(4,1)}), s8[4194304]{0:T(1024)(128)(4,1)S(1)}, s32[]{:S(2)}) async-start(s8[8388608]{0:T(1024)(128)(4,1)} %bitcast.2), calls=%async_computation.3 | async-start | bytes 8388608
  30.1 2.3 %copy-start = (bf16[416,512]{1,0:T(8,128)(2,1)S(1)}, bf16[416,512]{1,0:T(8,128)(2,1)}, u32[]{:S(2)}) copy-start(bf16[416,512]{1,0:T(8,128)(2,1)} %get-tuple-element.15.refs_0_) | copy-start | bytes 1277956
  30.1 6.0 %collective-permute-start.8 = (bf16[208,512]{1,0:T(8,128)(2,1)S(1)}, bf16[208,512]{1,0:T(8,128)(2,1)S(1)}, u32[]{:S(2)}, u32[]{:S(2)}) collective-permute-start(bf16[208,512]{1,0:T(8,128)(2,1)S(1)} %slice.8), channel_id=1, source_target_pairs={{0,1},{1,2},{2,3},{3,0},{4,5},{5,6},{6,7},{7,4},{8,9},{9,10},{10,1... | collective-permute-start | bytes 638984 | tf_op jit(solution)/shard_map/ppermute | solution.py:286
  32.4 3.7 %copy-start.1 = (bf16[16,16,512]{2,1,0:T(8,128)(2,1)S(1)}, bf16[16,16,512]{2,1,0:T(8,128)(2,1)}, u32[]{:S(2)}) copy-start(bf16[16,16,512]{2,1,0:T(8,128)(2,1)} %get-tuple-element.17.inner) | copy-start | bytes 786436
  36.1 34.4 %copy-start.5 = (s32[1024]{0:T(1024)S(1)}, s32[1024]{0:T(1024)}, u32[]{:S(2)}) copy-start(s32[1024]{0:T(1024)} %constant.2.clone) | copy-start | bytes 12292
  38.9 39.5 %copy-start.2 = (s32[2,2]{1,0:T(2,128)S(1)}, s32[2,2]{1,0:T(2,128)}, u32[]{:S(2)}) copy-start(s32[2,2]{1,0:T(2,128)} %ladder_tiles.1) | copy-start | bytes 52
  38.9 39.5 %copy-start.3 = (s32[2,2]{1,0:T(2,128)S(1)}, s32[2,2]{1,0:T(2,128)}, u32[]{:S(2)}) copy-start(s32[2,2]{1,0:T(2,128)} %cycle_tiles.1) | copy-start | bytes 52
  38.9 39.5 %copy-start.4 = (s32[8]{0:T(128)S(1)}, s32[8]{0:T(128)}, u32[]{:S(2)}) copy-start(s32[8]{0:T(128)} %partner.1) | copy-start | bytes 100
  38.9 24.6 %collective-permute-start.10 = (bf16[8,128,128]{2,1,0:T(8,128)(2,1)S(1)}, bf16[8,128,128]{2,1,0:T(8,128)(2,1)}, u32[]{:S(2)}, u32[]{:S(2)}) collective-permute-start(bf16[8,128,128]{2,1,0:T(8,128)(2,1)S(1)} %get-tuple-element.23), channel_id=1, source_target_pairs={{0,0},{8,64},{16,128},{24,192},{32,32},{40,96},{48,160},{56,224},{... | collective-permute-start | bytes 786440 | tf_op jit(solution)/shard_map/ppermute | solution.py:329
  62.8 14.6 %collective-permute-start.11 = (bf16[8,128,128]{2,1,0:T(8,128)(2,1)}, bf16[8,128,128]{2,1,0:T(8,128)(2,1)}, u32[]{:S(2)}, u32[]{:S(2)}) collective-permute-start(bf16[8,128,128]{2,1,0:T(8,128)(2,1)} %all_to_all.10), channel_id=1, source_target_pairs={{0,32},{8,96},{16,160},{24,224},{32,0},{40,64},{48,128},{56,192},{... | collective-permute-start | bytes 786440 | tf_op jit(solution)/shard_map/ppermute | solution.py:332
  63.5 14.8 %all-to-all-start = ((bf16[8,128,128]{2,1,0:T(8,128)(2,1)}), bf16[8,128,128]{2,1,0:T(8,128)(2,1)S(1)}, u32[]{:S(2)}, u32[]{:S(2)}) async-start(bf16[8,128,128]{2,1,0:T(8,128)(2,1)} %collective-permute-done.10), calls=%async_computation | async-start | bytes 524288 | tf_op jit(solution)/shard_map/all_to_all | solution.py:331

commit v9 on v8

--- a/solution.py
+++ b/solution.py
@@ -26,10 +26,44 @@
 DOWN = vert_moves(lambda h, y: h * 4 + (y + 3) % 4)
 
 
-def pair_moves(k):
+def pair_moves(k, dx):
     return [
-        (p * 4 + q, (2 * q + ((p % 2) ^ k)) * 4 + p // 2) for p in range(8) for q in range(4)
+        ((p * 4 + q) * 8 + v, ((2 * q + ((p % 2) ^ k)) * 4 + p // 2) * 8 + (v ^ (4 * dx)))
+        for p in range(8)
+        for q in range(4)
+        for v in range(8)
     ]
+
+
+def to_transposed(block, k, dx):
+    return lax.ppermute(block, ("pi", "pj", "vert"), pair_moves(k, dx))
+
+
+def along_y(block, dy):
+    return lax.ppermute(block, "vert", vert_moves(lambda h, y: h * 4 + (y + dy) % 4))
+
+
+def peers(sign):
+    vert = lax.axis_index("vert")
+    h, y = vert // 4, vert % 4
+    found = []
+    for dx in range(2):
+        for dy in range(4):
+            there = (h if dx == 0 else 1 - h) * 4 + (y + (dy if sign > 0 else 4 - dy)) % 4
+            found.append((dx, dy, pl.multiple_of(there * 128, 128)))
+    return found
+
+
+def split_kernel(same, other, first, second, third):
+    for dy, ref in enumerate((first, second, third), 1):
+        ref[0] = same[dy]
+        ref[1] = other[dy]
+
+
+def join_kernel(own, first, second, third, same, other):
+    for dy, ref in enumerate((own, first, second, third)):
+        same[dy] = ref[0]
+        other[dy] = ref[1]
 
 
 def swap_kernel(after, swap_ref):
@@ -156,7 +190,7 @@
 
 
 def main_kernel(ladder_ints, near, before, inner, after, swap, *refs):
-    total, first_ref, second_ref, ints = refs[9:]
+    total, same_ref, other_ref, *late_refs, ints, lanes_buf = refs[9:]
     far = far_pieces(refs[4:9])
     for w, pieces in enumerate(near_pieces(refs[:4])):
         for source, ref, first in pieces + far[w]:
@@ -201,27 +235,29 @@
     for which in range(2):
         lanes = slice(which * LANES, (which + 1) * LANES)
         total[:, lanes] = ladder_part(which, far[which], ladder_ints, near[:, lanes])
+    both = jnp.concatenate([total[:, :1024], total[:, 1024:]], axis=0).astype(BF)
+    lanes_buf[...] = jnp.dot(both, swap[...], preferred_element_type=F32).astype(BF)
     parity = lax.axis_index("pi") % 2
     for s in range(2):
-        sent = jnp.dot(
-            total[:, s * 1024 : (s + 1) * 1024].astype(BF), swap[...], preferred_element_type=F32
-        ).astype(BF)
-        upper, under = sent[:64], sent[64:]
-        halves = (jnp.where(parity == 0, upper, under), jnp.where(parity == 0, under, upper))
-        for half, ref in zip(halves, (first_ref, second_ref)):
-            for v in range(8):
-                ref[v, s * 64 : (s + 1) * 64, :] = half[:, v * 128 : (v + 1) * 128]
-
-
-def finish_kernel(
-    ladder_tiles, cycle_tiles, partner, total, place, first, second, out_ref, mirrored, held, sems
-):
+        early = pl.ds(pl.multiple_of(s * 128 + parity * 64, 64), 64)
+        late = pl.ds(pl.multiple_of(s * 128 + (1 - parity) * 64, 64), 64)
+        rows = slice(s * 64, (s + 1) * 64)
+        for dx, dy, start in peers(1):
+            (same_ref, other_ref)[dx][dy, rows, :] = lanes_buf[early, pl.ds(start, 128)]
+            late_refs[dy][dx, rows, :] = lanes_buf[late, pl.ds(start, 128)]
+
+
+def finish_kernel(ladder_tiles, cycle_tiles, partner, total, place, *refs):
+    arrived, (out_ref, mirrored, wide, held, sems) = refs[:7], refs[7:]
     parity = lax.axis_index("pi") % 2
-    for k, arrived in enumerate((first, second)):
-        wide = jnp.concatenate([arrived[v] for v in range(8)], axis=1)
-        moved = jnp.dot(wide, place[...], preferred_element_type=F32)
+    for dx, dy, start in peers(-1):
+        early = arrived[dx][0] if dy == 0 else arrived[1 + dy][dx]
+        wide[:128, pl.ds(start, 128)] = early
+        wide[128:, pl.ds(start, 128)] = arrived[5 + dx][dy]
+    moved = jnp.dot(wide[...], place[...], preferred_element_type=F32)
+    for k in range(2):
         for s in range(2):
-            mirrored[s, parity ^ k] = moved[s * 64 : (s + 1) * 64]
+            mirrored[s, parity ^ k] = moved[k * 128 + s * 64 : k * 128 + (s + 1) * 64]
     dests = [ladder_tiles[0, 0], ladder_tiles[1, 0], cycle_tiles[0, 0], cycle_tiles[1, 0]]
     tile = lax.broadcasted_iota(jnp.int32, (8, LANES), 0)
     own = [(tile == dest).astype(F32) for dest in dests]
@@ -316,34 +352,36 @@
     begun = call(
         near_kernel, [VMEM] * 5, shape((PAIRS, 1024), F32), VMEM, [], 8, 10**9
     )(ladder_ints, *near)
-    block = shape((8, 128, 128), BF)
-    total, sent_0, sent_1 = call(
+    four, two = shape((4, 128, 128), BF), shape((2, 128, 128), BF)
+    total, same, other, late_0, late_1, late_2, late_3 = call(
         main_kernel,
         [VMEM] * 15,
-        [shape((PAIRS, 2048), F32), block, block],
-        [VMEM] * 3,
-        [pltpu.VMEM((8, 160, LANES), F32)],
+        [shape((PAIRS, 2048), F32), four, four, two, two, two, two],
+        [VMEM] * 7,
+        [pltpu.VMEM((8, 160, LANES), F32), pltpu.VMEM((256, 1024), BF)],
         12,
         2 * 10**9,
     )(ladder_ints, begun, before, inner, after, swap, *near, *far)
-    moved_0 = lax.ppermute(sent_0, ("pi", "pj"), pair_moves(0))
-    arrived_1 = lax.all_to_all(sent_1, "vert", 0, 0)
-    arrived_0 = lax.all_to_all(moved_0, "vert", 0, 0)
-    moved_1 = lax.ppermute(arrived_1, ("pi", "pj"), pair_moves(1))
-    whole = shape((8, 16, 8, LANES), F32)
+    same, other = to_transposed(same, 0, 0), to_transposed(other, 0, 1)
+    late = [along_y(block, dy) for dy, block in ((1, late_1), (2, late_2), (3, late_3))]
+    joined = call(join_kernel, [VMEM] * 4, [four] * 2, [VMEM] * 2, [], 4, 10**7)(late_0, *late)
+    joined = [to_transposed(block, 1, dx) for dx, block in enumerate(joined)]
+    early = call(split_kernel, [VMEM] * 2, [two] * 3, [VMEM] * 3, [], 4, 10**7)(same, other)
+    early = [along_y(block, dy) for dy, block in enumerate(early, 1)]
     return call(
         finish_kernel,
-        [SMEM, SMEM, SMEM] + [VMEM] * 4,
-        whole,
+        [SMEM, SMEM, SMEM] + [VMEM] * 9,
+        shape((8, 16, 8, LANES), F32),
         HBM,
         [
             pltpu.VMEM((2, 2, 64, 1024), F32),
+            pltpu.VMEM((256, 1024), BF),
             pltpu.VMEM((8, 16, 8, LANES), F32),
             pltpu.SemaphoreType.DMA((8,)),
         ],
         12,
         10**9,
-    )(ladder_tiles, cycle_tiles, partner, total, place_matrix(), arrived_0, moved_1)
+    )(ladder_tiles, cycle_tiles, partner, total, place_matrix(), same, other, *early, *joined)
 
 
 def solution(mesh):

time: 83.3 us -> 79.8 us (0.958)
  the two profiles are of different devices: /device:TPU:3 before, /device:TPU:6 now
where the time goes in v9:
time: 79.8 us; the launch traced here: 79.7 us
  starting transfers between devices  44.4 us (56%)
  waiting for transfers between devices  21.2 us (27%)
  Pallas kernels  12 us (15%)
  local copies, waits for them, and re-layouts  1.38 us (2%)
    ppermute x4, starting transfers between devices, to_transposed(): return lax.ppermute(block, ('pi', 'pj', 'vert'), pair_moves(k, dx))  17.7 us
    ppermute x6, starting transfers between devices, along_y(): lax.ppermute(block, 'vert', vert_moves(lambda h, y: h * 4 + (y + dy) % 4))  7.41 us
    ppermute x1, waiting for transfers between devices, gather(): down_2 = lax.ppermute(to_down, 'vert', DOWN)  5.52 us
    ppermute x4, waiting for transfers between devices, to_transposed(): return lax.ppermute(block, ('pi', 'pj', 'vert'), pair_moves(k, dx))  4.51 us
    ppermute x6, waiting for transfers between devices, along_y(): lax.ppermute(block, 'vert', vert_moves(lambda h, y: h * 4 + (y + dy) % 4))  3.8 us
    ppermute x1, starting transfers between devices, gather(): down_3 = lax.ppermute(down_2[:HALF], 'vert', DOWN)  3.77 us
    ppermute x1, starting transfers between devices, body(): after = lax.ppermute(first, 'pj', [(q + 1, q) for q in range(3)])  3.64 us
    ppermute x1, waiting for transfers between devices, gather(): up_3 = lax.ppermute(side_2[:HALF], 'vert', UP)  3.37 us
  transfers between devices with their start and end apart: 20, of which 9 were waited for; matrix products, arithmetic and copies ran while one was open for 1% of the time, Pallas kernels for 3%

profile of v9, /device:TPU:6, one launch (start us, length us, event | category | flops | bytes accessed | tf_op | source)
XLA Modules:
  0.0 79.7 jit_solution(182809806672137103)
XLA Ops:
  0.0 3.2 %shard_map.73 = (bf16[416,512]{1,0:T(8,128)(2,1)}, bf16[16,16,512]{2,1,0:T(8,128)(2,1)}, bf16[2,16,512]{2,1,0:T(8,128)(2,1)}, bf16[2,16,512]{2,1,0:T(8,128)(2,1)}) custom-call(s32[2,2]{1,0:T(2,128)} %ladder_tiles.1, s32[2,2]{1,0:T(2,128)} %cycle_tiles.1, bf16[1024,512]{1,0:T(8,128)(2,1)} %bitcast.4, bf16[80,2,512]{2,1,0:T(2,128)(2,1)} %bitcast.5), custom_call_target="tpu_custom_call" | custom-call | flops 1000000000 | bytes 4194304 | tf_op jit(solution)/shard_map/pallas_call | solution.py:329
  3.2 1.5 %collective-permute-start.2 = (bf16[416,512]{1,0:T(8,128)(2,1)}, bf16[416,512]{1,0:T(8,128)(2,1)S(1)}, u32[]{:S(2)}, u32[]{:S(2)}) collective-permute-start(bf16[416,512]{1,0:T(8,128)(2,1)} %get-tuple-element.24.refs_0_), channel_id=1, source_target_pairs={{0,4},{1,5},{2,6},{3,7},{4,0},{5,1},{6,2},{7,3},{8,12},{9,13},{10,... | collective-permute-start | bytes 1277960 | tf_op jit(solution)/shard_map/ppermute | solution.py:308
  4.7 1.6 %collective-permute-start.1 = (bf16[416,512]{1,0:T(8,128)(2,1)}, bf16[416,512]{1,0:T(8,128)(2,1)S(1)}, u32[]{:S(2)}, u32[]{:S(2)}) collective-permute-start(bf16[416,512]{1,0:T(8,128)(2,1)} %get-tuple-element.24.refs_0_), channel_id=1, source_target_pairs={{0,1},{1,2},{2,3},{3,0},{4,5},{5,6},{6,7},{7,4},{8,9},{9,10},{10,1... | collective-permute-start | bytes 1277960 | tf_op jit(solution)/shard_map/ppermute | solution.py:307
  6.2 1.7 %collective-permute-start = (bf16[416,512]{1,0:T(8,128)(2,1)}, bf16[416,512]{1,0:T(8,128)(2,1)S(1)}, u32[]{:S(2)}, u32[]{:S(2)}) collective-permute-start(bf16[416,512]{1,0:T(8,128)(2,1)} %get-tuple-element.24.refs_0_), channel_id=1, source_target_pairs={{0,3},{1,0},{2,1},{3,2},{4,7},{5,4},{6,5},{7,6},{8,11},{9,8},{10,9... | collective-permute-start | bytes 1277960 | tf_op jit(solution)/shard_map/ppermute | solution.py:306
  7.9 1.9 %collective-permute-start.3 = (bf16[2,16,512]{2,1,0:T(8,128)(2,1)}, bf16[2,16,512]{2,1,0:T(8,128)(2,1)S(1)}, u32[]{:S(2)}, u32[]{:S(2)}) collective-permute-start(bf16[2,16,512]{2,1,0:T(8,128)(2,1)} %get-tuple-element.25), channel_id=1, source_target_pairs={{0,8},{8,16},{16,24},{1,9},{9,17},{17,25},{2,10},{10,18},{18,26},{... | collective-permute-start | bytes 98312 | tf_op jit(solution)/shard_map/ppermute | solution.py:346
  9.8 3.6 %collective-permute-start.4 = (bf16[2,16,512]{2,1,0:T(8,128)(2,1)}, bf16[2,16,512]{2,1,0:T(8,128)(2,1)S(1)}, u32[]{:S(2)}, u32[]{:S(2)}) collective-permute-start(bf16[2,16,512]{2,1,0:T(8,128)(2,1)} %get-tuple-element.27), channel_id=1, source_target_pairs={{8,0},{16,8},{24,16},{9,1},{17,9},{25,17},{10,2},{18,10},{26,18},{... | collective-permute-start | bytes 98312 | tf_op jit(solution)/shard_map/ppermute | solution.py:347
  13.5 0.3 collective-permute-done.3.before
  13.7 1.6 %collective-permute-done.4.after = bf16[2,16,512]{2,1,0:T(8,128)(2,1)S(1)} collective-permute-done((bf16[2,16,512]{2,1,0:T(8,128)(2,1)}, bf16[2,16,512]{2,1,0:T(8,128)(2,1)S(1)}, u32[]{:S(2)}, u32[]{:S(2)}) %collective-permute-start.4) | collective-permute-done | bytes 32800 | tf_op jit(solution)/shard_map/ppermute | solution.py:347
  15.3 1.2 %collective-permute-done.2.refs_3_.flip = bf16[416,512]{1,0:T(8,128)(2,1)S(1)} collective-permute-done((bf16[416,512]{1,0:T(8,128)(2,1)}, bf16[416,512]{1,0:T(8,128)(2,1)S(1)}, u32[]{:S(2)}, u32[]{:S(2)}) %collective-permute-start.2) | collective-permute-done | bytes 426016 | tf_op jit(solution)/shard_map/ppermute | solution.py:308
  16.5 0.9 %collective-permute-done.1.refs_2_.up = bf16[416,512]{1,0:T(8,128)(2,1)S(1)} collective-permute-done((bf16[416,512]{1,0:T(8,128)(2,1)}, bf16[416,512]{1,0:T(8,128)(2,1)S(1)}, u32[]{:S(2)}, u32[]{:S(2)}) %collective-permute-start.1) | collective-permute-done | bytes 426016 | tf_op jit(solution)/shard_map/ppermute | solution.py:307
  17.5 3.0 %collective-permute-start.6 = (bf16[416,512]{1,0:T(8,128)(2,1)S(1)}, bf16[416,512]{1,0:T(8,128)(2,1)S(1)}, u32[]{:S(2)}, u32[]{:S(2)}) collective-permute-start(bf16[416,512]{1,0:T(8,128)(2,1)S(1)} %get-tuple-element.29), channel_id=1, source_target_pairs={{0,3},{1,0},{2,1},{3,2},{4,7},{5,4},{6,5},{7,6},{8,11},{9,8},{10,9... | collective-permute-start | bytes 1277960 | tf_op jit(solution)/shard_map/ppermute | solution.py:321
  20.5 2.1 %collective-permute-start.7 = (bf16[416,512]{1,0:T(8,128)(2,1)S(1)}, bf16[416,512]{1,0:T(8,128)(2,1)S(1)}, u32[]{:S(2)}, u32[]{:S(2)}) collective-permute-start(bf16[416,512]{1,0:T(8,128)(2,1)S(1)} %get-tuple-element.30), channel_id=1, source_target_pairs={{0,4},{1,5},{2,6},{3,7},{4,0},{5,1},{6,2},{7,3},{8,12},{9,13},{10,... | collective-permute-start | bytes 1277960 | tf_op jit(solution)/shard_map/ppermute | solution.py:319
  22.7 5.5 %collective-permute-done.6.refs_5_ = bf16[416,512]{1,0:T(8,128)(2,1)S(1)} collective-permute-done((bf16[416,512]{1,0:T(8,128)(2,1)S(1)}, bf16[416,512]{1,0:T(8,128)(2,1)S(1)}, u32[]{:S(2)}, u32[]{:S(2)}) %collective-permute-start.6) | collective-permute-done | bytes 426016 | tf_op jit(solution)/shard_map/ppermute | solution.py:321
  28.2 3.8 %collective-permute-start.9 = (bf16[208,512]{1,0:T(8,128)(2,1)S(1)}, bf16[208,512]{1,0:T(8,128)(2,1)S(1)}, u32[]{:S(2)}, u32[]{:S(2)}) collective-permute-start(bf16[208,512]{1,0:T(8,128)(2,1)S(1)} %slice.9), channel_id=1, source_target_pairs={{0,3},{1,0},{2,1},{3,2},{4,7},{5,4},{6,5},{7,6},{8,11},{9,8},{10,9... | collective-permute-start | bytes 638984 | tf_op jit(solution)/shard_map/ppermute | solution.py:323
  32.1 0.8 %shard_map.75.swap = bf16[1024,1024]{1,0:T(8,128)(2,1)S(1)} custom-call(bf16[416,512]{1,0:T(8,128)(2,1)S(1)} %collective-permute-done.refs_1_.after.down), custom_call_target="tpu_custom_call" | custom-call | flops 20000000000 | bytes 4194304 | tf_op jit(solution)/shard_map/pallas_call | solution.py:349
  33.0 1.2 %slice-done.1 = s8[4194304]{0:T(1024)(128)(4,1)S(1)} async-done(((s8[8388608]{0:T(1024)(128)(4,1)}), s8[4194304]{0:T(1024)(128)(4,1)S(1)}, s32[]{:S(2)}) %slice-start.1) | async-done | bytes 4194328
  34.3 1.5 %shard_map.74.near = f32[128,1024]{1,0:T(8,128)S(1)} custom-call(bf16[2,512,4096]{2,1,0:T(8,128)(2,1)S(1)} %bitcast.3, bf16[416,512]{1,0:T(8,128)(2,1)S(1)} %copy-done, bf16[416,512]{1,0:T(8,128)(2,1)S(1)} %collective-permute-done.refs_1_.after.down, bf16[416,512]{1,0:T(8,128)(2,1)S(1)} %collective-permute-done.1.refs_2_.up, ...), custom_call_target="tpu_custom_call" | custom-call | flops 1000000000 | bytes 4194304 | tf_op jit(solution)/shard_map/pallas_call | solution.py:352
  35.8 3.4 %collective-permute-done.8.refs_7_ = bf16[208,512]{1,0:T(8,128)(2,1)S(1)} collective-permute-done((bf16[208,512]{1,0:T(8,128)(2,1)S(1)}, bf16[208,512]{1,0:T(8,128)(2,1)S(1)}, u32[]{:S(2)}, u32[]{:S(2)}) %collective-permute-start.8) | collective-permute-done | bytes 213024 | tf_op jit(solution)/shard_map/ppermute | solution.py:322
  39.2 3.1 %shard_map.77 = (f32[128,2048]{1,0:T(8,128)S(1)}, bf16[4,128,128]{2,1,0:T(8,128)(2,1)S(1)}, bf16[4,128,128]{2,1,0:T(8,128)(2,1)S(1)}, bf16[2,128,128]{2,1,0:T(8,...) custom-call(bf16[2,512,4096]{2,1,0:T(8,128)(2,1)S(1)} %bitcast.3, ...), custom_call_target="tpu_custom_call" | custom-call | flops 2000000000 | bytes 4194304 | tf_op jit(solution)/shard_map/pallas_call | solution.py:356
  42.3 9.8 %collective-permute-start.10 = (bf16[4,128,128]{2,1,0:T(8,128)(2,1)S(1)}, bf16[4,128,128]{2,1,0:T(8,128)(2,1)S(1)}, u32[]{:S(2)}, u32[]{:S(2)}) collective-permute-start(bf16[4,128,128]{2,1,0:T(8,128)(2,1)S(1)} %get-tuple-element.32), channel_id=1, source_target_pairs={{0,0},{1,1},{2,2},{3,3},{4,4},{5,5},{6,6},{7,7},{8,64},{9,65},{10,... | collective-permute-start | bytes 393224 | tf_op jit(solution)/shard_map/ppermute | solution.py:39
  52.1 1.1 %collective-permute-start.11 = (bf16[4,128,128]{2,1,0:T(8,128)(2,1)S(1)}, bf16[4,128,128]{2,1,0:T(8,128)(2,1)S(1)}, u32[]{:S(2)}, u32[]{:S(2)}) collective-permute-start(bf16[4,128,128]{2,1,0:T(8,128)(2,1)S(1)} %get-tuple-element.33), channel_id=1, source_target_pairs={{0,4},{1,5},{2,6},{3,7},{4,0},{5,1},{6,2},{7,3},{8,68},{9,69},{10,... | collective-permute-start | bytes 393224 | tf_op jit(solution)/shard_map/ppermute | solution.py:39
  53.2 1.4 %collective-permute-start.16 = (bf16[2,128,128]{2,1,0:T(8,128)(2,1)S(1)}, bf16[2,128,128]{2,1,0:T(8,128)(2,1)S(1)}, u32[]{:S(2)}, u32[]{:S(2)}) collective-permute-start(bf16[2,128,128]{2,1,0:T(8,128)(2,1)S(1)} %get-tuple-element.39), channel_id=1, source_target_pairs={{0,2},{1,3},{2,0},{3,1},{4,6},{5,7},{6,4},{7,5},{8,10},{9,11},{10,... | collective-permute-start | bytes 196616 | tf_op jit(solution)/shard_map/ppermute | solution.py:43
  54.5 1.9 %collective-permute-start.17 = (bf16[2,128,128]{2,1,0:T(8,128)(2,1)S(1)}, bf16[2,128,128]{2,1,0:T(8,128)(2,1)S(1)}, u32[]{:S(2)}, u32[]{:S(2)}) collective-permute-start(bf16[2,128,128]{2,1,0:T(8,128)(2,1)S(1)} %get-tuple-element.40), channel_id=1, source_target_pairs={{0,3},{1,0},{2,1},{3,2},{4,7},{5,4},{6,5},{7,6},{8,11},{9,8},{10,9... | collective-permute-start | bytes 196616 | tf_op jit(solution)/shard_map/ppermute | solution.py:43
  56.4 2.9 %collective-permute-done.15.first = bf16[2,128,128]{2,1,0:T(8,128)(2,1)S(1)} collective-permute-done((bf16[2,128,128]{2,1,0:T(8,128)(2,1)S(1)}, bf16[2,128,128]{2,1,0:T(8,128)(2,1)S(1)}, u32[]{:S(2)}, u32[]{:S(2)}) %collective-permute-start.15) | collective-permute-done | bytes 65568 | tf_op jit(solution)/shard_map/ppermute | solution.py:43
  59.4 0.9 %collective-permute-done.17.third = bf16[2,128,128]{2,1,0:T(8,128)(2,1)S(1)} collective-permute-done((bf16[2,128,128]{2,1,0:T(8,128)(2,1)S(1)}, bf16[2,128,128]{2,1,0:T(8,128)(2,1)S(1)}, u32[]{:S(2)}, u32[]{:S(2)}) %collective-permute-start.17) | collective-permute-done | bytes 65568 | tf_op jit(solution)/shard_map/ppermute | solution.py:43
  60.3 5.9 %collective-permute-start.18 = (bf16[4,128,128]{2,1,0:T(8,128)(2,1)S(1)}, bf16[4,128,128]{2,1,0:T(8,128)(2,1)S(1)}, u32[]{:S(2)}, u32[]{:S(2)}) collective-permute-start(bf16[4,128,128]{2,1,0:T(8,128)(2,1)S(1)} %get-tuple-element.41), channel_id=1, source_target_pairs={{0,32},{1,33},{2,34},{3,35},{4,36},{5,37},{6,38},{7,39},{8,96},{9,... | collective-permute-start | bytes 393224 | tf_op jit(solution)/shard_map/ppermute | solution.py:39
  66.1 1.0 %collective-permute-start.19 = (bf16[4,128,128]{2,1,0:T(8,128)(2,1)S(1)}, bf16[4,128,128]{2,1,0:T(8,128)(2,1)S(1)}, u32[]{:S(2)}, u32[]{:S(2)}) collective-permute-start(bf16[4,128,128]{2,1,0:T(8,128)(2,1)S(1)} %get-tuple-element.42), channel_id=1, source_target_pairs={{0,36},{1,37},{2,38},{3,39},{4,32},{5,33},{6,34},{7,35},{8,100},{9... | collective-permute-start | bytes 393224 | tf_op jit(solution)/shard_map/ppermute | solution.py:39
  67.1 1.4 %collective-permute-start.12 = (bf16[2,128,128]{2,1,0:T(8,128)(2,1)S(1)}, bf16[2,128,128]{2,1,0:T(8,128)(2,1)S(1)}, u32[]{:S(2)}, u32[]{:S(2)}) collective-permute-start(bf16[2,128,128]{2,1,0:T(8,128)(2,1)S(1)} %get-tuple-element.34), channel_id=1, source_target_pairs={{0,1},{1,2},{2,3},{3,0},{4,5},{5,6},{6,7},{7,4},{8,9},{9,10},{10,1... | collective-permute-start | bytes 196616 | tf_op jit(solution)/shard_map/ppermute | solution.py:43
  68.5 2.5 %collective-permute-start.13 = (bf16[2,128,128]{2,1,0:T(8,128)(2,1)S(1)}, bf16[2,128,128]{2,1,0:T(8,128)(2,1)S(1)}, u32[]{:S(2)}, u32[]{:S(2)}) collective-permute-start(bf16[2,128,128]{2,1,0:T(8,128)(2,1)S(1)} %get-tuple-element.35), channel_id=1, source_target_pairs={{0,2},{1,3},{2,0},{3,1},{4,6},{5,7},{6,4},{7,5},{8,10},{9,11},{10,... | collective-permute-start | bytes 196616 | tf_op jit(solution)/shard_map/ppermute | solution.py:43
  71.3 0.4 fusion.place
  71.7 4.5 %collective-permute-done.19.refs_6_ = bf16[4,128,128]{2,1,0:T(8,128)(2,1)S(1)} collective-permute-done((bf16[4,128,128]{2,1,0:T(8,128)(2,1)S(1)}, bf16[4,128,128]{2,1,0:T(8,128)(2,1)S(1)}, u32[]{:S(2)}, u32[]{:S(2)}) %collective-permute-start.19) | collective-permute-done | bytes 131104 | tf_op jit(solution)/shard_map/ppermute | solution.py:39
  76.2 3.3 %shard_map.80 = f32[8,16,8,512]{3,2,1,0:T(8,128)} custom-call(s32[2,2]{1,0:T(2,128)S(1)} %copy-done.2, s32[2,2]{1,0:T(2,128)S(1)} %copy-done.3, s32[8]{0:T(128)S(1)} %copy-done.4, f32[128,2048]{1,0:T(8,128)S(1)} %get-tuple-element.31.total, bf16[1024,1024]{1,0:T(8,128)(2,1)S(1)} %fusion.place, bf16[4,128,128]{2,1,0:T(8,128)(2,1)S(1)} %collective-permute-done.10.same.refs_0_, ...), custom_call_target="tpu_custom_call" | custom-call | flops 1000000000 | bytes 4194304 | tf_op jit(solution)/shard_map/pallas_call | solution.py:371
  (36 shorter events, 0.6 us)
Async XLA Ops:
  3.2 13.4 %collective-permute-start.2 = (bf16[416,512]{1,0:T(8,128)(2,1)}, bf16[416,512]{1,0:T(8,128)(2,1)S(1)}, u32[]{:S(2)}, u32[]{:S(2)}) collective-permute-start(bf16[416,512]{1,0:T(8,128)(2,1)} %get-tuple-element.24.refs_0_), channel_id=1, source_target_pairs={{0,4},{1,5},{2,6},{3,7},{4,0},{5,1},{6,2},{7,3},{8,12},{9,13},{10,... | collective-permute-start | bytes 1277960 | tf_op jit(solution)/shard_map/ppermute | solution.py:308
  4.7 12.8 %collective-permute-start.1 = (bf16[416,512]{1,0:T(8,128)(2,1)}, bf16[416,512]{1,0:T(8,128)(2,1)S(1)}, u32[]{:S(2)}, u32[]{:S(2)}) collective-permute-start(bf16[416,512]{1,0:T(8,128)(2,1)} %get-tuple-element.24.refs_0_), channel_id=1, source_target_pairs={{0,1},{1,2},{2,3},{3,0},{4,5},{5,6},{6,7},{7,4},{8,9},{9,10},{10,1... | collective-permute-start | bytes 1277960 | tf_op jit(solution)/shard_map/ppermute | solution.py:307
  6.2 11.2 %collective-permute-start = (bf16[416,512]{1,0:T(8,128)(2,1)}, bf16[416,512]{1,0:T(8,128)(2,1)S(1)}, u32[]{:S(2)}, u32[]{:S(2)}) collective-permute-start(bf16[416,512]{1,0:T(8,128)(2,1)} %get-tuple-element.24.refs_0_), channel_id=1, source_target_pairs={{0,3},{1,0},{2,1},{3,2},{4,7},{5,4},{6,5},{7,6},{8,11},{9,8},{10,9... | collective-permute-start | bytes 1277960 | tf_op jit(solution)/shard_map/ppermute | solution.py:306
  7.9 5.8 %collective-permute-start.3 = (bf16[2,16,512]{2,1,0:T(8,128)(2,1)}, bf16[2,16,512]{2,1,0:T(8,128)(2,1)S(1)}, u32[]{:S(2)}, u32[]{:S(2)}) collective-permute-start(bf16[2,16,512]{2,1,0:T(8,128)(2,1)} %get-tuple-element.25), channel_id=1, source_target_pairs={{0,8},{8,16},{16,24},{1,9},{9,17},{17,25},{2,10},{10,18},{18,26},{... | collective-permute-start | bytes 98312 | tf_op jit(solution)/shard_map/ppermute | solution.py:346
  9.8 5.5 %collective-permute-start.4 = (bf16[2,16,512]{2,1,0:T(8,128)(2,1)}, bf16[2,16,512]{2,1,0:T(8,128)(2,1)S(1)}, u32[]{:S(2)}, u32[]{:S(2)}) collective-permute-start(bf16[2,16,512]{2,1,0:T(8,128)(2,1)} %get-tuple-element.27), channel_id=1, source_target_pairs={{8,0},{16,8},{24,16},{9,1},{17,9},{25,17},{10,2},{18,10},{26,18},{... | collective-permute-start | bytes 98312 | tf_op jit(solution)/shard_map/ppermute | solution.py:347
  17.5 10.6 %collective-permute-start.6 = (bf16[416,512]{1,0:T(8,128)(2,1)S(1)}, bf16[416,512]{1,0:T(8,128)(2,1)S(1)}, u32[]{:S(2)}, u32[]{:S(2)}) collective-permute-start(bf16[416,512]{1,0:T(8,128)(2,1)S(1)} %get-tuple-element.29), channel_id=1, source_target_pairs={{0,3},{1,0},{2,1},{3,2},{4,7},{5,4},{6,5},{7,6},{8,11},{9,8},{10,9... | collective-permute-start | bytes 1277960 | tf_op jit(solution)/shard_map/ppermute | solution.py:321
  20.5 11.4 %collective-permute-start.7 = (bf16[416,512]{1,0:T(8,128)(2,1)S(1)}, bf16[416,512]{1,0:T(8,128)(2,1)S(1)}, u32[]{:S(2)}, u32[]{:S(2)}) collective-permute-start(bf16[416,512]{1,0:T(8,128)(2,1)S(1)} %get-tuple-element.30), channel_id=1, source_target_pairs={{0,4},{1,5},{2,6},{3,7},{4,0},{5,1},{6,2},{7,3},{8,12},{9,13},{10,... | collective-permute-start | bytes 1277960 | tf_op jit(solution)/shard_map/ppermute | solution.py:319
  22.7 13.1 %collective-permute-start.5 = (bf16[416,512]{1,0:T(8,128)(2,1)S(1)}, bf16[416,512]{1,0:T(8,128)(2,1)S(1)}, u32[]{:S(2)}, u32[]{:S(2)}) collective-permute-start(bf16[416,512]{1,0:T(8,128)(2,1)S(1)} %get-tuple-element.28), channel_id=1, source_target_pairs={{0,1},{1,2},{2,3},{3,0},{4,5},{5,6},{6,7},{7,4},{8,9},{9,10},{10,1... | collective-permute-start | bytes 1277960 | tf_op jit(solution)/shard_map/ppermute | solution.py:320
  28.2 4.8 %slice-start = ((s8[8388608]{0:T(1024)(128)(4,1)}), s8[4194304]{0:T(1024)(128)(4,1)S(1)}, s32[]{:S(2)}) async-start(s8[8388608]{0:T(1024)(128)(4,1)} %bitcast.2), calls=%async_computation | async-start | bytes 8388608
  28.2 7.6 %collective-permute-start.9 = (bf16[208,512]{1,0:T(8,128)(2,1)S(1)}, bf16[208,512]{1,0:T(8,128)(2,1)S(1)}, u32[]{:S(2)}, u32[]{:S(2)}) collective-permute-start(bf16[208,512]{1,0:T(8,128)(2,1)S(1)} %slice.9), channel_id=1, source_target_pairs={{0,3},{1,0},{2,1},{3,2},{4,7},{5,4},{6,5},{7,6},{8,11},{9,8},{10,9... | collective-permute-start | bytes 638984 | tf_op jit(solution)/shard_map/ppermute | solution.py:323
  32.0 2.2 %slice-start.1 = ((s8[8388608]{0:T(1024)(128)(4,1)}), s8[4194304]{0:T(1024)(128)(4,1)S(1)}, s32[]{:S(2)}) async-start(s8[8388608]{0:T(1024)(128)(4,1)} %bitcast.2), calls=%async_computation.1 | async-start | bytes 8388608
  32.0 2.3 %copy-start = (bf16[416,512]{1,0:T(8,128)(2,1)S(1)}, bf16[416,512]{1,0:T(8,128)(2,1)}, u32[]{:S(2)}) copy-start(bf16[416,512]{1,0:T(8,128)(2,1)} %get-tuple-element.24.refs_0_) | copy-start | bytes 1277956
  32.0 7.1 %collective-permute-start.8 = (bf16[208,512]{1,0:T(8,128)(2,1)S(1)}, bf16[208,512]{1,0:T(8,128)(2,1)S(1)}, u32[]{:S(2)}, u32[]{:S(2)}) collective-permute-start(bf16[208,512]{1,0:T(8,128)(2,1)S(1)} %slice.8), channel_id=1, source_target_pairs={{0,1},{1,2},{2,3},{3,0},{4,5},{5,6},{6,7},{7,4},{8,9},{9,10},{10,1... | collective-permute-start | bytes 638984 | tf_op jit(solution)/shard_map/ppermute | solution.py:322
  34.3 4.9 %copy-start.1 = (bf16[16,16,512]{2,1,0:T(8,128)(2,1)S(1)}, bf16[16,16,512]{2,1,0:T(8,128)(2,1)}, u32[]{:S(2)}) copy-start(bf16[16,16,512]{2,1,0:T(8,128)(2,1)} %get-tuple-element.26.inner) | copy-start | bytes 786436
  39.2 32.1 %copy-start.5 = (s32[1024]{0:T(1024)S(1)}, s32[1024]{0:T(1024)}, u32[]{:S(2)}) copy-start(s32[1024]{0:T(1024)} %constant.2.clone) | copy-start | bytes 12292
  42.3 33.9 %copy-start.2 = (s32[2,2]{1,0:T(2,128)S(1)}, s32[2,2]{1,0:T(2,128)}, u32[]{:S(2)}) copy-start(s32[2,2]{1,0:T(2,128)} %ladder_tiles.1) | copy-start | bytes 52
  42.3 33.9 %copy-start.3 = (s32[2,2]{1,0:T(2,128)S(1)}, s32[2,2]{1,0:T(2,128)}, u32[]{:S(2)}) copy-start(s32[2,2]{1,0:T(2,128)} %cycle_tiles.1) | copy-start | bytes 52
  42.3 33.9 %copy-start.4 = (s32[8]{0:T(128)S(1)}, s32[8]{0:T(128)}, u32[]{:S(2)}) copy-start(s32[8]{0:T(128)} %partner.1) | copy-start | bytes 100
  42.3 24.8 %collective-permute-start.10 = (bf16[4,128,128]{2,1,0:T(8,128)(2,1)S(1)}, bf16[4,128,128]{2,1,0:T(8,128)(2,1)S(1)}, u32[]{:S(2)}, u32[]{:S(2)}) collective-permute-start(bf16[4,128,128]{2,1,0:T(8,128)(2,1)S(1)} %get-tuple-element.32), channel_id=1, source_target_pairs={{0,0},{1,1},{2,2},{3,3},{4,4},{5,5},{6,6},{7,7},{8,64},{9,65},{10,... | collective-permute-start | bytes 393224 | tf_op jit(solution)/shard_map/ppermute | solution.py:39
  52.1 14.9 %collective-permute-start.11 = (bf16[4,128,128]{2,1,0:T(8,128)(2,1)S(1)}, bf16[4,128,128]{2,1,0:T(8,128)(2,1)S(1)}, u32[]{:S(2)}, u32[]{:S(2)}) collective-permute-start(bf16[4,128,128]{2,1,0:T(8,128)(2,1)S(1)} %get-tuple-element.33), channel_id=1, source_target_pairs={{0,4},{1,5},{2,6},{3,7},{4,0},{5,1},{6,2},{7,3},{8,68},{9,69},{10,... | collective-permute-start | bytes 393224 | tf_op jit(solution)/shard_map/ppermute | solution.py:39
  53.2 6.2 %collective-permute-start.15 = (bf16[2,128,128]{2,1,0:T(8,128)(2,1)S(1)}, bf16[2,128,128]{2,1,0:T(8,128)(2,1)S(1)}, u32[]{:S(2)}, u32[]{:S(2)}) collective-permute-start(bf16[2,128,128]{2,1,0:T(8,128)(2,1)S(1)} %get-tuple-element.38), channel_id=1, source_target_pairs={{0,1},{1,2},{2,3},{3,0},{4,5},{5,6},{6,7},{7,4},{8,9},{9,10},{10,1... | collective-permute-start | bytes 196616 | tf_op jit(solution)/shard_map/ppermute | solution.py:43
  53.2 6.2 %collective-permute-start.16 = (bf16[2,128,128]{2,1,0:T(8,128)(2,1)S(1)}, bf16[2,128,128]{2,1,0:T(8,128)(2,1)S(1)}, u32[]{:S(2)}, u32[]{:S(2)}) collective-permute-start(bf16[2,128,128]{2,1,0:T(8,128)(2,1)S(1)} %get-tuple-element.39), channel_id=1, source_target_pairs={{0,2},{1,3},{2,0},{3,1},{4,6},{5,7},{6,4},{7,5},{8,10},{9,11},{10,... | collective-permute-start | bytes 196616 | tf_op jit(solution)/shard_map/ppermute | solution.py:43
  54.5 5.7 %collective-permute-start.17 = (bf16[2,128,128]{2,1,0:T(8,128)(2,1)S(1)}, bf16[2,128,128]{2,1,0:T(8,128)(2,1)S(1)}, u32[]{:S(2)}, u32[]{:S(2)}) collective-permute-start(bf16[2,128,128]{2,1,0:T(8,128)(2,1)S(1)} %get-tuple-element.40), channel_id=1, source_target_pairs={{0,3},{1,0},{2,1},{3,2},{4,7},{5,4},{6,5},{7,6},{8,11},{9,8},{10,9... | collective-permute-start | bytes 196616 | tf_op jit(solution)/shard_map/ppermute | solution.py:43
  60.3 11.4 %collective-permute-start.18 = (bf16[4,128,128]{2,1,0:T(8,128)(2,1)S(1)}, bf16[4,128,128]{2,1,0:T(8,128)(2,1)S(1)}, u32[]{:S(2)}, u32[]{:S(2)}) collective-permute-start(bf16[4,128,128]{2,1,0:T(8,128)(2,1)S(1)} %get-tuple-element.41), channel_id=1, source_target_pairs={{0,32},{1,33},{2,34},{3,35},{4,36},{5,37},{6,38},{7,39},{8,96},{9,... | collective-permute-start | bytes 393224 | tf_op jit(solution)/shard_map/ppermute | solution.py:39
  66.1 10.1 %collective-permute-start.19 = (bf16[4,128,128]{2,1,0:T(8,128)(2,1)S(1)}, bf16[4,128,128]{2,1,0:T(8,128)(2,1)S(1)}, u32[]{:S(2)}, u32[]{:S(2)}) collective-permute-start(bf16[4,128,128]{2,1,0:T(8,128)(2,1)S(1)} %get-tuple-element.42), channel_id=1, source_target_pairs={{0,36},{1,37},{2,38},{3,39},{4,32},{5,33},{6,34},{7,35},{8,100},{9... | collective-permute-start | bytes 393224 | tf_op jit(solution)/shard_map/ppermute | solution.py:39
  67.1 9.1 %collective-permute-start.12 = (bf16[2,128,128]{2,1,0:T(8,128)(2,1)S(1)}, bf16[2,128,128]{2,1,0:T(8,128)(2,1)S(1)}, u32[]{:S(2)}, u32[]{:S(2)}) collective-permute-start(bf16[2,128,128]{2,1,0:T(8,128)(2,1)S(1)} %get-tuple-element.34), channel_id=1, source_target_pairs={{0,1},{1,2},{2,3},{3,0},{4,5},{5,6},{6,7},{7,4},{8,9},{9,10},{10,1... | collective-permute-start | bytes 196616 | tf_op jit(solution)/shard_map/ppermute | solution.py:43
  68.5 7.7 %collective-permute-start.13 = (bf16[2,128,128]{2,1,0:T(8,128)(2,1)S(1)}, bf16[2,128,128]{2,1,0:T(8,128)(2,1)S(1)}, u32[]{:S(2)}, u32[]{:S(2)}) collective-permute-start(bf16[2,128,128]{2,1,0:T(8,128)(2,1)S(1)} %get-tuple-element.35), channel_id=1, source_target_pairs={{0,2},{1,3},{2,0},{3,1},{4,6},{5,7},{6,4},{7,5},{8,10},{9,11},{10,... | collective-permute-start | bytes 196616 | tf_op jit(solution)/shard_map/ppermute | solution.py:43
  71.0 5.2 %collective-permute-start.14 = (bf16[2,128,128]{2,1,0:T(8,128)(2,1)S(1)}, bf16[2,128,128]{2,1,0:T(8,128)(2,1)S(1)}, u32[]{:S(2)}, u32[]{:S(2)}) collective-permute-start(bf16[2,128,128]{2,1,0:T(8,128)(2,1)S(1)} %get-tuple-element.36), channel_id=1, source_target_pairs={{0,3},{1,0},{2,1},{3,2},{4,7},{5,4},{6,5},{7,6},{8,11},{9,8},{10,9... | collective-permute-start | bytes 196616 | tf_op jit(solution)/shard_map/ppermute | solution.py:43

commit v10 on v9

--- a/solution.py
+++ b/solution.py
@@ -35,6 +35,28 @@
     ]
 
 
+def crosses(device):
+    p, q = device // 32, (device // 8) % 4
+    return p // 4 != q // 2
+
+
+def direct_moves(k, dx):
+    return [(a, b) for a, b in pair_moves(k, dx) if not crosses(a)]
+
+
+def relay_moves(k, dx):
+    over, along = [], []
+    for a, b in pair_moves(k, dx):
+        if crosses(a):
+            over.append((a, a ^ 16))
+            along.append((a ^ 16, b))
+    return over, along
+
+
+def along_moves(block, moves):
+    return lax.ppermute(block, ("pi", "pj", "vert"), moves)
+
+
 def to_transposed(block, k, dx):
     return lax.ppermute(block, ("pi", "pj", "vert"), pair_moves(k, dx))
 
@@ -54,10 +76,14 @@
     return found
 
 
-def split_kernel(same, other, first, second, third):
+def crossed():
+    return lax.axis_index("pi") // 4 != lax.axis_index("pj") // 2
+
+
+def split_kernel(same, direct, relayed, first, second, third):
     for dy, ref in enumerate((first, second, third), 1):
         ref[0] = same[dy]
-        ref[1] = other[dy]
+        ref[1] = jnp.where(crossed(), relayed[dy], direct[dy])
 
 
 def join_kernel(own, first, second, third, same, other):
@@ -248,12 +274,18 @@
 
 
 def finish_kernel(ladder_tiles, cycle_tiles, partner, total, place, *refs):
-    arrived, (out_ref, mirrored, wide, held, sems) = refs[:7], refs[7:]
+    arrived, (out_ref, mirrored, wide, held, sems) = refs[:8], refs[8:]
     parity = lax.axis_index("pi") % 2
+    same, direct, relayed = arrived[:3]
     for dx, dy, start in peers(-1):
-        early = arrived[dx][0] if dy == 0 else arrived[1 + dy][dx]
+        if dy > 0:
+            early = arrived[2 + dy][dx]
+        elif dx == 0:
+            early = same[0]
+        else:
+            early = jnp.where(crossed(), relayed[0], direct[0])
         wide[:128, pl.ds(start, 128)] = early
-        wide[128:, pl.ds(start, 128)] = arrived[5 + dx][dy]
+        wide[128:, pl.ds(start, 128)] = arrived[6 + dx][dy]
     moved = jnp.dot(wide[...], place[...], preferred_element_type=F32)
     for k in range(2):
         for s in range(2):
@@ -362,15 +394,19 @@
         12,
         2 * 10**9,
     )(ladder_ints, begun, before, inner, after, swap, *near, *far)
-    same, other = to_transposed(same, 0, 0), to_transposed(other, 0, 1)
+    over, along = relay_moves(0, 1)
+    relayed = along_moves(along_moves(other, over), along)
+    same, other = to_transposed(same, 0, 0), along_moves(other, direct_moves(0, 1))
     late = [along_y(block, dy) for dy, block in ((1, late_1), (2, late_2), (3, late_3))]
     joined = call(join_kernel, [VMEM] * 4, [four] * 2, [VMEM] * 2, [], 4, 10**7)(late_0, *late)
     joined = [to_transposed(block, 1, dx) for dx, block in enumerate(joined)]
-    early = call(split_kernel, [VMEM] * 2, [two] * 3, [VMEM] * 3, [], 4, 10**7)(same, other)
+    early = call(split_kernel, [VMEM] * 3, [two] * 3, [VMEM] * 3, [], 4, 10**7)(
+        same, other, relayed
+    )
     early = [along_y(block, dy) for dy, block in enumerate(early, 1)]
     return call(
         finish_kernel,
-        [SMEM, SMEM, SMEM] + [VMEM] * 9,
+        [SMEM, SMEM, SMEM] + [VMEM] * 10,
         shape((8, 16, 8, LANES), F32),
         HBM,
         [
@@ -381,7 +417,7 @@
         ],
         12,
         10**9,
-    )(ladder_tiles, cycle_tiles, partner, total, place_matrix(), same, other, *early, *joined)
+    )(ladder_tiles, cycle_tiles, partner, total, place_matrix(), same, other, relayed, *early, *joined)
 
 
 def solution(mesh):

time: 79.8 us -> 85.3 us (1.069)
  the two profiles are of different devices: /device:TPU:6 before, /device:TPU:1 now
where the time goes in v10:
time: 85.3 us; the launch traced here: 85.1 us
  starting transfers between devices  49.8 us (58%)
  waiting for transfers between devices  21.1 us (25%)
  Pallas kernels  12 us (14%)
  local copies, waits for them, and re-layouts  1.38 us (2%)
    ppermute x3, starting transfers between devices, along_moves(): return lax.ppermute(block, ('pi', 'pj', 'vert'), moves)  17 us
    ppermute x6, starting transfers between devices, along_y(): lax.ppermute(block, 'vert', vert_moves(lambda h, y: h * 4 + (y + dy) % 4))  7 us
    ppermute x3, starting transfers between devices, to_transposed(): return lax.ppermute(block, ('pi', 'pj', 'vert'), pair_moves(k, dx))  6.96 us
    ppermute x3, waiting for transfers between devices, to_transposed(): return lax.ppermute(block, ('pi', 'pj', 'vert'), pair_moves(k, dx))  5.94 us
    ppermute x1, waiting for transfers between devices, gather(): down_2 = lax.ppermute(to_down, 'vert', DOWN)  5.93 us
    ppermute x1, starting transfers between devices, gather(): flip = lax.ppermute(own, 'vert', FLIP)  3.66 us
    ppermute x1, starting transfers between devices, body(): before = lax.ppermute(last, 'pj', [(q, q + 1) for q in range(3)])  3.55 us
    pallas_call x1, Pallas kernels, body(): call(finish_kernel, [SMEM, SMEM, SMEM] + [VMEM] * 10, shape((8, 16, 8, LA...  3.31 us
  transfers between devices with their start and end apart: 22, of which 7 were waited for; matrix products, arithmetic and copies ran while one was open for 1% of the time, Pallas kernels for 3%

profile of v10, /device:TPU:1, one launch (start us, length us, event | category | flops | bytes accessed | tf_op | source)
XLA Modules:
  0.0 85.1 jit_solution(3042746714591804098)
XLA Ops:
  0.0 3.2 %shard_map.73 = (bf16[416,512]{1,0:T(8,128)(2,1)}, bf16[16,16,512]{2,1,0:T(8,128)(2,1)}, bf16[2,16,512]{2,1,0:T(8,128)(2,1)}, bf16[2,16,512]{2,1,0:T(8,128)(2,1)}) custom-call(s32[2,2]{1,0:T(2,128)} %ladder_tiles.1, s32[2,2]{1,0:T(2,128)} %cycle_tiles.1, bf16[1024,512]{1,0:T(8,128)(2,1)} %bitcast.4, bf16[80,2,512]{2,1,0:T(2,128)(2,1)} %bitcast.5), custom_call_target="tpu_custom_call" | custom-call | flops 1000000000 | bytes 4194304 | tf_op jit(solution)/shard_map/pallas_call | solution.py:361
  3.2 3.7 %collective-permute-start.2 = (bf16[416,512]{1,0:T(8,128)(2,1)}, bf16[416,512]{1,0:T(8,128)(2,1)S(1)}, u32[]{:S(2)}, u32[]{:S(2)}) collective-permute-start(bf16[416,512]{1,0:T(8,128)(2,1)} %get-tuple-element.24.refs_0_), channel_id=1, source_target_pairs={{0,4},{1,5},{2,6},{3,7},{4,0},{5,1},{6,2},{7,3},{8,12},{9,13},{10,... | collective-permute-start | bytes 1277960 | tf_op jit(solution)/shard_map/ppermute | solution.py:340
  6.8 1.3 %collective-permute-start.1 = (bf16[416,512]{1,0:T(8,128)(2,1)}, bf16[416,512]{1,0:T(8,128)(2,1)S(1)}, u32[]{:S(2)}, u32[]{:S(2)}) collective-permute-start(bf16[416,512]{1,0:T(8,128)(2,1)} %get-tuple-element.24.refs_0_), channel_id=1, source_target_pairs={{0,1},{1,2},{2,3},{3,0},{4,5},{5,6},{6,7},{7,4},{8,9},{9,10},{10,1... | collective-permute-start | bytes 1277960 | tf_op jit(solution)/shard_map/ppermute | solution.py:339
  8.1 1.4 %collective-permute-start = (bf16[416,512]{1,0:T(8,128)(2,1)}, bf16[416,512]{1,0:T(8,128)(2,1)S(1)}, u32[]{:S(2)}, u32[]{:S(2)}) collective-permute-start(bf16[416,512]{1,0:T(8,128)(2,1)} %get-tuple-element.24.refs_0_), channel_id=1, source_target_pairs={{0,3},{1,0},{2,1},{3,2},{4,7},{5,4},{6,5},{7,6},{8,11},{9,8},{10,9... | collective-permute-start | bytes 1277960 | tf_op jit(solution)/shard_map/ppermute | solution.py:338
  9.6 3.5 %collective-permute-start.3 = (bf16[2,16,512]{2,1,0:T(8,128)(2,1)}, bf16[2,16,512]{2,1,0:T(8,128)(2,1)S(1)}, u32[]{:S(2)}, u32[]{:S(2)}) collective-permute-start(bf16[2,16,512]{2,1,0:T(8,128)(2,1)} %get-tuple-element.25), channel_id=1, source_target_pairs={{0,8},{8,16},{16,24},{1,9},{9,17},{17,25},{2,10},{10,18},{18,26},{... | collective-permute-start | bytes 98312 | tf_op jit(solution)/shard_map/ppermute | solution.py:378
  13.1 1.9 %collective-permute-start.4 = (bf16[2,16,512]{2,1,0:T(8,128)(2,1)}, bf16[2,16,512]{2,1,0:T(8,128)(2,1)S(1)}, u32[]{:S(2)}, u32[]{:S(2)}) collective-permute-start(bf16[2,16,512]{2,1,0:T(8,128)(2,1)} %get-tuple-element.27), channel_id=1, source_target_pairs={{8,0},{16,8},{24,16},{9,1},{17,9},{25,17},{10,2},{18,10},{26,18},{... | collective-permute-start | bytes 98312 | tf_op jit(solution)/shard_map/ppermute | solution.py:379
  15.0 1.3 %collective-permute-done.3.before = bf16[2,16,512]{2,1,0:T(8,128)(2,1)S(1)} collective-permute-done((bf16[2,16,512]{2,1,0:T(8,128)(2,1)}, bf16[2,16,512]{2,1,0:T(8,128)(2,1)S(1)}, u32[]{:S(2)}, u32[]{:S(2)}) %collective-permute-start.3) | collective-permute-done | bytes 32800 | tf_op jit(solution)/shard_map/ppermute | solution.py:378
  16.3 2.5 %collective-permute-done.4.after = bf16[2,16,512]{2,1,0:T(8,128)(2,1)S(1)} collective-permute-done((bf16[2,16,512]{2,1,0:T(8,128)(2,1)}, bf16[2,16,512]{2,1,0:T(8,128)(2,1)S(1)}, u32[]{:S(2)}, u32[]{:S(2)}) %collective-permute-start.4) | collective-permute-done | bytes 32800 | tf_op jit(solution)/shard_map/ppermute | solution.py:379
  19.0 2.3 %collective-permute-start.6 = (bf16[416,512]{1,0:T(8,128)(2,1)S(1)}, bf16[416,512]{1,0:T(8,128)(2,1)S(1)}, u32[]{:S(2)}, u32[]{:S(2)}) collective-permute-start(bf16[416,512]{1,0:T(8,128)(2,1)S(1)} %get-tuple-element.29), channel_id=1, source_target_pairs={{0,3},{1,0},{2,1},{3,2},{4,7},{5,4},{6,5},{7,6},{8,11},{9,8},{10,9... | collective-permute-start | bytes 1277960 | tf_op jit(solution)/shard_map/ppermute | solution.py:353
  21.3 1.4 %collective-permute-start.7 = (bf16[416,512]{1,0:T(8,128)(2,1)S(1)}, bf16[416,512]{1,0:T(8,128)(2,1)S(1)}, u32[]{:S(2)}, u32[]{:S(2)}) collective-permute-start(bf16[416,512]{1,0:T(8,128)(2,1)S(1)} %get-tuple-element.30), channel_id=1, source_target_pairs={{0,4},{1,5},{2,6},{3,7},{4,0},{5,1},{6,2},{7,3},{8,12},{9,13},{10,... | collective-permute-start | bytes 1277960 | tf_op jit(solution)/shard_map/ppermute | solution.py:351
  22.7 5.9 %collective-permute-done.6.refs_5_ = bf16[416,512]{1,0:T(8,128)(2,1)S(1)} collective-permute-done((bf16[416,512]{1,0:T(8,128)(2,1)S(1)}, bf16[416,512]{1,0:T(8,128)(2,1)S(1)}, u32[]{:S(2)}, u32[]{:S(2)}) %collective-permute-start.6) | collective-permute-done | bytes 426016 | tf_op jit(solution)/shard_map/ppermute | solution.py:353
  28.7 3.1 %collective-permute-start.9 = (bf16[208,512]{1,0:T(8,128)(2,1)S(1)}, bf16[208,512]{1,0:T(8,128)(2,1)S(1)}, u32[]{:S(2)}, u32[]{:S(2)}) collective-permute-start(bf16[208,512]{1,0:T(8,128)(2,1)S(1)} %slice.9), channel_id=1, source_target_pairs={{0,3},{1,0},{2,1},{3,2},{4,7},{5,4},{6,5},{7,6},{8,11},{9,8},{10,9... | collective-permute-start | bytes 638984 | tf_op jit(solution)/shard_map/ppermute | solution.py:355
  31.9 0.8 shard_map.75.swap
  32.8 1.2 %slice-done.1 = s8[4194304]{0:T(1024)(128)(4,1)S(1)} async-done(((s8[8388608]{0:T(1024)(128)(4,1)}), s8[4194304]{0:T(1024)(128)(4,1)S(1)}, s32[]{:S(2)}) %slice-start.1) | async-done | bytes 4194328
  34.1 1.5 %shard_map.74.near = f32[128,1024]{1,0:T(8,128)S(1)} custom-call(bf16[2,512,4096]{2,1,0:T(8,128)(2,1)S(1)} %bitcast.3, bf16[416,512]{1,0:T(8,128)(2,1)S(1)} %copy-done, bf16[416,512]{1,0:T(8,128)(2,1)S(1)} %collective-permute-done.refs_1_.after.down, bf16[416,512]{1,0:T(8,128)(2,1)S(1)} %collective-permute-done.1.refs_2_.up, ...), custom_call_target="tpu_custom_call" | custom-call | flops 1000000000 | bytes 4194304 | tf_op jit(solution)/shard_map/pallas_call | solution.py:384
  35.6 2.2 %collective-permute-done.8.refs_7_ = bf16[208,512]{1,0:T(8,128)(2,1)S(1)} collective-permute-done((bf16[208,512]{1,0:T(8,128)(2,1)S(1)}, bf16[208,512]{1,0:T(8,128)(2,1)S(1)}, u32[]{:S(2)}, u32[]{:S(2)}) %collective-permute-start.8) | collective-permute-done | bytes 213024 | tf_op jit(solution)/shard_map/ppermute | solution.py:354
  37.8 3.1 %shard_map.77 = (f32[128,2048]{1,0:T(8,128)S(1)}, bf16[4,128,128]{2,1,0:T(8,128)(2,1)S(1)}, bf16[4,128,128]{2,1,0:T(8,128)(2,1)S(1)}, bf16[2,128,128]{2,1,0:T(8,...) custom-call(bf16[2,512,4096]{2,1,0:T(8,128)(2,1)S(1)} %bitcast.3, ...), custom_call_target="tpu_custom_call" | custom-call | flops 2000000000 | bytes 4194304 | tf_op jit(solution)/shard_map/pallas_call | solution.py:388
  41.0 1.4 %collective-permute-start.12 = (bf16[4,128,128]{2,1,0:T(8,128)(2,1)S(1)}, bf16[4,128,128]{2,1,0:T(8,128)(2,1)S(1)}, u32[]{:S(2)}, u32[]{:S(2)}) collective-permute-start(bf16[4,128,128]{2,1,0:T(8,128)(2,1)S(1)} %get-tuple-element.33), channel_id=1, source_target_pairs={{16,0},{17,1},{18,2},{19,3},{20,4},{21,5},{22,6},{23,7},{24,8},{25... | collective-permute-start | bytes 393224 | tf_op jit(solution)/shard_map/ppermute | solution.py:57
  42.5 10.4 %collective-permute-start.11 = (bf16[4,128,128]{2,1,0:T(8,128)(2,1)S(1)}, bf16[4,128,128]{2,1,0:T(8,128)(2,1)S(1)}, u32[]{:S(2)}, u32[]{:S(2)}) collective-permute-start(bf16[4,128,128]{2,1,0:T(8,128)(2,1)S(1)} %get-tuple-element.33), channel_id=1, source_target_pairs={{0,4},{1,5},{2,6},{3,7},{4,0},{5,1},{6,2},{7,3},{8,68},{9,69},{10,... | collective-permute-start | bytes 393224 | tf_op jit(solution)/shard_map/ppermute | solution.py:57
  52.9 1.9 %collective-permute-start.10 = (bf16[4,128,128]{2,1,0:T(8,128)(2,1)S(1)}, bf16[4,128,128]{2,1,0:T(8,128)(2,1)S(1)}, u32[]{:S(2)}, u32[]{:S(2)}) collective-permute-start(bf16[4,128,128]{2,1,0:T(8,128)(2,1)S(1)} %get-tuple-element.32), channel_id=1, source_target_pairs={{0,0},{1,1},{2,2},{3,3},{4,4},{5,5},{6,6},{7,7},{8,64},{9,65},{10,... | collective-permute-start | bytes 393224 | tf_op jit(solution)/shard_map/ppermute | solution.py:61
  54.8 5.2 %collective-permute-start.13 = (bf16[4,128,128]{2,1,0:T(8,128)(2,1)S(1)}, bf16[4,128,128]{2,1,0:T(8,128)(2,1)S(1)}, u32[]{:S(2)}, u32[]{:S(2)}) collective-permute-start(bf16[4,128,128]{2,1,0:T(8,128)(2,1)S(1)} %collective-permute-done.12), channel_id=1, source_target_pairs={{0,132},{1,133},{2,134},{3,135},{4,128},{5,129},{6,130},{7,131},{8... | collective-permute-start | bytes 393224 | tf_op jit(solution)/shard_map/ppermute | solution.py:57
  60.1 1.3 %collective-permute-start.18 = (bf16[2,128,128]{2,1,0:T(8,128)(2,1)S(1)}, bf16[2,128,128]{2,1,0:T(8,128)(2,1)S(1)}, u32[]{:S(2)}, u32[]{:S(2)}) collective-permute-start(bf16[2,128,128]{2,1,0:T(8,128)(2,1)S(1)} %get-tuple-element.39), channel_id=1, source_target_pairs={{0,2},{1,3},{2,0},{3,1},{4,6},{5,7},{6,4},{7,5},{8,10},{9,11},{10,... | collective-permute-start | bytes 196616 | tf_op jit(solution)/shard_map/ppermute | solution.py:65
  61.4 2.0 %collective-permute-start.19 = (bf16[2,128,128]{2,1,0:T(8,128)(2,1)S(1)}, bf16[2,128,128]{2,1,0:T(8,128)(2,1)S(1)}, u32[]{:S(2)}, u32[]{:S(2)}) collective-permute-start(bf16[2,128,128]{2,1,0:T(8,128)(2,1)S(1)} %get-tuple-element.40), channel_id=1, source_target_pairs={{0,3},{1,0},{2,1},{3,2},{4,7},{5,4},{6,5},{7,6},{8,11},{9,8},{10,9... | collective-permute-start | bytes 196616 | tf_op jit(solution)/shard_map/ppermute | solution.py:65
  63.4 1.6 %collective-permute-done.18.second = bf16[2,128,128]{2,1,0:T(8,128)(2,1)S(1)} collective-permute-done((bf16[2,128,128]{2,1,0:T(8,128)(2,1)S(1)}, bf16[2,128,128]{2,1,0:T(8,128)(2,1)S(1)}, u32[]{:S(2)}, u32[]{:S(2)}) %collective-permute-start.18) | collective-permute-done | bytes 65568 | tf_op jit(solution)/shard_map/ppermute | solution.py:65
  64.9 1.5 %collective-permute-done.19.third = bf16[2,128,128]{2,1,0:T(8,128)(2,1)S(1)} collective-permute-done((bf16[2,128,128]{2,1,0:T(8,128)(2,1)S(1)}, bf16[2,128,128]{2,1,0:T(8,128)(2,1)S(1)}, u32[]{:S(2)}, u32[]{:S(2)}) %collective-permute-start.19) | collective-permute-done | bytes 65568 | tf_op jit(solution)/shard_map/ppermute | solution.py:65
  66.5 3.7 %collective-permute-start.20 = (bf16[4,128,128]{2,1,0:T(8,128)(2,1)S(1)}, bf16[4,128,128]{2,1,0:T(8,128)(2,1)S(1)}, u32[]{:S(2)}, u32[]{:S(2)}) collective-permute-start(bf16[4,128,128]{2,1,0:T(8,128)(2,1)S(1)} %get-tuple-element.41), channel_id=1, source_target_pairs={{0,32},{1,33},{2,34},{3,35},{4,36},{5,37},{6,38},{7,39},{8,96},{9,... | collective-permute-start | bytes 393224 | tf_op jit(solution)/shard_map/ppermute | solution.py:61
  70.2 1.4 %collective-permute-start.21 = (bf16[4,128,128]{2,1,0:T(8,128)(2,1)S(1)}, bf16[4,128,128]{2,1,0:T(8,128)(2,1)S(1)}, u32[]{:S(2)}, u32[]{:S(2)}) collective-permute-start(bf16[4,128,128]{2,1,0:T(8,128)(2,1)S(1)} %get-tuple-element.42), channel_id=1, source_target_pairs={{0,36},{1,37},{2,38},{3,39},{4,32},{5,33},{6,34},{7,35},{8,100},{9... | collective-permute-start | bytes 393224 | tf_op jit(solution)/shard_map/ppermute | solution.py:61
  71.6 1.1 %collective-permute-start.14 = (bf16[2,128,128]{2,1,0:T(8,128)(2,1)S(1)}, bf16[2,128,128]{2,1,0:T(8,128)(2,1)S(1)}, u32[]{:S(2)}, u32[]{:S(2)}) collective-permute-start(bf16[2,128,128]{2,1,0:T(8,128)(2,1)S(1)} %get-tuple-element.34), channel_id=1, source_target_pairs={{0,1},{1,2},{2,3},{3,0},{4,5},{5,6},{6,7},{7,4},{8,9},{9,10},{10,1... | collective-permute-start | bytes 196616 | tf_op jit(solution)/shard_map/ppermute | solution.py:65
  72.7 2.3 %collective-permute-start.15 = (bf16[2,128,128]{2,1,0:T(8,128)(2,1)S(1)}, bf16[2,128,128]{2,1,0:T(8,128)(2,1)S(1)}, u32[]{:S(2)}, u32[]{:S(2)}) collective-permute-start(bf16[2,128,128]{2,1,0:T(8,128)(2,1)S(1)} %get-tuple-element.35), channel_id=1, source_target_pairs={{0,2},{1,3},{2,0},{3,1},{4,6},{5,7},{6,4},{7,5},{8,10},{9,11},{10,... | collective-permute-start | bytes 196616 | tf_op jit(solution)/shard_map/ppermute | solution.py:65
  75.2 0.4 fusion.place
  75.6 5.9 %collective-permute-done.21.refs_7_ = bf16[4,128,128]{2,1,0:T(8,128)(2,1)S(1)} collective-permute-done((bf16[4,128,128]{2,1,0:T(8,128)(2,1)S(1)}, bf16[4,128,128]{2,1,0:T(8,128)(2,1)S(1)}, u32[]{:S(2)}, u32[]{:S(2)}) %collective-permute-start.21) | collective-permute-done | bytes 131104 | tf_op jit(solution)/shard_map/ppermute | solution.py:61
  81.6 3.3 %shard_map.80 = f32[8,16,8,512]{3,2,1,0:T(8,128)} custom-call(s32[2,2]{1,0:T(2,128)S(1)} %copy-done.2, s32[2,2]{1,0:T(2,128)S(1)} %copy-done.3, s32[8]{0:T(128)S(1)} %copy-done.4, f32[128,2048]{1,0:T(8,128)S(1)} %get-tuple-element.31.total, bf16[1024,1024]{1,0:T(8,128)(2,1)S(1)} %fusion.place, bf16[4,128,128]{2,1,0:T(8,128)(2,1)S(1)} %collective-permute-done.10.same.refs_0_, ...), custom_call_target="tpu_custom_call" | custom-call | flops 1000000000 | bytes 4194304 | tf_op jit(solution)/shard_map/pallas_call | solution.py:407
  (40 shorter events, 0.7 us)
Async XLA Ops:
  3.2 15.7 %collective-permute-start.2 = (bf16[416,512]{1,0:T(8,128)(2,1)}, bf16[416,512]{1,0:T(8,128)(2,1)S(1)}, u32[]{:S(2)}, u32[]{:S(2)}) collective-permute-start(bf16[416,512]{1,0:T(8,128)(2,1)} %get-tuple-element.24.refs_0_), channel_id=1, source_target_pairs={{0,4},{1,5},{2,6},{3,7},{4,0},{5,1},{6,2},{7,3},{8,12},{9,13},{10,... | collective-permute-start | bytes 1277960 | tf_op jit(solution)/shard_map/ppermute | solution.py:340
  6.8 12.0 %collective-permute-start.1 = (bf16[416,512]{1,0:T(8,128)(2,1)}, bf16[416,512]{1,0:T(8,128)(2,1)S(1)}, u32[]{:S(2)}, u32[]{:S(2)}) collective-permute-start(bf16[416,512]{1,0:T(8,128)(2,1)} %get-tuple-element.24.refs_0_), channel_id=1, source_target_pairs={{0,1},{1,2},{2,3},{3,0},{4,5},{5,6},{6,7},{7,4},{8,9},{9,10},{10,1... | collective-permute-start | bytes 1277960 | tf_op jit(solution)/shard_map/ppermute | solution.py:339
  8.1 10.7 %collective-permute-start = (bf16[416,512]{1,0:T(8,128)(2,1)}, bf16[416,512]{1,0:T(8,128)(2,1)S(1)}, u32[]{:S(2)}, u32[]{:S(2)}) collective-permute-start(bf16[416,512]{1,0:T(8,128)(2,1)} %get-tuple-element.24.refs_0_), channel_id=1, source_target_pairs={{0,3},{1,0},{2,1},{3,2},{4,7},{5,4},{6,5},{7,6},{8,11},{9,8},{10,9... | collective-permute-start | bytes 1277960 | tf_op jit(solution)/shard_map/ppermute | solution.py:338
  9.6 6.8 %collective-permute-start.3 = (bf16[2,16,512]{2,1,0:T(8,128)(2,1)}, bf16[2,16,512]{2,1,0:T(8,128)(2,1)S(1)}, u32[]{:S(2)}, u32[]{:S(2)}) collective-permute-start(bf16[2,16,512]{2,1,0:T(8,128)(2,1)} %get-tuple-element.25), channel_id=1, source_target_pairs={{0,8},{8,16},{16,24},{1,9},{9,17},{17,25},{2,10},{10,18},{18,26},{... | collective-permute-start | bytes 98312 | tf_op jit(solution)/shard_map/ppermute | solution.py:378
  13.1 5.7 %collective-permute-start.4 = (bf16[2,16,512]{2,1,0:T(8,128)(2,1)}, bf16[2,16,512]{2,1,0:T(8,128)(2,1)S(1)}, u32[]{:S(2)}, u32[]{:S(2)}) collective-permute-start(bf16[2,16,512]{2,1,0:T(8,128)(2,1)} %get-tuple-element.27), channel_id=1, source_target_pairs={{8,0},{16,8},{24,16},{9,1},{17,9},{25,17},{10,2},{18,10},{26,18},{... | collective-permute-start | bytes 98312 | tf_op jit(solution)/shard_map/ppermute | solution.py:379
  19.0 9.7 %collective-permute-start.6 = (bf16[416,512]{1,0:T(8,128)(2,1)S(1)}, bf16[416,512]{1,0:T(8,128)(2,1)S(1)}, u32[]{:S(2)}, u32[]{:S(2)}) collective-permute-start(bf16[416,512]{1,0:T(8,128)(2,1)S(1)} %get-tuple-element.29), channel_id=1, source_target_pairs={{0,3},{1,0},{2,1},{3,2},{4,7},{5,4},{6,5},{7,6},{8,11},{9,8},{10,9... | collective-permute-start | bytes 1277960 | tf_op jit(solution)/shard_map/ppermute | solution.py:353
  21.3 10.5 %collective-permute-start.7 = (bf16[416,512]{1,0:T(8,128)(2,1)S(1)}, bf16[416,512]{1,0:T(8,128)(2,1)S(1)}, u32[]{:S(2)}, u32[]{:S(2)}) collective-permute-start(bf16[416,512]{1,0:T(8,128)(2,1)S(1)} %get-tuple-element.30), channel_id=1, source_target_pairs={{0,4},{1,5},{2,6},{3,7},{4,0},{5,1},{6,2},{7,3},{8,12},{9,13},{10,... | collective-permute-start | bytes 1277960 | tf_op jit(solution)/shard_map/ppermute | solution.py:351
  22.7 12.9 %collective-permute-start.5 = (bf16[416,512]{1,0:T(8,128)(2,1)S(1)}, bf16[416,512]{1,0:T(8,128)(2,1)S(1)}, u32[]{:S(2)}, u32[]{:S(2)}) collective-permute-start(bf16[416,512]{1,0:T(8,128)(2,1)S(1)} %get-tuple-element.28), channel_id=1, source_target_pairs={{0,1},{1,2},{2,3},{3,0},{4,5},{5,6},{6,7},{7,4},{8,9},{9,10},{10,1... | collective-permute-start | bytes 1277960 | tf_op jit(solution)/shard_map/ppermute | solution.py:352
  28.6 4.1 %slice-start = ((s8[8388608]{0:T(1024)(128)(4,1)}), s8[4194304]{0:T(1024)(128)(4,1)S(1)}, s32[]{:S(2)}) async-start(s8[8388608]{0:T(1024)(128)(4,1)} %bitcast.2), calls=%async_computation | async-start | bytes 8388608
  28.7 6.9 %collective-permute-start.9 = (bf16[208,512]{1,0:T(8,128)(2,1)S(1)}, bf16[208,512]{1,0:T(8,128)(2,1)S(1)}, u32[]{:S(2)}, u32[]{:S(2)}) collective-permute-start(bf16[208,512]{1,0:T(8,128)(2,1)S(1)} %slice.9), channel_id=1, source_target_pairs={{0,3},{1,0},{2,1},{3,2},{4,7},{5,4},{6,5},{7,6},{8,11},{9,8},{10,9... | collective-permute-start | bytes 638984 | tf_op jit(solution)/shard_map/ppermute | solution.py:355
  31.8 2.2 %slice-start.1 = ((s8[8388608]{0:T(1024)(128)(4,1)}), s8[4194304]{0:T(1024)(128)(4,1)S(1)}, s32[]{:S(2)}) async-start(s8[8388608]{0:T(1024)(128)(4,1)} %bitcast.2), calls=%async_computation.1 | async-start | bytes 8388608
  31.8 2.3 %copy-start = (bf16[416,512]{1,0:T(8,128)(2,1)S(1)}, bf16[416,512]{1,0:T(8,128)(2,1)}, u32[]{:S(2)}) copy-start(bf16[416,512]{1,0:T(8,128)(2,1)} %get-tuple-element.24.refs_0_) | copy-start | bytes 1277956
  31.9 6.0 %collective-permute-start.8 = (bf16[208,512]{1,0:T(8,128)(2,1)S(1)}, bf16[208,512]{1,0:T(8,128)(2,1)S(1)}, u32[]{:S(2)}, u32[]{:S(2)}) collective-permute-start(bf16[208,512]{1,0:T(8,128)(2,1)S(1)} %slice.8), channel_id=1, source_target_pairs={{0,1},{1,2},{2,3},{3,0},{4,5},{5,6},{6,7},{7,4},{8,9},{9,10},{10,1... | collective-permute-start | bytes 638984 | tf_op jit(solution)/shard_map/ppermute | solution.py:354
  34.1 3.7 %copy-start.1 = (bf16[16,16,512]{2,1,0:T(8,128)(2,1)S(1)}, bf16[16,16,512]{2,1,0:T(8,128)(2,1)}, u32[]{:S(2)}) copy-start(bf16[16,16,512]{2,1,0:T(8,128)(2,1)} %get-tuple-element.26.inner) | copy-start | bytes 786436
  37.8 37.4 %copy-start.5 = (s32[1024]{0:T(1024)S(1)}, s32[1024]{0:T(1024)}, u32[]{:S(2)}) copy-start(s32[1024]{0:T(1024)} %constant.2.clone) | copy-start | bytes 12292
  41.0 40.6 %copy-start.2 = (s32[2,2]{1,0:T(2,128)S(1)}, s32[2,2]{1,0:T(2,128)}, u32[]{:S(2)}) copy-start(s32[2,2]{1,0:T(2,128)} %ladder_tiles.1) | copy-start | bytes 52
  41.0 40.6 %copy-start.3 = (s32[2,2]{1,0:T(2,128)S(1)}, s32[2,2]{1,0:T(2,128)}, u32[]{:S(2)}) copy-start(s32[2,2]{1,0:T(2,128)} %cycle_tiles.1) | copy-start | bytes 52
  41.0 40.6 %copy-start.4 = (s32[8]{0:T(128)S(1)}, s32[8]{0:T(128)}, u32[]{:S(2)}) copy-start(s32[8]{0:T(128)} %partner.1) | copy-start | bytes 100
  41.0 13.8 %collective-permute-start.12 = (bf16[4,128,128]{2,1,0:T(8,128)(2,1)S(1)}, bf16[4,128,128]{2,1,0:T(8,128)(2,1)S(1)}, u32[]{:S(2)}, u32[]{:S(2)}) collective-permute-start(bf16[4,128,128]{2,1,0:T(8,128)(2,1)S(1)} %get-tuple-element.33), channel_id=1, source_target_pairs={{16,0},{17,1},{18,2},{19,3},{20,4},{21,5},{22,6},{23,7},{24,8},{25... | collective-permute-start | bytes 393224 | tf_op jit(solution)/shard_map/ppermute | solution.py:57
  42.4 19.0 %collective-permute-start.17 = (bf16[2,128,128]{2,1,0:T(8,128)(2,1)S(1)}, bf16[2,128,128]{2,1,0:T(8,128)(2,1)S(1)}, u32[]{:S(2)}, u32[]{:S(2)}) collective-permute-start(bf16[2,128,128]{2,1,0:T(8,128)(2,1)S(1)} %get-tuple-element.38), channel_id=1, source_target_pairs={{0,1},{1,2},{2,3},{3,0},{4,5},{5,6},{6,7},{7,4},{8,9},{9,10},{10,1... | collective-permute-start | bytes 196616 | tf_op jit(solution)/shard_map/ppermute | solution.py:65
  42.5 29.0 %collective-permute-start.11 = (bf16[4,128,128]{2,1,0:T(8,128)(2,1)S(1)}, bf16[4,128,128]{2,1,0:T(8,128)(2,1)S(1)}, u32[]{:S(2)}, u32[]{:S(2)}) collective-permute-start(bf16[4,128,128]{2,1,0:T(8,128)(2,1)S(1)} %get-tuple-element.33), channel_id=1, source_target_pairs={{0,4},{1,5},{2,6},{3,7},{4,0},{5,1},{6,2},{7,3},{8,68},{9,69},{10,... | collective-permute-start | bytes 393224 | tf_op jit(solution)/shard_map/ppermute | solution.py:57
  52.9 18.6 %collective-permute-start.10 = (bf16[4,128,128]{2,1,0:T(8,128)(2,1)S(1)}, bf16[4,128,128]{2,1,0:T(8,128)(2,1)S(1)}, u32[]{:S(2)}, u32[]{:S(2)}) collective-permute-start(bf16[4,128,128]{2,1,0:T(8,128)(2,1)S(1)} %get-tuple-element.32), channel_id=1, source_target_pairs={{0,0},{1,1},{2,2},{3,3},{4,4},{5,5},{6,6},{7,7},{8,64},{9,65},{10,... | collective-permute-start | bytes 393224 | tf_op jit(solution)/shard_map/ppermute | solution.py:61
  54.8 16.7 %collective-permute-start.13 = (bf16[4,128,128]{2,1,0:T(8,128)(2,1)S(1)}, bf16[4,128,128]{2,1,0:T(8,128)(2,1)S(1)}, u32[]{:S(2)}, u32[]{:S(2)}) collective-permute-start(bf16[4,128,128]{2,1,0:T(8,128)(2,1)S(1)} %collective-permute-done.12), channel_id=1, source_target_pairs={{0,132},{1,133},{2,134},{3,135},{4,128},{5,129},{6,130},{7,131},{8... | collective-permute-start | bytes 393224 | tf_op jit(solution)/shard_map/ppermute | solution.py:57
  60.1 4.9 %collective-permute-start.18 = (bf16[2,128,128]{2,1,0:T(8,128)(2,1)S(1)}, bf16[2,128,128]{2,1,0:T(8,128)(2,1)S(1)}, u32[]{:S(2)}, u32[]{:S(2)}) collective-permute-start(bf16[2,128,128]{2,1,0:T(8,128)(2,1)S(1)} %get-tuple-element.39), channel_id=1, source_target_pairs={{0,2},{1,3},{2,0},{3,1},{4,6},{5,7},{6,4},{7,5},{8,10},{9,11},{10,... | collective-permute-start | bytes 196616 | tf_op jit(solution)/shard_map/ppermute | solution.py:65
  61.4 5.1 %collective-permute-start.19 = (bf16[2,128,128]{2,1,0:T(8,128)(2,1)S(1)}, bf16[2,128,128]{2,1,0:T(8,128)(2,1)S(1)}, u32[]{:S(2)}, u32[]{:S(2)}) collective-permute-start(bf16[2,128,128]{2,1,0:T(8,128)(2,1)S(1)} %get-tuple-element.40), channel_id=1, source_target_pairs={{0,3},{1,0},{2,1},{3,2},{4,7},{5,4},{6,5},{7,6},{8,11},{9,8},{10,9... | collective-permute-start | bytes 196616 | tf_op jit(solution)/shard_map/ppermute | solution.py:65
  66.5 9.1 %collective-permute-start.20 = (bf16[4,128,128]{2,1,0:T(8,128)(2,1)S(1)}, bf16[4,128,128]{2,1,0:T(8,128)(2,1)S(1)}, u32[]{:S(2)}, u32[]{:S(2)}) collective-permute-start(bf16[4,128,128]{2,1,0:T(8,128)(2,1)S(1)} %get-tuple-element.41), channel_id=1, source_target_pairs={{0,32},{1,33},{2,34},{3,35},{4,36},{5,37},{6,38},{7,39},{8,96},{9,... | collective-permute-start | bytes 393224 | tf_op jit(solution)/shard_map/ppermute | solution.py:61
  70.2 11.4 %collective-permute-start.21 = (bf16[4,128,128]{2,1,0:T(8,128)(2,1)S(1)}, bf16[4,128,128]{2,1,0:T(8,128)(2,1)S(1)}, u32[]{:S(2)}, u32[]{:S(2)}) collective-permute-start(bf16[4,128,128]{2,1,0:T(8,128)(2,1)S(1)} %get-tuple-element.42), channel_id=1, source_target_pairs={{0,36},{1,37},{2,38},{3,39},{4,32},{5,33},{6,34},{7,35},{8,100},{9... | collective-permute-start | bytes 393224 | tf_op jit(solution)/shard_map/ppermute | solution.py:61
  71.6 10.0 %collective-permute-start.14 = (bf16[2,128,128]{2,1,0:T(8,128)(2,1)S(1)}, bf16[2,128,128]{2,1,0:T(8,128)(2,1)S(1)}, u32[]{:S(2)}, u32[]{:S(2)}) collective-permute-start(bf16[2,128,128]{2,1,0:T(8,128)(2,1)S(1)} %get-tuple-element.34), channel_id=1, source_target_pairs={{0,1},{1,2},{2,3},{3,0},{4,5},{5,6},{6,7},{7,4},{8,9},{9,10},{10,1... | collective-permute-start | bytes 196616 | tf_op jit(solution)/shard_map/ppermute | solution.py:65
  72.7 8.9 %collective-permute-start.15 = (bf16[2,128,128]{2,1,0:T(8,128)(2,1)S(1)}, bf16[2,128,128]{2,1,0:T(8,128)(2,1)S(1)}, u32[]{:S(2)}, u32[]{:S(2)}) collective-permute-start(bf16[2,128,128]{2,1,0:T(8,128)(2,1)S(1)} %get-tuple-element.35), channel_id=1, source_target_pairs={{0,2},{1,3},{2,0},{3,1},{4,6},{5,7},{6,4},{7,5},{8,10},{9,11},{10,... | collective-permute-start | bytes 196616 | tf_op jit(solution)/shard_map/ppermute | solution.py:65
  75.1 6.5 %collective-permute-start.16 = (bf16[2,128,128]{2,1,0:T(8,128)(2,1)S(1)}, bf16[2,128,128]{2,1,0:T(8,128)(2,1)S(1)}, u32[]{:S(2)}, u32[]{:S(2)}) collective-permute-start(bf16[2,128,128]{2,1,0:T(8,128)(2,1)S(1)} %get-tuple-element.36), channel_id=1, source_target_pairs={{0,3},{1,0},{2,1},{3,2},{4,7},{5,4},{6,5},{7,6},{8,11},{9,8},{10,9... | collective-permute-start | bytes 196616 | tf_op jit(solution)/shard_map/ppermute | solution.py:65

commit v11 on v9

--- a/solution.py
+++ b/solution.py
@@ -1,3 +1,5 @@
+import functools
+
 import jax
 import jax.numpy as jnp
 import numpy as np
@@ -247,33 +249,36 @@
             late_refs[dy][dx, rows, :] = lanes_buf[late, pl.ds(start, 128)]
 
 
-def finish_kernel(ladder_tiles, cycle_tiles, partner, total, place, *refs):
-    arrived, (out_ref, mirrored, wide, held, sems) = refs[:7], refs[7:]
-    parity = lax.axis_index("pi") % 2
+def finish_kernel(k, ladder_tiles, cycle_tiles, partner, total, place, *refs):
+    arrived, (out_ref, mirrored, wide, held, sems) = refs[:-5], refs[-5:]
+    half = (lax.axis_index("pi") % 2) ^ k
     for dx, dy, start in peers(-1):
-        early = arrived[dx][0] if dy == 0 else arrived[1 + dy][dx]
-        wide[:128, pl.ds(start, 128)] = early
-        wide[128:, pl.ds(start, 128)] = arrived[5 + dx][dy]
-    moved = jnp.dot(wide[...], place[...], preferred_element_type=F32)
-    for k in range(2):
-        for s in range(2):
-            mirrored[s, parity ^ k] = moved[k * 128 + s * 64 : k * 128 + (s + 1) * 64]
+        if k == 1:
+            block = arrived[dx][dy]
+        elif dy == 0:
+            block = arrived[dx][0]
+        else:
+            block = arrived[1 + dy][dx]
+        wide[:, pl.ds(start, 128)] = block
+    mirrored[...] = jnp.dot(wide[...], place[...], preferred_element_type=F32)
     dests = [ladder_tiles[0, 0], ladder_tiles[1, 0], cycle_tiles[0, 0], cycle_tiles[1, 0]]
     tile = lax.broadcasted_iota(jnp.int32, (8, LANES), 0)
     own = [(tile == dest).astype(F32) for dest in dests]
     other = [(tile == partner[dest]).astype(F32) for dest in dests]
 
     def store(i):
-        return pltpu.make_async_copy(held.at[i], out_ref.at[i], sems.at[i])
+        where = out_ref.at[i, pl.ds(pl.multiple_of(half * 8, 8), 8)]
+        return pltpu.make_async_copy(held.at[i], where, sems.at[i])
 
     def one(i):
-        for j in range(16):
+        for j in range(8):
             acc = None
             for s in range(4):
                 lanes = slice((s % 2) * LANES, (s % 2 + 1) * LANES)
-                term = own[s] * total[pl.ds(j * 8 + i, 1), s * LANES : (s + 1) * LANES]
+                mine = total[pl.ds(half * 64 + j * 8 + i, 1), s * LANES : (s + 1) * LANES]
+                term = own[s] * mine
                 acc = term if acc is None else acc + term
-                acc = acc + other[s] * mirrored[s // 2, j // 8, pl.ds(i * 8 + j % 8, 1), lanes]
+                acc = acc + other[s] * mirrored[pl.ds((s // 2) * 64 + i * 8 + j, 1), lanes]
             held[i, j] = acc
         store(i).start()
 
@@ -286,13 +291,14 @@
 HBM = pl.BlockSpec(memory_space=pltpu.HBM)
 
 
-def call(kernel, ins, outs, out_specs, scratch, limit, flops):
+def call(kernel, ins, outs, out_specs, scratch, limit, flops, aliases=None):
     return pl.pallas_call(
         kernel,
         out_shape=outs,
         in_specs=ins,
         out_specs=out_specs,
         scratch_shapes=scratch,
+        input_output_aliases=aliases or {},
         compiler_params=pltpu.CompilerParams(vmem_limit_bytes=limit * MIB),
         cost_estimate=pl.CostEstimate(flops=flops, bytes_accessed=4 * MIB, transcendentals=0),
     )
@@ -368,20 +374,33 @@
     joined = [to_transposed(block, 1, dx) for dx, block in enumerate(joined)]
     early = call(split_kernel, [VMEM] * 2, [two] * 3, [VMEM] * 3, [], 4, 10**7)(same, other)
     early = [along_y(block, dy) for dy, block in enumerate(early, 1)]
-    return call(
-        finish_kernel,
-        [SMEM, SMEM, SMEM] + [VMEM] * 9,
-        shape((8, 16, 8, LANES), F32),
+    scratch = [
+        pltpu.VMEM((128, 1024), F32),
+        pltpu.VMEM((128, 1024), BF),
+        pltpu.VMEM((8, 8, 8, LANES), F32),
+        pltpu.SemaphoreType.DMA((8,)),
+    ]
+    whole = shape((8, 16, 8, LANES), F32)
+    common = (ladder_tiles, cycle_tiles, partner, total, place_matrix())
+    begun = call(
+        functools.partial(finish_kernel, 0),
+        [SMEM] * 3 + [VMEM] * 7,
+        whole,
         HBM,
-        [
-            pltpu.VMEM((2, 2, 64, 1024), F32),
-            pltpu.VMEM((256, 1024), BF),
-            pltpu.VMEM((8, 16, 8, LANES), F32),
-            pltpu.SemaphoreType.DMA((8,)),
-        ],
+        scratch,
         12,
         10**9,
-    )(ladder_tiles, cycle_tiles, partner, total, place_matrix(), same, other, *early, *joined)
+    )(*common, same, other, *early)
+    return call(
+        functools.partial(finish_kernel, 1),
+        [SMEM] * 3 + [VMEM] * 4 + [HBM],
+        whole,
+        HBM,
+        scratch,
+        12,
+        10**9,
+        {7: 0},
+    )(*common, *joined, begun)
 
 
 def solution(mesh):

time: 79.8 us -> 82.3 us (1.031)
  the two profiles are of different devices: /device:TPU:6 before, /device:TPU:3 now
where the time goes in v11:
time: 82.3 us; the launch traced here: 80.9 us
  starting transfers between devices  42.7 us (52%)
  waiting for transfers between devices  23.7 us (29%)
  Pallas kernels  13.5 us (16%)
    ppermute x4, starting transfers between devices, to_transposed(): return lax.ppermute(block, ('pi', 'pj', 'vert'), pair_moves(k, dx))  17.9 us
    ppermute x6, starting transfers between devices, along_y(): lax.ppermute(block, 'vert', vert_moves(lambda h, y: h * 4 + (y + dy) % 4))  7.45 us
    ppermute x1, waiting for transfers between devices, gather(): side_2 = lax.ppermute(to_side, 'vert', FLIP)  6.72 us
    ppermute x6, waiting for transfers between devices, along_y(): lax.ppermute(block, 'vert', vert_moves(lambda h, y: h * 4 + (y + dy) % 4))  6.12 us
    ppermute x1, starting transfers between devices, body(): after = lax.ppermute(first, 'pj', [(q + 1, q) for q in range(3)])  3.77 us
    ppermute x1, starting transfers between devices, gather(): down_3 = lax.ppermute(down_2[:HALF], 'vert', DOWN)  3.3 us
    pallas_call x1, Pallas kernels, body(): call(prepare_kernel, [HBM] * 4, [shape((2 * HALF, LANES), BF), shape((16,...  3.15 us
    pallas_call x1, Pallas kernels, body(): call(main_kernel, [VMEM] * 15, [shape((PAIRS, 2048), F32), four, four, tw...  3.12 us
  transfers between devices with their start and end apart: 20, of which 13 were waited for; matrix products, arithmetic and copies ran while one was open for 1% of the time, Pallas kernels for 6%

profile of v11, /device:TPU:3, one launch (start us, length us, event | category | flops | bytes accessed | tf_op | source)
XLA Modules:
  0.0 80.9 jit_solution(5513040423099798924)
XLA Ops:
  0.0 3.2 %shard_map.73 = (bf16[416,512]{1,0:T(8,128)(2,1)}, bf16[16,16,512]{2,1,0:T(8,128)(2,1)}, bf16[2,16,512]{2,1,0:T(8,128)(2,1)}, bf16[2,16,512]{2,1,0:T(8,128)(2,1)}) custom-call(s32[2,2]{1,0:T(2,128)} %ladder_tiles.3, s32[2,2]{1,0:T(2,128)} %cycle_tiles.3, bf16[1024,512]{1,0:T(8,128)(2,1)} %bitcast.4, bf16[80,2,512]{2,1,0:T(2,128)(2,1)} %bitcast.5), custom_call_target="tpu_custom_call" | custom-call | flops 1000000000 | bytes 4194304 | tf_op jit(solution)/shard_map/pallas_call | solution.py:335
  3.2 2.8 %collective-permute-start = (bf16[416,512]{1,0:T(8,128)(2,1)}, bf16[416,512]{1,0:T(8,128)(2,1)S(1)}, u32[]{:S(2)}, u32[]{:S(2)}) collective-permute-start(bf16[416,512]{1,0:T(8,128)(2,1)} %get-tuple-element.24.refs_0_), channel_id=1, source_target_pairs={{0,3},{1,0},{2,1},{3,2},{4,7},{5,4},{6,5},{7,6},{8,11},{9,8},{10,9... | collective-permute-start | bytes 1277960 | tf_op jit(solution)/shard_map/ppermute | solution.py:312
  6.0 1.8 %collective-permute-start.2 = (bf16[416,512]{1,0:T(8,128)(2,1)}, bf16[416,512]{1,0:T(8,128)(2,1)S(1)}, u32[]{:S(2)}, u32[]{:S(2)}) collective-permute-start(bf16[416,512]{1,0:T(8,128)(2,1)} %get-tuple-element.24.refs_0_), channel_id=1, source_target_pairs={{0,4},{1,5},{2,6},{3,7},{4,0},{5,1},{6,2},{7,3},{8,12},{9,13},{10,... | collective-permute-start | bytes 1277960 | tf_op jit(solution)/shard_map/ppermute | solution.py:314
  7.8 1.3 %collective-permute-start.3 = (bf16[2,16,512]{2,1,0:T(8,128)(2,1)}, bf16[2,16,512]{2,1,0:T(8,128)(2,1)S(1)}, u32[]{:S(2)}, u32[]{:S(2)}) collective-permute-start(bf16[2,16,512]{2,1,0:T(8,128)(2,1)} %get-tuple-element.25), channel_id=1, source_target_pairs={{0,8},{8,16},{16,24},{1,9},{9,17},{17,25},{2,10},{10,18},{18,26},{... | collective-permute-start | bytes 98312 | tf_op jit(solution)/shard_map/ppermute | solution.py:352
  9.1 3.8 %collective-permute-start.4 = (bf16[2,16,512]{2,1,0:T(8,128)(2,1)}, bf16[2,16,512]{2,1,0:T(8,128)(2,1)S(1)}, u32[]{:S(2)}, u32[]{:S(2)}) collective-permute-start(bf16[2,16,512]{2,1,0:T(8,128)(2,1)} %get-tuple-element.27), channel_id=1, source_target_pairs={{8,0},{16,8},{24,16},{9,1},{17,9},{25,17},{10,2},{18,10},{26,18},{... | collective-permute-start | bytes 98312 | tf_op jit(solution)/shard_map/ppermute | solution.py:353
  12.9 1.0 %collective-permute-done.4.after = bf16[2,16,512]{2,1,0:T(8,128)(2,1)S(1)} collective-permute-done((bf16[2,16,512]{2,1,0:T(8,128)(2,1)}, bf16[2,16,512]{2,1,0:T(8,128)(2,1)S(1)}, u32[]{:S(2)}, u32[]{:S(2)}) %collective-permute-start.4) | collective-permute-done | bytes 32800 | tf_op jit(solution)/shard_map/ppermute | solution.py:353
  13.9 0.8 %collective-permute-done.refs_1_.after.down = bf16[416,512]{1,0:T(8,128)(2,1)S(1)} collective-permute-done((bf16[416,512]{1,0:T(8,128)(2,1)}, bf16[416,512]{1,0:T(8,128)(2,1)S(1)}, u32[]{:S(2)}, u32[]{:S(2)}) %collective-permute-start) | collective-permute-done | bytes 426016 | tf_op jit(solution)/shard_map/ppermute | solution.py:312
  14.8 3.0 %collective-permute-done.1.refs_2_.up = bf16[416,512]{1,0:T(8,128)(2,1)S(1)} collective-permute-done((bf16[416,512]{1,0:T(8,128)(2,1)}, bf16[416,512]{1,0:T(8,128)(2,1)S(1)}, u32[]{:S(2)}, u32[]{:S(2)}) %collective-permute-start.1) | collective-permute-done | bytes 426016 | tf_op jit(solution)/shard_map/ppermute | solution.py:313
  17.8 0.3 collective-permute-done.2.refs_3_.flip
  18.1 1.9 %collective-permute-start.7 = (bf16[416,512]{1,0:T(8,128)(2,1)S(1)}, bf16[416,512]{1,0:T(8,128)(2,1)S(1)}, u32[]{:S(2)}, u32[]{:S(2)}) collective-permute-start(bf16[416,512]{1,0:T(8,128)(2,1)S(1)} %get-tuple-element.30), channel_id=1, source_target_pairs={{0,4},{1,5},{2,6},{3,7},{4,0},{5,1},{6,2},{7,3},{8,12},{9,13},{10,... | collective-permute-start | bytes 1277960 | tf_op jit(solution)/shard_map/ppermute | solution.py:325
  20.1 2.4 %collective-permute-start.6 = (bf16[416,512]{1,0:T(8,128)(2,1)S(1)}, bf16[416,512]{1,0:T(8,128)(2,1)S(1)}, u32[]{:S(2)}, u32[]{:S(2)}) collective-permute-start(bf16[416,512]{1,0:T(8,128)(2,1)S(1)} %get-tuple-element.29), channel_id=1, source_target_pairs={{0,3},{1,0},{2,1},{3,2},{4,7},{5,4},{6,5},{7,6},{8,11},{9,8},{10,9... | collective-permute-start | bytes 1277960 | tf_op jit(solution)/shard_map/ppermute | solution.py:327
  22.5 6.7 %collective-permute-done.7.refs_6_ = bf16[416,512]{1,0:T(8,128)(2,1)S(1)} collective-permute-done((bf16[416,512]{1,0:T(8,128)(2,1)S(1)}, bf16[416,512]{1,0:T(8,128)(2,1)S(1)}, u32[]{:S(2)}, u32[]{:S(2)}) %collective-permute-start.7) | collective-permute-done | bytes 426016 | tf_op jit(solution)/shard_map/ppermute | solution.py:325
  29.4 3.3 %collective-permute-start.9 = (bf16[208,512]{1,0:T(8,128)(2,1)S(1)}, bf16[208,512]{1,0:T(8,128)(2,1)S(1)}, u32[]{:S(2)}, u32[]{:S(2)}) collective-permute-start(bf16[208,512]{1,0:T(8,128)(2,1)S(1)} %slice.9), channel_id=1, source_target_pairs={{0,3},{1,0},{2,1},{3,2},{4,7},{5,4},{6,5},{7,6},{8,11},{9,8},{10,9... | collective-permute-start | bytes 638984 | tf_op jit(solution)/shard_map/ppermute | solution.py:329
  32.7 0.8 %shard_map.75.swap = bf16[1024,1024]{1,0:T(8,128)(2,1)S(1)} custom-call(bf16[416,512]{1,0:T(8,128)(2,1)S(1)} %collective-permute-done.refs_1_.after.down), custom_call_target="tpu_custom_call" | custom-call | flops 20000000000 | bytes 4194304 | tf_op jit(solution)/shard_map/pallas_call | solution.py:355
  33.5 1.5 %shard_map.74.near = f32[128,1024]{1,0:T(8,128)S(1)} custom-call(bf16[2,512,4096]{2,1,0:T(8,128)(2,1)S(1)} %bitcast.3, bf16[416,512]{1,0:T(8,128)(2,1)S(1)} %copy-done, bf16[416,512]{1,0:T(8,128)(2,1)S(1)} %collective-permute-done.refs_1_.after.down, bf16[416,512]{1,0:T(8,128)(2,1)S(1)} %collective-permute-done.1.refs_2_.up, ...), custom_call_target="tpu_custom_call" | custom-call | flops 1000000000 | bytes 4194304 | tf_op jit(solution)/shard_map/pallas_call | solution.py:358
  35.1 2.8 %collective-permute-done.8.refs_7_ = bf16[208,512]{1,0:T(8,128)(2,1)S(1)} collective-permute-done((bf16[208,512]{1,0:T(8,128)(2,1)S(1)}, bf16[208,512]{1,0:T(8,128)(2,1)S(1)}, u32[]{:S(2)}, u32[]{:S(2)}) %collective-permute-start.8) | collective-permute-done | bytes 213024 | tf_op jit(solution)/shard_map/ppermute | solution.py:328
  37.8 3.1 %shard_map.77 = (f32[128,2048]{1,0:T(8,128)S(1)}, bf16[4,128,128]{2,1,0:T(8,128)(2,1)S(1)}, bf16[4,128,128]{2,1,0:T(8,128)(2,1)S(1)}, bf16[2,128,128]{2,1,0:T(8,...) custom-call(bf16[2,512,4096]{2,1,0:T(8,128)(2,1)S(1)} %bitcast.3, ...), custom_call_target="tpu_custom_call" | custom-call | flops 2000000000 | bytes 4194304 | tf_op jit(solution)/shard_map/pallas_call | solution.py:362
  41.0 12.7 %collective-permute-start.15 = (bf16[4,128,128]{2,1,0:T(8,128)(2,1)S(1)}, bf16[4,128,128]{2,1,0:T(8,128)(2,1)S(1)}, u32[]{:S(2)}, u32[]{:S(2)}) collective-permute-start(bf16[4,128,128]{2,1,0:T(8,128)(2,1)S(1)} %get-tuple-element.38), channel_id=1, source_target_pairs={{0,0},{1,1},{2,2},{3,3},{4,4},{5,5},{6,6},{7,7},{8,64},{9,65},{10,... | collective-permute-start | bytes 393224 | tf_op jit(solution)/shard_map/ppermute | solution.py:41
  53.8 0.3 collective-permute-start.10
  54.0 3.8 %collective-permute-start.11 = (bf16[2,128,128]{2,1,0:T(8,128)(2,1)S(1)}, bf16[2,128,128]{2,1,0:T(8,128)(2,1)S(1)}, u32[]{:S(2)}, u32[]{:S(2)}) collective-permute-start(bf16[2,128,128]{2,1,0:T(8,128)(2,1)S(1)} %get-tuple-element.34), channel_id=1, source_target_pairs={{0,2},{1,3},{2,0},{3,1},{4,6},{5,7},{6,4},{7,5},{8,10},{9,11},{10,... | collective-permute-start | bytes 196616 | tf_op jit(solution)/shard_map/ppermute | solution.py:45
  57.9 0.5 collective-permute-done.10.first
  58.4 1.9 %collective-permute-done.11.second = bf16[2,128,128]{2,1,0:T(8,128)(2,1)S(1)} collective-permute-done((bf16[2,128,128]{2,1,0:T(8,128)(2,1)S(1)}, bf16[2,128,128]{2,1,0:T(8,128)(2,1)S(1)}, u32[]{:S(2)}, u32[]{:S(2)}) %collective-permute-start.11) | collective-permute-done | bytes 65568 | tf_op jit(solution)/shard_map/ppermute | solution.py:45
  60.3 1.6 %collective-permute-done.12.third = bf16[2,128,128]{2,1,0:T(8,128)(2,1)S(1)} collective-permute-done((bf16[2,128,128]{2,1,0:T(8,128)(2,1)S(1)}, bf16[2,128,128]{2,1,0:T(8,128)(2,1)S(1)}, u32[]{:S(2)}, u32[]{:S(2)}) %collective-permute-start.12) | collective-permute-done | bytes 65568 | tf_op jit(solution)/shard_map/ppermute | solution.py:45
  61.9 5.1 %collective-permute-start.13 = (bf16[4,128,128]{2,1,0:T(8,128)(2,1)S(1)}, bf16[4,128,128]{2,1,0:T(8,128)(2,1)S(1)}, u32[]{:S(2)}, u32[]{:S(2)}) collective-permute-start(bf16[4,128,128]{2,1,0:T(8,128)(2,1)S(1)} %get-tuple-element.36), channel_id=1, source_target_pairs={{0,32},{1,33},{2,34},{3,35},{4,36},{5,37},{6,38},{7,39},{8,96},{9,... | collective-permute-start | bytes 393224 | tf_op jit(solution)/shard_map/ppermute | solution.py:41
  67.2 2.5 %collective-permute-start.18 = (bf16[2,128,128]{2,1,0:T(8,128)(2,1)S(1)}, bf16[2,128,128]{2,1,0:T(8,128)(2,1)S(1)}, u32[]{:S(2)}, u32[]{:S(2)}) collective-permute-start(bf16[2,128,128]{2,1,0:T(8,128)(2,1)S(1)} %get-tuple-element.41), channel_id=1, source_target_pairs={{0,2},{1,3},{2,0},{3,1},{4,6},{5,7},{6,4},{7,5},{8,10},{9,11},{10,... | collective-permute-start | bytes 196616 | tf_op jit(solution)/shard_map/ppermute | solution.py:45
  69.6 0.8 %collective-permute-start.19 = (bf16[2,128,128]{2,1,0:T(8,128)(2,1)S(1)}, bf16[2,128,128]{2,1,0:T(8,128)(2,1)S(1)}, u32[]{:S(2)}, u32[]{:S(2)}) collective-permute-start(bf16[2,128,128]{2,1,0:T(8,128)(2,1)S(1)} %get-tuple-element.42), channel_id=1, source_target_pairs={{0,3},{1,0},{2,1},{3,2},{4,7},{5,4},{6,5},{7,6},{8,11},{9,8},{10,9... | collective-permute-start | bytes 196616 | tf_op jit(solution)/shard_map/ppermute | solution.py:45
  70.5 0.4 fusion.place
  70.9 1.6 %collective-permute-done.17.refs_2_ = bf16[2,128,128]{2,1,0:T(8,128)(2,1)S(1)} collective-permute-done((bf16[2,128,128]{2,1,0:T(8,128)(2,1)S(1)}, bf16[2,128,128]{2,1,0:T(8,128)(2,1)S(1)}, u32[]{:S(2)}, u32[]{:S(2)}) %collective-permute-start.17) | collective-permute-done | bytes 65568 | tf_op jit(solution)/shard_map/ppermute | solution.py:45
  72.5 0.5 collective-permute-done.19.refs_4_
  73.0 2.4 %shard_map.80.refs_2_ = f32[8,16,8,512]{3,2,1,0:T(8,128)} custom-call(s32[2,2]{1,0:T(2,128)S(1)} %copy-done.2, s32[2,2]{1,0:T(2,128)S(1)} %copy-done.3, s32[8]{0:T(128)S(1)} %copy-done.4, f32[128,2048]{1,0:T(8,128)S(1)} %get-tuple-element.31.total, bf16[1024,1024]{1,0:T(8,128)(2,1)S(1)} %fusion.place, ...), custom_call_target="tpu_custom_call" | custom-call | flops 1000000000 | bytes 4194304 | tf_op jit(solution)/shard_map/pallas_call | solution.py:385
  75.5 2.8 %collective-permute-done.14.refs_1_ = bf16[4,128,128]{2,1,0:T(8,128)(2,1)S(1)} collective-permute-done((bf16[4,128,128]{2,1,0:T(8,128)(2,1)S(1)}, bf16[4,128,128]{2,1,0:T(8,128)(2,1)S(1)}, u32[]{:S(2)}, u32[]{:S(2)}) %collective-permute-start.14) | collective-permute-done | bytes 131104 | tf_op jit(solution)/shard_map/ppermute | solution.py:41
  78.3 2.4 %shard_map.81 = f32[8,16,8,512]{3,2,1,0:T(8,128)} custom-call(s32[2,2]{1,0:T(2,128)S(1)} %copy-done.2, s32[2,2]{1,0:T(2,128)S(1)} %copy-done.3, s32[8]{0:T(128)S(1)} %copy-done.4, f32[128,2048]{1,0:T(8,128)S(1)} %get-tuple-element.31.total, bf16[1024,1024]{1,0:T(8,128)(2,1)S(1)} %fusion.place, ...), custom_call_target="tpu_custom_call", output_to_operand_aliasing={{}: (7, {})} | custom-call | flops 1000000000 | bytes 4194304 | tf_op jit(solution)/shard_map/pallas_call | solution.py:394
  (37 shorter events, 0.7 us)
Async XLA Ops:
  3.2 11.6 %collective-permute-start = (bf16[416,512]{1,0:T(8,128)(2,1)}, bf16[416,512]{1,0:T(8,128)(2,1)S(1)}, u32[]{:S(2)}, u32[]{:S(2)}) collective-permute-start(bf16[416,512]{1,0:T(8,128)(2,1)} %get-tuple-element.24.refs_0_), channel_id=1, source_target_pairs={{0,3},{1,0},{2,1},{3,2},{4,7},{5,4},{6,5},{7,6},{8,11},{9,8},{10,9... | collective-permute-start | bytes 1277960 | tf_op jit(solution)/shard_map/ppermute | solution.py:312
  6.0 11.8 %collective-permute-start.1 = (bf16[416,512]{1,0:T(8,128)(2,1)}, bf16[416,512]{1,0:T(8,128)(2,1)S(1)}, u32[]{:S(2)}, u32[]{:S(2)}) collective-permute-start(bf16[416,512]{1,0:T(8,128)(2,1)} %get-tuple-element.24.refs_0_), channel_id=1, source_target_pairs={{0,1},{1,2},{2,3},{3,0},{4,5},{5,6},{6,7},{7,4},{8,9},{9,10},{10,1... | collective-permute-start | bytes 1277960 | tf_op jit(solution)/shard_map/ppermute | solution.py:313
  6.0 12.1 %collective-permute-start.2 = (bf16[416,512]{1,0:T(8,128)(2,1)}, bf16[416,512]{1,0:T(8,128)(2,1)S(1)}, u32[]{:S(2)}, u32[]{:S(2)}) collective-permute-start(bf16[416,512]{1,0:T(8,128)(2,1)} %get-tuple-element.24.refs_0_), channel_id=1, source_target_pairs={{0,4},{1,5},{2,6},{3,7},{4,0},{5,1},{6,2},{7,3},{8,12},{9,13},{10,... | collective-permute-start | bytes 1277960 | tf_op jit(solution)/shard_map/ppermute | solution.py:314
  7.8 5.1 %collective-permute-start.3 = (bf16[2,16,512]{2,1,0:T(8,128)(2,1)}, bf16[2,16,512]{2,1,0:T(8,128)(2,1)S(1)}, u32[]{:S(2)}, u32[]{:S(2)}) collective-permute-start(bf16[2,16,512]{2,1,0:T(8,128)(2,1)} %get-tuple-element.25), channel_id=1, source_target_pairs={{0,8},{8,16},{16,24},{1,9},{9,17},{17,25},{2,10},{10,18},{18,26},{... | collective-permute-start | bytes 98312 | tf_op jit(solution)/shard_map/ppermute | solution.py:352
  9.1 4.8 %collective-permute-start.4 = (bf16[2,16,512]{2,1,0:T(8,128)(2,1)}, bf16[2,16,512]{2,1,0:T(8,128)(2,1)S(1)}, u32[]{:S(2)}, u32[]{:S(2)}) collective-permute-start(bf16[2,16,512]{2,1,0:T(8,128)(2,1)} %get-tuple-element.27), channel_id=1, source_target_pairs={{8,0},{16,8},{24,16},{9,1},{17,9},{25,17},{10,2},{18,10},{26,18},{... | collective-permute-start | bytes 98312 | tf_op jit(solution)/shard_map/ppermute | solution.py:353
  18.1 11.0 %collective-permute-start.7 = (bf16[416,512]{1,0:T(8,128)(2,1)S(1)}, bf16[416,512]{1,0:T(8,128)(2,1)S(1)}, u32[]{:S(2)}, u32[]{:S(2)}) collective-permute-start(bf16[416,512]{1,0:T(8,128)(2,1)S(1)} %get-tuple-element.30), channel_id=1, source_target_pairs={{0,4},{1,5},{2,6},{3,7},{4,0},{5,1},{6,2},{7,3},{8,12},{9,13},{10,... | collective-permute-start | bytes 1277960 | tf_op jit(solution)/shard_map/ppermute | solution.py:325
  20.1 9.2 %collective-permute-start.6 = (bf16[416,512]{1,0:T(8,128)(2,1)S(1)}, bf16[416,512]{1,0:T(8,128)(2,1)S(1)}, u32[]{:S(2)}, u32[]{:S(2)}) collective-permute-start(bf16[416,512]{1,0:T(8,128)(2,1)S(1)} %get-tuple-element.29), channel_id=1, source_target_pairs={{0,3},{1,0},{2,1},{3,2},{4,7},{5,4},{6,5},{7,6},{8,11},{9,8},{10,9... | collective-permute-start | bytes 1277960 | tf_op jit(solution)/shard_map/ppermute | solution.py:327
  22.5 12.6 %collective-permute-start.5 = (bf16[416,512]{1,0:T(8,128)(2,1)S(1)}, bf16[416,512]{1,0:T(8,128)(2,1)S(1)}, u32[]{:S(2)}, u32[]{:S(2)}) collective-permute-start(bf16[416,512]{1,0:T(8,128)(2,1)S(1)} %get-tuple-element.28), channel_id=1, source_target_pairs={{0,1},{1,2},{2,3},{3,0},{4,5},{5,6},{6,7},{7,4},{8,9},{9,10},{10,1... | collective-permute-start | bytes 1277960 | tf_op jit(solution)/shard_map/ppermute | solution.py:326
  29.2 4.3 %slice-start = ((s8[8388608]{0:T(1024)(128)(4,1)}), s8[4194304]{0:T(1024)(128)(4,1)S(1)}, s32[]{:S(2)}) async-start(s8[8388608]{0:T(1024)(128)(4,1)} %bitcast.2), calls=%async_computation | async-start | bytes 8388608
  29.2 8.6 %collective-permute-start.8 = (bf16[208,512]{1,0:T(8,128)(2,1)S(1)}, bf16[208,512]{1,0:T(8,128)(2,1)S(1)}, u32[]{:S(2)}, u32[]{:S(2)}) collective-permute-start(bf16[208,512]{1,0:T(8,128)(2,1)S(1)} %slice.8), channel_id=1, source_target_pairs={{0,1},{1,2},{2,3},{3,0},{4,5},{5,6},{6,7},{7,4},{8,9},{9,10},{10,1... | collective-permute-start | bytes 638984 | tf_op jit(solution)/shard_map/ppermute | solution.py:328
  29.3 4.2 %slice-start.1 = ((s8[8388608]{0:T(1024)(128)(4,1)}), s8[4194304]{0:T(1024)(128)(4,1)S(1)}, s32[]{:S(2)}) async-start(s8[8388608]{0:T(1024)(128)(4,1)} %bitcast.2), calls=%async_computation.1 | async-start | bytes 8388608
  29.3 4.2 %copy-start = (bf16[416,512]{1,0:T(8,128)(2,1)S(1)}, bf16[416,512]{1,0:T(8,128)(2,1)}, u32[]{:S(2)}) copy-start(bf16[416,512]{1,0:T(8,128)(2,1)} %get-tuple-element.24.refs_0_) | copy-start | bytes 1277956
  29.4 8.5 %collective-permute-start.9 = (bf16[208,512]{1,0:T(8,128)(2,1)S(1)}, bf16[208,512]{1,0:T(8,128)(2,1)S(1)}, u32[]{:S(2)}, u32[]{:S(2)}) collective-permute-start(bf16[208,512]{1,0:T(8,128)(2,1)S(1)} %slice.9), channel_id=1, source_target_pairs={{0,3},{1,0},{2,1},{3,2},{4,7},{5,4},{6,5},{7,6},{8,11},{9,8},{10,9... | collective-permute-start | bytes 638984 | tf_op jit(solution)/shard_map/ppermute | solution.py:329
  33.5 4.3 %copy-start.1 = (bf16[16,16,512]{2,1,0:T(8,128)(2,1)S(1)}, bf16[16,16,512]{2,1,0:T(8,128)(2,1)}, u32[]{:S(2)}) copy-start(bf16[16,16,512]{2,1,0:T(8,128)(2,1)} %get-tuple-element.26.inner) | copy-start | bytes 786436
  37.8 32.6 %copy-start.5 = (s32[1024]{0:T(1024)S(1)}, s32[1024]{0:T(1024)}, u32[]{:S(2)}) copy-start(s32[1024]{0:T(1024)} %constant.2.clone) | copy-start | bytes 12292
  41.0 32.0 %copy-start.2 = (s32[2,2]{1,0:T(2,128)S(1)}, s32[2,2]{1,0:T(2,128)}, u32[]{:S(2)}) copy-start(s32[2,2]{1,0:T(2,128)} %ladder_tiles.3) | copy-start | bytes 52
  41.0 32.0 %copy-start.3 = (s32[2,2]{1,0:T(2,128)S(1)}, s32[2,2]{1,0:T(2,128)}, u32[]{:S(2)}) copy-start(s32[2,2]{1,0:T(2,128)} %cycle_tiles.3) | copy-start | bytes 52
  41.0 32.0 %copy-start.4 = (s32[8]{0:T(128)S(1)}, s32[8]{0:T(128)}, u32[]{:S(2)}) copy-start(s32[8]{0:T(128)} %partner.3) | copy-start | bytes 100
  41.0 26.1 %collective-permute-start.15 = (bf16[4,128,128]{2,1,0:T(8,128)(2,1)S(1)}, bf16[4,128,128]{2,1,0:T(8,128)(2,1)S(1)}, u32[]{:S(2)}, u32[]{:S(2)}) collective-permute-start(bf16[4,128,128]{2,1,0:T(8,128)(2,1)S(1)} %get-tuple-element.38), channel_id=1, source_target_pairs={{0,0},{1,1},{2,2},{3,3},{4,4},{5,5},{6,6},{7,7},{8,64},{9,65},{10,... | collective-permute-start | bytes 393224 | tf_op jit(solution)/shard_map/ppermute | solution.py:41
  53.7 13.4 %collective-permute-start.16 = (bf16[4,128,128]{2,1,0:T(8,128)(2,1)S(1)}, bf16[4,128,128]{2,1,0:T(8,128)(2,1)S(1)}, u32[]{:S(2)}, u32[]{:S(2)}) collective-permute-start(bf16[4,128,128]{2,1,0:T(8,128)(2,1)S(1)} %get-tuple-element.39), channel_id=1, source_target_pairs={{0,4},{1,5},{2,6},{3,7},{4,0},{5,1},{6,2},{7,3},{8,68},{9,69},{10,... | collective-permute-start | bytes 393224 | tf_op jit(solution)/shard_map/ppermute | solution.py:41
  53.8 4.6 %collective-permute-start.10 = (bf16[2,128,128]{2,1,0:T(8,128)(2,1)S(1)}, bf16[2,128,128]{2,1,0:T(8,128)(2,1)S(1)}, u32[]{:S(2)}, u32[]{:S(2)}) collective-permute-start(bf16[2,128,128]{2,1,0:T(8,128)(2,1)S(1)} %get-tuple-element.33), channel_id=1, source_target_pairs={{0,1},{1,2},{2,3},{3,0},{4,5},{5,6},{6,7},{7,4},{8,9},{9,10},{10,1... | collective-permute-start | bytes 196616 | tf_op jit(solution)/shard_map/ppermute | solution.py:45
  54.0 6.2 %collective-permute-start.11 = (bf16[2,128,128]{2,1,0:T(8,128)(2,1)S(1)}, bf16[2,128,128]{2,1,0:T(8,128)(2,1)S(1)}, u32[]{:S(2)}, u32[]{:S(2)}) collective-permute-start(bf16[2,128,128]{2,1,0:T(8,128)(2,1)S(1)} %get-tuple-element.34), channel_id=1, source_target_pairs={{0,2},{1,3},{2,0},{3,1},{4,6},{5,7},{6,4},{7,5},{8,10},{9,11},{10,... | collective-permute-start | bytes 196616 | tf_op jit(solution)/shard_map/ppermute | solution.py:45
  57.8 4.1 %collective-permute-start.12 = (bf16[2,128,128]{2,1,0:T(8,128)(2,1)S(1)}, bf16[2,128,128]{2,1,0:T(8,128)(2,1)S(1)}, u32[]{:S(2)}, u32[]{:S(2)}) collective-permute-start(bf16[2,128,128]{2,1,0:T(8,128)(2,1)S(1)} %get-tuple-element.35), channel_id=1, source_target_pairs={{0,3},{1,0},{2,1},{3,2},{4,7},{5,4},{6,5},{7,6},{8,11},{9,8},{10,9... | collective-permute-start | bytes 196616 | tf_op jit(solution)/shard_map/ppermute | solution.py:45
  61.9 13.6 %collective-permute-start.13 = (bf16[4,128,128]{2,1,0:T(8,128)(2,1)S(1)}, bf16[4,128,128]{2,1,0:T(8,128)(2,1)S(1)}, u32[]{:S(2)}, u32[]{:S(2)}) collective-permute-start(bf16[4,128,128]{2,1,0:T(8,128)(2,1)S(1)} %get-tuple-element.36), channel_id=1, source_target_pairs={{0,32},{1,33},{2,34},{3,35},{4,36},{5,37},{6,38},{7,39},{8,96},{9,... | collective-permute-start | bytes 393224 | tf_op jit(solution)/shard_map/ppermute | solution.py:41
  67.0 11.3 %collective-permute-start.14 = (bf16[4,128,128]{2,1,0:T(8,128)(2,1)S(1)}, bf16[4,128,128]{2,1,0:T(8,128)(2,1)S(1)}, u32[]{:S(2)}, u32[]{:S(2)}) collective-permute-start(bf16[4,128,128]{2,1,0:T(8,128)(2,1)S(1)} %get-tuple-element.37), channel_id=1, source_target_pairs={{0,36},{1,37},{2,38},{3,39},{4,32},{5,33},{6,34},{7,35},{8,100},{9... | collective-permute-start | bytes 393224 | tf_op jit(solution)/shard_map/ppermute | solution.py:41
  67.1 5.4 %collective-permute-start.17 = (bf16[2,128,128]{2,1,0:T(8,128)(2,1)S(1)}, bf16[2,128,128]{2,1,0:T(8,128)(2,1)S(1)}, u32[]{:S(2)}, u32[]{:S(2)}) collective-permute-start(bf16[2,128,128]{2,1,0:T(8,128)(2,1)S(1)} %get-tuple-element.40), channel_id=1, source_target_pairs={{0,1},{1,2},{2,3},{3,0},{4,5},{5,6},{6,7},{7,4},{8,9},{9,10},{10,1... | collective-permute-start | bytes 196616 | tf_op jit(solution)/shard_map/ppermute | solution.py:45
  67.2 5.3 %collective-permute-start.18 = (bf16[2,128,128]{2,1,0:T(8,128)(2,1)S(1)}, bf16[2,128,128]{2,1,0:T(8,128)(2,1)S(1)}, u32[]{:S(2)}, u32[]{:S(2)}) collective-permute-start(bf16[2,128,128]{2,1,0:T(8,128)(2,1)S(1)} %get-tuple-element.41), channel_id=1, source_target_pairs={{0,2},{1,3},{2,0},{3,1},{4,6},{5,7},{6,4},{7,5},{8,10},{9,11},{10,... | collective-permute-start | bytes 196616 | tf_op jit(solution)/shard_map/ppermute | solution.py:45
  69.6 3.3 %collective-permute-start.19 = (bf16[2,128,128]{2,1,0:T(8,128)(2,1)S(1)}, bf16[2,128,128]{2,1,0:T(8,128)(2,1)S(1)}, u32[]{:S(2)}, u32[]{:S(2)}) collective-permute-start(bf16[2,128,128]{2,1,0:T(8,128)(2,1)S(1)} %get-tuple-element.42), channel_id=1, source_target_pairs={{0,3},{1,0},{2,1},{3,2},{4,7},{5,4},{6,5},{7,6},{8,11},{9,8},{10,9... | collective-permute-start | bytes 196616 | tf_op jit(solution)/shard_map/ppermute | solution.py:45

commit v12 on v9

--- a/solution.py
+++ b/solution.py
@@ -183,9 +183,10 @@
 
 
 def near_kernel(ladder_ints, *refs):
+    far = far_pieces(list(refs[4:7]) + [None, None])
     for which, pieces in enumerate(near_pieces(refs[:4])):
-        refs[4][:, which * LANES : (which + 1) * LANES] = ladder_part(
-            which, pieces, ladder_ints, None
+        refs[7][:, which * LANES : (which + 1) * LANES] = ladder_part(
+            which, pieces + far[which][:3], ladder_ints, None
         )
 
 
@@ -234,7 +235,7 @@
                 total[j * 8 : j * 8 + 8, lane : lane + 128] = jnp.where(low, even, odd)
     for which in range(2):
         lanes = slice(which * LANES, (which + 1) * LANES)
-        total[:, lanes] = ladder_part(which, far[which], ladder_ints, near[:, lanes])
+        total[:, lanes] = ladder_part(which, far[which][3:], ladder_ints, near[:, lanes])
     both = jnp.concatenate([total[:, :1024], total[:, 1024:]], axis=0).astype(BF)
     lanes_buf[...] = jnp.dot(both, swap[...], preferred_element_type=F32).astype(BF)
     parity = lax.axis_index("pi") % 2
@@ -350,8 +351,8 @@
         swap_kernel, [HBM], shape((1024, 1024), BF), VMEM, [], 8, 2 * 10**10
     )(near[1])
     begun = call(
-        near_kernel, [VMEM] * 5, shape((PAIRS, 1024), F32), VMEM, [], 8, 10**9
-    )(ladder_ints, *near)
+        near_kernel, [VMEM] * 8, shape((PAIRS, 1024), F32), VMEM, [], 8, 10**9
+    )(ladder_ints, *near, *far[:3])
     four, two = shape((4, 128, 128), BF), shape((2, 128, 128), BF)
     total, same, other, late_0, late_1, late_2, late_3 = call(
         main_kernel,

time: 79.8 us -> 78.8 us (0.987)
    pallas_call x1, Pallas kernels: 3.1 us -> 2.07 us  [body(): call(main_kernel, [VMEM] * 15, [shape((PAIRS, 2048), F32), four, four, tw...]
    pallas_call x1, Pallas kernels: 1.48 us -> 2.49 us  [body(): call(near_kernel, [VMEM] * 8, shape((PAIRS, 1024), F32), VMEM, [], 8, 10...]
    ppermute x1, waiting for transfers between devices: 3.37 us -> 2.37 us  [gather(): up_3 = lax.ppermute(side_2[:HALF], 'vert', UP)]
  transfers between devices with their start and end apart: 20 -> 20, of which waited for: 9 -> 10; matrix products, arithmetic and copies ran while one was open for 1% -> 1% of each run, Pallas kernels for 3% -> 4%
where the time goes in v12:
time: 78.8 us; the launch traced here: 78.6 us
  starting transfers between devices  44.4 us (56%)
  waiting for transfers between devices  21 us (27%)
  Pallas kernels  11.9 us (15%)
    ppermute x4, starting transfers between devices, to_transposed(): return lax.ppermute(block, ('pi', 'pj', 'vert'), pair_moves(k, dx))  17.7 us
    ppermute x6, starting transfers between devices, along_y(): lax.ppermute(block, 'vert', vert_moves(lambda h, y: h * 4 + (y + dy) % 4))  7.41 us
    ppermute x1, waiting for transfers between devices, gather(): down_2 = lax.ppermute(to_down, 'vert', DOWN)  5.52 us
    ppermute x4, waiting for transfers between devices, to_transposed(): return lax.ppermute(block, ('pi', 'pj', 'vert'), pair_moves(k, dx))  4.51 us
    ppermute x6, waiting for transfers between devices, along_y(): lax.ppermute(block, 'vert', vert_moves(lambda h, y: h * 4 + (y + dy) % 4))  3.8 us
    ppermute x1, starting transfers between devices, gather(): down_3 = lax.ppermute(down_2[:HALF], 'vert', DOWN)  3.77 us
    ppermute x1, starting transfers between devices, body(): after = lax.ppermute(first, 'pj', [(q + 1, q) for q in range(3)])  3.64 us
    pallas_call x1, Pallas kernels, body(): call(finish_kernel, [SMEM, SMEM, SMEM] + [VMEM] * 9, shape((8, 16, 8, LAN...  3.28 us
  transfers between devices with their start and end apart: 20, of which 10 were waited for; matrix products, arithmetic and copies ran while one was open for 1% of the time, Pallas kernels for 4%

profile of v12, /device:TPU:6, one launch (start us, length us, event | category | flops | bytes accessed | tf_op | source)
XLA Modules:
  0.0 78.6 jit_solution(17149755510291822012)
XLA Ops:
  0.0 3.2 %shard_map.73 = (bf16[416,512]{1,0:T(8,128)(2,1)}, bf16[16,16,512]{2,1,0:T(8,128)(2,1)}, bf16[2,16,512]{2,1,0:T(8,128)(2,1)}, bf16[2,16,512]{2,1,0:T(8,128)(2,1)}) custom-call(s32[2,2]{1,0:T(2,128)} %ladder_tiles.1, s32[2,2]{1,0:T(2,128)} %cycle_tiles.1, bf16[1024,512]{1,0:T(8,128)(2,1)} %bitcast.4, bf16[80,2,512]{2,1,0:T(2,128)(2,1)} %bitcast.5), custom_call_target="tpu_custom_call" | custom-call | flops 1000000000 | bytes 4194304 | tf_op jit(solution)/shard_map/pallas_call | solution.py:330
  3.2 1.5 %collective-permute-start.2 = (bf16[416,512]{1,0:T(8,128)(2,1)}, bf16[416,512]{1,0:T(8,128)(2,1)S(1)}, u32[]{:S(2)}, u32[]{:S(2)}) collective-permute-start(bf16[416,512]{1,0:T(8,128)(2,1)} %get-tuple-element.24.refs_0_), channel_id=1, source_target_pairs={{0,4},{1,5},{2,6},{3,7},{4,0},{5,1},{6,2},{7,3},{8,12},{9,13},{10,... | collective-permute-start | bytes 1277960 | tf_op jit(solution)/shard_map/ppermute | solution.py:309
  4.7 1.6 %collective-permute-start.1 = (bf16[416,512]{1,0:T(8,128)(2,1)}, bf16[416,512]{1,0:T(8,128)(2,1)S(1)}, u32[]{:S(2)}, u32[]{:S(2)}) collective-permute-start(bf16[416,512]{1,0:T(8,128)(2,1)} %get-tuple-element.24.refs_0_), channel_id=1, source_target_pairs={{0,1},{1,2},{2,3},{3,0},{4,5},{5,6},{6,7},{7,4},{8,9},{9,10},{10,1... | collective-permute-start | bytes 1277960 | tf_op jit(solution)/shard_map/ppermute | solution.py:308
  6.2 1.7 %collective-permute-start = (bf16[416,512]{1,0:T(8,128)(2,1)}, bf16[416,512]{1,0:T(8,128)(2,1)S(1)}, u32[]{:S(2)}, u32[]{:S(2)}) collective-permute-start(bf16[416,512]{1,0:T(8,128)(2,1)} %get-tuple-element.24.refs_0_), channel_id=1, source_target_pairs={{0,3},{1,0},{2,1},{3,2},{4,7},{5,4},{6,5},{7,6},{8,11},{9,8},{10,9... | collective-permute-start | bytes 1277960 | tf_op jit(solution)/shard_map/ppermute | solution.py:307
  7.9 1.9 %collective-permute-start.3 = (bf16[2,16,512]{2,1,0:T(8,128)(2,1)}, bf16[2,16,512]{2,1,0:T(8,128)(2,1)S(1)}, u32[]{:S(2)}, u32[]{:S(2)}) collective-permute-start(bf16[2,16,512]{2,1,0:T(8,128)(2,1)} %get-tuple-element.25), channel_id=1, source_target_pairs={{0,8},{8,16},{16,24},{1,9},{9,17},{17,25},{2,10},{10,18},{18,26},{... | collective-permute-start | bytes 98312 | tf_op jit(solution)/shard_map/ppermute | solution.py:347
  9.8 3.6 %collective-permute-start.4 = (bf16[2,16,512]{2,1,0:T(8,128)(2,1)}, bf16[2,16,512]{2,1,0:T(8,128)(2,1)S(1)}, u32[]{:S(2)}, u32[]{:S(2)}) collective-permute-start(bf16[2,16,512]{2,1,0:T(8,128)(2,1)} %get-tuple-element.26), channel_id=1, source_target_pairs={{8,0},{16,8},{24,16},{9,1},{17,9},{25,17},{10,2},{18,10},{26,18},{... | collective-permute-start | bytes 98312 | tf_op jit(solution)/shard_map/ppermute | solution.py:348
  13.7 1.6 %collective-permute-done.4.after = bf16[2,16,512]{2,1,0:T(8,128)(2,1)S(1)} collective-permute-done((bf16[2,16,512]{2,1,0:T(8,128)(2,1)}, bf16[2,16,512]{2,1,0:T(8,128)(2,1)S(1)}, u32[]{:S(2)}, u32[]{:S(2)}) %collective-permute-start.4) | collective-permute-done | bytes 32800 | tf_op jit(solution)/shard_map/ppermute | solution.py:348
  15.3 1.2 %collective-permute-done.2.flip.refs_3_ = bf16[416,512]{1,0:T(8,128)(2,1)S(1)} collective-permute-done((bf16[416,512]{1,0:T(8,128)(2,1)}, bf16[416,512]{1,0:T(8,128)(2,1)S(1)}, u32[]{:S(2)}, u32[]{:S(2)}) %collective-permute-start.2) | collective-permute-done | bytes 426016 | tf_op jit(solution)/shard_map/ppermute | solution.py:309
  16.5 0.9 %collective-permute-done.1.up.refs_2_ = bf16[416,512]{1,0:T(8,128)(2,1)S(1)} collective-permute-done((bf16[416,512]{1,0:T(8,128)(2,1)}, bf16[416,512]{1,0:T(8,128)(2,1)S(1)}, u32[]{:S(2)}, u32[]{:S(2)}) %collective-permute-start.1) | collective-permute-done | bytes 426016 | tf_op jit(solution)/shard_map/ppermute | solution.py:308
  17.5 3.0 %collective-permute-start.6 = (bf16[416,512]{1,0:T(8,128)(2,1)S(1)}, bf16[416,512]{1,0:T(8,128)(2,1)S(1)}, u32[]{:S(2)}, u32[]{:S(2)}) collective-permute-start(bf16[416,512]{1,0:T(8,128)(2,1)S(1)} %get-tuple-element.28), channel_id=1, source_target_pairs={{0,3},{1,0},{2,1},{3,2},{4,7},{5,4},{6,5},{7,6},{8,11},{9,8},{10,9... | collective-permute-start | bytes 1277960 | tf_op jit(solution)/shard_map/ppermute | solution.py:322
  20.5 2.1 %collective-permute-start.7 = (bf16[416,512]{1,0:T(8,128)(2,1)S(1)}, bf16[416,512]{1,0:T(8,128)(2,1)S(1)}, u32[]{:S(2)}, u32[]{:S(2)}) collective-permute-start(bf16[416,512]{1,0:T(8,128)(2,1)S(1)} %get-tuple-element.29), channel_id=1, source_target_pairs={{0,4},{1,5},{2,6},{3,7},{4,0},{5,1},{6,2},{7,3},{8,12},{9,13},{10,... | collective-permute-start | bytes 1277960 | tf_op jit(solution)/shard_map/ppermute | solution.py:320
  22.7 5.5 %collective-permute-done.6.refs_5_ = bf16[416,512]{1,0:T(8,128)(2,1)S(1)} collective-permute-done((bf16[416,512]{1,0:T(8,128)(2,1)S(1)}, bf16[416,512]{1,0:T(8,128)(2,1)S(1)}, u32[]{:S(2)}, u32[]{:S(2)}) %collective-permute-start.6) | collective-permute-done | bytes 426016 | tf_op jit(solution)/shard_map/ppermute | solution.py:322
  28.2 3.8 %collective-permute-start.9 = (bf16[208,512]{1,0:T(8,128)(2,1)S(1)}, bf16[208,512]{1,0:T(8,128)(2,1)S(1)}, u32[]{:S(2)}, u32[]{:S(2)}) collective-permute-start(bf16[208,512]{1,0:T(8,128)(2,1)S(1)} %slice.9), channel_id=1, source_target_pairs={{0,3},{1,0},{2,1},{3,2},{4,7},{5,4},{6,5},{7,6},{8,11},{9,8},{10,9... | collective-permute-start | bytes 638984 | tf_op jit(solution)/shard_map/ppermute | solution.py:324
  32.1 0.8 %shard_map.76.swap = bf16[1024,1024]{1,0:T(8,128)(2,1)S(1)} custom-call(bf16[416,512]{1,0:T(8,128)(2,1)S(1)} %collective-permute-done.down.refs_1_.after), custom_call_target="tpu_custom_call" | custom-call | flops 20000000000 | bytes 4194304 | tf_op jit(solution)/shard_map/pallas_call | solution.py:350
  33.0 0.8 collective-permute-done.5.refs_4_
  33.7 0.5 slice-done.1
  34.3 2.5 %shard_map.75.near = f32[128,1024]{1,0:T(8,128)S(1)} custom-call(bf16[2,512,4096]{2,1,0:T(8,128)(2,1)S(1)} %bitcast.3, bf16[416,512]{1,0:T(8,128)(2,1)S(1)} %copy-done, bf16[416,512]{1,0:T(8,128)(2,1)S(1)} %collective-permute-done.down.refs_1_.after, bf16[416,512]{1,0:T(8,128)(2,1)S(1)} %collective-permute-done.1.up.refs_2_, ...), custom_call_target="tpu_custom_call" | custom-call | flops 1000000000 | bytes 4194304 | tf_op jit(solution)/shard_map/pallas_call | solution.py:353
  36.8 2.4 %collective-permute-done.8.refs_7_ = bf16[208,512]{1,0:T(8,128)(2,1)S(1)} collective-permute-done((bf16[208,512]{1,0:T(8,128)(2,1)S(1)}, bf16[208,512]{1,0:T(8,128)(2,1)S(1)}, u32[]{:S(2)}, u32[]{:S(2)}) %collective-permute-start.8) | collective-permute-done | bytes 213024 | tf_op jit(solution)/shard_map/ppermute | solution.py:323
  39.2 2.1 %shard_map.77 = (f32[128,2048]{1,0:T(8,128)S(1)}, bf16[4,128,128]{2,1,0:T(8,128)(2,1)S(1)}, bf16[4,128,128]{2,1,0:T(8,128)(2,1)S(1)}, bf16[2,128,128]{2,1,0:T(8,...) custom-call(bf16[2,512,4096]{2,1,0:T(8,128)(2,1)S(1)} %bitcast.3, ...), custom_call_target="tpu_custom_call" | custom-call | flops 2000000000 | bytes 4194304 | tf_op jit(solution)/shard_map/pallas_call | solution.py:357
  41.3 9.8 %collective-permute-start.10 = (bf16[4,128,128]{2,1,0:T(8,128)(2,1)S(1)}, bf16[4,128,128]{2,1,0:T(8,128)(2,1)S(1)}, u32[]{:S(2)}, u32[]{:S(2)}) collective-permute-start(bf16[4,128,128]{2,1,0:T(8,128)(2,1)S(1)} %get-tuple-element.32), channel_id=1, source_target_pairs={{0,0},{1,1},{2,2},{3,3},{4,4},{5,5},{6,6},{7,7},{8,64},{9,65},{10,... | collective-permute-start | bytes 393224 | tf_op jit(solution)/shard_map/ppermute | solution.py:39
  51.1 1.1 %collective-permute-start.11 = (bf16[4,128,128]{2,1,0:T(8,128)(2,1)S(1)}, bf16[4,128,128]{2,1,0:T(8,128)(2,1)S(1)}, u32[]{:S(2)}, u32[]{:S(2)}) collective-permute-start(bf16[4,128,128]{2,1,0:T(8,128)(2,1)S(1)} %get-tuple-element.33), channel_id=1, source_target_pairs={{0,4},{1,5},{2,6},{3,7},{4,0},{5,1},{6,2},{7,3},{8,68},{9,69},{10,... | collective-permute-start | bytes 393224 | tf_op jit(solution)/shard_map/ppermute | solution.py:39
  52.2 1.4 %collective-permute-start.16 = (bf16[2,128,128]{2,1,0:T(8,128)(2,1)S(1)}, bf16[2,128,128]{2,1,0:T(8,128)(2,1)S(1)}, u32[]{:S(2)}, u32[]{:S(2)}) collective-permute-start(bf16[2,128,128]{2,1,0:T(8,128)(2,1)S(1)} %get-tuple-element.39), channel_id=1, source_target_pairs={{0,2},{1,3},{2,0},{3,1},{4,6},{5,7},{6,4},{7,5},{8,10},{9,11},{10,... | collective-permute-start | bytes 196616 | tf_op jit(solution)/shard_map/ppermute | solution.py:43
  53.5 1.9 %collective-permute-start.17 = (bf16[2,128,128]{2,1,0:T(8,128)(2,1)S(1)}, bf16[2,128,128]{2,1,0:T(8,128)(2,1)S(1)}, u32[]{:S(2)}, u32[]{:S(2)}) collective-permute-start(bf16[2,128,128]{2,1,0:T(8,128)(2,1)S(1)} %get-tuple-element.40), channel_id=1, source_target_pairs={{0,3},{1,0},{2,1},{3,2},{4,7},{5,4},{6,5},{7,6},{8,11},{9,8},{10,9... | collective-permute-start | bytes 196616 | tf_op jit(solution)/shard_map/ppermute | solution.py:43
  55.4 2.9 %collective-permute-done.15.first = bf16[2,128,128]{2,1,0:T(8,128)(2,1)S(1)} collective-permute-done((bf16[2,128,128]{2,1,0:T(8,128)(2,1)S(1)}, bf16[2,128,128]{2,1,0:T(8,128)(2,1)S(1)}, u32[]{:S(2)}, u32[]{:S(2)}) %collective-permute-start.15) | collective-permute-done | bytes 65568 | tf_op jit(solution)/shard_map/ppermute | solution.py:43
  58.3 0.9 %collective-permute-done.17.third = bf16[2,128,128]{2,1,0:T(8,128)(2,1)S(1)} collective-permute-done((bf16[2,128,128]{2,1,0:T(8,128)(2,1)S(1)}, bf16[2,128,128]{2,1,0:T(8,128)(2,1)S(1)}, u32[]{:S(2)}, u32[]{:S(2)}) %collective-permute-start.17) | collective-permute-done | bytes 65568 | tf_op jit(solution)/shard_map/ppermute | solution.py:43
  59.2 5.9 %collective-permute-start.18 = (bf16[4,128,128]{2,1,0:T(8,128)(2,1)S(1)}, bf16[4,128,128]{2,1,0:T(8,128)(2,1)S(1)}, u32[]{:S(2)}, u32[]{:S(2)}) collective-permute-start(bf16[4,128,128]{2,1,0:T(8,128)(2,1)S(1)} %get-tuple-element.41), channel_id=1, source_target_pairs={{0,32},{1,33},{2,34},{3,35},{4,36},{5,37},{6,38},{7,39},{8,96},{9,... | collective-permute-start | bytes 393224 | tf_op jit(solution)/shard_map/ppermute | solution.py:39
  65.1 1.0 %collective-permute-start.19 = (bf16[4,128,128]{2,1,0:T(8,128)(2,1)S(1)}, bf16[4,128,128]{2,1,0:T(8,128)(2,1)S(1)}, u32[]{:S(2)}, u32[]{:S(2)}) collective-permute-start(bf16[4,128,128]{2,1,0:T(8,128)(2,1)S(1)} %get-tuple-element.42), channel_id=1, source_target_pairs={{0,36},{1,37},{2,38},{3,39},{4,32},{5,33},{6,34},{7,35},{8,100},{9... | collective-permute-start | bytes 393224 | tf_op jit(solution)/shard_map/ppermute | solution.py:39
  66.1 1.4 %collective-permute-start.12 = (bf16[2,128,128]{2,1,0:T(8,128)(2,1)S(1)}, bf16[2,128,128]{2,1,0:T(8,128)(2,1)S(1)}, u32[]{:S(2)}, u32[]{:S(2)}) collective-permute-start(bf16[2,128,128]{2,1,0:T(8,128)(2,1)S(1)} %get-tuple-element.34), channel_id=1, source_target_pairs={{0,1},{1,2},{2,3},{3,0},{4,5},{5,6},{6,7},{7,4},{8,9},{9,10},{10,1... | collective-permute-start | bytes 196616 | tf_op jit(solution)/shard_map/ppermute | solution.py:43
  67.5 2.5 %collective-permute-start.13 = (bf16[2,128,128]{2,1,0:T(8,128)(2,1)S(1)}, bf16[2,128,128]{2,1,0:T(8,128)(2,1)S(1)}, u32[]{:S(2)}, u32[]{:S(2)}) collective-permute-start(bf16[2,128,128]{2,1,0:T(8,128)(2,1)S(1)} %get-tuple-element.35), channel_id=1, source_target_pairs={{0,2},{1,3},{2,0},{3,1},{4,6},{5,7},{6,4},{7,5},{8,10},{9,11},{10,... | collective-permute-start | bytes 196616 | tf_op jit(solution)/shard_map/ppermute | solution.py:43
  70.2 0.4 fusion.place
  70.7 4.5 %collective-permute-done.19.refs_6_ = bf16[4,128,128]{2,1,0:T(8,128)(2,1)S(1)} collective-permute-done((bf16[4,128,128]{2,1,0:T(8,128)(2,1)S(1)}, bf16[4,128,128]{2,1,0:T(8,128)(2,1)S(1)}, u32[]{:S(2)}, u32[]{:S(2)}) %collective-permute-start.19) | collective-permute-done | bytes 131104 | tf_op jit(solution)/shard_map/ppermute | solution.py:39
  75.2 3.3 %shard_map.80 = f32[8,16,8,512]{3,2,1,0:T(8,128)} custom-call(s32[2,2]{1,0:T(2,128)S(1)} %copy-done.2, s32[2,2]{1,0:T(2,128)S(1)} %copy-done.3, s32[8]{0:T(128)S(1)} %copy-done.4, f32[128,2048]{1,0:T(8,128)S(1)} %get-tuple-element.31.total, bf16[1024,1024]{1,0:T(8,128)(2,1)S(1)} %fusion.place, bf16[4,128,128]{2,1,0:T(8,128)(2,1)S(1)} %collective-permute-done.10.same.refs_0_, ...), custom_call_target="tpu_custom_call" | custom-call | flops 1000000000 | bytes 4194304 | tf_op jit(solution)/shard_map/pallas_call | solution.py:372
  (36 shorter events, 0.9 us)
Async XLA Ops:
  3.2 13.4 %collective-permute-start.2 = (bf16[416,512]{1,0:T(8,128)(2,1)}, bf16[416,512]{1,0:T(8,128)(2,1)S(1)}, u32[]{:S(2)}, u32[]{:S(2)}) collective-permute-start(bf16[416,512]{1,0:T(8,128)(2,1)} %get-tuple-element.24.refs_0_), channel_id=1, source_target_pairs={{0,4},{1,5},{2,6},{3,7},{4,0},{5,1},{6,2},{7,3},{8,12},{9,13},{10,... | collective-permute-start | bytes 1277960 | tf_op jit(solution)/shard_map/ppermute | solution.py:309
  4.7 12.8 %collective-permute-start.1 = (bf16[416,512]{1,0:T(8,128)(2,1)}, bf16[416,512]{1,0:T(8,128)(2,1)S(1)}, u32[]{:S(2)}, u32[]{:S(2)}) collective-permute-start(bf16[416,512]{1,0:T(8,128)(2,1)} %get-tuple-element.24.refs_0_), channel_id=1, source_target_pairs={{0,1},{1,2},{2,3},{3,0},{4,5},{5,6},{6,7},{7,4},{8,9},{9,10},{10,1... | collective-permute-start | bytes 1277960 | tf_op jit(solution)/shard_map/ppermute | solution.py:308
  6.2 11.2 %collective-permute-start = (bf16[416,512]{1,0:T(8,128)(2,1)}, bf16[416,512]{1,0:T(8,128)(2,1)S(1)}, u32[]{:S(2)}, u32[]{:S(2)}) collective-permute-start(bf16[416,512]{1,0:T(8,128)(2,1)} %get-tuple-element.24.refs_0_), channel_id=1, source_target_pairs={{0,3},{1,0},{2,1},{3,2},{4,7},{5,4},{6,5},{7,6},{8,11},{9,8},{10,9... | collective-permute-start | bytes 1277960 | tf_op jit(solution)/shard_map/ppermute | solution.py:307
  7.9 5.8 %collective-permute-start.3 = (bf16[2,16,512]{2,1,0:T(8,128)(2,1)}, bf16[2,16,512]{2,1,0:T(8,128)(2,1)S(1)}, u32[]{:S(2)}, u32[]{:S(2)}) collective-permute-start(bf16[2,16,512]{2,1,0:T(8,128)(2,1)} %get-tuple-element.25), channel_id=1, source_target_pairs={{0,8},{8,16},{16,24},{1,9},{9,17},{17,25},{2,10},{10,18},{18,26},{... | collective-permute-start | bytes 98312 | tf_op jit(solution)/shard_map/ppermute | solution.py:347
  9.8 5.5 %collective-permute-start.4 = (bf16[2,16,512]{2,1,0:T(8,128)(2,1)}, bf16[2,16,512]{2,1,0:T(8,128)(2,1)S(1)}, u32[]{:S(2)}, u32[]{:S(2)}) collective-permute-start(bf16[2,16,512]{2,1,0:T(8,128)(2,1)} %get-tuple-element.26), channel_id=1, source_target_pairs={{8,0},{16,8},{24,16},{9,1},{17,9},{25,17},{10,2},{18,10},{26,18},{... | collective-permute-start | bytes 98312 | tf_op jit(solution)/shard_map/ppermute | solution.py:348
  17.5 10.6 %collective-permute-start.6 = (bf16[416,512]{1,0:T(8,128)(2,1)S(1)}, bf16[416,512]{1,0:T(8,128)(2,1)S(1)}, u32[]{:S(2)}, u32[]{:S(2)}) collective-permute-start(bf16[416,512]{1,0:T(8,128)(2,1)S(1)} %get-tuple-element.28), channel_id=1, source_target_pairs={{0,3},{1,0},{2,1},{3,2},{4,7},{5,4},{6,5},{7,6},{8,11},{9,8},{10,9... | collective-permute-start | bytes 1277960 | tf_op jit(solution)/shard_map/ppermute | solution.py:322
  20.5 11.4 %collective-permute-start.7 = (bf16[416,512]{1,0:T(8,128)(2,1)S(1)}, bf16[416,512]{1,0:T(8,128)(2,1)S(1)}, u32[]{:S(2)}, u32[]{:S(2)}) collective-permute-start(bf16[416,512]{1,0:T(8,128)(2,1)S(1)} %get-tuple-element.29), channel_id=1, source_target_pairs={{0,4},{1,5},{2,6},{3,7},{4,0},{5,1},{6,2},{7,3},{8,12},{9,13},{10,... | collective-permute-start | bytes 1277960 | tf_op jit(solution)/shard_map/ppermute | solution.py:320
  22.7 11.1 %collective-permute-start.5 = (bf16[416,512]{1,0:T(8,128)(2,1)S(1)}, bf16[416,512]{1,0:T(8,128)(2,1)S(1)}, u32[]{:S(2)}, u32[]{:S(2)}) collective-permute-start(bf16[416,512]{1,0:T(8,128)(2,1)S(1)} %get-tuple-element.27), channel_id=1, source_target_pairs={{0,1},{1,2},{2,3},{3,0},{4,5},{5,6},{6,7},{7,4},{8,9},{9,10},{10,1... | collective-permute-start | bytes 1277960 | tf_op jit(solution)/shard_map/ppermute | solution.py:321
  28.2 5.5 %slice-start = ((s8[8388608]{0:T(1024)(128)(4,1)}), s8[4194304]{0:T(1024)(128)(4,1)S(1)}, s32[]{:S(2)}) async-start(s8[8388608]{0:T(1024)(128)(4,1)} %bitcast.2), calls=%async_computation | async-start | bytes 8388608
  28.2 8.6 %collective-permute-start.9 = (bf16[208,512]{1,0:T(8,128)(2,1)S(1)}, bf16[208,512]{1,0:T(8,128)(2,1)S(1)}, u32[]{:S(2)}, u32[]{:S(2)}) collective-permute-start(bf16[208,512]{1,0:T(8,128)(2,1)S(1)} %slice.9), channel_id=1, source_target_pairs={{0,3},{1,0},{2,1},{3,2},{4,7},{5,4},{6,5},{7,6},{8,11},{9,8},{10,9... | collective-permute-start | bytes 638984 | tf_op jit(solution)/shard_map/ppermute | solution.py:324
  32.0 2.2 %slice-start.1 = ((s8[8388608]{0:T(1024)(128)(4,1)}), s8[4194304]{0:T(1024)(128)(4,1)S(1)}, s32[]{:S(2)}) async-start(s8[8388608]{0:T(1024)(128)(4,1)} %bitcast.2), calls=%async_computation.1 | async-start | bytes 8388608
  32.0 2.3 %copy-start = (bf16[416,512]{1,0:T(8,128)(2,1)S(1)}, bf16[416,512]{1,0:T(8,128)(2,1)}, u32[]{:S(2)}) copy-start(bf16[416,512]{1,0:T(8,128)(2,1)} %get-tuple-element.24.refs_0_) | copy-start | bytes 1277956
  32.0 7.1 %collective-permute-start.8 = (bf16[208,512]{1,0:T(8,128)(2,1)S(1)}, bf16[208,512]{1,0:T(8,128)(2,1)S(1)}, u32[]{:S(2)}, u32[]{:S(2)}) collective-permute-start(bf16[208,512]{1,0:T(8,128)(2,1)S(1)} %slice.8), channel_id=1, source_target_pairs={{0,1},{1,2},{2,3},{3,0},{4,5},{5,6},{6,7},{7,4},{8,9},{9,10},{10,1... | collective-permute-start | bytes 638984 | tf_op jit(solution)/shard_map/ppermute | solution.py:323
  32.9 6.2 %copy-start.1 = (bf16[16,16,512]{2,1,0:T(8,128)(2,1)S(1)}, bf16[16,16,512]{2,1,0:T(8,128)(2,1)}, u32[]{:S(2)}) copy-start(bf16[16,16,512]{2,1,0:T(8,128)(2,1)} %get-tuple-element.30.inner) | copy-start | bytes 786436
  39.2 31.1 %copy-start.5 = (s32[1024]{0:T(1024)S(1)}, s32[1024]{0:T(1024)}, u32[]{:S(2)}) copy-start(s32[1024]{0:T(1024)} %constant.2.clone) | copy-start | bytes 12292
  41.2 33.9 %copy-start.2 = (s32[2,2]{1,0:T(2,128)S(1)}, s32[2,2]{1,0:T(2,128)}, u32[]{:S(2)}) copy-start(s32[2,2]{1,0:T(2,128)} %ladder_tiles.1) | copy-start | bytes 52
  41.3 33.9 %copy-start.3 = (s32[2,2]{1,0:T(2,128)S(1)}, s32[2,2]{1,0:T(2,128)}, u32[]{:S(2)}) copy-start(s32[2,2]{1,0:T(2,128)} %cycle_tiles.1) | copy-start | bytes 52
  41.3 33.9 %copy-start.4 = (s32[8]{0:T(128)S(1)}, s32[8]{0:T(128)}, u32[]{:S(2)}) copy-start(s32[8]{0:T(128)} %partner.1) | copy-start | bytes 100
  41.3 24.8 %collective-permute-start.10 = (bf16[4,128,128]{2,1,0:T(8,128)(2,1)S(1)}, bf16[4,128,128]{2,1,0:T(8,128)(2,1)S(1)}, u32[]{:S(2)}, u32[]{:S(2)}) collective-permute-start(bf16[4,128,128]{2,1,0:T(8,128)(2,1)S(1)} %get-tuple-element.32), channel_id=1, source_target_pairs={{0,0},{1,1},{2,2},{3,3},{4,4},{5,5},{6,6},{7,7},{8,64},{9,65},{10,... | collective-permute-start | bytes 393224 | tf_op jit(solution)/shard_map/ppermute | solution.py:39
  51.1 14.9 %collective-permute-start.11 = (bf16[4,128,128]{2,1,0:T(8,128)(2,1)S(1)}, bf16[4,128,128]{2,1,0:T(8,128)(2,1)S(1)}, u32[]{:S(2)}, u32[]{:S(2)}) collective-permute-start(bf16[4,128,128]{2,1,0:T(8,128)(2,1)S(1)} %get-tuple-element.33), channel_id=1, source_target_pairs={{0,4},{1,5},{2,6},{3,7},{4,0},{5,1},{6,2},{7,3},{8,68},{9,69},{10,... | collective-permute-start | bytes 393224 | tf_op jit(solution)/shard_map/ppermute | solution.py:39
  52.2 6.2 %collective-permute-start.15 = (bf16[2,128,128]{2,1,0:T(8,128)(2,1)S(1)}, bf16[2,128,128]{2,1,0:T(8,128)(2,1)S(1)}, u32[]{:S(2)}, u32[]{:S(2)}) collective-permute-start(bf16[2,128,128]{2,1,0:T(8,128)(2,1)S(1)} %get-tuple-element.38), channel_id=1, source_target_pairs={{0,1},{1,2},{2,3},{3,0},{4,5},{5,6},{6,7},{7,4},{8,9},{9,10},{10,1... | collective-permute-start | bytes 196616 | tf_op jit(solution)/shard_map/ppermute | solution.py:43
  52.2 6.2 %collective-permute-start.16 = (bf16[2,128,128]{2,1,0:T(8,128)(2,1)S(1)}, bf16[2,128,128]{2,1,0:T(8,128)(2,1)S(1)}, u32[]{:S(2)}, u32[]{:S(2)}) collective-permute-start(bf16[2,128,128]{2,1,0:T(8,128)(2,1)S(1)} %get-tuple-element.39), channel_id=1, source_target_pairs={{0,2},{1,3},{2,0},{3,1},{4,6},{5,7},{6,4},{7,5},{8,10},{9,11},{10,... | collective-permute-start | bytes 196616 | tf_op jit(solution)/shard_map/ppermute | solution.py:43
  53.5 5.7 %collective-permute-start.17 = (bf16[2,128,128]{2,1,0:T(8,128)(2,1)S(1)}, bf16[2,128,128]{2,1,0:T(8,128)(2,1)S(1)}, u32[]{:S(2)}, u32[]{:S(2)}) collective-permute-start(bf16[2,128,128]{2,1,0:T(8,128)(2,1)S(1)} %get-tuple-element.40), channel_id=1, source_target_pairs={{0,3},{1,0},{2,1},{3,2},{4,7},{5,4},{6,5},{7,6},{8,11},{9,8},{10,9... | collective-permute-start | bytes 196616 | tf_op jit(solution)/shard_map/ppermute | solution.py:43
  59.2 11.4 %collective-permute-start.18 = (bf16[4,128,128]{2,1,0:T(8,128)(2,1)S(1)}, bf16[4,128,128]{2,1,0:T(8,128)(2,1)S(1)}, u32[]{:S(2)}, u32[]{:S(2)}) collective-permute-start(bf16[4,128,128]{2,1,0:T(8,128)(2,1)S(1)} %get-tuple-element.41), channel_id=1, source_target_pairs={{0,32},{1,33},{2,34},{3,35},{4,36},{5,37},{6,38},{7,39},{8,96},{9,... | collective-permute-start | bytes 393224 | tf_op jit(solution)/shard_map/ppermute | solution.py:39
  65.1 10.1 %collective-permute-start.19 = (bf16[4,128,128]{2,1,0:T(8,128)(2,1)S(1)}, bf16[4,128,128]{2,1,0:T(8,128)(2,1)S(1)}, u32[]{:S(2)}, u32[]{:S(2)}) collective-permute-start(bf16[4,128,128]{2,1,0:T(8,128)(2,1)S(1)} %get-tuple-element.42), channel_id=1, source_target_pairs={{0,36},{1,37},{2,38},{3,39},{4,32},{5,33},{6,34},{7,35},{8,100},{9... | collective-permute-start | bytes 393224 | tf_op jit(solution)/shard_map/ppermute | solution.py:39
  66.1 9.1 %collective-permute-start.12 = (bf16[2,128,128]{2,1,0:T(8,128)(2,1)S(1)}, bf16[2,128,128]{2,1,0:T(8,128)(2,1)S(1)}, u32[]{:S(2)}, u32[]{:S(2)}) collective-permute-start(bf16[2,128,128]{2,1,0:T(8,128)(2,1)S(1)} %get-tuple-element.34), channel_id=1, source_target_pairs={{0,1},{1,2},{2,3},{3,0},{4,5},{5,6},{6,7},{7,4},{8,9},{9,10},{10,1... | collective-permute-start | bytes 196616 | tf_op jit(solution)/shard_map/ppermute | solution.py:43
  67.5 7.7 %collective-permute-start.13 = (bf16[2,128,128]{2,1,0:T(8,128)(2,1)S(1)}, bf16[2,128,128]{2,1,0:T(8,128)(2,1)S(1)}, u32[]{:S(2)}, u32[]{:S(2)}) collective-permute-start(bf16[2,128,128]{2,1,0:T(8,128)(2,1)S(1)} %get-tuple-element.35), channel_id=1, source_target_pairs={{0,2},{1,3},{2,0},{3,1},{4,6},{5,7},{6,4},{7,5},{8,10},{9,11},{10,... | collective-permute-start | bytes 196616 | tf_op jit(solution)/shard_map/ppermute | solution.py:43
  70.0 5.2 %collective-permute-start.14 = (bf16[2,128,128]{2,1,0:T(8,128)(2,1)S(1)}, bf16[2,128,128]{2,1,0:T(8,128)(2,1)S(1)}, u32[]{:S(2)}, u32[]{:S(2)}) collective-permute-start(bf16[2,128,128]{2,1,0:T(8,128)(2,1)S(1)} %get-tuple-element.36), channel_id=1, source_target_pairs={{0,3},{1,0},{2,1},{3,2},{4,7},{5,4},{6,5},{7,6},{8,11},{9,8},{10,9... | collective-permute-start | bytes 196616 | tf_op jit(solution)/shard_map/ppermute | solution.py:43

commit v13 on v12

--- a/solution.py
+++ b/solution.py
@@ -182,21 +182,7 @@
     return acc
 
 
-def near_kernel(ladder_ints, *refs):
-    far = far_pieces(list(refs[4:7]) + [None, None])
-    for which, pieces in enumerate(near_pieces(refs[:4])):
-        refs[7][:, which * LANES : (which + 1) * LANES] = ladder_part(
-            which, pieces + far[which][:3], ladder_ints, None
-        )
-
-
-def main_kernel(ladder_ints, near, before, inner, after, swap, *refs):
-    total, same_ref, other_ref, *late_refs, ints, lanes_buf = refs[9:]
-    far = far_pieces(refs[4:9])
-    for w, pieces in enumerate(near_pieces(refs[:4])):
-        for source, ref, first in pieces + far[w]:
-            ints[source, w * 80 : (w + 1) * 80, :] = ref[first + PAIRS : first + HALF, :].astype(F32)
-
+def near_kernel(ladder_ints, before, inner, after, *refs):
     def rows_of(j):
         if j < REACH:
             return before[j]
@@ -204,12 +190,25 @@
             return inner[j - REACH]
         return after[j - REACH - 16]
 
-    laid = []
     for j in range(16 + 2 * REACH):
         block = rows_of(j)
-        laid.append(
-            jnp.concatenate([block[:, a * TILE : (a + 1) * TILE] for a in range(ROWS)], axis=0)
+        refs[8][j] = jnp.concatenate(
+            [block[:, a * TILE : (a + 1) * TILE] for a in range(ROWS)], axis=0
         )
+    far = far_pieces(list(refs[4:7]) + [None, None])
+    for which, pieces in enumerate(near_pieces(refs[:4])):
+        refs[7][:, which * LANES : (which + 1) * LANES] = ladder_part(
+            which, pieces + far[which][:3], ladder_ints, None
+        )
+
+
+def main_kernel(ladder_ints, near, laid, swap, *refs):
+    total, same_ref, other_ref, *late_refs, ints, lanes_buf = refs[9:]
+    far = far_pieces(refs[4:9])
+    for w, pieces in enumerate(near_pieces(refs[:4])):
+        for source, ref, first in pieces + far[w]:
+            ints[source, w * 80 : (w + 1) * 80, :] = ref[first + PAIRS : first + HALF, :].astype(F32)
+
     low = lax.broadcasted_iota(jnp.int32, (8, 128), 1) < TILE
     for j in range(16):
         left = jnp.concatenate([laid[j + o] for o in range(BAND)], axis=1)
@@ -350,19 +349,25 @@
     swap = call(
         swap_kernel, [HBM], shape((1024, 1024), BF), VMEM, [], 8, 2 * 10**10
     )(near[1])
-    begun = call(
-        near_kernel, [VMEM] * 8, shape((PAIRS, 1024), F32), VMEM, [], 8, 10**9
-    )(ladder_ints, *near, *far[:3])
+    begun, laid = call(
+        near_kernel,
+        [VMEM] * 11,
+        [shape((PAIRS, 1024), F32), shape((16 + 2 * REACH, PAIRS, TILE), BF)],
+        [VMEM] * 2,
+        [],
+        8,
+        10**9,
+    )(ladder_ints, before, inner, after, *near, *far[:3])
     four, two = shape((4, 128, 128), BF), shape((2, 128, 128), BF)
     total, same, other, late_0, late_1, late_2, late_3 = call(
         main_kernel,
-        [VMEM] * 15,
+        [VMEM] * 13,
         [shape((PAIRS, 2048), F32), four, four, two, two, two, two],
         [VMEM] * 7,
         [pltpu.VMEM((8, 160, LANES), F32), pltpu.VMEM((256, 1024), BF)],
         12,
         2 * 10**9,
-    )(ladder_ints, begun, before, inner, after, swap, *near, *far)
+    )(ladder_ints, begun, laid, swap, *near, *far)
     same, other = to_transposed(same, 0, 0), to_transposed(other, 0, 1)
     late = [along_y(block, dy) for dy, block in ((1, late_1), (2, late_2), (3, late_3))]
     joined = call(join_kernel, [VMEM] * 4, [four] * 2, [VMEM] * 2, [], 4, 10**7)(late_0, *late)

time: 78.8 us -> 78.6 us (level)
  no operation moved by 1% of the time
where the time goes in v13:
time: 78.6 us; the launch traced here: 78.4 us
  starting transfers between devices  44.3 us (56%)
  waiting for transfers between devices  20.9 us (27%)
  Pallas kernels  11.7 us (15%)
    ppermute x4, starting transfers between devices, to_transposed(): return lax.ppermute(block, ('pi', 'pj', 'vert'), pair_moves(k, dx))  17.7 us
    ppermute x6, starting transfers between devices, along_y(): lax.ppermute(block, 'vert', vert_moves(lambda h, y: h * 4 + (y + dy) % 4))  7.41 us
    ppermute x1, waiting for transfers between devices, gather(): down_2 = lax.ppermute(to_down, 'vert', DOWN)  5.52 us
    ppermute x4, waiting for transfers between devices, to_transposed(): return lax.ppermute(block, ('pi', 'pj', 'vert'), pair_moves(k, dx))  4.51 us
    ppermute x6, waiting for transfers between devices, along_y(): lax.ppermute(block, 'vert', vert_moves(lambda h, y: h * 4 + (y + dy) % 4))  3.8 us
    ppermute x1, starting transfers between devices, gather(): down_3 = lax.ppermute(down_2[:HALF], 'vert', DOWN)  3.77 us
    ppermute x1, starting transfers between devices, body(): after = lax.ppermute(first, 'pj', [(q + 1, q) for q in range(3)])  3.64 us
    pallas_call x1, Pallas kernels, body(): call(finish_kernel, [SMEM, SMEM, SMEM] + [VMEM] * 9, shape((8, 16, 8, LAN...  3.28 us
  transfers between devices with their start and end apart: 20, of which 10 were waited for; matrix products, arithmetic and copies ran while one was open for 1% of the time, Pallas kernels for 4%

profile of v13, /device:TPU:6, one launch (start us, length us, event | category | flops | bytes accessed | tf_op | source)
XLA Modules:
  0.0 78.4 jit_solution(796000540800080577)
XLA Ops:
  0.0 3.1 %shard_map.73 = (bf16[416,512]{1,0:T(8,128)(2,1)}, bf16[16,16,512]{2,1,0:T(8,128)(2,1)}, bf16[2,16,512]{2,1,0:T(8,128)(2,1)}, bf16[2,16,512]{2,1,0:T(8,128)(2,1)}) custom-call(s32[2,2]{1,0:T(2,128)} %ladder_tiles.1, s32[2,2]{1,0:T(2,128)} %cycle_tiles.1, bf16[1024,512]{1,0:T(8,128)(2,1)} %bitcast.4, bf16[80,2,512]{2,1,0:T(2,128)(2,1)} %bitcast.5), custom_call_target="tpu_custom_call" | custom-call | flops 1000000000 | bytes 4194304 | tf_op jit(solution)/shard_map/pallas_call | solution.py:329
  3.2 1.5 %collective-permute-start.4 = (bf16[416,512]{1,0:T(8,128)(2,1)}, bf16[416,512]{1,0:T(8,128)(2,1)S(1)}, u32[]{:S(2)}, u32[]{:S(2)}) collective-permute-start(bf16[416,512]{1,0:T(8,128)(2,1)} %get-tuple-element.29.refs_0_), channel_id=1, source_target_pairs={{0,4},{1,5},{2,6},{3,7},{4,0},{5,1},{6,2},{7,3},{8,12},{9,13},{10,... | collective-permute-start | bytes 1277960 | tf_op jit(solution)/shard_map/ppermute | solution.py:308
  4.6 1.6 %collective-permute-start.3 = (bf16[416,512]{1,0:T(8,128)(2,1)}, bf16[416,512]{1,0:T(8,128)(2,1)S(1)}, u32[]{:S(2)}, u32[]{:S(2)}) collective-permute-start(bf16[416,512]{1,0:T(8,128)(2,1)} %get-tuple-element.29.refs_0_), channel_id=1, source_target_pairs={{0,1},{1,2},{2,3},{3,0},{4,5},{5,6},{6,7},{7,4},{8,9},{9,10},{10,1... | collective-permute-start | bytes 1277960 | tf_op jit(solution)/shard_map/ppermute | solution.py:307
  6.2 1.7 %collective-permute-start.2 = (bf16[416,512]{1,0:T(8,128)(2,1)}, bf16[416,512]{1,0:T(8,128)(2,1)S(1)}, u32[]{:S(2)}, u32[]{:S(2)}) collective-permute-start(bf16[416,512]{1,0:T(8,128)(2,1)} %get-tuple-element.29.refs_0_), channel_id=1, source_target_pairs={{0,3},{1,0},{2,1},{3,2},{4,7},{5,4},{6,5},{7,6},{8,11},{9,8},{10,9... | collective-permute-start | bytes 1277960 | tf_op jit(solution)/shard_map/ppermute | solution.py:306
  7.9 1.9 %collective-permute-start = (bf16[2,16,512]{2,1,0:T(8,128)(2,1)}, bf16[2,16,512]{2,1,0:T(8,128)(2,1)S(1)}, u32[]{:S(2)}, u32[]{:S(2)}) collective-permute-start(bf16[2,16,512]{2,1,0:T(8,128)(2,1)} %get-tuple-element.26), channel_id=1, source_target_pairs={{0,8},{8,16},{16,24},{1,9},{9,17},{17,25},{2,10},{10,18},{18,26},{... | collective-permute-start | bytes 98312 | tf_op jit(solution)/shard_map/ppermute | solution.py:346
  9.8 3.6 %collective-permute-start.1 = (bf16[2,16,512]{2,1,0:T(8,128)(2,1)}, bf16[2,16,512]{2,1,0:T(8,128)(2,1)S(1)}, u32[]{:S(2)}, u32[]{:S(2)}) collective-permute-start(bf16[2,16,512]{2,1,0:T(8,128)(2,1)} %get-tuple-element.28), channel_id=1, source_target_pairs={{8,0},{16,8},{24,16},{9,1},{17,9},{25,17},{10,2},{18,10},{26,18},{... | collective-permute-start | bytes 98312 | tf_op jit(solution)/shard_map/ppermute | solution.py:347
  13.7 1.6 %collective-permute-done.1.after = bf16[2,16,512]{2,1,0:T(8,128)(2,1)S(1)} collective-permute-done((bf16[2,16,512]{2,1,0:T(8,128)(2,1)}, bf16[2,16,512]{2,1,0:T(8,128)(2,1)S(1)}, u32[]{:S(2)}, u32[]{:S(2)}) %collective-permute-start.1) | collective-permute-done | bytes 32800 | tf_op jit(solution)/shard_map/ppermute | solution.py:347
  15.3 1.2 %collective-permute-done.4.flip.refs_3_ = bf16[416,512]{1,0:T(8,128)(2,1)S(1)} collective-permute-done((bf16[416,512]{1,0:T(8,128)(2,1)}, bf16[416,512]{1,0:T(8,128)(2,1)S(1)}, u32[]{:S(2)}, u32[]{:S(2)}) %collective-permute-start.4) | collective-permute-done | bytes 426016 | tf_op jit(solution)/shard_map/ppermute | solution.py:308
  16.5 0.9 %collective-permute-done.3.up.refs_2_ = bf16[416,512]{1,0:T(8,128)(2,1)S(1)} collective-permute-done((bf16[416,512]{1,0:T(8,128)(2,1)}, bf16[416,512]{1,0:T(8,128)(2,1)S(1)}, u32[]{:S(2)}, u32[]{:S(2)}) %collective-permute-start.3) | collective-permute-done | bytes 426016 | tf_op jit(solution)/shard_map/ppermute | solution.py:307
  17.5 3.0 %collective-permute-start.6 = (bf16[416,512]{1,0:T(8,128)(2,1)S(1)}, bf16[416,512]{1,0:T(8,128)(2,1)S(1)}, u32[]{:S(2)}, u32[]{:S(2)}) collective-permute-start(bf16[416,512]{1,0:T(8,128)(2,1)S(1)} %get-tuple-element.31), channel_id=1, source_target_pairs={{0,3},{1,0},{2,1},{3,2},{4,7},{5,4},{6,5},{7,6},{8,11},{9,8},{10,9... | collective-permute-start | bytes 1277960 | tf_op jit(solution)/shard_map/ppermute | solution.py:321
  20.5 2.1 %collective-permute-start.7 = (bf16[416,512]{1,0:T(8,128)(2,1)S(1)}, bf16[416,512]{1,0:T(8,128)(2,1)S(1)}, u32[]{:S(2)}, u32[]{:S(2)}) collective-permute-start(bf16[416,512]{1,0:T(8,128)(2,1)S(1)} %get-tuple-element.32), channel_id=1, source_target_pairs={{0,4},{1,5},{2,6},{3,7},{4,0},{5,1},{6,2},{7,3},{8,12},{9,13},{10,... | collective-permute-start | bytes 1277960 | tf_op jit(solution)/shard_map/ppermute | solution.py:319
  22.7 5.5 %collective-permute-done.6.refs_5_ = bf16[416,512]{1,0:T(8,128)(2,1)S(1)} collective-permute-done((bf16[416,512]{1,0:T(8,128)(2,1)S(1)}, bf16[416,512]{1,0:T(8,128)(2,1)S(1)}, u32[]{:S(2)}, u32[]{:S(2)}) %collective-permute-start.6) | collective-permute-done | bytes 426016 | tf_op jit(solution)/shard_map/ppermute | solution.py:321
  28.2 3.8 %collective-permute-start.9 = (bf16[208,512]{1,0:T(8,128)(2,1)S(1)}, bf16[208,512]{1,0:T(8,128)(2,1)S(1)}, u32[]{:S(2)}, u32[]{:S(2)}) collective-permute-start(bf16[208,512]{1,0:T(8,128)(2,1)S(1)} %slice.9), channel_id=1, source_target_pairs={{0,3},{1,0},{2,1},{3,2},{4,7},{5,4},{6,5},{7,6},{8,11},{9,8},{10,9... | collective-permute-start | bytes 638984 | tf_op jit(solution)/shard_map/ppermute | solution.py:323
  32.1 0.8 %shard_map.76.swap = bf16[1024,1024]{1,0:T(8,128)(2,1)S(1)} custom-call(bf16[416,512]{1,0:T(8,128)(2,1)S(1)} %collective-permute-done.2.down.refs_1_.after), custom_call_target="tpu_custom_call" | custom-call | flops 20000000000 | bytes 4194304 | tf_op jit(solution)/shard_map/pallas_call | solution.py:349
  32.9 0.7 collective-permute-done.5.refs_4_
  33.7 0.5 slice-done.1
  34.3 2.5 %shard_map.75 = (f32[128,1024]{1,0:T(8,128)S(1)}, bf16[20,128,64]{2,1,0:T(8,128)(2,1)S(1)}) custom-call(bf16[2,512,4096]{2,1,0:T(8,128)(2,1)S(1)} %bitcast.3, bf16[2,16,512]{2,1,0:T(8,128)(2,1)S(1)} %collective-permute-done.before, bf16[16,16,512]{2,1,0:T(8,128)(2,1)S(1)} %copy-done.1, bf16[2,16,512]{2,1,0:T(8,128)(2,1)S(1)} %collective-permute-done.1.after, ...), custom_call_target="tpu_custom_call" | custom-call | flops 1000000000 | bytes 4194304 | tf_op jit(solution)/shard_map/pallas_call | solution.py:352
  36.8 2.3 %collective-permute-done.8.refs_7_ = bf16[208,512]{1,0:T(8,128)(2,1)S(1)} collective-permute-done((bf16[208,512]{1,0:T(8,128)(2,1)S(1)}, bf16[208,512]{1,0:T(8,128)(2,1)S(1)}, u32[]{:S(2)}, u32[]{:S(2)}) %collective-permute-start.8) | collective-permute-done | bytes 213024 | tf_op jit(solution)/shard_map/ppermute | solution.py:322
  39.2 1.8 %shard_map.77 = (f32[128,2048]{1,0:T(8,128)S(1)}, bf16[4,128,128]{2,1,0:T(8,128)(2,1)S(1)}, bf16[4,128,128]{2,1,0:T(8,128)(2,1)S(1)}, bf16[2,128,128]{2,1,0:T(8,...) custom-call(bf16[2,512,4096]{2,1,0:T(8,128)(2,1)S(1)} %bitcast.3, ...), custom_call_target="tpu_custom_call" | custom-call | flops 2000000000 | bytes 4194304 | tf_op jit(solution)/shard_map/pallas_call | solution.py:362
  41.0 9.8 %collective-permute-start.10 = (bf16[4,128,128]{2,1,0:T(8,128)(2,1)S(1)}, bf16[4,128,128]{2,1,0:T(8,128)(2,1)S(1)}, u32[]{:S(2)}, u32[]{:S(2)}) collective-permute-start(bf16[4,128,128]{2,1,0:T(8,128)(2,1)S(1)} %get-tuple-element.36), channel_id=1, source_target_pairs={{0,0},{1,1},{2,2},{3,3},{4,4},{5,5},{6,6},{7,7},{8,64},{9,65},{10,... | collective-permute-start | bytes 393224 | tf_op jit(solution)/shard_map/ppermute | solution.py:39
  50.8 1.1 %collective-permute-start.11 = (bf16[4,128,128]{2,1,0:T(8,128)(2,1)S(1)}, bf16[4,128,128]{2,1,0:T(8,128)(2,1)S(1)}, u32[]{:S(2)}, u32[]{:S(2)}) collective-permute-start(bf16[4,128,128]{2,1,0:T(8,128)(2,1)S(1)} %get-tuple-element.37), channel_id=1, source_target_pairs={{0,4},{1,5},{2,6},{3,7},{4,0},{5,1},{6,2},{7,3},{8,68},{9,69},{10,... | collective-permute-start | bytes 393224 | tf_op jit(solution)/shard_map/ppermute | solution.py:39
  51.9 1.3 %collective-permute-start.16 = (bf16[2,128,128]{2,1,0:T(8,128)(2,1)S(1)}, bf16[2,128,128]{2,1,0:T(8,128)(2,1)S(1)}, u32[]{:S(2)}, u32[]{:S(2)}) collective-permute-start(bf16[2,128,128]{2,1,0:T(8,128)(2,1)S(1)} %get-tuple-element.43), channel_id=1, source_target_pairs={{0,2},{1,3},{2,0},{3,1},{4,6},{5,7},{6,4},{7,5},{8,10},{9,11},{10,... | collective-permute-start | bytes 196616 | tf_op jit(solution)/shard_map/ppermute | solution.py:43
  53.3 1.9 %collective-permute-start.17 = (bf16[2,128,128]{2,1,0:T(8,128)(2,1)S(1)}, bf16[2,128,128]{2,1,0:T(8,128)(2,1)S(1)}, u32[]{:S(2)}, u32[]{:S(2)}) collective-permute-start(bf16[2,128,128]{2,1,0:T(8,128)(2,1)S(1)} %get-tuple-element.44), channel_id=1, source_target_pairs={{0,3},{1,0},{2,1},{3,2},{4,7},{5,4},{6,5},{7,6},{8,11},{9,8},{10,9... | collective-permute-start | bytes 196616 | tf_op jit(solution)/shard_map/ppermute | solution.py:43
  55.1 2.9 %collective-permute-done.15.first = bf16[2,128,128]{2,1,0:T(8,128)(2,1)S(1)} collective-permute-done((bf16[2,128,128]{2,1,0:T(8,128)(2,1)S(1)}, bf16[2,128,128]{2,1,0:T(8,128)(2,1)S(1)}, u32[]{:S(2)}, u32[]{:S(2)}) %collective-permute-start.15) | collective-permute-done | bytes 65568 | tf_op jit(solution)/shard_map/ppermute | solution.py:43
  58.1 0.9 %collective-permute-done.17.third = bf16[2,128,128]{2,1,0:T(8,128)(2,1)S(1)} collective-permute-done((bf16[2,128,128]{2,1,0:T(8,128)(2,1)S(1)}, bf16[2,128,128]{2,1,0:T(8,128)(2,1)S(1)}, u32[]{:S(2)}, u32[]{:S(2)}) %collective-permute-start.17) | collective-permute-done | bytes 65568 | tf_op jit(solution)/shard_map/ppermute | solution.py:43
  59.0 5.9 %collective-permute-start.18 = (bf16[4,128,128]{2,1,0:T(8,128)(2,1)S(1)}, bf16[4,128,128]{2,1,0:T(8,128)(2,1)S(1)}, u32[]{:S(2)}, u32[]{:S(2)}) collective-permute-start(bf16[4,128,128]{2,1,0:T(8,128)(2,1)S(1)} %get-tuple-element.45), channel_id=1, source_target_pairs={{0,32},{1,33},{2,34},{3,35},{4,36},{5,37},{6,38},{7,39},{8,96},{9,... | collective-permute-start | bytes 393224 | tf_op jit(solution)/shard_map/ppermute | solution.py:39
  64.8 1.0 %collective-permute-start.19 = (bf16[4,128,128]{2,1,0:T(8,128)(2,1)S(1)}, bf16[4,128,128]{2,1,0:T(8,128)(2,1)S(1)}, u32[]{:S(2)}, u32[]{:S(2)}) collective-permute-start(bf16[4,128,128]{2,1,0:T(8,128)(2,1)S(1)} %get-tuple-element.46), channel_id=1, source_target_pairs={{0,36},{1,37},{2,38},{3,39},{4,32},{5,33},{6,34},{7,35},{8,100},{9... | collective-permute-start | bytes 393224 | tf_op jit(solution)/shard_map/ppermute | solution.py:39
  65.8 1.4 %collective-permute-start.12 = (bf16[2,128,128]{2,1,0:T(8,128)(2,1)S(1)}, bf16[2,128,128]{2,1,0:T(8,128)(2,1)S(1)}, u32[]{:S(2)}, u32[]{:S(2)}) collective-permute-start(bf16[2,128,128]{2,1,0:T(8,128)(2,1)S(1)} %get-tuple-element.38), channel_id=1, source_target_pairs={{0,1},{1,2},{2,3},{3,0},{4,5},{5,6},{6,7},{7,4},{8,9},{9,10},{10,1... | collective-permute-start | bytes 196616 | tf_op jit(solution)/shard_map/ppermute | solution.py:43
  67.2 2.5 %collective-permute-start.13 = (bf16[2,128,128]{2,1,0:T(8,128)(2,1)S(1)}, bf16[2,128,128]{2,1,0:T(8,128)(2,1)S(1)}, u32[]{:S(2)}, u32[]{:S(2)}) collective-permute-start(bf16[2,128,128]{2,1,0:T(8,128)(2,1)S(1)} %get-tuple-element.39), channel_id=1, source_target_pairs={{0,2},{1,3},{2,0},{3,1},{4,6},{5,7},{6,4},{7,5},{8,10},{9,11},{10,... | collective-permute-start | bytes 196616 | tf_op jit(solution)/shard_map/ppermute | solution.py:43
  70.0 0.4 fusion.place
  70.4 4.5 %collective-permute-done.19.refs_6_ = bf16[4,128,128]{2,1,0:T(8,128)(2,1)S(1)} collective-permute-done((bf16[4,128,128]{2,1,0:T(8,128)(2,1)S(1)}, bf16[4,128,128]{2,1,0:T(8,128)(2,1)S(1)}, u32[]{:S(2)}, u32[]{:S(2)}) %collective-permute-start.19) | collective-permute-done | bytes 131104 | tf_op jit(solution)/shard_map/ppermute | solution.py:39
  74.9 3.3 %shard_map.80 = f32[8,16,8,512]{3,2,1,0:T(8,128)} custom-call(s32[2,2]{1,0:T(2,128)S(1)} %copy-done.2, s32[2,2]{1,0:T(2,128)S(1)} %copy-done.3, s32[8]{0:T(128)S(1)} %copy-done.4, f32[128,2048]{1,0:T(8,128)S(1)} %get-tuple-element.35.total, bf16[1024,1024]{1,0:T(8,128)(2,1)S(1)} %fusion.place, bf16[4,128,128]{2,1,0:T(8,128)(2,1)S(1)} %collective-permute-done.10.same.refs_0_, ...), custom_call_target="tpu_custom_call" | custom-call | flops 1000000000 | bytes 4194304 | tf_op jit(solution)/shard_map/pallas_call | solution.py:377
  (36 shorter events, 1.0 us)
Async XLA Ops:
  3.2 13.4 %collective-permute-start.4 = (bf16[416,512]{1,0:T(8,128)(2,1)}, bf16[416,512]{1,0:T(8,128)(2,1)S(1)}, u32[]{:S(2)}, u32[]{:S(2)}) collective-permute-start(bf16[416,512]{1,0:T(8,128)(2,1)} %get-tuple-element.29.refs_0_), channel_id=1, source_target_pairs={{0,4},{1,5},{2,6},{3,7},{4,0},{5,1},{6,2},{7,3},{8,12},{9,13},{10,... | collective-permute-start | bytes 1277960 | tf_op jit(solution)/shard_map/ppermute | solution.py:308
  4.6 12.8 %collective-permute-start.3 = (bf16[416,512]{1,0:T(8,128)(2,1)}, bf16[416,512]{1,0:T(8,128)(2,1)S(1)}, u32[]{:S(2)}, u32[]{:S(2)}) collective-permute-start(bf16[416,512]{1,0:T(8,128)(2,1)} %get-tuple-element.29.refs_0_), channel_id=1, source_target_pairs={{0,1},{1,2},{2,3},{3,0},{4,5},{5,6},{6,7},{7,4},{8,9},{9,10},{10,1... | collective-permute-start | bytes 1277960 | tf_op jit(solution)/shard_map/ppermute | solution.py:307
  6.2 11.2 %collective-permute-start.2 = (bf16[416,512]{1,0:T(8,128)(2,1)}, bf16[416,512]{1,0:T(8,128)(2,1)S(1)}, u32[]{:S(2)}, u32[]{:S(2)}) collective-permute-start(bf16[416,512]{1,0:T(8,128)(2,1)} %get-tuple-element.29.refs_0_), channel_id=1, source_target_pairs={{0,3},{1,0},{2,1},{3,2},{4,7},{5,4},{6,5},{7,6},{8,11},{9,8},{10,9... | collective-permute-start | bytes 1277960 | tf_op jit(solution)/shard_map/ppermute | solution.py:306
  7.9 5.8 %collective-permute-start = (bf16[2,16,512]{2,1,0:T(8,128)(2,1)}, bf16[2,16,512]{2,1,0:T(8,128)(2,1)S(1)}, u32[]{:S(2)}, u32[]{:S(2)}) collective-permute-start(bf16[2,16,512]{2,1,0:T(8,128)(2,1)} %get-tuple-element.26), channel_id=1, source_target_pairs={{0,8},{8,16},{16,24},{1,9},{9,17},{17,25},{2,10},{10,18},{18,26},{... | collective-permute-start | bytes 98312 | tf_op jit(solution)/shard_map/ppermute | solution.py:346
  9.8 5.5 %collective-permute-start.1 = (bf16[2,16,512]{2,1,0:T(8,128)(2,1)}, bf16[2,16,512]{2,1,0:T(8,128)(2,1)S(1)}, u32[]{:S(2)}, u32[]{:S(2)}) collective-permute-start(bf16[2,16,512]{2,1,0:T(8,128)(2,1)} %get-tuple-element.28), channel_id=1, source_target_pairs={{8,0},{16,8},{24,16},{9,1},{17,9},{25,17},{10,2},{18,10},{26,18},{... | collective-permute-start | bytes 98312 | tf_op jit(solution)/shard_map/ppermute | solution.py:347
  17.5 10.6 %collective-permute-start.6 = (bf16[416,512]{1,0:T(8,128)(2,1)S(1)}, bf16[416,512]{1,0:T(8,128)(2,1)S(1)}, u32[]{:S(2)}, u32[]{:S(2)}) collective-permute-start(bf16[416,512]{1,0:T(8,128)(2,1)S(1)} %get-tuple-element.31), channel_id=1, source_target_pairs={{0,3},{1,0},{2,1},{3,2},{4,7},{5,4},{6,5},{7,6},{8,11},{9,8},{10,9... | collective-permute-start | bytes 1277960 | tf_op jit(solution)/shard_map/ppermute | solution.py:321
  20.5 11.4 %collective-permute-start.7 = (bf16[416,512]{1,0:T(8,128)(2,1)S(1)}, bf16[416,512]{1,0:T(8,128)(2,1)S(1)}, u32[]{:S(2)}, u32[]{:S(2)}) collective-permute-start(bf16[416,512]{1,0:T(8,128)(2,1)S(1)} %get-tuple-element.32), channel_id=1, source_target_pairs={{0,4},{1,5},{2,6},{3,7},{4,0},{5,1},{6,2},{7,3},{8,12},{9,13},{10,... | collective-permute-start | bytes 1277960 | tf_op jit(solution)/shard_map/ppermute | solution.py:319
  22.7 11.0 %collective-permute-start.5 = (bf16[416,512]{1,0:T(8,128)(2,1)S(1)}, bf16[416,512]{1,0:T(8,128)(2,1)S(1)}, u32[]{:S(2)}, u32[]{:S(2)}) collective-permute-start(bf16[416,512]{1,0:T(8,128)(2,1)S(1)} %get-tuple-element.30), channel_id=1, source_target_pairs={{0,1},{1,2},{2,3},{3,0},{4,5},{5,6},{6,7},{7,4},{8,9},{9,10},{10,1... | collective-permute-start | bytes 1277960 | tf_op jit(solution)/shard_map/ppermute | solution.py:320
  28.2 5.5 %slice-start = ((s8[8388608]{0:T(1024)(128)(4,1)}), s8[4194304]{0:T(1024)(128)(4,1)S(1)}, s32[]{:S(2)}) async-start(s8[8388608]{0:T(1024)(128)(4,1)} %bitcast.2), calls=%async_computation | async-start | bytes 8388608
  28.2 8.6 %collective-permute-start.9 = (bf16[208,512]{1,0:T(8,128)(2,1)S(1)}, bf16[208,512]{1,0:T(8,128)(2,1)S(1)}, u32[]{:S(2)}, u32[]{:S(2)}) collective-permute-start(bf16[208,512]{1,0:T(8,128)(2,1)S(1)} %slice.9), channel_id=1, source_target_pairs={{0,3},{1,0},{2,1},{3,2},{4,7},{5,4},{6,5},{7,6},{8,11},{9,8},{10,9... | collective-permute-start | bytes 638984 | tf_op jit(solution)/shard_map/ppermute | solution.py:323
  32.0 2.2 %slice-start.1 = ((s8[8388608]{0:T(1024)(128)(4,1)}), s8[4194304]{0:T(1024)(128)(4,1)S(1)}, s32[]{:S(2)}) async-start(s8[8388608]{0:T(1024)(128)(4,1)} %bitcast.2), calls=%async_computation.1 | async-start | bytes 8388608
  32.0 2.3 %copy-start = (bf16[416,512]{1,0:T(8,128)(2,1)S(1)}, bf16[416,512]{1,0:T(8,128)(2,1)}, u32[]{:S(2)}) copy-start(bf16[416,512]{1,0:T(8,128)(2,1)} %get-tuple-element.29.refs_0_) | copy-start | bytes 1277956
  32.0 2.3 %copy-start.1 = (bf16[16,16,512]{2,1,0:T(8,128)(2,1)S(1)}, bf16[16,16,512]{2,1,0:T(8,128)(2,1)}, u32[]{:S(2)}) copy-start(bf16[16,16,512]{2,1,0:T(8,128)(2,1)} %get-tuple-element.27.inner) | copy-start | bytes 786436
  32.0 7.1 %collective-permute-start.8 = (bf16[208,512]{1,0:T(8,128)(2,1)S(1)}, bf16[208,512]{1,0:T(8,128)(2,1)S(1)}, u32[]{:S(2)}, u32[]{:S(2)}) collective-permute-start(bf16[208,512]{1,0:T(8,128)(2,1)S(1)} %slice.8), channel_id=1, source_target_pairs={{0,1},{1,2},{2,3},{3,0},{4,5},{5,6},{6,7},{7,4},{8,9},{9,10},{10,1... | collective-permute-start | bytes 638984 | tf_op jit(solution)/shard_map/ppermute | solution.py:322
  39.2 30.8 %copy-start.5 = (s32[1024]{0:T(1024)S(1)}, s32[1024]{0:T(1024)}, u32[]{:S(2)}) copy-start(s32[1024]{0:T(1024)} %constant.2.clone) | copy-start | bytes 12292
  41.0 33.9 %copy-start.2 = (s32[2,2]{1,0:T(2,128)S(1)}, s32[2,2]{1,0:T(2,128)}, u32[]{:S(2)}) copy-start(s32[2,2]{1,0:T(2,128)} %ladder_tiles.1) | copy-start | bytes 52
  41.0 33.9 %copy-start.3 = (s32[2,2]{1,0:T(2,128)S(1)}, s32[2,2]{1,0:T(2,128)}, u32[]{:S(2)}) copy-start(s32[2,2]{1,0:T(2,128)} %cycle_tiles.1) | copy-start | bytes 52
  41.0 33.9 %copy-start.4 = (s32[8]{0:T(128)S(1)}, s32[8]{0:T(128)}, u32[]{:S(2)}) copy-start(s32[8]{0:T(128)} %partner.1) | copy-start | bytes 100
  41.0 24.8 %collective-permute-start.10 = (bf16[4,128,128]{2,1,0:T(8,128)(2,1)S(1)}, bf16[4,128,128]{2,1,0:T(8,128)(2,1)S(1)}, u32[]{:S(2)}, u32[]{:S(2)}) collective-permute-start(bf16[4,128,128]{2,1,0:T(8,128)(2,1)S(1)} %get-tuple-element.36), channel_id=1, source_target_pairs={{0,0},{1,1},{2,2},{3,3},{4,4},{5,5},{6,6},{7,7},{8,64},{9,65},{10,... | collective-permute-start | bytes 393224 | tf_op jit(solution)/shard_map/ppermute | solution.py:39
  50.8 14.9 %collective-permute-start.11 = (bf16[4,128,128]{2,1,0:T(8,128)(2,1)S(1)}, bf16[4,128,128]{2,1,0:T(8,128)(2,1)S(1)}, u32[]{:S(2)}, u32[]{:S(2)}) collective-permute-start(bf16[4,128,128]{2,1,0:T(8,128)(2,1)S(1)} %get-tuple-element.37), channel_id=1, source_target_pairs={{0,4},{1,5},{2,6},{3,7},{4,0},{5,1},{6,2},{7,3},{8,68},{9,69},{10,... | collective-permute-start | bytes 393224 | tf_op jit(solution)/shard_map/ppermute | solution.py:39
  51.9 6.2 %collective-permute-start.15 = (bf16[2,128,128]{2,1,0:T(8,128)(2,1)S(1)}, bf16[2,128,128]{2,1,0:T(8,128)(2,1)S(1)}, u32[]{:S(2)}, u32[]{:S(2)}) collective-permute-start(bf16[2,128,128]{2,1,0:T(8,128)(2,1)S(1)} %get-tuple-element.42), channel_id=1, source_target_pairs={{0,1},{1,2},{2,3},{3,0},{4,5},{5,6},{6,7},{7,4},{8,9},{9,10},{10,1... | collective-permute-start | bytes 196616 | tf_op jit(solution)/shard_map/ppermute | solution.py:43
  51.9 6.2 %collective-permute-start.16 = (bf16[2,128,128]{2,1,0:T(8,128)(2,1)S(1)}, bf16[2,128,128]{2,1,0:T(8,128)(2,1)S(1)}, u32[]{:S(2)}, u32[]{:S(2)}) collective-permute-start(bf16[2,128,128]{2,1,0:T(8,128)(2,1)S(1)} %get-tuple-element.43), channel_id=1, source_target_pairs={{0,2},{1,3},{2,0},{3,1},{4,6},{5,7},{6,4},{7,5},{8,10},{9,11},{10,... | collective-permute-start | bytes 196616 | tf_op jit(solution)/shard_map/ppermute | solution.py:43
  53.3 5.7 %collective-permute-start.17 = (bf16[2,128,128]{2,1,0:T(8,128)(2,1)S(1)}, bf16[2,128,128]{2,1,0:T(8,128)(2,1)S(1)}, u32[]{:S(2)}, u32[]{:S(2)}) collective-permute-start(bf16[2,128,128]{2,1,0:T(8,128)(2,1)S(1)} %get-tuple-element.44), channel_id=1, source_target_pairs={{0,3},{1,0},{2,1},{3,2},{4,7},{5,4},{6,5},{7,6},{8,11},{9,8},{10,9... | collective-permute-start | bytes 196616 | tf_op jit(solution)/shard_map/ppermute | solution.py:43
  59.0 11.4 %collective-permute-start.18 = (bf16[4,128,128]{2,1,0:T(8,128)(2,1)S(1)}, bf16[4,128,128]{2,1,0:T(8,128)(2,1)S(1)}, u32[]{:S(2)}, u32[]{:S(2)}) collective-permute-start(bf16[4,128,128]{2,1,0:T(8,128)(2,1)S(1)} %get-tuple-element.45), channel_id=1, source_target_pairs={{0,32},{1,33},{2,34},{3,35},{4,36},{5,37},{6,38},{7,39},{8,96},{9,... | collective-permute-start | bytes 393224 | tf_op jit(solution)/shard_map/ppermute | solution.py:39
  64.8 10.1 %collective-permute-start.19 = (bf16[4,128,128]{2,1,0:T(8,128)(2,1)S(1)}, bf16[4,128,128]{2,1,0:T(8,128)(2,1)S(1)}, u32[]{:S(2)}, u32[]{:S(2)}) collective-permute-start(bf16[4,128,128]{2,1,0:T(8,128)(2,1)S(1)} %get-tuple-element.46), channel_id=1, source_target_pairs={{0,36},{1,37},{2,38},{3,39},{4,32},{5,33},{6,34},{7,35},{8,100},{9... | collective-permute-start | bytes 393224 | tf_op jit(solution)/shard_map/ppermute | solution.py:39
  65.8 9.1 %collective-permute-start.12 = (bf16[2,128,128]{2,1,0:T(8,128)(2,1)S(1)}, bf16[2,128,128]{2,1,0:T(8,128)(2,1)S(1)}, u32[]{:S(2)}, u32[]{:S(2)}) collective-permute-start(bf16[2,128,128]{2,1,0:T(8,128)(2,1)S(1)} %get-tuple-element.38), channel_id=1, source_target_pairs={{0,1},{1,2},{2,3},{3,0},{4,5},{5,6},{6,7},{7,4},{8,9},{9,10},{10,1... | collective-permute-start | bytes 196616 | tf_op jit(solution)/shard_map/ppermute | solution.py:43
  67.2 7.7 %collective-permute-start.13 = (bf16[2,128,128]{2,1,0:T(8,128)(2,1)S(1)}, bf16[2,128,128]{2,1,0:T(8,128)(2,1)S(1)}, u32[]{:S(2)}, u32[]{:S(2)}) collective-permute-start(bf16[2,128,128]{2,1,0:T(8,128)(2,1)S(1)} %get-tuple-element.39), channel_id=1, source_target_pairs={{0,2},{1,3},{2,0},{3,1},{4,6},{5,7},{6,4},{7,5},{8,10},{9,11},{10,... | collective-permute-start | bytes 196616 | tf_op jit(solution)/shard_map/ppermute | solution.py:43
  69.7 5.2 %collective-permute-start.14 = (bf16[2,128,128]{2,1,0:T(8,128)(2,1)S(1)}, bf16[2,128,128]{2,1,0:T(8,128)(2,1)S(1)}, u32[]{:S(2)}, u32[]{:S(2)}) collective-permute-start(bf16[2,128,128]{2,1,0:T(8,128)(2,1)S(1)} %get-tuple-element.40), channel_id=1, source_target_pairs={{0,3},{1,0},{2,1},{3,2},{4,7},{5,4},{6,5},{7,6},{8,11},{9,8},{10,9... | collective-permute-start | bytes 196616 | tf_op jit(solution)/shard_map/ppermute | solution.py:43
